TPU v7x, 32 devices: a whole 2x2x4 slice. The times are simulated.
32 devices in a mesh: section: 2 (over core), dp: 4 (over y, x), tensor: 4 (over z).
Axes of the slice: x: 2, y: 2, z: 4, core: 2. Of those that a mesh axis runs over, the one named last changes fastest.
Arguments:
- token_ids: int32 [8, 1024], P('dp'), may hold values from 0 to 32767
- target_ids: int32 [8, 1024], P('dp'), may hold values from 0 to 32767
- lengths: int32 [8], replicated, may hold values from 204 to 1024, as said below
- embedding: bfloat16 [32768, 1024], P('tensor'), may hold values from -0.375 to 0.375
- outer_gain: float32 [2, 1024], P('section'), may hold values from 0.5 to 1.5
- outer_bias: float32 [2, 1024], P('section'), may hold values from -1.2 to 1.2
- norm_gain: float32 [2, 2, 1024], P('section'), may hold values from 0.5 to 1.5
- norm_bias: float32 [2, 2, 1024], P('section'), may hold values from -1.2 to 1.2
- qkv_weight: bfloat16 [2, 3, 1024, 1024], P('section', None, None, 'tensor'), may hold values from -0.1875 to 0.1875
- qv_bias: float32 [2, 2, 1024], P('section', None, 'tensor'), may hold values from -1.8 to 1.8
- out_weight: bfloat16 [2, 1024, 1024], P('section', 'tensor'), may hold values from -0.375 to 0.375
- up_weight: bfloat16 [2, 1024, 4096], P('section', None, 'tensor'), may hold values from -0.1875 to 0.1875
- up_bias: float32 [2, 4096], P('section', 'tensor'), may hold values from -1.8 to 1.8
- down_weight: bfloat16 [2, 4096, 1024], P('section', 'tensor'), may hold values from -0.09375 to 0.09375
- row_bias: float32 [2, 2, 1024], P('section'), may hold values from -1.2 to 1.2
Outputs:
- loss: float32 [], replicated
- grad_embedding: float32 [32768, 1024], P('tensor')
- grad_outer_gain: float32 [2, 1024], P('section')
- grad_outer_bias: float32 [2, 1024], P('section')
- grad_norm_gain: float32 [2, 2, 1024], P('section')
- grad_norm_bias: float32 [2, 2, 1024], P('section')
- grad_qkv_weight: float32 [2, 3, 1024, 1024], P('section', None, None, 'tensor')
- grad_qv_bias: float32 [2, 2, 1024], P('section', None, 'tensor')
- grad_out_weight: float32 [2, 1024, 1024], P('section', 'tensor')
- grad_up_weight: float32 [2, 1024, 4096], P('section', None, 'tensor')
- grad_up_bias: float32 [2, 4096], P('section', 'tensor')
- grad_down_weight: float32 [2, 4096, 1024], P('section', 'tensor')
- grad_row_bias: float32 [2, 2, 1024], P('section')
Inputs may be any that keep to these rules, and one draw needn't show every extreme that they name: `lengths`: in each aligned block of 2 rows (one data group's rows) one row, drawn from the seed, has 1024 tokens.
All inputs are finite; a program needn't handle non-finite values.
Results may differ from a plain program's by a relative error of at most 0.005.
Values may be sent and summed in bfloat16 or wider, within the bound.
A program may use at most 704 MiB of HBM per device.

v0:
```python
import jax
import jax.numpy as jnp
from jax import lax
from jax.sharding import PartitionSpec as P

HEADS = 16
HEAD_DIM = 64


EPS = 1e-05
NEG = -1e30


def from_partner(block, axis, stride):
    count = lax.axis_size(axis)
    route = []
    for low in range(count):
        high = low | 1 << stride
        if high != low and high < count:
            route += [(low, high), (high, low)]
    return lax.ppermute(block, axis, route)


def layer_norm(inputs, weight, offset):
    centre = inputs - jnp.mean(inputs, axis=-1, keepdims=True)
    spread = jnp.mean(centre * centre, axis=-1, keepdims=True)
    return centre * lax.rsqrt(spread + EPS) * weight + offset


def gelu_tanh(inputs):
    return jax.nn.gelu(inputs, approximate=True)


def alibi_slopes(first_head, count_heads):
    number = (first_head + jnp.arange(count_heads) + 1).astype(jnp.float32)
    return jnp.exp2(-8.0 * number / HEADS)


def mask_scores(raw_scores, slopes, length):
    seq_len = raw_scores.shape[-1]
    places = jnp.arange(seq_len)
    distance = (places[:, None] - places[None, :]).astype(jnp.float32)
    scores = raw_scores * HEAD_DIM ** (-0.5) - slopes[:, None, None] * distance[None]
    allowed = (places[None, :] <= places[:, None]) & (places[None, :] < length)
    return jnp.where(allowed[None], scores, NEG)


def to_low(inputs):
    return inputs.astype(jnp.bfloat16)


def matmul(former, latter):
    return jnp.dot(former, latter, preferred_element_type=jnp.float32)


def matmul_t(former, latter):
    return lax.dot_general(
        former, latter, (((1,), (1,)), ((), ())), preferred_element_type=jnp.float32
    )


def outer_sum(former, latter):
    return lax.dot_general(
        former, latter, (((0,), (0,)), ((), ())), preferred_element_type=jnp.float32
    )


def split_heads(inputs):
    return inputs.reshape(inputs.shape[0], inputs.shape[1] // HEAD_DIM, HEAD_DIM)


def whole_rows(part_input):
    return lax.all_gather(part_input, "tensor", axis=0, tiled=True)


def summed_rows(row_term, part_rows):
    return lax.psum_scatter(
        row_term(jnp.int32(0), part_rows * lax.axis_size("tensor")),
        "tensor",
        scatter_dimension=0,
        tiled=True,
    )


def row_window(full_rows):

    def partial_rows(leading_row, row_count):
        return full_rows

    return partial_rows


def sliced_product(full_rows, weight):

    def partial_rows(leading_row, row_count):
        return matmul(full_rows, weight)

    return partial_rows


def sliced_product_t(full_rows, weight):

    def partial_rows(leading_row, row_count):
        return matmul_t(full_rows, weight)

    return partial_rows


def layer_forward(section_in, params, length, slopes):
    (
        norm_gains,
        norm_offsets,
        qkv_mats,
        qv_offsets,
        out_mat,
        up_mat,
        up_offset,
        down_mat,
        row_offsets,
    ) = params
    part_rows = section_in.shape[0]
    normed = to_low(layer_norm(section_in, norm_gains[0], norm_offsets[0]))
    normed_full = whole_rows(normed)
    queries = to_low(matmul(normed_full, qkv_mats[0]) + qv_offsets[0])
    key_rows = to_low(matmul(normed_full, qkv_mats[1]))
    value_rows = to_low(matmul(normed_full, qkv_mats[2]) + qv_offsets[1])
    raw_scores = jnp.einsum(
        "qhd,khd->hqk",
        split_heads(queries),
        split_heads(key_rows),
        preferred_element_type=jnp.float32,
    )
    scores = mask_scores(raw_scores, slopes, length)
    highest = jnp.max(scores, axis=-1, keepdims=True)
    log_total = jnp.log(jnp.sum(jnp.exp(scores - highest), axis=-1, keepdims=True)) + highest
    weights_low = to_low(jnp.exp(scores - log_total))
    attended = jnp.einsum(
        "hqk,khd->qhd", weights_low, split_heads(value_rows), preferred_element_type=jnp.float32
    )
    mixed_rows = to_low(attended.reshape(attended.shape[0], -1))
    middle = (
        section_in + summed_rows(sliced_product(mixed_rows, out_mat), part_rows) + row_offsets[0]
    )
    second = to_low(layer_norm(middle, norm_gains[1], norm_offsets[1]))
    second_full = whole_rows(second)
    before = matmul(second_full, up_mat) + up_offset
    active = to_low(gelu_tanh(before))
    section_out = middle + summed_rows(sliced_product(active, down_mat), part_rows) + row_offsets[1]
    kept_state = (
        normed_full,
        queries,
        key_rows,
        value_rows,
        log_total,
        mixed_rows,
        middle,
        second_full,
        before,
        active,
    )
    return (section_out, kept_state)


def layer_backward(grad_out, section_in, kept_state, params, length, slopes):
    (
        norm_gains,
        norm_offsets,
        qkv_mats,
        qv_offsets,
        out_mat,
        up_mat,
        up_offset,
        down_mat,
        row_offsets,
    ) = params
    (
        normed_full,
        queries,
        key_rows,
        value_rows,
        log_total,
        mixed_rows,
        middle,
        second_full,
        before,
        active,
    ) = kept_state
    part_rows = grad_out.shape[0]
    grad_down_full = whole_rows(to_low(grad_out))
    grad_down = outer_sum(active, grad_down_full)
    _, gelu_back = jax.vjp(gelu_tanh, before)
    grad_before = gelu_back(matmul_t(grad_down_full, down_mat))[0]
    before_low = to_low(grad_before)
    grad_up = outer_sum(second_full, before_low)
    grad_second = summed_rows(sliced_product_t(before_low, up_mat), part_rows)
    _, norm_back_two = jax.vjp(layer_norm, middle, norm_gains[1], norm_offsets[1])
    grad_middle, gain_two, offset_two = norm_back_two(grad_second)
    grad_middle = grad_middle + grad_out
    grad_mid_full = whole_rows(to_low(grad_middle))
    grad_out_mat = outer_sum(mixed_rows, grad_mid_full)
    grad_mixed = split_heads(to_low(matmul_t(grad_mid_full, out_mat)))
    raw_scores = jnp.einsum(
        "qhd,khd->hqk",
        split_heads(queries),
        split_heads(key_rows),
        preferred_element_type=jnp.float32,
    )
    weights_full = jnp.exp(mask_scores(raw_scores, slopes, length) - log_total)
    grad_weights = jnp.einsum(
        "qhd,khd->hqk", grad_mixed, split_heads(value_rows), preferred_element_type=jnp.float32
    )
    grad_values = jnp.einsum(
        "hqk,qhd->khd", to_low(weights_full), grad_mixed, preferred_element_type=jnp.float32
    )
    inner_sum = jnp.sum(weights_full * grad_weights, axis=-1, keepdims=True)
    grad_scores = to_low(weights_full * (grad_weights - inner_sum) * HEAD_DIM ** (-0.5))
    grad_queries = jnp.einsum(
        "hqk,khd->qhd", grad_scores, split_heads(key_rows), preferred_element_type=jnp.float32
    )
    grad_keys = jnp.einsum(
        "hqk,qhd->khd", grad_scores, split_heads(queries), preferred_element_type=jnp.float32
    )
    seq_len = grad_queries.shape[0]
    flat_queries = grad_queries.reshape(seq_len, -1)
    flat_keys = grad_keys.reshape(seq_len, -1)
    flat_values = grad_values.reshape(seq_len, -1)
    grad_qv = jnp.stack([jnp.sum(flat_queries, axis=0), jnp.sum(flat_values, axis=0)])
    grad_rows = to_low(jnp.stack([flat_queries, flat_keys, flat_values]))
    grad_qkv = jnp.einsum("sd,isk->idk", normed_full, grad_rows, preferred_element_type=jnp.float32)

    def back_rows(leading_row, row_count):
        return jnp.einsum("isk,idk->sd", grad_rows, qkv_mats, preferred_element_type=jnp.float32)

    grad_first = summed_rows(back_rows, part_rows)
    _, norm_back_one = jax.vjp(layer_norm, section_in, norm_gains[0], norm_offsets[0])
    grad_in, gain_one, offset_one = norm_back_one(grad_first)
    grad_in = grad_in + grad_middle
    layer_part = (grad_qkv, grad_qv, grad_out_mat, grad_up, jnp.sum(grad_before, axis=0), grad_down)
    norm_part = (
        jnp.stack([gain_one, gain_two]),
        jnp.stack([offset_one, offset_two]),
        jnp.stack([jnp.sum(grad_middle, axis=0), jnp.sum(grad_out, axis=0)]),
    )
    return (grad_in, layer_part, norm_part)


def guarded_addition(cumulative_sums, extra_terms, row_is_present):
    return tuple(
        (
            running_total + jnp.where(row_is_present, extra_term, 0.0)
            for running_total, extra_term in zip(cumulative_sums, extra_terms)
        )
    )


def pick_row(source, index_value):
    return lax.dynamic_index_in_dim(source, index_value, 0, keepdims=False)


def per_device(
    token_ids,
    target_ids,
    lengths,
    embedding,
    outer_gain,
    outer_bias,
    norm_gain,
    norm_bias,
    qkv_weight,
    qv_bias,
    out_weight,
    up_weight,
    up_bias,
    down_weight,
    row_bias,
):
    section_index = lax.axis_index("section")
    is_first = section_index == 0
    tensor_index = lax.axis_index("tensor")
    vocab_rows = embedding.shape[0]
    model_width = embedding.shape[1]
    vocab_start = tensor_index * vocab_rows
    micro_rows = token_ids.shape[0]
    seq_len = token_ids.shape[1]
    part_rows = seq_len // lax.axis_size("tensor")
    row_base = lax.axis_index("dp") * micro_rows
    params = (
        norm_gain[0],
        norm_bias[0],
        qkv_weight[0],
        qv_bias[0],
        out_weight[0],
        up_weight[0],
        up_bias[0],
        down_weight[0],
        row_bias[0],
    )
    local_heads = qkv_weight.shape[-1] // HEAD_DIM
    slopes = alibi_slopes(tensor_index * local_heads, local_heads)
    outer_weight = outer_gain[0]
    outer_offset = outer_bias[0]
    token_count = jnp.sum(lengths).astype(jnp.float32)
    inverse = 1.0 / token_count
    vocab_columns = jnp.arange(vocab_rows)
    places = jnp.arange(seq_len)
    arrived = jnp.zeros((part_rows, model_width), jnp.float32)
    layer_totals = tuple(
        (
            jnp.zeros(array.shape[1:], jnp.float32)
            for array in (qkv_weight, qv_bias, out_weight, up_weight, up_bias, down_weight)
        )
    )
    norm_totals = (
        jnp.zeros(norm_gain.shape[1:], jnp.float32),
        jnp.zeros(norm_bias.shape[1:], jnp.float32),
        jnp.zeros(row_bias.shape[1:], jnp.float32),
    )
    outer_gain_total = jnp.zeros((model_width,), jnp.float32)
    outer_bias_total = jnp.zeros((model_width,), jnp.float32)
    embed_total = jnp.zeros((vocab_rows, model_width), jnp.float32)
    loss_total = jnp.zeros((), jnp.float32)
    inputs_hist = []
    embed_hist = []
    kept_hist = []
    for tick_index in range(micro_rows + 2):
        fwd_micro = tick_index - section_index
        fwd_live = (fwd_micro >= 0) & (fwd_micro < micro_rows)
        fwd_slot = jnp.clip(fwd_micro, 0, micro_rows - 1)
        fwd_ids = pick_row(token_ids, fwd_slot)
        fwd_length = pick_row(lengths, row_base + fwd_slot)
        local_ids = fwd_ids - vocab_start
        inside = (local_ids >= 0) & (local_ids < vocab_rows)
        looked = jnp.where(
            inside[:, None], jnp.take(embedding, jnp.clip(local_ids, 0, vocab_rows - 1), axis=0), 0
        ).astype(jnp.float32)
        embed_part = summed_rows(row_window(looked), part_rows)
        section_in = jnp.where(
            is_first, layer_norm(embed_part, outer_weight, outer_offset), arrived
        )
        section_out, kept_state = layer_forward(section_in, params, fwd_length, slopes)
        inputs_hist.append(section_in)
        embed_hist.append(embed_part)
        kept_hist.append(kept_state)
        head_live = jnp.logical_not(is_first) & fwd_live
        final_full = whole_rows(to_low(layer_norm(section_out, outer_weight, outer_offset)))
        target_col = pick_row(target_ids, fwd_slot) - vocab_start
        target_hits = vocab_columns[None, :] == target_col[:, None]

        def head_logits(final_input):
            logit_rows = matmul_t(final_input, embedding)
            return (
                logit_rows,
                jnp.max(logit_rows, axis=-1),
                jnp.sum(jnp.where(target_hits, logit_rows, 0.0), axis=-1),
            )

        def head_empty(final_input):
            return (
                jnp.zeros((seq_len, vocab_rows), jnp.float32),
                jnp.zeros((seq_len,), jnp.float32),
                jnp.zeros((seq_len,), jnp.float32),
            )

        logits, local_top, local_pick = lax.cond(head_live, head_logits, head_empty, final_full)
        top_all = lax.pmax(local_top, "tensor")
        sum_all, pick_all = lax.psum(
            (jnp.sum(jnp.exp(logits - top_all[:, None]), axis=-1), local_pick), "tensor"
        )
        log_norm = top_all + jnp.log(sum_all)
        valid_rows = places < fwd_length
        loss_total = loss_total + jnp.where(
            head_live, jnp.sum(jnp.where(valid_rows, log_norm - pick_all, 0.0)), 0.0
        )
        row_weight = jnp.where(valid_rows, inverse, 0.0)

        def head_grads(logit_rows):
            grad_logits = to_low(
                (jnp.exp(logit_rows - log_norm[:, None]) - target_hits.astype(jnp.float32))
                * row_weight[:, None]
            )
            return (grad_logits, outer_sum(grad_logits, final_full))

        def head_none(logit_rows):
            return (
                jnp.zeros((seq_len, vocab_rows), jnp.bfloat16),
                jnp.zeros((vocab_rows, model_width), jnp.float32),
            )

        grad_logits, head_table = lax.cond(head_live, head_grads, head_none, logits)
        embed_total = embed_total + head_table
        grad_final = summed_rows(sliced_product(grad_logits, embedding), part_rows)
        _, final_back = jax.vjp(layer_norm, section_out, outer_weight, outer_offset)
        grad_top, final_gain, final_offset = final_back(grad_final)
        bwd_micro = tick_index - 2 + section_index
        bwd_live = (bwd_micro >= 0) & (bwd_micro < micro_rows)
        bwd_slot = jnp.clip(bwd_micro, 0, micro_rows - 1)
        bwd_length = pick_row(lengths, row_base + bwd_slot)
        past_tick = max(tick_index - 2, 0)
        bwd_in = jnp.where(is_first, inputs_hist[past_tick], section_in)
        grad_out = jnp.where(is_first, arrived, grad_top)
        _, bwd_kept = layer_forward(bwd_in, params, bwd_length, slopes)
        grad_in, layer_part, norm_part = layer_backward(
            grad_out, bwd_in, bwd_kept, params, bwd_length, slopes
        )
        layer_totals = guarded_addition(layer_totals, layer_part, bwd_live)
        norm_totals = guarded_addition(norm_totals, norm_part, bwd_live)
        embed_live = is_first & bwd_live
        _, embed_back = jax.vjp(layer_norm, embed_hist[past_tick], outer_weight, outer_offset)
        grad_embed_rows, embed_gain, embed_offset = embed_back(grad_in)
        outer_gain_total = (
            outer_gain_total
            + jnp.where(head_live, final_gain, 0.0)
            + jnp.where(embed_live, embed_gain, 0.0)
        )
        outer_bias_total = (
            outer_bias_total
            + jnp.where(head_live, final_offset, 0.0)
            + jnp.where(embed_live, embed_offset, 0.0)
        )
        bwd_ids = pick_row(token_ids, bwd_slot)
        chosen = bwd_ids - vocab_start
        within = (chosen >= 0) & (chosen < vocab_rows)
        embed_total = embed_total.at[jnp.clip(chosen, 0, vocab_rows - 1)].add(
            jnp.where(
                within[:, None],
                lax.all_gather(
                    jnp.where(embed_live, grad_embed_rows, 0.0), "tensor", axis=0, tiled=True
                ),
                0.0,
            )
        )
        if tick_index < micro_rows + 1:
            arrived = from_partner(jnp.where(is_first, section_out, grad_in), "section", 0)
    layer_sums = lax.psum(
        (
            layer_totals[0],
            layer_totals[1],
            layer_totals[2],
            layer_totals[3],
            layer_totals[4],
            layer_totals[5],
        ),
        "dp",
    )
    norm_sums = lax.psum(
        (norm_totals[0], norm_totals[1], norm_totals[2], outer_gain_total, outer_bias_total),
        ("dp", "tensor"),
    )
    embed_sum, loss_sum = lax.psum((embed_total, loss_total), ("section", "dp"))
    return (
        loss_sum / token_count,
        embed_sum,
        norm_sums[3][None],
        norm_sums[4][None],
        norm_sums[0][None],
        norm_sums[1][None],
        layer_sums[0][None],
        layer_sums[1][None],
        layer_sums[2][None],
        layer_sums[3][None],
        layer_sums[4][None],
        layer_sums[5][None],
        norm_sums[2][None],
    )


def solution(mesh):
    return jax.shard_map(
        per_device,
        mesh=mesh,
        in_specs=(
            P("dp", None),
            P("dp", None),
            P(),
            P("tensor", None),
            P("section", None),
            P("section", None),
            P("section", None, None),
            P("section", None, None),
            P("section", None, None, "tensor"),
            P("section", None, "tensor"),
            P("section", "tensor", None),
            P("section", None, "tensor"),
            P("section", "tensor"),
            P("section", "tensor", None),
            P("section", None, None),
        ),
        out_specs=(
            P(),
            P("tensor", None),
            P("section", None),
            P("section", None),
            P("section", None, None),
            P("section", None, None),
            P("section", None, None, "tensor"),
            P("section", None, "tensor"),
            P("section", "tensor", None),
            P("section", None, "tensor"),
            P("section", "tensor"),
            P("section", "tensor", None),
            P("section", None, None),
        ),
        check_vma=False,
    )
```

profile of v0, /device:TPU:1, one launch (start us, length us, event | category | flops | bytes accessed | tf_op | source)
XLA Modules:
  0.0 5472.6 jit_solution(13915368243051739434)
XLA Ops:
  28.6 78.9 %reduce-scatter.29.cloned.1.call-done = f32[256,1024]{1,0:T(8,128)} async-done(((f32[1024,1024]{1,0:T(8,128)}), f32[256,1024]{1,0:T(8,128)}) %reduce-scatter.29.cloned.1.call-update) | async-done | bytes 1048592 | tf_op jit(solution)/shard_map/reduce_scatter | solution.py:77
  207.2 60.5 %reduce-scatter.31.cloned.1.call-done = f32[256,1024]{1,0:T(8,128)} async-done(((f32[1024,1024]{1,0:T(8,128)}), f32[256,1024]{1,0:T(8,128)}) %reduce-scatter.31.cloned.1.call-update) | async-done | bytes 1048592 | tf_op jit(solution)/shard_map/reduce_scatter | solution.py:77
  267.7 80.0 %reduce-scatter.39.cloned.1.call-done = f32[256,1024]{1,0:T(8,128)} async-done(((f32[1024,1024]{1,0:T(8,128)}), f32[256,1024]{1,0:T(8,128)}) %reduce-scatter.39.cloned.1.call-update) | async-done | bytes 1048592 | tf_op jit(solution)/shard_map/reduce_scatter | solution.py:77
  352.6 46.3 all-gather.34.cloned.1.call-done
  408.1 75.6 %reduce-scatter.33.cloned.1.call-done = f32[256,1024]{1,0:T(8,128)} async-done(((f32[1024,1024]{1,0:T(8,128)}), f32[256,1024]{1,0:T(8,128)}) %reduce-scatter.33.cloned.1.call-update) | async-done | bytes 1048592 | tf_op jit(solution)/shard_map/reduce_scatter | solution.py:77
  626.4 78.9 %reduce-scatter.37.cloned.1.call-done = f32[256,1024]{1,0:T(8,128)} async-done(((f32[1024,1024]{1,0:T(8,128)}), f32[256,1024]{1,0:T(8,128)}) %reduce-scatter.37.cloned.1.call-update) | async-done | bytes 1048592 | tf_op jit(solution)/shard_map/reduce_scatter | solution.py:77
  711.7 41.7 all-gather.40.cloned.1.call-done
  814.8 75.6 %reduce-scatter.41.cloned.1.call-done = f32[256,1024]{1,0:T(8,128)} async-done(((f32[1024,1024]{1,0:T(8,128)}), f32[256,1024]{1,0:T(8,128)}) %reduce-scatter.41.cloned.1.call-update) | async-done | bytes 1048592 | tf_op jit(solution)/shard_map/reduce_scatter | solution.py:77
  897.7 46.3 all-gather.42.cloned.1.call-done
  1043.1 56.3 %reduce-scatter.43.cloned.1.call-done = f32[256,1024]{1,0:T(8,128)} async-done(((f32[1024,1024]{1,0:T(8,128)}), f32[256,1024]{1,0:T(8,128)}) %reduce-scatter.43.cloned.1.call-update) | async-done | bytes 1048592 | tf_op jit(solution)/shard_map/reduce_scatter | solution.py:77
  1106.2 72.8 %reduce-scatter.35.cloned.1.call-done = f32[256,1024]{1,0:T(8,128)} async-done(((f32[1024,1024]{1,0:T(8,128)}), f32[256,1024]{1,0:T(8,128)}) %reduce-scatter.35.cloned.1.call-update) | async-done | bytes 1048592 | tf_op jit(solution)/shard_map/reduce_scatter | solution.py:77
  1194.5 44.9 all-gather.44.cloned.1.call-done
  1321.6 41.5 reduce-scatter.45.cloned.1.call-done
  1363.2 80.1 %reduce-scatter.53.cloned.1.call-done = f32[256,1024]{1,0:T(8,128)} async-done(((f32[1024,1024]{1,0:T(8,128)}), f32[256,1024]{1,0:T(8,128)}) %reduce-scatter.53.cloned.1.call-update) | async-done | bytes 1048592 | tf_op jit(solution)/shard_map/reduce_scatter | solution.py:77
  1448.7 46.1 all-gather.46.cloned.1.call-done
  1503.9 75.6 %reduce-scatter.47.cloned.1.call-done = f32[256,1024]{1,0:T(8,128)} async-done(((f32[1024,1024]{1,0:T(8,128)}), f32[256,1024]{1,0:T(8,128)}) %reduce-scatter.47.cloned.1.call-update) | async-done | bytes 1048592 | tf_op jit(solution)/shard_map/reduce_scatter | solution.py:77
  1687.7 50.4 conditional.11
  1762.5 74.6 %reduce-scatter.51.cloned.1.call-done = f32[256,1024]{1,0:T(8,128)} async-done(((f32[1024,1024]{1,0:T(8,128)}), f32[256,1024]{1,0:T(8,128)}) %reduce-scatter.51.cloned.1.call-update) | async-done | bytes 1048592 | tf_op jit(solution)/shard_map/reduce_scatter | solution.py:77
  1946.4 75.6 %reduce-scatter.55.cloned.1.call-done = f32[256,1024]{1,0:T(8,128)} async-done(((f32[1024,1024]{1,0:T(8,128)}), f32[256,1024]{1,0:T(8,128)}) %reduce-scatter.55.cloned.1.call-update) | async-done | bytes 1048592 | tf_op jit(solution)/shard_map/reduce_scatter | solution.py:77
  2029.3 46.3 all-gather.56.cloned.1.call-done
  2173.0 55.2 %reduce-scatter.57.cloned.1.call-done = f32[256,1024]{1,0:T(8,128)} async-done(((f32[1024,1024]{1,0:T(8,128)}), f32[256,1024]{1,0:T(8,128)}) %reduce-scatter.57.cloned.1.call-update) | async-done | bytes 1048592 | tf_op jit(solution)/shard_map/reduce_scatter | solution.py:77
  2234.4 73.3 %reduce-scatter.49.cloned.1.call-done = f32[256,1024]{1,0:T(8,128)} async-done(((f32[1024,1024]{1,0:T(8,128)}), f32[256,1024]{1,0:T(8,128)}) %reduce-scatter.49.cloned.1.call-update) | async-done | bytes 1048592 | tf_op jit(solution)/shard_map/reduce_scatter | solution.py:77
  2322.8 44.8 all-gather.58.cloned.1.call-done
  2449.8 41.8 reduce-scatter.59.cloned.1.call-done
  2491.7 80.2 %reduce-scatter.67.cloned.1.call-done = f32[256,1024]{1,0:T(8,128)} async-done(((f32[1024,1024]{1,0:T(8,128)}), f32[256,1024]{1,0:T(8,128)}) %reduce-scatter.67.cloned.1.call-update) | async-done | bytes 1048592 | tf_op jit(solution)/shard_map/reduce_scatter | solution.py:77
  2577.1 46.3 all-gather.60.cloned.1.call-done
  2632.5 75.6 %reduce-scatter.61.cloned.1.call-done = f32[256,1024]{1,0:T(8,128)} async-done(((f32[1024,1024]{1,0:T(8,128)}), f32[256,1024]{1,0:T(8,128)}) %reduce-scatter.61.cloned.1.call-update) | async-done | bytes 1048592 | tf_op jit(solution)/shard_map/reduce_scatter | solution.py:77
  2816.5 50.3 conditional.13
  2891.0 74.7 %reduce-scatter.65.cloned.1.call-done = f32[256,1024]{1,0:T(8,128)} async-done(((f32[1024,1024]{1,0:T(8,128)}), f32[256,1024]{1,0:T(8,128)}) %reduce-scatter.65.cloned.1.call-update) | async-done | bytes 1048592 | tf_op jit(solution)/shard_map/reduce_scatter | solution.py:77
  3075.3 75.6 %reduce-scatter.69.cloned.1.call-done = f32[256,1024]{1,0:T(8,128)} async-done(((f32[1024,1024]{1,0:T(8,128)}), f32[256,1024]{1,0:T(8,128)}) %reduce-scatter.69.cloned.1.call-update) | async-done | bytes 1048592 | tf_op jit(solution)/shard_map/reduce_scatter | solution.py:77
  3158.4 46.1 all-gather.70.cloned.1.call-done
  3300.6 56.4 %reduce-scatter.71.cloned.1.call-done = f32[256,1024]{1,0:T(8,128)} async-done(((f32[1024,1024]{1,0:T(8,128)}), f32[256,1024]{1,0:T(8,128)}) %reduce-scatter.71.cloned.1.call-update) | async-done | bytes 1048592 | tf_op jit(solution)/shard_map/reduce_scatter | solution.py:77
  3362.9 73.8 %reduce-scatter.63.cloned.1.call-done = f32[256,1024]{1,0:T(8,128)} async-done(((f32[1024,1024]{1,0:T(8,128)}), f32[256,1024]{1,0:T(8,128)}) %reduce-scatter.63.cloned.1.call-update) | async-done | bytes 1048592 | tf_op jit(solution)/shard_map/reduce_scatter | solution.py:77
  3451.1 44.3 all-gather.72.cloned.1.call-done
  3577.9 42.1 reduce-scatter.73.cloned.1.call-done
  3620.0 80.1 %reduce-scatter.79.cloned.1.call-done = f32[256,1024]{1,0:T(8,128)} async-done(((f32[1024,1024]{1,0:T(8,128)}), f32[256,1024]{1,0:T(8,128)}) %reduce-scatter.79.cloned.1.call-update) | async-done | bytes 1048592 | tf_op jit(solution)/shard_map/reduce_scatter | solution.py:77
  3705.3 46.3 all-gather.74.cloned.1.call-done
  3760.7 75.6 %reduce-scatter.75.cloned.1.call-done = f32[256,1024]{1,0:T(8,128)} async-done(((f32[1024,1024]{1,0:T(8,128)}), f32[256,1024]{1,0:T(8,128)}) %reduce-scatter.75.cloned.1.call-update) | async-done | bytes 1048592 | tf_op jit(solution)/shard_map/reduce_scatter | solution.py:77
  3975.2 80.8 %reduce-scatter.77.cloned.1.call-done = f32[256,1024]{1,0:T(8,128)} async-done(((f32[1024,1024]{1,0:T(8,128)}), f32[256,1024]{1,0:T(8,128)}) %reduce-scatter.77.cloned.1.call-update) | async-done | bytes 1048592 | tf_op jit(solution)/shard_map/reduce_scatter | solution.py:77
  4165.3 75.6 %reduce-scatter.81.cloned.1.call-done = f32[256,1024]{1,0:T(8,128)} async-done(((f32[1024,1024]{1,0:T(8,128)}), f32[256,1024]{1,0:T(8,128)}) %reduce-scatter.81.cloned.1.call-update) | async-done | bytes 1048592 | tf_op jit(solution)/shard_map/reduce_scatter | solution.py:77
  4248.1 46.3 all-gather.90.cloned.1.call-done
  4371.4 75.6 %reduce-scatter.83.cloned.1.call-done = f32[256,1024]{1,0:T(8,128)} async-done(((f32[1024,1024]{1,0:T(8,128)}), f32[256,1024]{1,0:T(8,128)}) %reduce-scatter.83.cloned.1.call-update) | async-done | bytes 1048592 | tf_op jit(solution)/shard_map/reduce_scatter | solution.py:77
  4528.1 55.7 %add_add_fusion = f32[8192,1024]{1,0:T(8,128)} fusion(f32[8192,1024]{1,0:T(8,128)} %get-tuple-element.180, f32[8192,1024]{1,0:T(8,128)} %get-tuple-element.179, f32[8192,1024]{1,0:T(8,128)} %get-tuple-element.177, f32[8192,1024]{1,0:T(8,128)} %get-tuple-element.178), kind=kLoop, calls=%fused_computation.31 | loop fusion | flops 25165824 | bytes 167772160 | tf_op jit(solution)/shard_map/add.142
  4654.9 46.8 all-gather.82.cloned.1.call-done
  4735.2 47.8 all-gather.92.cloned.1.call-done
  4858.8 61.1 %all-reduce = (f32[1,1024]{1,0:T(1,128)}, f32[1,1024]{1,0:T(1,128)}, f32[1,2,1024]{2,1,0:T(2,128)}, f32[1,2,1024]{2,1,0:T(2,128)}, f32[1,2,1024]{2,1,0:T(2,128)}) all-reduce(f32[1,1024]{1,0:T(1,128)S(1)} %bitcast.638, f32[1,1024]{1,0:T(1,128)S(1)} %bitcast.637, ...), channel_id=1, replica_groups=mesh['section'=2,'dp'=4,'tensor'=4] {'dp','tensor'}, use_global_device_ids=true, to_apply=%region_185.187 | all-reduce | flops 8192 | bytes 65536 | tf_op jit(solution)/shard_map/psum | solution.py:445
  4919.9 110.3 %all-reduce.9.cloned.1.call-done = (f32[1,3,1024,256]{2,3,1,0:T(8,128)}, f32[1,256,1024]{2,1,0:T(8,128)}, f32[1,1024,1024]{2,1,0:T(8,128)}, f32[1,1024,1024]{2,1,0:T(8,128)}) async-done(((f32[1,3,1024,256]{2,3,1,0:T(8,128)}, f32[1,256,1024]{2,1,0:T(8,128)}, f32[1,1024,1024]{2,1,0:T(8,128)}, f32[1,1024,1024]{2,1,0:T(8,128)}), (f32[1,3,1024,256]{2,3,1,0:T(8,128)}, f32[1,256,1024]{2,1,0:T(8,128)}, ...) | async-done | bytes 12582928 | tf_op jit(solution)/shard_map/psum | solution.py:434
  5033.7 399.4 %all-reduce.7.cloned.1.call-done = f32[8192,1024]{1,0:T(8,128)} async-done(((f32[8192,1024]{1,0:T(8,128)}), f32[8192,1024]{1,0:T(8,128)}) %all-reduce.7.cloned.1.call-update) | async-done | bytes 33554448 | tf_op jit(solution)/shard_map/psum | solution.py:449
  (1364 shorter events, 2331.9 us)
Async XLA Ops:
  28.4 134.0 %all-gather.32.cloned.1.call-start = ((), (), s32[]{:S(2)}) async-start(), calls=%async_computation.29 | async-start | bytes 2621440 | tf_op jit(solution)/shard_map/all_gather | solution.py:73
  115.9 151.8 %reduce-scatter.31.cloned.1.call-start = ((), (), s32[]{:S(2)}) async-start(), calls=%async_computation.30 | async-start | bytes 5242880 | tf_op jit(solution)/shard_map/reduce_scatter | solution.py:77
  192.0 155.7 %reduce-scatter.39.cloned.1.call-start = ((), (), s32[]{:S(2)}) async-start(), calls=%async_computation.37 | async-start | bytes 5242880 | tf_op jit(solution)/shard_map/reduce_scatter | solution.py:77
  206.5 192.5 %all-gather.34.cloned.1.call-start = ((), (), s32[]{:S(2)}) async-start(), calls=%async_computation.31 | async-start | bytes 2621440 | tf_op jit(solution)/shard_map/all_gather | solution.py:73
  352.4 131.3 %reduce-scatter.33.cloned.1.call-start = ((), (), s32[]{:S(2)}) async-start(), calls=%async_computation.32 | async-start | bytes 5242880 | tf_op jit(solution)/shard_map/reduce_scatter | solution.py:77
  487.1 218.1 %reduce-scatter.37.cloned.1.call-start = ((), (), s32[]{:S(2)}) async-start(), calls=%async_computation.35 | async-start | bytes 5242880 | tf_op jit(solution)/shard_map/reduce_scatter | solution.py:77
  626.3 173.8 %all-gather.38.cloned.1.call-start = ((), (), s32[]{:S(2)}) async-start(), calls=%async_computation.36 | async-start | bytes 2621440 | tf_op jit(solution)/shard_map/all_gather | solution.py:73
  711.7 178.8 %reduce-scatter.41.cloned.1.call-start = ((), (), s32[]{:S(2)}) async-start(), calls=%async_computation.39 | async-start | bytes 5242880 | tf_op jit(solution)/shard_map/reduce_scatter | solution.py:77
  814.8 129.3 %all-gather.42.cloned.1.call-start = ((), (), s32[]{:S(2)}) async-start(), calls=%async_computation.40 | async-start | bytes 2621440 | tf_op jit(solution)/shard_map/all_gather | solution.py:73
  897.5 202.0 %reduce-scatter.43.cloned.1.call-start = ((), (), s32[]{:S(2)}) async-start(), calls=%async_computation.41 | async-start | bytes 5242880 | tf_op jit(solution)/shard_map/reduce_scatter | solution.py:77
  1023.8 155.2 %reduce-scatter.35.cloned.1.call-start = ((), (), s32[]{:S(2)}) async-start(), calls=%async_computation.34 | async-start | bytes 5242880 | tf_op jit(solution)/shard_map/reduce_scatter | solution.py:77
  1043.1 196.3 %all-gather.44.cloned.1.call-start = ((), (), s32[]{:S(2)}) async-start(), calls=%async_computation.42 | async-start | bytes 2621440 | tf_op jit(solution)/shard_map/all_gather | solution.py:73
  1194.2 168.9 %reduce-scatter.45.cloned.1.call-start = ((), (), s32[]{:S(2)}) async-start(), calls=%async_computation.43 | async-start | bytes 5242880 | tf_op jit(solution)/shard_map/reduce_scatter | solution.py:77
  1274.7 168.6 %reduce-scatter.53.cloned.1.call-start = ((), (), s32[]{:S(2)}) async-start(), calls=%async_computation.51 | async-start | bytes 5242880 | tf_op jit(solution)/shard_map/reduce_scatter | solution.py:77
  1321.6 173.2 %all-gather.46.cloned.1.call-start = ((), (), s32[]{:S(2)}) async-start(), calls=%async_computation.44 | async-start | bytes 2621440 | tf_op jit(solution)/shard_map/all_gather | solution.py:73
  1448.3 131.3 %reduce-scatter.47.cloned.1.call-start = ((), (), s32[]{:S(2)}) async-start(), calls=%async_computation.45 | async-start | bytes 5242880 | tf_op jit(solution)/shard_map/reduce_scatter | solution.py:77
  1583.0 254.0 %reduce-scatter.51.cloned.1.call-start = ((), (), s32[]{:S(2)}) async-start(), calls=%async_computation.49 | async-start | bytes 5242880 | tf_op jit(solution)/shard_map/reduce_scatter | solution.py:77
  1762.4 169.3 %all-gather.52.cloned.1.call-start = ((), (), s32[]{:S(2)}) async-start(), calls=%async_computation.50 | async-start | bytes 2621440 | tf_op jit(solution)/shard_map/all_gather | solution.py:73
  1843.6 178.5 %reduce-scatter.55.cloned.1.call-start = ((), (), s32[]{:S(2)}) async-start(), calls=%async_computation.53 | async-start | bytes 5242880 | tf_op jit(solution)/shard_map/reduce_scatter | solution.py:77
  2029.1 199.1 %reduce-scatter.57.cloned.1.call-start = ((), (), s32[]{:S(2)}) async-start(), calls=%async_computation.55 | async-start | bytes 5242880 | tf_op jit(solution)/shard_map/reduce_scatter | solution.py:77
  2152.5 155.2 %reduce-scatter.49.cloned.1.call-start = ((), (), s32[]{:S(2)}) async-start(), calls=%async_computation.47 | async-start | bytes 5242880 | tf_op jit(solution)/shard_map/reduce_scatter | solution.py:77
  2172.9 194.7 %all-gather.58.cloned.1.call-start = ((), (), s32[]{:S(2)}) async-start(), calls=%async_computation.56 | async-start | bytes 2621440 | tf_op jit(solution)/shard_map/all_gather | solution.py:73
  2322.3 169.4 %reduce-scatter.59.cloned.1.call-start = ((), (), s32[]{:S(2)}) async-start(), calls=%async_computation.57 | async-start | bytes 5242880 | tf_op jit(solution)/shard_map/reduce_scatter | solution.py:77
  2402.8 169.1 %reduce-scatter.67.cloned.1.call-start = ((), (), s32[]{:S(2)}) async-start(), calls=%async_computation.65 | async-start | bytes 5242880 | tf_op jit(solution)/shard_map/reduce_scatter | solution.py:77
  2449.8 173.6 %all-gather.60.cloned.1.call-start = ((), (), s32[]{:S(2)}) async-start(), calls=%async_computation.58 | async-start | bytes 2621440 | tf_op jit(solution)/shard_map/all_gather | solution.py:73
  2576.9 131.3 %reduce-scatter.61.cloned.1.call-start = ((), (), s32[]{:S(2)}) async-start(), calls=%async_computation.59 | async-start | bytes 5242880 | tf_op jit(solution)/shard_map/reduce_scatter | solution.py:77
  2711.6 254.1 %reduce-scatter.65.cloned.1.call-start = ((), (), s32[]{:S(2)}) async-start(), calls=%async_computation.63 | async-start | bytes 5242880 | tf_op jit(solution)/shard_map/reduce_scatter | solution.py:77
  2891.0 169.6 %all-gather.66.cloned.1.call-start = ((), (), s32[]{:S(2)}) async-start(), calls=%async_computation.64 | async-start | bytes 2621440 | tf_op jit(solution)/shard_map/all_gather | solution.py:73
  2972.3 178.6 %reduce-scatter.69.cloned.1.call-start = ((), (), s32[]{:S(2)}) async-start(), calls=%async_computation.67 | async-start | bytes 5242880 | tf_op jit(solution)/shard_map/reduce_scatter | solution.py:77
  3075.2 129.3 %all-gather.70.cloned.1.call-start = ((), (), s32[]{:S(2)}) async-start(), calls=%async_computation.68 | async-start | bytes 2621440 | tf_op jit(solution)/shard_map/all_gather | solution.py:73
  3157.9 199.0 %reduce-scatter.71.cloned.1.call-start = ((), (), s32[]{:S(2)}) async-start(), calls=%async_computation.69 | async-start | bytes 5242880 | tf_op jit(solution)/shard_map/reduce_scatter | solution.py:77
  3281.3 155.4 %reduce-scatter.63.cloned.1.call-start = ((), (), s32[]{:S(2)}) async-start(), calls=%async_computation.61 | async-start | bytes 5242880 | tf_op jit(solution)/shard_map/reduce_scatter | solution.py:77
  3300.5 195.0 %all-gather.72.cloned.1.call-start = ((), (), s32[]{:S(2)}) async-start(), calls=%async_computation.70 | async-start | bytes 2621440 | tf_op jit(solution)/shard_map/all_gather | solution.py:73
  3450.9 169.1 %reduce-scatter.73.cloned.1.call-start = ((), (), s32[]{:S(2)}) async-start(), calls=%async_computation.71 | async-start | bytes 5242880 | tf_op jit(solution)/shard_map/reduce_scatter | solution.py:77
  3530.7 169.4 %reduce-scatter.79.cloned.1.call-start = ((), (), s32[]{:S(2)}) async-start(), calls=%async_computation.81 | async-start | bytes 5242880 | tf_op jit(solution)/shard_map/reduce_scatter | solution.py:77
  3577.9 173.8 %all-gather.74.cloned.1.call-start = ((), (), s32[]{:S(2)}) async-start(), calls=%async_computation.72 | async-start | bytes 2621440 | tf_op jit(solution)/shard_map/all_gather | solution.py:73
  3705.1 131.3 %reduce-scatter.75.cloned.1.call-start = ((), (), s32[]{:S(2)}) async-start(), calls=%async_computation.73 | async-start | bytes 5242880 | tf_op jit(solution)/shard_map/reduce_scatter | solution.py:77
  3839.8 216.2 %reduce-scatter.77.cloned.1.call-start = ((), (), s32[]{:S(2)}) async-start(), calls=%async_computation.79 | async-start | bytes 5242880 | tf_op jit(solution)/shard_map/reduce_scatter | solution.py:77
  3974.5 129.3 %all-gather.88.cloned.1.call-start = ((), (), s32[]{:S(2)}) async-start(), calls=%async_computation.82 | async-start | bytes 2621440 | tf_op jit(solution)/shard_map/all_gather | solution.py:73
  3975.1 175.6 %all-gather.86.cloned.1.call-start = ((), (), s32[]{:S(2)}) async-start(), calls=%async_computation.80 | async-start | bytes 2621440 | tf_op jit(solution)/shard_map/all_gather | solution.py:73
  4062.5 178.4 %reduce-scatter.81.cloned.1.call-start = ((), (), s32[]{:S(2)}) async-start(), calls=%async_computation.83 | async-start | bytes 5242880 | tf_op jit(solution)/shard_map/reduce_scatter | solution.py:77
  4247.9 199.1 %reduce-scatter.83.cloned.1.call-start = ((), (), s32[]{:S(2)}) async-start(), calls=%async_computation.85 | async-start | bytes 5242880 | tf_op jit(solution)/shard_map/reduce_scatter | solution.py:77
  4371.3 212.5 %all-gather.78.cloned.1.call-start = ((), (), s32[]{:S(2)}) async-start(), calls=%async_computation.75 | async-start | bytes 5242880 | tf_op jit(solution)/shard_map/all_gather | solution.py:426
  4458.7 162.3 %all-gather.80.cloned.1.call-start = ((), (), s32[]{:S(2)}) async-start(), calls=%async_computation.76 | async-start | bytes 5242880 | tf_op jit(solution)/shard_map/all_gather | solution.py:426
  4459.4 242.3 %all-gather.82.cloned.1.call-start = ((), (), s32[]{:S(2)}) async-start(), calls=%async_computation.77 | async-start | bytes 5242880 | tf_op jit(solution)/shard_map/all_gather | solution.py:426
  4460.0 323.0 %all-gather.92.cloned.1.call-start = ((), (), s32[]{:S(2)}) async-start(), calls=%async_computation.86 | async-start | bytes 5242880 | tf_op jit(solution)/shard_map/all_gather | solution.py:426
  4488.3 541.8 %all-reduce.9.cloned.1.call-start = ((), (), s32[]{:S(2)}) async-start(), calls=%async_computation.88 | async-start | bytes 25165824 | tf_op jit(solution)/shard_map/psum | solution.py:434
  4527.3 905.8 %all-reduce.7.cloned.1.call-start = ((), (), s32[]{:S(2)}) async-start(), calls=%async_computation.87 | async-start | bytes 67108864 | tf_op jit(solution)/shard_map/psum | solution.py:449
  (415 other events, 16181.9 us)
Sparse Core Ops, SparseCore 0:
  28.5 78.8 reduce-scatter.28
  192.1 75.4 reduce-scatter.30
  270.4 77.2 reduce-scatter.38
  352.5 46.4 all-gather.33
  408.1 75.4 reduce-scatter.32
  487.3 46.4 all-gather.35
  625.7 79.5 reduce-scatter.36
  706.9 46.4 all-gather.39
  814.9 75.5 reduce-scatter.40
  897.6 46.4 all-gather.41
  1023.9 75.4 reduce-scatter.42
  1101.7 77.2 reduce-scatter.34
  1287.6 75.4 reduce-scatter.44
  1366.0 77.2 reduce-scatter.52
  1448.4 46.4 all-gather.45
  1504.0 75.5 reduce-scatter.46
  1583.2 46.3 all-gather.47
  1761.8 75.2 reduce-scatter.50
  1946.5 75.5 reduce-scatter.54
  2029.2 46.3 all-gather.55
  2152.6 75.5 reduce-scatter.56
  2230.5 77.2 reduce-scatter.48
  2416.2 75.4 reduce-scatter.58
  2494.6 77.2 reduce-scatter.66
  2577.0 46.4 all-gather.59
  2632.6 75.5 reduce-scatter.60
  2711.8 46.3 all-gather.61
  2890.5 75.1 reduce-scatter.64
  2967.3 46.4 all-gather.67
  3075.3 75.5 reduce-scatter.68
  3281.4 75.4 reduce-scatter.70
  3359.4 77.2 reduce-scatter.62
  3449.0 46.3 all-gather.71
  3544.4 75.4 reduce-scatter.72
  3622.8 77.2 reduce-scatter.78
  3760.8 75.5 reduce-scatter.74
  3839.9 46.3 all-gather.75
  3974.7 81.2 reduce-scatter.76
  4057.4 46.4 all-gather.87
  4165.4 75.4 reduce-scatter.80
  4248.0 46.4 all-gather.89
  4371.4 75.5 reduce-scatter.82
  4458.8 81.2 all-gather.77
  4541.6 79.2 all-gather.79
  4622.4 79.2 all-gather.81
  4703.7 79.2 all-gather.91
  4788.1 242.0 all-reduce.8
  5034.5 398.5 all-reduce.6
  (13 shorter events, 589.5 us)
where the time goes:
time: 5480 us; the launch traced here: 5470 us
  waiting for transfers between devices  3620 us (66%)
  matrix products  872 us (16%)
  other arithmetic  576 us (11%)
  local copies, waits for them, and re-layouts  211 us (4%)
  blocking collectives  149 us (3%)
    reduce_scatter x28, waiting for transfers between devices, summed_rows(): lax.psum_scatter(row_term(jnp.int32(0), part_rows * lax.axis_size('tensor...  1960 us
    all_gather x27, waiting for transfers between devices, whole_rows(): return lax.all_gather(part_input, 'tensor', axis=0, tiled=True)  1040 us
    psum x1, waiting for transfers between devices, per_device(): embed_sum, loss_sum = lax.psum((embed_total, loss_total), ('section', 'dp'))  399 us
    dot_general x41, matrix products, matmul(): return jnp.dot(former, latter, preferred_element_type=jnp.float32)  225 us
    scatter-add x4, other arithmetic, per_device(): embed_total.at[jnp.clip(chosen, 0, vocab_rows - 1)]  134 us
    dot_general x14, matrix products, matmul_t(): lax.dot_general(former, latter, (((1,), (1,)), ((), ())), preferred_eleme...  120 us
    psum x1, waiting for transfers between devices, per_device(): lax.psum((layer_totals[0], layer_totals[1], layer_totals[2], layer_totals...  110 us
  transfers between devices with their start and end apart: 64, of which 60 were waited for; matrix products, arithmetic and copies ran while one was open for 12% of the time, Pallas kernels for 0%

commit v1 on v0

v1 whole, which is shorter than its diff:
```python
import functools
import math

import jax
import jax.numpy as jnp
from jax import lax
from jax.experimental import pallas as pl
from jax.experimental.pallas import tpu as pltpu
from jax.sharding import PartitionSpec as P

HEADS = 16
HEAD_DIM = 64
EPS = 1e-05
NEG = -1e30
MESH = pl.DeviceIdType.MESH
F32 = jnp.float32
BF16 = jnp.bfloat16


def matmul(former, latter):
    return jnp.dot(former, latter, preferred_element_type=F32)


def matmul_t(former, latter):
    return lax.dot_general(
        former, latter, (((1,), (1,)), ((), ())), preferred_element_type=F32
    )


def outer_sum(former, latter):
    return lax.dot_general(
        former, latter, (((0,), (0,)), ((), ())), preferred_element_type=F32
    )


def layer_norm(inputs, weight, offset):
    centre = inputs - jnp.mean(inputs, axis=-1, keepdims=True)
    spread = jnp.mean(centre * centre, axis=-1, keepdims=True)
    return centre * lax.rsqrt(spread + EPS) * weight + offset


def gelu_tanh(inputs):
    return jax.nn.gelu(inputs, approximate=True)


class Group:
    def __init__(self, axes, sizes):
        self.axes = axes
        self.sizes = sizes
        self.count = math.prod(sizes)

    def me(self):
        place = 0
        for axis, size in zip(self.axes, self.sizes):
            place = place * size + lax.axis_index(axis)
        return place

    def device(self, place):
        spot = {}
        for axis, size in reversed(list(zip(self.axes, self.sizes))):
            spot[axis] = lax.rem(place, size)
            place = lax.div(place, size)
        return spot

    def peers(self):
        me = self.me()
        return [lax.rem(me + step, self.count) for step in range(1, self.count)]


def greet(groups):
    barrier = pltpu.get_barrier_semaphore()
    total = 0
    for group in groups:
        for peer in group.peers():
            pl.semaphore_signal(
                barrier, inc=1, device_id=group.device(peer), device_id_type=MESH
            )
            total += 1
    pl.semaphore_wait(barrier, total)


def send(group, peer, step, src, dst, send_sem, recv_sem):
    copy = pltpu.make_async_remote_copy(
        src_ref=src,
        dst_ref=dst,
        send_sem=send_sem.at[step],
        recv_sem=recv_sem.at[step],
        device_id=group.device(peer),
        device_id_type=MESH,
    )
    copy.start()
    return copy


def gather_body(group, x_ref, out_ref, local_sem, send_sem, recv_sem):
    me = group.me()
    greet([group])
    copies = [
        send(group, peer, step, x_ref, out_ref.at[me], send_sem, recv_sem)
        for step, peer in enumerate(group.peers())
    ]
    own = pltpu.make_async_copy(x_ref, out_ref.at[me], local_sem)
    own.start()
    for copy in copies:
        copy.wait()
    own.wait()


def gather(group, x, ident):
    if group.count == 1:
        return x[None]
    others = group.count - 1
    return pl.pallas_call(
        functools.partial(gather_body, group),
        out_shape=jax.ShapeDtypeStruct((group.count,) + x.shape, x.dtype),
        in_specs=[pl.BlockSpec(memory_space=pl.ANY)],
        out_specs=pl.BlockSpec(memory_space=pl.ANY),
        scratch_shapes=[
            pltpu.SemaphoreType.DMA,
            pltpu.SemaphoreType.DMA((others,)),
            pltpu.SemaphoreType.DMA((others,)),
        ],
        compiler_params=pltpu.CompilerParams(collective_id=ident, has_side_effects=True),
    )(x)


def scatter_body(group, x_ref, out_ref, own, slots, local_sem, send_sem, recv_sem):
    me = group.me()
    greet([group])
    copies = [
        send(group, peer, step, x_ref.at[peer], slots.at[step], send_sem, recv_sem)
        for step, peer in enumerate(group.peers())
    ]
    kept = pltpu.make_async_copy(x_ref.at[me], own, local_sem)
    kept.start()
    kept.wait()
    for copy in copies:
        copy.wait()
    total = own[...].astype(F32)
    for step in range(group.count - 1):
        total = total + slots[step].astype(F32)
    out_ref[...] = total


def scatter_sum(group, x, ident):
    if group.count == 1:
        return x[0].astype(F32)
    others = group.count - 1
    block = x.shape[1:]
    return pl.pallas_call(
        functools.partial(scatter_body, group),
        out_shape=jax.ShapeDtypeStruct(block, F32),
        in_specs=[pl.BlockSpec(memory_space=pl.ANY)],
        out_specs=pl.BlockSpec(memory_space=pltpu.VMEM),
        scratch_shapes=[
            pltpu.VMEM(block, x.dtype),
            pltpu.VMEM((others,) + block, x.dtype),
            pltpu.SemaphoreType.DMA,
            pltpu.SemaphoreType.DMA((others,)),
            pltpu.SemaphoreType.DMA((others,)),
        ],
        compiler_params=pltpu.CompilerParams(
            collective_id=ident, has_side_effects=True, vmem_limit_bytes=32 * 2**20
        ),
    )(x)


def all_sum_body(groups, x_ref, out_ref, *scratch):
    greet(groups)
    out_ref[...] = x_ref[...]
    count = len(groups)
    for number, group in enumerate(groups):
        kept, slots, send_sem, recv_sem = scratch[4 * number : 4 * number + 4]
        kept[...] = out_ref[...]
        copies = [
            send(group, peer, step, kept, slots.at[step], send_sem, recv_sem)
            for step, peer in enumerate(group.peers())
        ]
        for copy in copies:
            copy.wait()
        me = group.me()
        total = jnp.zeros_like(out_ref)
        for place in range(group.count):
            step = lax.rem(me - place + group.count, group.count) - 1
            term = slots[jnp.maximum(step, 0)]
            total = total + jnp.where(place == me, kept[...], term)
        out_ref[...] = total


def all_sum(groups, x, ident):
    groups = [group for group in groups if group.count > 1]
    scratch = []
    for group in groups:
        others = group.count - 1
        scratch += [
            pltpu.VMEM(x.shape, x.dtype),
            pltpu.VMEM((others,) + x.shape, x.dtype),
            pltpu.SemaphoreType.DMA((others,)),
            pltpu.SemaphoreType.DMA((others,)),
        ]
    return pl.pallas_call(
        functools.partial(all_sum_body, groups),
        out_shape=jax.ShapeDtypeStruct(x.shape, x.dtype),
        in_specs=[pl.BlockSpec(memory_space=pltpu.VMEM)],
        out_specs=pl.BlockSpec(memory_space=pltpu.VMEM),
        scratch_shapes=scratch,
        compiler_params=pltpu.CompilerParams(
            collective_id=ident, has_side_effects=True, vmem_limit_bytes=32 * 2**20
        ),
    )(x)


BLOCK = 256


def masked_scores(queries, keys, slope, length, first):
    rows, cols = queries.shape[0], keys.shape[0]
    raw = matmul_t(queries, keys)
    i = first + lax.broadcasted_iota(jnp.int32, (rows, cols), 0)
    j = lax.broadcasted_iota(jnp.int32, (rows, cols), 1)
    scores = raw * HEAD_DIM ** (-0.5) - slope * (i - j).astype(F32)
    return jnp.where((j <= i) & (j < length), scores, NEG)


def attend_body(length_ref, slope_ref, q_ref, k_ref, v_ref, o_ref, lse_ref):
    seq, width = q_ref.shape
    for head in range(width // HEAD_DIM):
        lanes = slice(head * HEAD_DIM, (head + 1) * HEAD_DIM)
        slope = slope_ref[head]
        keys, values = k_ref[:, lanes], v_ref[:, lanes]
        for first in range(0, seq, BLOCK):
            upto = first + BLOCK
            scores = masked_scores(
                q_ref[first:upto, lanes], keys[:upto], slope, length_ref[0], first
            )
            highest = jnp.max(scores, axis=-1, keepdims=True)
            powers = jnp.exp(scores - highest)
            total = jnp.sum(powers, axis=-1, keepdims=True)
            probs = (powers * (1.0 / total)).astype(BF16)
            o_ref[first:upto, lanes] = matmul(probs, values[:upto]).astype(BF16)
            lse_ref[head, first:upto, :] = highest + jnp.log(total)


def attend(length, slopes, q, k, v):
    seq, width = q.shape
    heads = width // HEAD_DIM
    smem = pl.BlockSpec(memory_space=pltpu.SMEM)
    vmem = pl.BlockSpec(memory_space=pltpu.VMEM)
    return pl.pallas_call(
        attend_body,
        out_shape=(
            jax.ShapeDtypeStruct((seq, width), BF16),
            jax.ShapeDtypeStruct((heads, seq, 1), F32),
        ),
        in_specs=[smem, smem, vmem, vmem, vmem],
        out_specs=(vmem, vmem),
        compiler_params=pltpu.CompilerParams(vmem_limit_bytes=40 * 2**20),
    )(length, slopes, q, k, v)


def attend_back_body(
    length_ref, slope_ref, q_ref, k_ref, v_ref, go_ref, lse_ref, gq_ref, gk_ref, gv_ref
):
    seq, width = q_ref.shape
    gk_ref[...] = jnp.zeros_like(gk_ref)
    gv_ref[...] = jnp.zeros_like(gv_ref)
    for head in range(width // HEAD_DIM):
        lanes = slice(head * HEAD_DIM, (head + 1) * HEAD_DIM)
        slope = slope_ref[head]
        keys, values = k_ref[:, lanes], v_ref[:, lanes]
        for first in range(0, seq, BLOCK):
            upto = first + BLOCK
            queries = q_ref[first:upto, lanes]
            grads = go_ref[first:upto, lanes]
            scores = masked_scores(queries, keys[:upto], slope, length_ref[0], first)
            probs = jnp.exp(scores - lse_ref[head, first:upto, :])
            grad_probs = matmul_t(grads, values[:upto])
            inner = jnp.sum(probs * grad_probs, axis=-1, keepdims=True)
            grad_scores = (probs * (grad_probs - inner) * HEAD_DIM ** (-0.5)).astype(BF16)
            gq_ref[first:upto, lanes] = matmul(grad_scores, keys[:upto])
            gk_ref[:upto, lanes] += outer_sum(grad_scores, queries)
            gv_ref[:upto, lanes] += outer_sum(probs.astype(BF16), grads)


def attend_back(length, slopes, q, k, v, go, lse):
    smem = pl.BlockSpec(memory_space=pltpu.SMEM)
    vmem = pl.BlockSpec(memory_space=pltpu.VMEM)
    return pl.pallas_call(
        attend_back_body,
        out_shape=(jax.ShapeDtypeStruct(q.shape, F32),) * 3,
        in_specs=[smem, smem] + [vmem] * 5,
        out_specs=(vmem,) * 3,
        compiler_params=pltpu.CompilerParams(vmem_limit_bytes=40 * 2**20),
    )(length, slopes, q, k, v, go, lse)


def per_device(
    mesh_shape,
    token_ids,
    target_ids,
    lengths,
    embedding,
    outer_gain,
    outer_bias,
    norm_gain,
    norm_bias,
    qkv_weight,
    qv_bias,
    out_weight,
    up_weight,
    up_bias,
    down_weight,
    row_bias,
):
    sections, groups, shards = (mesh_shape[name] for name in ("section", "dp", "tensor"))
    s, j, z = (lax.axis_index(name) for name in ("section", "dp", "tensor"))
    by_section = Group(("section",), (sections,))
    by_dp = Group(("dp",), (groups,))
    by_tensor = Group(("tensor",), (shards,))
    layers = sections
    vocab, width = embedding.shape
    seq = token_ids.shape[1]
    rows = token_ids.shape[0] * groups
    local_cols = qkv_weight.shape[-1]
    planes = rows == sections * shards and local_cols % (groups * HEAD_DIM) == 0
    team = by_dp if planes else by_tensor
    cut = groups if planes else 1
    part = seq // team.count
    cols = local_cols // cut
    hidden = up_weight.shape[-1] // cut
    cut_index = j if planes else 0
    my_part = j if planes else z
    my_row = z * sections + s if planes else j * sections + s

    if planes:
        both = gather(by_dp, jnp.stack([token_ids, target_ids]), 1)
        both = jnp.swapaxes(both, 0, 1).reshape(2, shards, sections, groups, part)
        both = lax.dynamic_index_in_dim(
            lax.dynamic_index_in_dim(both, s, 2, keepdims=False), j, 2, keepdims=False
        )
        ids, targets = both[0].reshape(-1), both[1].reshape(-1)
        group_lengths = lax.dynamic_index_in_dim(
            lengths.reshape(shards, sections), s, 1, keepdims=False
        )
        places = jnp.broadcast_to(j * part + jnp.arange(part), (shards, part))
        valid = (places < group_lengths[:, None]).reshape(-1)
    else:
        ids, targets = token_ids[s], target_ids[s]
        valid = jnp.arange(seq) < lengths[my_row]
    length = lax.dynamic_slice(lengths, (my_row,), (1,))
    token_count = jnp.sum(lengths).astype(F32)
    vocab_start = z * vocab

    def chosen_cols(array, size):
        piece = lax.dynamic_slice_in_dim(array, cut_index * size, size, array.ndim - 1)
        return jnp.swapaxes(piece, -1, -2)

    def chosen_rows(array, size):
        return lax.dynamic_slice_in_dim(array, cut_index * size, size, 0)

    def spread_weights(piece):
        if planes:
            piece = lax.all_gather(piece, "tensor", axis=0)
        else:
            piece = piece[None]
        return lax.all_gather(piece, "section", axis=0)

    attn_piece = jnp.concatenate(
        [chosen_cols(qkv_weight[0], cols), chosen_rows(out_weight[0], cols)[None]]
    )
    feed_piece = jnp.stack(
        [chosen_cols(up_weight[0], hidden), chosen_rows(down_weight[0], hidden)]
    )
    attn_all = spread_weights(attn_piece)
    feed_all = spread_weights(feed_piece)
    fan = attn_all.shape[1]

    def pad_rows(array, count):
        return jnp.pad(array, ((0, count - array.shape[0]), (0, width - array.shape[1])))

    qv_piece = lax.dynamic_slice_in_dim(qv_bias[0], cut_index * cols, cols, 1)
    up_piece = lax.dynamic_slice_in_dim(up_bias[0], cut_index * hidden, hidden, 0)
    small = jnp.concatenate(
        [
            outer_gain,
            outer_bias,
            norm_gain[0],
            norm_bias[0],
            row_bias[0],
            pad_rows(qv_piece, 2),
            pad_rows(up_piece[None], 6),
        ]
    )
    if planes:
        small_all = gather(Group(("section", "tensor"), (sections, shards)), small, 2)
        small_all = small_all.reshape((sections, shards) + small.shape)
    else:
        small_all = gather(by_section, small, 2)[:, None]
    outer_gains = [small_all[l, 0, 0] for l in range(layers)]
    outer_offsets = [small_all[l, 0, 1] for l in range(layers)]
    params = []
    for l in range(layers):
        attn = jnp.swapaxes(attn_all[l], 0, 1).reshape(4, fan * cols, width)
        feed = jnp.swapaxes(feed_all[l], 0, 1).reshape(2, fan * hidden, width)
        params.append(
            dict(
                gains=small_all[l, 0, 2:4],
                offsets=small_all[l, 0, 4:6],
                row_bias=small_all[l, 0, 6:8],
                q=attn[0],
                k=attn[1],
                v=attn[2],
                o=attn[3],
                up=feed[0],
                down=feed[1],
                q_bias=small_all[l, :, 8, :cols].reshape(-1),
                v_bias=small_all[l, :, 9, :cols].reshape(-1),
                up_bias=small_all[l, :, 10, :hidden].reshape(-1),
            )
        )
    head_number = (
        (jnp.arange(fan)[:, None] if planes else z) * (local_cols // HEAD_DIM)
        + cut_index * (cols // HEAD_DIM)
        + jnp.arange(cols // HEAD_DIM)
    ).reshape(-1)
    slopes = jnp.exp2(-8.0 * (head_number + 1).astype(F32) / HEADS)

    def whole(block):
        return gather(team, block.astype(BF16), 3).reshape(seq, width)

    def summed(terms):
        return scatter_sum(team, terms.astype(BF16).reshape(team.count, part, width), 4)

    local_ids = ids - vocab_start
    inside = (local_ids >= 0) & (local_ids < vocab)
    looked = jnp.where(
        inside[:, None], jnp.take(embedding, jnp.clip(local_ids, 0, vocab - 1), axis=0), 0
    )
    group_part = looked.shape[0] // shards
    x = scatter_sum(by_tensor, looked.reshape(shards, group_part, width), 5)
    h = layer_norm(x, outer_gains[0], outer_offsets[0])

    kept = []
    for p in params:
        normed = whole(layer_norm(h, p["gains"][0], p["offsets"][0]))
        q = (matmul_t(normed, p["q"]) + p["q_bias"]).astype(BF16)
        k = matmul_t(normed, p["k"]).astype(BF16)
        v = (matmul_t(normed, p["v"]) + p["v_bias"]).astype(BF16)
        mixed, lse = attend(length, slopes, q, k, v)
        middle = h + summed(matmul(mixed, p["o"])) + p["row_bias"][0]
        second = whole(layer_norm(middle, p["gains"][1], p["offsets"][1]))
        before = matmul_t(second, p["up"]) + p["up_bias"]
        active = gelu_tanh(before).astype(BF16)
        kept.append((h, normed, q, k, v, mixed, lse, middle, second, before, active))
        h = middle + summed(matmul(active, p["down"])) + p["row_bias"][1]

    final = gather(by_tensor, layer_norm(h, outer_gains[-1], outer_offsets[-1]).astype(BF16), 6)
    final = final.reshape(-1, width)
    tokens = final.shape[0]
    hits = jnp.arange(vocab)[None, :] == (targets - vocab_start)[:, None]
    logits = matmul_t(final, embedding)
    top = jnp.max(logits, axis=-1)
    total = jnp.sum(jnp.exp(logits - top[:, None]), axis=-1)
    pick = jnp.sum(jnp.where(hits, logits, 0.0), axis=-1)
    stats = gather(by_tensor, pad_rows(jnp.stack([top, total, pick]), 8), 7)
    top_all = jnp.max(stats[:, 0], axis=0)
    log_norm = top_all + jnp.log(jnp.sum(stats[:, 1] * jnp.exp(stats[:, 0] - top_all), axis=0))
    terms = jnp.where(valid, log_norm - jnp.sum(stats[:, 2], axis=0), 0.0)
    loss_part = jnp.sum(
        lax.dynamic_index_in_dim(terms.reshape(shards, -1), z, 0, keepdims=False)
    )
    row_weight = jnp.where(valid, 1.0 / token_count, 0.0)
    grad_logits = (
        (jnp.exp(logits - log_norm[:, None]) - hits.astype(F32)) * row_weight[:, None]
    ).astype(BF16)
    grad_final = scatter_sum(
        by_tensor,
        matmul(grad_logits, embedding).astype(BF16).reshape(shards, group_part, width),
        5,
    )
    table = outer_sum(grad_logits, final)
    _, final_back = jax.vjp(layer_norm, h, outer_gains[-1], outer_offsets[-1])
    grad, final_gain, final_offset = final_back(grad_final)

    layer_grads, small_rows = [None] * layers, [None] * layers
    for l in reversed(range(layers)):
        p = params[l]
        section_in, normed, q, k, v, mixed, lse, middle, second, before, active = kept[l]
        grad_down_full = whole(grad)
        g_down = outer_sum(active, grad_down_full)
        _, gelu_back = jax.vjp(gelu_tanh, before)
        grad_before = gelu_back(matmul_t(grad_down_full, p["down"]))[0]
        before_low = grad_before.astype(BF16)
        g_up = outer_sum(before_low, second)
        _, norm_back = jax.vjp(layer_norm, middle, p["gains"][1], p["offsets"][1])
        grad_mid, gain_two, offset_two = norm_back(summed(matmul(before_low, p["up"])))
        grad_mid = grad_mid + grad
        grad_mid_full = whole(grad_mid)
        g_out = outer_sum(mixed, grad_mid_full)
        grad_mixed = matmul_t(grad_mid_full, p["o"]).astype(BF16)
        gq, gk, gv = attend_back(length, slopes, q, k, v, grad_mixed, lse)
        gq_sum, gv_sum = jnp.sum(gq, axis=0), jnp.sum(gv, axis=0)
        gq, gk, gv = gq.astype(BF16), gk.astype(BF16), gv.astype(BF16)
        g_qkvo = [outer_sum(gq, normed), outer_sum(gk, normed), outer_sum(gv, normed), g_out]
        back = matmul(gq, p["q"]) + matmul(gk, p["k"]) + matmul(gv, p["v"])
        _, norm_back = jax.vjp(layer_norm, section_in, p["gains"][0], p["offsets"][0])
        grad_in, gain_one, offset_one = norm_back(summed(back))
        bias_two = jnp.sum(grad, axis=0)
        grad = grad_in + grad_mid
        layer_grads[l] = jnp.concatenate(
            [g.reshape(fan, cols, width) for g in g_qkvo]
            + [g_up.reshape(fan, hidden, width), g_down.reshape(fan, hidden, width)],
            axis=1,
        )

        def placed(values, size, full):
            out = jnp.zeros((fan if planes else shards, cut, size), F32)
            if planes:
                return lax.dynamic_update_slice(
                    out, values.reshape(fan, 1, size), (0, j, 0)
                ).reshape(-1)
            return lax.dynamic_update_slice(
                out, values.reshape(1, 1, size), (z, 0, 0)
            ).reshape(-1)

        small_rows[l] = [
            gain_one[None],
            gain_two[None],
            offset_one[None],
            offset_two[None],
            jnp.sum(grad_mid, axis=0)[None],
            bias_two[None],
            placed(gq_sum, cols, width).reshape(-1, width),
            placed(gv_sum, cols, width).reshape(-1, width),
            placed(jnp.sum(grad_before, axis=0), hidden, width).reshape(-1, width),
        ]

    _, embed_back = jax.vjp(layer_norm, x, outer_gains[0], outer_offsets[0])
    grad_rows, embed_gain, embed_offset = embed_back(grad)
    grad_rows = gather(by_tensor, grad_rows.astype(BF16), 6).reshape(tokens, width)
    table = table.at[jnp.clip(local_ids, 0, vocab - 1)].add(
        jnp.where(inside[:, None], grad_rows.astype(F32), 0.0)
    )

    packed = jnp.concatenate(
        [row for l in range(layers) for row in small_rows[l]]
        + [embed_gain[None], final_gain[None], embed_offset[None], final_offset[None]]
        + [jnp.broadcast_to(loss_part, (1, width))]
    )
    used = packed.shape[0]
    packed = jnp.pad(packed, ((0, -used % 8), (0, 0)))
    packed = all_sum([by_section, by_dp, by_tensor], packed, 8)
    per_layer = (used - 5) // layers
    mine = lax.dynamic_slice_in_dim(packed, s * per_layer, per_layer, 0)
    qv_rows = mine[6:8].reshape(2, -1)
    ff_row = mine[8:].reshape(-1)
    grad_qv = lax.dynamic_slice_in_dim(qv_rows, z * local_cols, local_cols, 1)
    grad_up_bias = lax.dynamic_slice_in_dim(ff_row, z * hidden * cut, hidden * cut, 0)
    base = per_layer * layers
    grad_outer_gain = lax.dynamic_slice_in_dim(packed, base + s, 1, 0)
    grad_outer_bias = lax.dynamic_slice_in_dim(packed, base + 2 + s, 1, 0)
    loss = packed[base + 4, 0] / token_count

    layer_sum = lax.psum_scatter(
        jnp.stack(layer_grads), "section", scatter_dimension=0, tiled=False
    )
    if planes:
        layer_sum = lax.psum_scatter(
            layer_sum.astype(BF16), "tensor", scatter_dimension=0, tiled=False
        )
        layer_sum = lax.all_gather(layer_sum, "dp", axis=0)
    else:
        layer_sum = lax.psum(layer_sum.astype(BF16), "dp")
    layer_sum = layer_sum.astype(F32)

    def as_cols(array):
        return jnp.moveaxis(array, 0, -2).swapaxes(-1, -3).swapaxes(-1, -2)

    def columns(array):
        return array.reshape(-1, width).T

    grad_qkv = jnp.stack(
        [columns(layer_sum[:, i * cols : (i + 1) * cols]) for i in range(3)]
    )
    grad_out_mat = layer_sum[:, 3 * cols : 4 * cols].reshape(-1, width)
    grad_up = columns(layer_sum[:, 4 * cols : 4 * cols + hidden])
    grad_down = layer_sum[:, 4 * cols + hidden :].reshape(-1, width)
    embed_sum = lax.psum(table.astype(BF16), ("section", "dp")).astype(F32)
    return (
        loss,
        embed_sum,
        grad_outer_gain,
        grad_outer_bias,
        mine[0:2][None],
        mine[2:4][None],
        grad_qkv[None],
        grad_qv[None],
        grad_out_mat[None],
        grad_up[None],
        grad_up_bias[None],
        grad_down[None],
        mine[4:6][None],
    )


def solution(mesh):
    return jax.shard_map(
        functools.partial(per_device, dict(mesh.shape)),
        mesh=mesh,
        in_specs=(
            P("dp", None),
            P("dp", None),
            P(),
            P("tensor", None),
            P("section", None),
            P("section", None),
            P("section", None, None),
            P("section", None, None),
            P("section", None, None, "tensor"),
            P("section", None, "tensor"),
            P("section", "tensor", None),
            P("section", None, "tensor"),
            P("section", "tensor"),
            P("section", "tensor", None),
            P("section", None, None),
        ),
        out_specs=(
            P(),
            P("tensor", None),
            P("section", None),
            P("section", None),
            P("section", None, None),
            P("section", None, None),
            P("section", None, None, "tensor"),
            P("section", None, "tensor"),
            P("section", "tensor", None),
            P("section", None, "tensor"),
            P("section", "tensor"),
            P("section", "tensor", None),
            P("section", None, None),
        ),
        check_vma=False,
    )
```

time: 5480 us -> 1610 us (0.29)
  waiting for transfers between devices: 3620 us -> 410 us
  Pallas kernels: 0 us -> 737 us
  matrix products: 872 us -> 161 us
  other arithmetic: 576 us -> 169 us
  blocking collectives: 149 us -> 0 us
  local copies, waits for them, and re-layouts: 211 us -> 111 us
    reduce_scatter x28 -> x2, waiting for transfers between devices: 1960 us -> 45.8 us  [the longest x1 45.8 us: per_device(): lax.psum_scatter(jnp.stack(layer_grads), 'section', scatter_dimension=0,...]
    all_gather x31 -> x5, waiting for transfers between devices: 1140 us -> 174 us  [the longest x2 122 us: spread_weights(): piece = lax.all_gather(piece, 'tensor', axis=0)]
    pallas_call x0 -> x28, Pallas kernels: none -> 737 us  [the longest x13 353 us: gather(): pl.pallas_call(functools.partial(gather_body, group), out_shape=jax.Shape...]
    dot_general x80 -> x13, matrix products: 648 us -> 46.2 us  [matmul(): return jnp.dot(former, latter, preferred_element_type=F32)]
    psum x2 -> x1, waiting for transfers between devices: 510 us -> 189 us  [per_device(): embed_sum = lax.psum(table.astype(BF16), ('section', 'dp')).astype(F32)]
    psum x7 -> x0, blocking collectives: 118 us -> none  [the longest x1 61.1 us: per_device(): lax.psum((norm_totals[0], norm_totals[1], norm_totals[2], outer_gain_tota...]
    scatter-add x4 -> x1, other arithmetic: 134 us -> 32.1 us  [per_device(): table.at[jnp.clip(local_ids, 0, vocab - 1)]]
    reduce_sum x24 -> x11, other arithmetic: 125 us -> 33.6 us  [the longest x1 16.5 us: per_device(): total = jnp.sum(jnp.exp(logits - top[:, None]), axis=-1)]
  transfers between devices with their start and end apart: 64 -> 8, of which waited for: 60 -> 5; matrix products, arithmetic and copies ran while one was open for 12% -> 9% of each run, Pallas kernels for 0% -> 19%
where the time goes in v1:
time: 1610 us
  Pallas kernels  737 us (46%)
  waiting for transfers between devices  410 us (25%)
  other arithmetic  169 us (10%)
  matrix products  161 us (10%)
  local copies, waits for them, and re-layouts  111 us (7%)
  between operations  19.4 us (1%)
    pallas_call x13, Pallas kernels, gather(): pl.pallas_call(functools.partial(gather_body, group), out_shape=jax.Shape...  353 us
    pallas_call x10, Pallas kernels, scatter_sum(): pl.pallas_call(functools.partial(scatter_body, group), out_shape=jax.Shap...  273 us
    psum x1, waiting for transfers between devices, per_device(): embed_sum = lax.psum(table.astype(BF16), ('section', 'dp')).astype(F32)  189 us
    all_gather x2, waiting for transfers between devices, spread_weights(): piece = lax.all_gather(piece, 'tensor', axis=0)  122 us
    dot_general x13, matrix products, matmul_t(): lax.dot_general(former, latter, (((1,), (1,)), ((), ())), preferred_eleme...  68.8 us
    pallas_call x1, Pallas kernels, all_sum(): pl.pallas_call(functools.partial(all_sum_body, groups), out_shape=jax.Sha...  61.5 us
    all_gather x1, waiting for transfers between devices, per_device(): layer_sum = lax.all_gather(layer_sum, 'dp', axis=0)  52.9 us
    dot_general x13, matrix products, matmul(): return jnp.dot(former, latter, preferred_element_type=F32)  46.2 us
  transfers between devices with their start and end apart: 8, of which 5 were waited for; matrix products, arithmetic and copies ran while one was open for 9% of the time, Pallas kernels for 19%

profile of v1, /device:TPU:1, one launch (start us, length us, event | category | flops | bytes accessed | tf_op | source)
XLA Modules:
  0.0 1607.9 jit_solution(328516093285856190)
XLA Ops:
  13.5 45.6 %all-gather.12.cloned.1.call-done = bf16[16,64,1024]{2,1,0:T(8,128)(2,1)} async-done(((bf16[4,64,1024]{2,1,0:T(8,128)(2,1)}), bf16[16,64,1024]{2,1,0:T(8,128)(2,1)}) %all-gather.12.cloned.1.call-update) | async-done | bytes 2097168 | tf_op jit(solution)/shard_map/all_gather | solution.py:363
  64.7 76.0 %all-gather.16.cloned.1.call-done = bf16[8,256,1024]{2,1,0:T(8,128)(2,1)} async-done(((bf16[2,256,1024]{2,1,0:T(8,128)(2,1)}), bf16[8,256,1024]{2,1,0:T(8,128)(2,1)}) %all-gather.16.cloned.1.call-update) | async-done | bytes 4194320 | tf_op jit(solution)/shard_map/all_gather | solution.py:363
  142.2 13.3 gather_fusion
  156.0 36.7 %shard_map.247 = f32[256,1024]{1,0:T(8,128)S(1)} custom-call(bf16[4,256,1024]{2,1,0:T(8,128)(2,1)S(1)} %select_select_fusion.x_ref), custom_call_target="tpu_custom_call" | custom-call | tf_op jit(solution)/shard_map/pallas_call | solution.py:150
  194.8 25.2 %shard_map.248 = f32[8,16,1024]{2,1,0:T(8,128)} custom-call(f32[16,1024]{1,0:T(8,128)} %concatenate.15.x_ref), custom_call_target="tpu_custom_call" | custom-call | tf_op jit(solution)/shard_map/pallas_call | solution.py:113
  224.9 26.3 %shard_map.249 = bf16[4,256,1024]{2,1,0:T(8,128)(2,1)} custom-call(bf16[256,1024]{1,0:T(8,128)(2,1)} %add_convert_fusion.7.x_ref), custom_call_target="tpu_custom_call" | custom-call | tf_op jit(solution)/shard_map/pallas_call | solution.py:113
  264.7 10.5 shard_map.250
  276.0 25.6 %shard_map.251 = f32[256,1024]{1,0:T(8,128)S(1)} custom-call(bf16[4,256,1024]{2,1,0:T(8,128)(2,1)S(1)} %bitcast.342), custom_call_target="tpu_custom_call" | custom-call | tf_op jit(solution)/shard_map/pallas_call | solution.py:150
  303.4 24.6 %shard_map.252 = bf16[4,256,1024]{2,1,0:T(8,128)(2,1)} custom-call(bf16[256,1024]{1,0:T(8,128)(2,1)} %add_convert_fusion.6.x_ref), custom_call_target="tpu_custom_call" | custom-call | tf_op jit(solution)/shard_map/pallas_call | solution.py:113
  355.4 24.5 %shard_map.253 = f32[256,1024]{1,0:T(8,128)S(1)} custom-call(bf16[4,256,1024]{2,1,0:T(8,128)(2,1)S(1)} %bitcast.348), custom_call_target="tpu_custom_call" | custom-call | tf_op jit(solution)/shard_map/pallas_call | solution.py:150
  381.5 24.6 %shard_map.254 = bf16[4,256,1024]{2,1,0:T(8,128)(2,1)} custom-call(bf16[256,1024]{1,0:T(8,128)(2,1)} %add_convert_fusion.5.x_ref), custom_call_target="tpu_custom_call" | custom-call | tf_op jit(solution)/shard_map/pallas_call | solution.py:113
  410.7 10.1 shard_map.255
  421.5 24.5 %shard_map.256 = f32[256,1024]{1,0:T(8,128)S(1)} custom-call(bf16[4,256,1024]{2,1,0:T(8,128)(2,1)S(1)} %bitcast.343), custom_call_target="tpu_custom_call" | custom-call | tf_op jit(solution)/shard_map/pallas_call | solution.py:150
  447.6 24.6 %shard_map.257 = bf16[4,256,1024]{2,1,0:T(8,128)(2,1)} custom-call(bf16[256,1024]{1,0:T(8,128)(2,1)} %add_convert_fusion.4.x_ref), custom_call_target="tpu_custom_call" | custom-call | tf_op jit(solution)/shard_map/pallas_call | solution.py:113
  472.1 6.5 broadcast_add_fusion
  489.6 24.5 %shard_map.258 = f32[256,1024]{1,0:T(8,128)S(1)} custom-call(bf16[4,256,1024]{2,1,0:T(8,128)(2,1)S(1)} %bitcast.349), custom_call_target="tpu_custom_call" | custom-call | tf_op jit(solution)/shard_map/pallas_call | solution.py:150
  516.3 39.0 %shard_map.259 = bf16[4,256,1024]{2,1,0:T(8,128)(2,1)} custom-call(bf16[256,1024]{1,0:T(8,128)(2,1)} %add_convert_fusion.3.x_ref), custom_call_target="tpu_custom_call" | custom-call | tf_op jit(solution)/shard_map/pallas_call | solution.py:113
  555.3 26.3 %fusion.124 = (f32[1024]{0:T(1024)S(1)}, f32[1024,8192]{1,0:T(8,128)}) fusion(bf16[1024,1024]{1,0:T(8,128)(2,1)} %bitcast.383, bf16[8192,1024]{1,0:T(8,128)(2,1)} %param.18), kind=kOutput, calls=%fused_computation.292 | convolution fusion | flops 17188257792 | bytes 52432896 | tf_op jit(solution)/shard_map/dot_general | solution.py:25
  581.6 16.5 %exponential_reduce_fusion = (f32[1024]{0:T(1024)S(1)}, f32[1024]{0:T(1024)S(1)}) fusion(f32[1024,8192]{1,0:T(8,128)} %get-tuple-element.158, f32[1024]{0:T(1024)S(1)} %get-tuple-element.157, s32[1024]{0:T(1024)S(1)} %bitcast.466), kind=kLoop, calls=%fused_computation.5 | loop fusion | flops 41940992 | bytes 33570816 | tf_op jit(solution)/shard_map/reduce_sum | solution.py:463
  598.7 15.3 shard_map.260
  615.8 15.6 multiply_convert_fusion
  631.4 23.7 %convolution_convert_fusion = bf16[1024,1024]{1,0:T(8,128)(2,1)S(1)} fusion(bf16[1024,8192]{1,0:T(8,128)(2,1)S(1)} %multiply_convert_fusion, bf16[8192,1024]{1,0:T(8,128)(2,1)} %param.18), kind=kOutput, calls=%fused_computation.90 | convolution fusion | flops 17180917760 | bytes 35651584 | tf_op jit(solution)/shard_map/dot_general | solution.py:21
  655.1 36.6 %shard_map.261 = f32[256,1024]{1,0:T(8,128)S(1)} custom-call(bf16[4,256,1024]{2,1,0:T(8,128)(2,1)S(1)} %bitcast.350), custom_call_target="tpu_custom_call" | custom-call | tf_op jit(solution)/shard_map/pallas_call | solution.py:150
  695.7 24.6 %shard_map.262 = bf16[4,256,1024]{2,1,0:T(8,128)(2,1)} custom-call(bf16[256,1024]{1,0:T(8,128)(2,1)} %get-tuple-element.121.x_ref), custom_call_target="tpu_custom_call" | custom-call | tf_op jit(solution)/shard_map/pallas_call | solution.py:113
  720.2 11.4 fusion.27
  737.1 6.0 fusion.100
  745.4 24.5 %shard_map.263 = f32[256,1024]{1,0:T(8,128)S(1)} custom-call(bf16[4,256,1024]{2,1,0:T(8,128)(2,1)S(1)} %bitcast.346), custom_call_target="tpu_custom_call" | custom-call | tf_op jit(solution)/shard_map/pallas_call | solution.py:150
  773.9 24.6 %shard_map.264 = bf16[4,256,1024]{2,1,0:T(8,128)(2,1)} custom-call(bf16[256,1024]{1,0:T(8,128)(2,1)} %convert_element_type.191.x_ref), custom_call_target="tpu_custom_call" | custom-call | tf_op jit(solution)/shard_map/pallas_call | solution.py:113
  801.1 14.9 shard_map.265
  822.1 24.5 %shard_map.266 = f32[256,1024]{1,0:T(8,128)S(1)} custom-call(bf16[4,256,1024]{2,1,0:T(8,128)(2,1)S(1)} %bitcast.344), custom_call_target="tpu_custom_call" | custom-call | tf_op jit(solution)/shard_map/pallas_call | solution.py:150
  849.6 24.6 %shard_map.267 = bf16[4,256,1024]{2,1,0:T(8,128)(2,1)} custom-call(bf16[256,1024]{1,0:T(8,128)(2,1)} %convert_element_type.197.x_ref), custom_call_target="tpu_custom_call" | custom-call | tf_op jit(solution)/shard_map/pallas_call | solution.py:113
  874.2 9.0 fusion.31
  896.4 24.5 %shard_map.268 = f32[256,1024]{1,0:T(8,128)S(1)} custom-call(bf16[4,256,1024]{2,1,0:T(8,128)(2,1)S(1)} %bitcast.347), custom_call_target="tpu_custom_call" | custom-call | tf_op jit(solution)/shard_map/pallas_call | solution.py:150
  922.9 24.6 %shard_map.269 = bf16[4,256,1024]{2,1,0:T(8,128)(2,1)} custom-call(bf16[256,1024]{1,0:T(8,128)(2,1)} %convert_element_type.200.x_ref), custom_call_target="tpu_custom_call" | custom-call | tf_op jit(solution)/shard_map/pallas_call | solution.py:113
  950.1 14.9 shard_map.270
  1000.7 8.8 pad_maximum_fusion
  1009.6 45.8 %reduce-scatter.3.cloned.1.call-done = f32[1,4,768,1024]{3,2,1,0:T(8,128)} async-done(((f32[2,4,768,1024]{3,2,1,0:T(8,128)}), f32[1,4,768,1024]{3,2,1,0:T(8,128)}) %reduce-scatter.3.cloned.1.call-update) | async-done | bytes 12582928 | tf_op jit(solution)/shard_map/reduce_scatter | solution.py:564
  1055.4 8.2 convert_bitcast_fusion
  1068.0 26.9 %shard_map.271 = f32[256,1024]{1,0:T(8,128)S(1)} custom-call(bf16[4,256,1024]{2,1,0:T(8,128)(2,1)S(1)} %bitcast.345), custom_call_target="tpu_custom_call" | custom-call | tf_op jit(solution)/shard_map/pallas_call | solution.py:150
  1098.2 71.0 %shard_map.273 = bf16[4,256,1024]{2,1,0:T(8,128)(2,1)} custom-call(bf16[256,1024]{1,0:T(8,128)(2,1)} %add_convert_fusion.2.x_ref), custom_call_target="tpu_custom_call" | custom-call | tf_op jit(solution)/shard_map/pallas_call | solution.py:113
  1169.2 28.4 %fusion.125 = f32[8192,1024]{1,0:T(8,128)} fusion(bf16[1024,8192]{1,0:T(8,128)(2,1)} %copy-done.32, bf16[1024,1024]{1,0:T(8,128)(2,1)} %bitcast.384), kind=kOutput, calls=%fused_computation.293 | convolution fusion | flops 17179869184 | bytes 52428800 | tf_op jit(solution)/shard_map/dot_general | solution.py:31
  1197.6 32.1 %scatter_custom_fusion = f32[8192,1024]{1,0:T(8,128)} fusion(f32[8192,1024]{1,0:T(8,128)} %fusion.125, s32[1024]{0:T(1024)} %bitcast.496, bf16[1024,1024]{1,0:T(8,128)(2,1)S(1)} %bitcast.368, f32[]{:T(128)} %constant.148.clone.1, pred[1024]{0:T(1024)(128)(4,1)S(1)} %and.28), kind=kCustom, calls=%fused_computation.45 | custom fusion | flops 3145728 | bytes 35653120 | tf_op jit(solution)/shard_map/scatter-add | solution.py:541
  1229.7 17.5 %convert_element_type.209 = bf16[8192,1024]{1,0:T(8,128)(2,1)} convert(f32[8192,1024]{1,0:T(8,128)} %scatter_custom_fusion) | non-fusion elementwise | flops 8388608 | bytes 50331648 | tf_op jit(solution)/shard_map/convert_element_type | solution.py:588
  1250.7 61.5 %shard_map.272 = f32[32,1024]{1,0:T(8,128)S(1)} custom-call(f32[32,1024]{1,0:T(8,128)S(1)} %pad.19.x_ref), custom_call_target="tpu_custom_call" | custom-call | tf_op jit(solution)/shard_map/pallas_call | solution.py:201
  1315.9 188.9 %all-reduce.6.cloned.1.call-done = bf16[8192,1024]{1,0:T(8,128)(2,1)} async-done(((bf16[8192,1024]{1,0:T(8,128)(2,1)}), bf16[8192,1024]{1,0:T(8,128)(2,1)}) %all-reduce.6.cloned.1.call-update) | async-done | bytes 16777232 | tf_op jit(solution)/shard_map/psum | solution.py:588
  1504.8 19.0 %convert_element_type.210 = f32[8192,1024]{1,0:T(8,128)} convert(bf16[8192,1024]{1,0:T(8,128)(2,1)} %all-reduce.6.cloned.1.call-done) | non-fusion elementwise | flops 8388608 | bytes 50331648 | tf_op jit(solution)/shard_map/convert_element_type | solution.py:588
  1523.9 52.9 %all-gather.10.cloned.1.call-done = bf16[4,768,1024]{2,1,0:T(8,128)(2,1)} async-done(((bf16[1,768,1024]{2,1,0:T(8,128)(2,1)}), bf16[4,768,1024]{2,1,0:T(8,128)(2,1)}) %all-gather.10.cloned.1.call-update) | async-done | bytes 6291472 | tf_op jit(solution)/shard_map/all_gather | solution.py:571
  1576.7 6.6 fusion.115
  (497 shorter events, 197.4 us)
Async XLA Ops:
  7.2 51.8 %all-gather.12.cloned.1.call-start = ((), (), s32[]{:S(2)}) async-start(), calls=%async_computation.6 | async-start | bytes 2621440 | tf_op jit(solution)/shard_map/all_gather | solution.py:363
  10.9 129.8 %all-gather.16.cloned.1.call-start = ((), (), s32[]{:S(2)}) async-start(), calls=%async_computation.8 | async-start | bytes 5242880 | tf_op jit(solution)/shard_map/all_gather | solution.py:363
  10.9 48.2 %copy-start.123 = (s32[2,1024]{1,0:T(2,128)S(1)}, s32[2,1024]{1,0:T(2,128)}, u32[]{:S(2)}) copy-start(s32[2,1024]{1,0:T(2,128)} %param.16) | copy-start | bytes 24580
  10.9 48.2 %copy-start.124 = (s32[2,1024]{1,0:T(2,128)S(1)}, s32[2,1024]{1,0:T(2,128)}, u32[]{:S(2)}) copy-start(s32[2,1024]{1,0:T(2,128)} %param.15) | copy-start | bytes 24580
  13.4 127.4 %copy-start.130 = (s32[8]{0:T(128)S(1)}, s32[8]{0:T(128)}, u32[]{:S(2)}) copy-start(s32[8]{0:T(128)} %param.17) | copy-start | bytes 100
  13.4 241.9 %all-gather.14.cloned.1.call-start = ((), (), s32[]{:S(2)}) async-start(), calls=%async_computation.7 | async-start | bytes 6291456 | tf_op jit(solution)/shard_map/all_gather | solution.py:366
  59.1 272.7 %all-gather.18.cloned.1.call-start = ((), (), s32[]{:S(2)}) async-start(), calls=%async_computation.9 | async-start | bytes 12582912 | tf_op jit(solution)/shard_map/all_gather | solution.py:366
  140.7 914.7 %reduce-scatter.3.cloned.1.call-start = ((), (), s32[]{:S(2)}) async-start(), calls=%async_computation.3 | async-start | bytes 37748736 | tf_op jit(solution)/shard_map/reduce_scatter | solution.py:564
  155.4 38.0 %copy-start.131 = (f32[1,2,256]{2,1,0:T(2,128)S(1)}, f32[1,2,256]{2,1,0:T(2,128)}, u32[]{:S(2)}) copy-start(f32[1,2,256]{2,1,0:T(2,128)} %param.24) | copy-start | bytes 6148
  155.4 38.1 %copy-start.120 = (f32[1,2,1024]{2,1,0:T(2,128)S(1)}, f32[1,2,1024]{2,1,0:T(2,128)}, u32[]{:S(2)}) copy-start(f32[1,2,1024]{2,1,0:T(2,128)} %param.21) | copy-start | bytes 24580
  155.5 38.1 %copy-start.121 = (f32[1,2,1024]{2,1,0:T(2,128)S(1)}, f32[1,2,1024]{2,1,0:T(2,128)}, u32[]{:S(2)}) copy-start(f32[1,2,1024]{2,1,0:T(2,128)} %param.22) | copy-start | bytes 24580
  155.5 38.1 %copy-start.122 = (f32[1,2,1024]{2,1,0:T(2,128)S(1)}, f32[1,2,1024]{2,1,0:T(2,128)}, u32[]{:S(2)}) copy-start(f32[1,2,1024]{2,1,0:T(2,128)} %param.29) | copy-start | bytes 24580
  155.5 38.1 %copy-start.125 = (f32[1,1024]{1,0:T(1,128)S(1)}, f32[1,1024]{1,0:T(1,128)}, u32[]{:S(2)}) copy-start(f32[1,1024]{1,0:T(1,128)} %param.19) | copy-start | bytes 12292
  155.5 38.1 %copy-start.126 = (f32[1,1024]{1,0:T(1,128)S(1)}, f32[1,1024]{1,0:T(1,128)}, u32[]{:S(2)}) copy-start(f32[1,1024]{1,0:T(1,128)} %param.20) | copy-start | bytes 12292
  192.7 108.9 %copy-start.2 = (f32[256,1024]{1,0:T(8,128)}, f32[256,1024]{1,0:T(8,128)S(1)}, u32[]{:S(2)}) copy-start(f32[256,1024]{1,0:T(8,128)S(1)} %shard_map.247) | copy-start | bytes 3145732
  220.2 81.4 %copy-start.78 = (f32[256]{0:T(256)}, f32[256]{0:T(256)S(1)}, u32[]{:S(2)}) copy-start(f32[256]{0:T(256)S(1)} %broadcast_multiply_fusion.5) | copy-start | bytes 3076
  221.0 80.6 %copy-start.80 = (f32[256]{0:T(256)}, f32[256]{0:T(256)S(1)}, u32[]{:S(2)}) copy-start(f32[256]{0:T(256)S(1)} %fusion.82) | copy-start | bytes 3076
  222.6 35.5 %copy-start.82 = (f32[1,1,1,1024]{3,2,1,0:T(1,128)}, f32[1,1,1,1024]{3,2,1,0:T(1,128)S(1)}, u32[]{:S(2)}) copy-start(f32[1,1,1,1024]{3,2,1,0:T(1,128)S(1)} %get-tuple-element.143) | copy-start | bytes 12292
  222.6 79.0 %copy-start.72 = (f32[1,1,1,1024]{3,2,1,0:T(1,128)}, f32[1,1,1,1024]{3,2,1,0:T(1,128)S(1)}, u32[]{:S(2)}) copy-start(f32[1,1,1,1024]{3,2,1,0:T(1,128)S(1)} %get-tuple-element.145) | copy-start | bytes 12292
  222.6 79.0 %copy-start.74 = (f32[1,1,1,1024]{3,2,1,0:T(1,128)}, f32[1,1,1,1024]{3,2,1,0:T(1,128)S(1)}, u32[]{:S(2)}) copy-start(f32[1,1,1,1024]{3,2,1,0:T(1,128)S(1)} %get-tuple-element.144) | copy-start | bytes 12292
  222.6 79.7 %copy-start.84 = (f32[1,1,1,1024]{3,2,1,0:T(1,128)}, f32[1,1,1,1024]{3,2,1,0:T(1,128)S(1)}, u32[]{:S(2)}) copy-start(f32[1,1,1,1024]{3,2,1,0:T(1,128)S(1)} %get-tuple-element.139) | copy-start | bytes 12292
  222.6 157.8 %copy-start.86 = (f32[1,1,1,1024]{3,2,1,0:T(1,128)}, f32[1,1,1,1024]{3,2,1,0:T(1,128)S(1)}, u32[]{:S(2)}) copy-start(f32[1,1,1,1024]{3,2,1,0:T(1,128)S(1)} %get-tuple-element.136) | copy-start | bytes 12292
  223.0 35.1 %copy-start.88 = (f32[256]{0:T(256)}, f32[256]{0:T(256)S(1)}, u32[]{:S(2)}) copy-start(f32[256]{0:T(256)S(1)} %broadcast_multiply_fusion.4) | copy-start | bytes 3076
  223.4 29.6 %copy-start.114 = (f32[256]{0:T(256)}, f32[256]{0:T(256)S(1)}, u32[]{:S(2)}) copy-start(f32[256]{0:T(256)S(1)} %multiply_reduce_fusion.16) | copy-start | bytes 3076
  223.4 34.7 %copy-start.103 = (f32[256]{0:T(256)}, f32[256]{0:T(256)S(1)}, u32[]{:S(2)}) copy-start(f32[256]{0:T(256)S(1)} %fusion.83) | copy-start | bytes 3076
  254.5 156.1 %copy-start.19 = (f32[4]{0:T(128)}, f32[4]{0:T(128)S(1)}, u32[]{:S(2)}) copy-start(f32[4]{0:T(128)S(1)} %multiply_exponential_fusion.slope_ref) | copy-start | bytes 52
  264.7 37.3 %copy-start.10 = (bf16[1024,256]{1,0:T(8,128)(2,1)}, bf16[1024,256]{1,0:T(8,128)(2,1)S(1)}, u32[]{:S(2)}) copy-start(bf16[1024,256]{1,0:T(8,128)(2,1)S(1)} %fusion.59.q_ref) | copy-start | bytes 1572868
  302.0 77.9 %copy-start.21 = (f32[256,1024]{1,0:T(8,128)}, f32[256,1024]{1,0:T(8,128)S(1)}, u32[]{:S(2)}) copy-start(f32[256,1024]{1,0:T(8,128)S(1)} %get-tuple-element.93) | copy-start | bytes 3145732
  331.7 77.0 %copy-start.55 = (bf16[1,4,64,1024]{3,2,1,0:T(8,128)(2,1)}, bf16[1,4,64,1024]{3,2,1,0:T(8,128)(2,1)S(1)}, u32[]{:S(2)}) copy-start(bf16[1,4,64,1024]{3,2,1,0:T(8,128)(2,1)S(1)} %get-tuple-element.113) | copy-start | bytes 1572868
  331.7 89.1 %copy-start.59 = (bf16[1,4,64,1024]{3,2,1,0:T(8,128)(2,1)}, bf16[1,4,64,1024]{3,2,1,0:T(8,128)(2,1)S(1)}, u32[]{:S(2)}) copy-start(bf16[1,4,64,1024]{3,2,1,0:T(8,128)(2,1)S(1)} %get-tuple-element.112) | copy-start | bytes 1572868
  380.2 28.5 %copy-start.23 = (f32[256,1024]{1,0:T(8,128)}, f32[256,1024]{1,0:T(8,128)S(1)}, u32[]{:S(2)}) copy-start(f32[256,1024]{1,0:T(8,128)S(1)} %get-tuple-element.91) | copy-start | bytes 3145732
  380.2 28.4 %copy-start.92 = (f32[256]{0:T(256)}, f32[256]{0:T(256)S(1)}, u32[]{:S(2)}) copy-start(f32[256]{0:T(256)S(1)} %broadcast_multiply_fusion.2) | copy-start | bytes 3076
  380.5 28.2 %copy-start.118 = (f32[256]{0:T(256)}, f32[256]{0:T(256)S(1)}, u32[]{:S(2)}) copy-start(f32[256]{0:T(256)S(1)} %multiply_reduce_fusion.14) | copy-start | bytes 3076
  380.5 28.2 %copy-start.107 = (f32[256]{0:T(256)}, f32[256]{0:T(256)S(1)}, u32[]{:S(2)}) copy-start(f32[256]{0:T(256)S(1)} %fusion.85) | copy-start | bytes 3076
  410.7 35.5 %copy-start.16 = (bf16[1024,256]{1,0:T(8,128)(2,1)}, bf16[1024,256]{1,0:T(8,128)(2,1)S(1)}, u32[]{:S(2)}) copy-start(bf16[1024,256]{1,0:T(8,128)(2,1)S(1)} %fusion.61.q_ref) | copy-start | bytes 1572868
  410.7 35.3 %copy-start.24 = (f32[256,1024]{1,0:T(8,128)S(1)}, f32[256,1024]{1,0:T(8,128)}, u32[]{:S(2)}) copy-start(f32[256,1024]{1,0:T(8,128)} %copy-done.23) | copy-start | bytes 3145732
  631.4 60.3 %copy-start.27 = (f32[256,1024]{1,0:T(8,128)S(1)}, f32[256,1024]{1,0:T(8,128)}, u32[]{:S(2)}) copy-start(f32[256,1024]{1,0:T(8,128)} %copy-done.26) | copy-start | bytes 3145732
  921.9 28.1 %copy-start.37 = (f32[256,1024]{1,0:T(8,128)}, f32[256,1024]{1,0:T(8,128)S(1)}, u32[]{:S(2)}) copy-start(f32[256,1024]{1,0:T(8,128)S(1)} %get-tuple-element.75) | copy-start | bytes 3145732
  1009.5 237.9 %reduce-scatter.5.cloned.1.call-start = ((), (), s32[]{:S(2)}) async-start(), calls=%async_computation.4 | async-start | bytes 7864320 | tf_op jit(solution)/shard_map/reduce_scatter | solution.py:568
  1063.7 441.2 %all-reduce.6.cloned.1.call-start = ((), (), s32[]{:S(2)}) async-start(), calls=%async_computation.2 | async-start | bytes 33554432 | tf_op jit(solution)/shard_map/psum | solution.py:588
  1067.2 27.7 %copy-start.79 = (f32[256]{0:T(256)S(1)}, f32[256]{0:T(256)}, u32[]{:S(2)}) copy-start(f32[256]{0:T(256)} %copy-done.78) | copy-start | bytes 3076
  1067.2 27.7 %copy-start.81 = (f32[256]{0:T(256)S(1)}, f32[256]{0:T(256)}, u32[]{:S(2)}) copy-start(f32[256]{0:T(256)} %copy-done.80) | copy-start | bytes 3076
  1067.2 27.7 %copy-start.83 = (f32[1,1,1,1024]{3,2,1,0:T(1,128)S(1)}, f32[1,1,1,1024]{3,2,1,0:T(1,128)}, u32[]{:S(2)}) copy-start(f32[1,1,1,1024]{3,2,1,0:T(1,128)} %copy-done.82) | copy-start | bytes 12292
  1067.2 27.7 %copy-start.89 = (f32[256]{0:T(256)S(1)}, f32[256]{0:T(256)}, u32[]{:S(2)}) copy-start(f32[256]{0:T(256)} %copy-done.88) | copy-start | bytes 3076
  1067.2 27.7 %copy-start.104 = (f32[256]{0:T(256)S(1)}, f32[256]{0:T(256)}, u32[]{:S(2)}) copy-start(f32[256]{0:T(256)} %copy-done.103) | copy-start | bytes 3076
  1068.0 28.2 %copy-start.38 = (f32[256,1024]{1,0:T(8,128)S(1)}, f32[256,1024]{1,0:T(8,128)}, u32[]{:S(2)}) copy-start(f32[256,1024]{1,0:T(8,128)} %copy-done.37) | copy-start | bytes 3145732
  1169.2 28.4 %copy-start.39 = (bf16[4,256,1024]{2,1,0:T(8,128)(2,1)S(1)}, bf16[4,256,1024]{2,1,0:T(8,128)(2,1)}, u32[]{:S(2)}) copy-start(bf16[4,256,1024]{2,1,0:T(8,128)(2,1)} %shard_map.273) | copy-start | bytes 6291460
  1247.4 329.4 %all-gather.10.cloned.1.call-start = ((), (), s32[]{:S(2)}) async-start(), calls=%async_computation.5 | async-start | bytes 7864320 | tf_op jit(solution)/shard_map/all_gather | solution.py:571
  (96 other events, 961.2 us)
Sparse Core Ops, SparseCore 0:
  11.0 48.0 all-gather.11
  61.2 79.4 all-gather.15
  142.3 12.5 all-gather.13
  156.2 21.0 all-gather.17
  1009.6 45.7 reduce-scatter.2
  1063.8 145.3 reduce-scatter.4
  1247.5 257.2 all-reduce.5
  1506.8 69.8 all-gather.9

commit v2 on v1

v2 whole, which is shorter than its diff:
```python
import functools
import math

import jax
import jax.numpy as jnp
from jax import lax
from jax.experimental import pallas as pl
from jax.experimental.pallas import tpu as pltpu
from jax.sharding import PartitionSpec as P

HEADS = 16
HEAD_DIM = 64
EPS = 1e-05
NEG = -1e30
MESH = pl.DeviceIdType.MESH
F32 = jnp.float32
BF16 = jnp.bfloat16


def matmul(former, latter):
    return jnp.dot(former, latter, preferred_element_type=F32)


def matmul_t(former, latter):
    return lax.dot_general(
        former, latter, (((1,), (1,)), ((), ())), preferred_element_type=F32
    )


def outer_sum(former, latter):
    return lax.dot_general(
        former, latter, (((0,), (0,)), ((), ())), preferred_element_type=F32
    )


def layer_norm(inputs, weight, offset):
    centre = inputs - jnp.mean(inputs, axis=-1, keepdims=True)
    spread = jnp.mean(centre * centre, axis=-1, keepdims=True)
    return centre * lax.rsqrt(spread + EPS) * weight + offset


def gelu_tanh(inputs):
    return jax.nn.gelu(inputs, approximate=True)


class Group:
    def __init__(self, axes, sizes):
        self.axes = axes
        self.sizes = sizes
        self.count = math.prod(sizes)

    def me(self):
        place = 0
        for axis, size in zip(self.axes, self.sizes):
            place = place * size + lax.axis_index(axis)
        return place

    def device(self, place):
        spot = {}
        for axis, size in reversed(list(zip(self.axes, self.sizes))):
            spot[axis] = lax.rem(place, size)
            place = lax.div(place, size)
        return spot

    def peers(self):
        me = self.me()
        return [lax.rem(me + step, self.count) for step in range(1, self.count)]


def greet(groups):
    barrier = pltpu.get_barrier_semaphore()
    total = 0
    for group in groups:
        for peer in group.peers():
            pl.semaphore_signal(
                barrier, inc=1, device_id=group.device(peer), device_id_type=MESH
            )
            total += 1
    pl.semaphore_wait(barrier, total)


def send(group, peer, step, src, dst, send_sem, recv_sem):
    copy = pltpu.make_async_remote_copy(
        src_ref=src,
        dst_ref=dst,
        send_sem=send_sem.at[step],
        recv_sem=recv_sem.at[step],
        device_id=group.device(peer),
        device_id_type=MESH,
    )
    copy.start()
    return copy


def tie(*arrays):
    return lax.optimization_barrier(arrays)


class Job:
    def __init__(self, kind, groups, x, axis=0):
        self.kind, self.groups, self.x, self.axis = kind, groups, x, axis
        count = groups[0].count
        rest = x.shape[:axis] + x.shape[axis + 1 :]
        dma = pltpu.SemaphoreType.DMA
        self.in_spec = pl.BlockSpec(memory_space=pl.ANY)
        self.out_spec = pl.BlockSpec(memory_space=pl.ANY)
        self.scratch = [dma((count - 1,)), dma((count - 1,)), dma]
        if kind in ("gather", "spread"):
            self.in_spec = pl.BlockSpec(memory_space=pltpu.VMEM)
        if kind == "gather":
            self.out = jax.ShapeDtypeStruct((count,) + x.shape, x.dtype)
        elif kind == "spread":
            self.out = jax.ShapeDtypeStruct((groups[1].count, count) + x.shape, x.dtype)
            self.scratch += [dma((count,)), dma((count,))]
        elif kind == "deal":
            self.out = jax.ShapeDtypeStruct((count - 1,) + rest, x.dtype)
        else:
            self.out = jax.ShapeDtypeStruct(rest, F32)
            self.out_spec = pl.BlockSpec(memory_space=pltpu.VMEM)
            self.scratch += [pltpu.VMEM(rest, x.dtype), pltpu.VMEM((count - 1,) + rest, x.dtype)]

    def key(self):
        return (self.kind, tuple(g.axes for g in self.groups), self.x.shape, str(self.x.dtype), self.axis)

    def start(self, x, out, send_sem, recv_sem, own_sem, *more):
        group = self.groups[0]
        me = group.me()
        peers = list(enumerate(group.peers()))

        def block(place):
            return x.at[(slice(None),) * self.axis + (place,)]

        if self.kind == "gather":
            copies = [send(group, p, k, x, out.at[me], send_sem, recv_sem) for k, p in peers]
            own = pltpu.make_async_copy(x, out.at[me], own_sem)
            own.start()

            def finish():
                for copy in copies + [own]:
                    copy.wait()

        elif self.kind == "spread":
            pair = self.groups[1]
            side = pair.me()
            fw_send, fw_recv = more
            home = out.at[side, me]
            copies = [send(group, p, k, x, home, send_sem, recv_sem) for k, p in peers]
            last = group.count - 1
            passed = [send(pair, 1 - side, last, x, home, fw_send, fw_recv)]
            own = pltpu.make_async_copy(x, home, own_sem)
            own.start()

            def finish():
                for k, copy in enumerate(copies):
                    copy.wait_recv()
                    place = out.at[side, lax.rem(me + group.count - 1 - k, group.count)]
                    passed.append(send(pair, 1 - side, k, place, place, fw_send, fw_recv))
                for copy in passed:
                    copy.wait()
                for copy in copies:
                    copy.wait_send()
                own.wait()

        elif self.kind == "deal":
            copies = [send(group, p, k, block(p), out.at[k], send_sem, recv_sem) for k, p in peers]

            def finish():
                for copy in copies:
                    copy.wait()

        else:
            kept, slots = more
            copies = [send(group, p, k, block(p), slots.at[k], send_sem, recv_sem) for k, p in peers]
            own = pltpu.make_async_copy(block(me), kept, own_sem)
            own.start()

            def finish():
                own.wait()
                for copy in copies:
                    copy.wait()
                total = kept[...].astype(F32)
                for k in range(group.count - 1):
                    total = total + slots[k].astype(F32)
                out[...] = total

        return finish


def job_groups(jobs):
    return [group for job in jobs for group in job.groups]


def split_scratch(jobs, scratch):
    parts, at = [], 0
    for job in jobs:
        parts.append(scratch[at : at + len(job.scratch)])
        at += len(job.scratch)
    return parts


def exchange_body(jobs, *refs):
    count = len(jobs)
    greet(job_groups(jobs))
    parts = split_scratch(jobs, refs[2 * count :])
    ends = [
        job.start(refs[n], refs[count + n], *parts[n]) for n, job in enumerate(jobs)
    ]
    for end in ends:
        end()


class Exchanges:
    def __init__(self):
        self.idents = {}

    def ident(self, key):
        return self.idents.setdefault(key, len(self.idents))

    def __call__(self, *jobs):
        jobs = list(jobs)
        return pl.pallas_call(
            functools.partial(exchange_body, jobs),
            out_shape=tuple(job.out for job in jobs),
            in_specs=[job.in_spec for job in jobs],
            out_specs=tuple(job.out_spec for job in jobs),
            scratch_shapes=[one for job in jobs for one in job.scratch],
            compiler_params=pltpu.CompilerParams(
                collective_id=self.ident(tuple(job.key() for job in jobs)),
                has_side_effects=True,
                vmem_limit_bytes=32 * 2**20,
            ),
        )(*[job.x for job in jobs])


def all_sum_body(groups, x_ref, out_ref, *scratch):
    greet(groups)
    out_ref[...] = x_ref[...]
    count = len(groups)
    for number, group in enumerate(groups):
        kept, slots, send_sem, recv_sem = scratch[4 * number : 4 * number + 4]
        kept[...] = out_ref[...]
        copies = [
            send(group, peer, step, kept, slots.at[step], send_sem, recv_sem)
            for step, peer in enumerate(group.peers())
        ]
        for copy in copies:
            copy.wait()
        me = group.me()
        total = jnp.zeros_like(out_ref)
        for place in range(group.count):
            step = lax.rem(me - place + group.count, group.count) - 1
            term = slots[jnp.maximum(step, 0)]
            total = total + jnp.where(place == me, kept[...], term)
        out_ref[...] = total


def all_sum(groups, x, ident):
    groups = [group for group in groups if group.count > 1]
    scratch = []
    for group in groups:
        others = group.count - 1
        scratch += [
            pltpu.VMEM(x.shape, x.dtype),
            pltpu.VMEM((others,) + x.shape, x.dtype),
            pltpu.SemaphoreType.DMA((others,)),
            pltpu.SemaphoreType.DMA((others,)),
        ]
    return pl.pallas_call(
        functools.partial(all_sum_body, groups),
        out_shape=jax.ShapeDtypeStruct(x.shape, x.dtype),
        in_specs=[pl.BlockSpec(memory_space=pltpu.VMEM)],
        out_specs=pl.BlockSpec(memory_space=pltpu.VMEM),
        scratch_shapes=scratch,
        compiler_params=pltpu.CompilerParams(
            collective_id=ident, has_side_effects=True, vmem_limit_bytes=32 * 2**20
        ),
    )(x)


CHUNK = 256


def table_body(
    by_section, by_dp, jobs, g_ref, ids_ref, u_ref, gx_ref, *refs
):
    riders = len(jobs)
    xs, (out_ref, *outs), refs = refs[:riders], refs[riders : 2 * riders + 1], refs[2 * riders + 1 :]
    (g_buf, to_partner, from_partner, to_dp, from_dp, own, result,
    g_sem, ps_send, ps_recv, dp_send, dp_recv, ag_send, ag_recv, fw_send, fw_recv, own_sem,
    ) = refs[:17]
    s, j = by_section.me(), by_dp.me()
    partner = 1 - s
    peers = by_dp.peers() + [j]
    count = by_dp.count
    block = own.shape[0]
    subs = block // CHUNK
    tokens = u_ref.shape[0]
    greet([by_section, by_dp] + job_groups(jobs))
    parts = split_scratch(jobs, refs[17:])
    ends = [job.start(xs[n], outs[n], *parts[n]) for n, job in enumerate(jobs)]

    def chunk(half, place, sub):
        return (half * count + place) * subs + sub

    order = [(number, half) for number in range(count) for half in (0, 1)]

    def fetch(index, sub, slot):
        number, away = order[index]
        half = partner if away == 0 else s
        return pltpu.make_async_copy(
            g_ref.at[chunk(half, peers[number], sub)], g_buf.at[slot], g_sem.at[slot]
        )

    def remote(group, peer, number, sub, src, dst, send_sem, recv_sem):
        return pltpu.make_async_remote_copy(
            src_ref=src,
            dst_ref=dst,
            send_sem=send_sem.at[number, sub],
            recv_sem=recv_sem.at[number, sub],
            device_id=group.device(peer),
            device_id_type=MESH,
        )

    def rows(sub):
        return pl.ds(pl.multiple_of(sub * CHUNK, CHUNK), CHUNK)

    def partner_copy(number, sub):
        return remote(
            by_section, partner, number, sub,
            to_partner.at[number, rows(sub)], from_partner.at[number, rows(sub)],
            ps_send, ps_recv,
        )

    def chip_copy(number, sub):
        return remote(
            by_dp, peers[number], number, sub,
            to_dp.at[number, rows(sub)], from_dp.at[number, rows(sub)], dp_send, dp_recv,
        )

    def spread_copy(number, sub):
        return remote(
            by_dp, peers[number], number, sub,
            result.at[rows(sub)], out_ref.at[chunk(s, j, sub)], ag_send, ag_recv,
        )

    sources = [lax.rem(j + count - 1 - number, count) for number in range(count - 1)] + [j]

    def forward_copy(number, sub):
        target = out_ref.at[chunk(s, sources[number], sub)]
        origin = result.at[rows(sub)] if number == count - 1 else target
        return remote(by_section, partner, number, sub, origin, target, fw_send, fw_recv)

    def own_copy(sub):
        return pltpu.make_async_copy(
            result.at[rows(sub)], out_ref.at[chunk(s, j, sub)], own_sem.at[sub]
        )

    fetch(0, 0, 0).start()
    for index, (number, away) in enumerate(order):
        half = partner if away == 0 else s

        def one(sub, carry, index=index, number=number, away=away, half=half):
            slot = lax.rem(sub, 2)
            fetch(index, sub, slot).wait()

            @pl.when(sub + 1 < subs)
            def _():
                fetch(index, sub + 1, 1 - slot).start()

            if index + 1 < len(order):

                @pl.when(sub + 1 == subs)
                def _():
                    fetch(index + 1, 0, 1 - slot).start()

            base = chunk(half, peers[number], sub) * CHUNK
            place = base + lax.broadcasted_iota(jnp.int32, (tokens, CHUNK), 1)
            chosen = jnp.where(place == ids_ref[...], 1.0, 0.0).astype(BF16)
            term = outer_sum(g_buf[slot], u_ref[...]) + outer_sum(chosen, gx_ref[...])
            if away == 0:
                to_partner[number, rows(sub), :] = term.astype(BF16)
                partner_copy(number, sub).start()
            else:
                partner_copy(number, sub).wait_recv()
                term = term + from_partner[number, rows(sub), :].astype(F32)
                if number < count - 1:
                    to_dp[number, rows(sub), :] = term.astype(BF16)
                    chip_copy(number, sub).start()
                else:
                    own[rows(sub), :] = term
            return carry

        lax.fori_loop(0, subs, one, 0)

    def finish(sub, carry):
        term = own[rows(sub), :]
        for number in range(count - 1):
            chip_copy(number, sub).wait_recv()
            term = term + from_dp[number, rows(sub), :].astype(F32)
        result[rows(sub), :] = term.astype(BF16)
        for number in range(count - 1):
            spread_copy(number, sub).start()
        forward_copy(count - 1, sub).start()
        own_copy(sub).start()
        return carry

    lax.fori_loop(0, subs, finish, 0)

    def take(sub, carry):
        for number in range(count - 1):
            spread_copy(number, sub).wait_recv()
            forward_copy(number, sub).start()
        return carry

    lax.fori_loop(0, subs, take, 0)

    def drain(sub, carry):
        own_copy(sub).wait()
        for number in range(count):
            partner_copy(number, sub).wait_send()
            forward_copy(number, sub).wait()
        for number in range(count - 1):
            chip_copy(number, sub).wait_send()
            spread_copy(number, sub).wait_send()
        return carry

    lax.fori_loop(0, subs, drain, 0)
    for end in ends:
        end()


def table_sum(by_section, by_dp, jobs, grads, ids, final, grad_rows, ident):
    chunks, tokens, _ = grads.shape
    width = final.shape[1]
    count = by_dp.count
    subs = chunks // (2 * count)
    block = subs * CHUNK
    assert subs % 2 == 0
    vmem = pl.BlockSpec(memory_space=pltpu.VMEM)
    hbm = pl.BlockSpec(memory_space=pl.ANY)
    dma = pltpu.SemaphoreType.DMA
    return pl.pallas_call(
        functools.partial(table_body, by_section, by_dp, jobs),
        out_shape=(jax.ShapeDtypeStruct((chunks, CHUNK, width), BF16),)
        + tuple(job.out for job in jobs),
        in_specs=[hbm, vmem, vmem, vmem] + [job.in_spec for job in jobs],
        out_specs=(hbm,) + tuple(job.out_spec for job in jobs),
        scratch_shapes=[
            pltpu.VMEM((2, tokens, CHUNK), BF16),
            pltpu.VMEM((count, block, width), BF16),
            pltpu.VMEM((count, block, width), BF16),
            pltpu.VMEM((count - 1, block, width), BF16),
            pltpu.VMEM((count - 1, block, width), BF16),
            pltpu.VMEM((block, width), F32),
            pltpu.VMEM((block, width), BF16),
            dma((2,)),
            dma((count, subs)),
            dma((count, subs)),
            dma((count - 1, subs)),
            dma((count - 1, subs)),
            dma((count - 1, subs)),
            dma((count - 1, subs)),
            dma((count, subs)),
            dma((count, subs)),
            dma((subs,)),
        ]
        + [one for job in jobs for one in job.scratch],
        compiler_params=pltpu.CompilerParams(
            collective_id=ident, has_side_effects=True, vmem_limit_bytes=56 * 2**20
        ),
    )(grads, ids, final, grad_rows, *[job.x for job in jobs])


LANES = 128


def head_logits_body(u_ref, e_ref, ids_ref, logits_ref, top_ref, total_ref, pick_ref):
    step = pl.program_id(0)
    tokens, tile = logits_ref.shape[1:]

    @pl.when(step == 0)
    def _():
        top_ref[...] = jnp.full_like(top_ref, NEG)
        total_ref[...] = jnp.zeros_like(total_ref)
        pick_ref[...] = jnp.zeros_like(pick_ref)

    logits = matmul_t(u_ref[...], e_ref[...])
    logits_ref[0] = logits
    place = step * tile + lax.broadcasted_iota(jnp.int32, (tokens, tile), 1)
    picked = jnp.where(place == ids_ref[...], logits, 0.0)
    pieces = [logits[:, at : at + LANES] for at in range(0, tile, LANES)]
    before = top_ref[...]
    top = functools.reduce(jnp.maximum, pieces, before)
    total = total_ref[...] * jnp.exp(before - top)
    pick = pick_ref[...]
    for number, piece in enumerate(pieces):
        total = total + jnp.exp(piece - top)
        pick = pick + picked[:, number * LANES : (number + 1) * LANES]
    top_ref[...] = top
    total_ref[...] = total
    pick_ref[...] = pick


def head_logits(final, embedding, ids):
    tokens, width = final.shape
    vocab = embedding.shape[0]
    fixed = pl.BlockSpec((tokens, LANES), lambda step: (0, 0))
    stat = jax.ShapeDtypeStruct((tokens, LANES), F32)
    return pl.pallas_call(
        head_logits_body,
        grid=(vocab // CHUNK,),
        out_shape=(
            jax.ShapeDtypeStruct((vocab // CHUNK, tokens, CHUNK), F32), stat, stat, stat
        ),
        in_specs=[
            pl.BlockSpec((tokens, width), lambda step: (0, 0)),
            pl.BlockSpec((CHUNK, width), lambda step: (step, 0)),
            pl.BlockSpec((tokens, 1), lambda step: (0, 0)),
        ],
        out_specs=(
            pl.BlockSpec((1, tokens, CHUNK), lambda step: (step, 0, 0)), fixed, fixed, fixed
        ),
        compiler_params=pltpu.CompilerParams(vmem_limit_bytes=40 * 2**20),
        cost_estimate=pl.CostEstimate(
            flops=2 * tokens * vocab * width,
            bytes_accessed=4 * tokens * vocab + 2 * vocab * width,
            transcendentals=tokens * vocab,
        ),
    )(final, embedding, ids)


def head_grads_body(logits_ref, e_ref, ids_ref, norm_ref, weight_ref, grads_ref, back_ref, acc):
    step = pl.program_id(0)
    tokens, tile = grads_ref.shape[1:]

    @pl.when(step == 0)
    def _():
        acc[...] = jnp.zeros_like(acc)

    place = step * tile + lax.broadcasted_iota(jnp.int32, (tokens, tile), 1)
    probs = jnp.exp(logits_ref[0] - norm_ref[...])
    grads = (jnp.where(place == ids_ref[...], probs - 1.0, probs) * weight_ref[...]).astype(BF16)
    grads_ref[0] = grads
    acc[...] += matmul(grads, e_ref[...])

    @pl.when(step == pl.num_programs(0) - 1)
    def _():
        back_ref[...] = acc[...].astype(BF16)


def head_grads(logits, embedding, ids, norm, weight):
    chunks, tokens, _ = logits.shape
    vocab, width = embedding.shape
    column = pl.BlockSpec((tokens, 1), lambda step: (0, 0))
    tile = pl.BlockSpec((1, tokens, CHUNK), lambda step: (step, 0, 0))
    return pl.pallas_call(
        head_grads_body,
        grid=(chunks,),
        out_shape=(
            jax.ShapeDtypeStruct(logits.shape, BF16),
            jax.ShapeDtypeStruct((tokens, width), BF16),
        ),
        in_specs=[
            tile, pl.BlockSpec((CHUNK, width), lambda step: (step, 0)), column, column, column
        ],
        out_specs=(tile, pl.BlockSpec((tokens, width), lambda step: (0, 0))),
        scratch_shapes=[pltpu.VMEM((tokens, width), F32)],
        compiler_params=pltpu.CompilerParams(vmem_limit_bytes=40 * 2**20),
        cost_estimate=pl.CostEstimate(
            flops=2 * tokens * vocab * width,
            bytes_accessed=6 * tokens * vocab + 2 * vocab * width,
            transcendentals=tokens * vocab,
        ),
    )(logits, embedding, ids, norm, weight)


BLOCK = 256


def masked_scores(queries, keys, slope, length, first):
    rows, cols = queries.shape[0], keys.shape[0]
    raw = matmul_t(queries, keys)
    i = first + lax.broadcasted_iota(jnp.int32, (rows, cols), 0)
    j = lax.broadcasted_iota(jnp.int32, (rows, cols), 1)
    scores = raw * HEAD_DIM ** (-0.5) - slope * (i - j).astype(F32)
    return jnp.where((j <= i) & (j < length), scores, NEG)


SMEM = pl.BlockSpec(memory_space=pltpu.SMEM)
VMEM = pl.BlockSpec(memory_space=pltpu.VMEM)


def attend_body(
    length_ref, slope_ref, a_ref, qk_ref, vo_ref, bias_ref,
    q_ref, k_ref, v_ref, mixed_ref, lse_ref, part_ref,
):
    seq, width = q_ref.shape

    def project(step, carry):
        rows = pl.ds(pl.multiple_of(step * BLOCK, BLOCK), BLOCK)
        block = a_ref[rows, :]
        q_ref[rows, :] = (matmul_t(block, qk_ref[0]) + bias_ref[0:1, :]).astype(BF16)
        k_ref[rows, :] = matmul_t(block, qk_ref[1]).astype(BF16)
        v_ref[rows, :] = (matmul_t(block, vo_ref[0]) + bias_ref[1:2, :]).astype(BF16)
        return carry

    lax.fori_loop(0, seq // BLOCK, project, 0)
    for first in range(0, seq, BLOCK):
        upto = first + BLOCK
        for head in range(width // HEAD_DIM):
            lanes = slice(head * HEAD_DIM, (head + 1) * HEAD_DIM)
            scores = masked_scores(
                q_ref[first:upto, lanes], k_ref[:upto, lanes], slope_ref[head], length_ref[0], first
            )
            highest = jnp.max(scores, axis=-1, keepdims=True)
            powers = jnp.exp(scores - highest)
            total = jnp.sum(powers, axis=-1, keepdims=True)
            probs = (powers * (1.0 / total)).astype(BF16)
            mixed_ref[first:upto, lanes] = matmul(probs, v_ref[:upto, lanes]).astype(BF16)
            lse_ref[head, first:upto, :] = highest + jnp.log(total)
        part_ref[first:upto, :] = matmul(mixed_ref[first:upto, :], vo_ref[1]).astype(BF16)


def attend(length, slopes, a, qk, vo, bias):
    seq, model = a.shape
    width = qk.shape[1]
    low = jax.ShapeDtypeStruct((seq, width), BF16)
    return pl.pallas_call(
        attend_body,
        out_shape=(
            low, low, low, low,
            jax.ShapeDtypeStruct((width // HEAD_DIM, seq, 1), F32),
            jax.ShapeDtypeStruct((seq, model), BF16),
        ),
        in_specs=[SMEM, SMEM, VMEM, VMEM, VMEM, VMEM],
        out_specs=(VMEM,) * 6,
        compiler_params=pltpu.CompilerParams(vmem_limit_bytes=48 * 2**20),
    )(length, slopes, a, qk, vo, bias)


def attend_back_body(
    length_ref, slope_ref, gy_ref, a_ref, qk_ref, vo_ref, q_ref, k_ref, v_ref, mixed_ref, lse_ref,
    part_ref, grads_ref, sums_ref, go, gq, gk, gv, gk_sum, gv_sum,
):
    seq, width = q_ref.shape
    heads = width // HEAD_DIM
    gk_sum[...] = jnp.zeros_like(gk_sum)
    gv_sum[...] = jnp.zeros_like(gv_sum)

    def open_block(step, carry):
        rows = pl.ds(pl.multiple_of(step * BLOCK, BLOCK), BLOCK)
        go[rows, :] = matmul_t(gy_ref[rows, :], vo_ref[1]).astype(BF16)
        return carry

    lax.fori_loop(0, seq // BLOCK, open_block, 0)
    grads_ref[3] = outer_sum(mixed_ref[...], gy_ref[...])
    for head in range(heads):
        lanes = slice(head * HEAD_DIM, (head + 1) * HEAD_DIM)
        gq_total = jnp.zeros((1, HEAD_DIM), F32)
        for first in range(0, seq, BLOCK):
            upto = first + BLOCK
            queries, grads = q_ref[first:upto, lanes], go[first:upto, lanes]
            keys, values = k_ref[:upto, lanes], v_ref[:upto, lanes]
            scores = masked_scores(queries, keys, slope_ref[head], length_ref[0], first)
            probs = jnp.exp(scores - lse_ref[head, first:upto, :])
            grad_probs = matmul_t(grads, values)
            inner = jnp.sum(probs * grad_probs, axis=-1, keepdims=True)
            grad_scores = (probs * (grad_probs - inner) * HEAD_DIM ** (-0.5)).astype(BF16)
            block = matmul(grad_scores, keys)
            gq_total = gq_total + jnp.sum(block, axis=0, keepdims=True)
            gq[first:upto, lanes] = block.astype(BF16)
            gk_sum[:upto, lanes] += outer_sum(grad_scores, queries)
            gv_sum[:upto, lanes] += outer_sum(probs.astype(BF16), grads)
        sums_ref[0:1, lanes] = gq_total
    sums_ref[1:2, :] = jnp.sum(gv_sum[...], axis=0, keepdims=True)
    gk[...] = gk_sum[...].astype(BF16)
    gv[...] = gv_sum[...].astype(BF16)
    grads_ref[0] = outer_sum(gq[...], a_ref[...])
    grads_ref[1] = outer_sum(gv[...], a_ref[...])
    grads_ref[2] = outer_sum(gk[...], a_ref[...])

    def close_block(step, carry):
        rows = pl.ds(pl.multiple_of(step * BLOCK, BLOCK), BLOCK)
        part_ref[rows, :] = (
            matmul(gq[rows, :], qk_ref[0]) + matmul(gk[rows, :], qk_ref[1])
            + matmul(gv[rows, :], vo_ref[0])
        ).astype(BF16)
        return carry

    lax.fori_loop(0, seq // BLOCK, close_block, 0)


def attend_back(length, slopes, gy, a, qk, vo, q, k, v, mixed, lse):
    seq, model = a.shape
    width = qk.shape[1]
    return pl.pallas_call(
        attend_back_body,
        out_shape=(
            jax.ShapeDtypeStruct((seq, model), BF16),
            jax.ShapeDtypeStruct((4, width, model), F32),
            jax.ShapeDtypeStruct((2, width), F32),
        ),
        in_specs=[SMEM, SMEM] + [VMEM] * 9,
        out_specs=(VMEM,) * 3,
        scratch_shapes=[pltpu.VMEM((seq, width), BF16)] * 4 + [pltpu.VMEM((seq, width), F32)] * 2,
        compiler_params=pltpu.CompilerParams(vmem_limit_bytes=52 * 2**20),
    )(length, slopes, gy, a, qk, vo, q, k, v, mixed, lse)


GELU_A = 0.7978845608028654
GELU_B = 0.044715


def feed_body(c_ref, up_ref, down_ref, bias_ref, before_ref, part_ref, total):
    seq = c_ref.shape[0]
    units = up_ref.shape[0]
    tile = min(units, BLOCK)

    def one(step, carry):
        rows = pl.ds(pl.multiple_of(step * BLOCK, BLOCK), BLOCK)
        block = c_ref[rows, :]
        for first in range(0, units, tile):
            lanes = slice(first, first + tile)
            before = matmul_t(block, up_ref[lanes, :]) + bias_ref[:, lanes]
            before_ref[rows, lanes] = before
            bend = jnp.tanh(GELU_A * (before + GELU_B * before * before * before))
            active = (0.5 * before * (1.0 + bend)).astype(BF16)
            term = matmul(active, down_ref[lanes, :])
            if first == 0:
                total[...] = term
            else:
                total[...] += term
        part_ref[rows, :] = total[...].astype(BF16)
        return carry

    lax.fori_loop(0, seq // BLOCK, one, 0)


def feed(c, up, down, bias):
    seq, model = c.shape
    units = up.shape[0]
    return pl.pallas_call(
        feed_body,
        out_shape=(
            jax.ShapeDtypeStruct((seq, units), F32),
            jax.ShapeDtypeStruct((seq, model), BF16),
        ),
        in_specs=[VMEM] * 4,
        out_specs=(VMEM, VMEM),
        scratch_shapes=[pltpu.VMEM((BLOCK, model), F32)],
        compiler_params=pltpu.CompilerParams(vmem_limit_bytes=48 * 2**20),
    )(c, up, down, bias)


def feed_back_body(
    gz_ref, c_ref, before_ref, up_ref, down_ref, part_ref, grads_ref, sums_ref, active, low
):
    seq = c_ref.shape[0]
    units = up_ref.shape[0]
    tile = min(units, BLOCK)
    sums_ref[...] = jnp.zeros_like(sums_ref)

    def one(step, carry):
        rows = pl.ds(pl.multiple_of(step * BLOCK, BLOCK), BLOCK)
        gz = gz_ref[rows, :]
        for first in range(0, units, tile):
            lanes = slice(first, first + tile)
            before = before_ref[rows, lanes]
            square = before * before
            bend = jnp.tanh(GELU_A * before * (1.0 + GELU_B * square))
            half = 0.5 * (1.0 + bend)
            slope = half + 0.5 * before * (1.0 - bend * bend) * (
                GELU_A * (1.0 + 3.0 * GELU_B * square)
            )
            grad = matmul_t(gz, down_ref[lanes, :]) * slope
            sums_ref[:, lanes] += jnp.sum(grad, axis=0, keepdims=True)
            active[rows, lanes] = (before * half).astype(BF16)
            low[rows, lanes] = grad.astype(BF16)
        part_ref[rows, :] = matmul(low[rows, :], up_ref[...]).astype(BF16)
        return carry

    lax.fori_loop(0, seq // BLOCK, one, 0)
    for first in range(0, units, tile):
        lanes = slice(first, first + tile)
        grads_ref[0, lanes, :] = outer_sum(low[:, lanes], c_ref[...])
        grads_ref[1, lanes, :] = outer_sum(active[:, lanes], gz_ref[...])


def feed_back(gz, c, before, up, down):
    seq, model = c.shape
    units = up.shape[0]
    return pl.pallas_call(
        feed_back_body,
        out_shape=(
            jax.ShapeDtypeStruct((seq, model), BF16),
            jax.ShapeDtypeStruct((2, units, model), F32),
            jax.ShapeDtypeStruct((1, units), F32),
        ),
        in_specs=[VMEM] * 5,
        out_specs=(VMEM,) * 3,
        scratch_shapes=[pltpu.VMEM((seq, units), BF16)] * 2,
        compiler_params=pltpu.CompilerParams(vmem_limit_bytes=52 * 2**20),
    )(gz, c, before, up, down)


def per_device(
    mesh_shape,
    token_ids,
    target_ids,
    lengths,
    embedding,
    outer_gain,
    outer_bias,
    norm_gain,
    norm_bias,
    qkv_weight,
    qv_bias,
    out_weight,
    up_weight,
    up_bias,
    down_weight,
    row_bias,
):
    sections, groups, shards = (mesh_shape[name] for name in ("section", "dp", "tensor"))
    s, j, z = (lax.axis_index(name) for name in ("section", "dp", "tensor"))
    by_section = Group(("section",), (sections,))
    by_dp = Group(("dp",), (groups,))
    by_tensor = Group(("tensor",), (shards,))
    exchange = Exchanges()
    layers = sections
    vocab, width = embedding.shape
    seq = token_ids.shape[1]
    rows = token_ids.shape[0] * groups
    local_cols = qkv_weight.shape[-1]
    planes = rows == sections * shards and local_cols % (groups * HEAD_DIM) == 0
    team = by_dp if planes else by_tensor
    cut = groups if planes else 1
    fan = shards if planes else 1
    halves = 2 if planes else 1
    part = seq // team.count
    cols = local_cols // cut
    hidden = up_weight.shape[-1] // cut
    strip = hidden // halves
    cut_index = j if planes else 0
    my_row = z * sections + s if planes else j * sections + s
    length = lax.dynamic_slice(lengths, (my_row,), (1,))
    token_count = jnp.sum(lengths).astype(F32)
    vocab_start = z * vocab

    def chosen_cols(array, size):
        return lax.dynamic_slice_in_dim(array, cut_index * size, size, array.ndim - 1).T

    def chosen_rows(array, size):
        return lax.dynamic_slice_in_dim(array, cut_index * size, size, 0)

    def pad_rows(array, count):
        return jnp.pad(array, ((0, count - array.shape[0]), (0, width - array.shape[1])))

    sides = jnp.stack(
        [
            jnp.concatenate(
                [
                    chosen_cols(qkv_weight[0, 0], cols),
                    chosen_cols(qkv_weight[0, 2], cols),
                    chosen_cols(up_weight[0], hidden),
                ]
            ),
            jnp.concatenate(
                [
                    chosen_cols(qkv_weight[0, 1], cols),
                    chosen_rows(out_weight[0], cols),
                    chosen_rows(down_weight[0], hidden),
                ]
            ),
        ]
    )
    qv_piece = lax.dynamic_slice_in_dim(qv_bias[0], cut_index * cols, cols, 1)
    up_piece = lax.dynamic_slice_in_dim(up_bias[0], cut_index * hidden, hidden, 0)
    small = jnp.concatenate(
        [
            outer_gain,
            outer_bias,
            norm_gain[0],
            norm_bias[0],
            row_bias[0],
            pad_rows(qv_piece, 2),
            pad_rows(up_piece[None], 6),
        ]
    )

    def gather(group, x):
        return Job("gather", [group], x)

    def deal(group, x, axis=0):
        return Job("deal", [group], x, axis)

    def own_and_dealt(x, dealt, place, axis=0):
        own = lax.dynamic_index_in_dim(x, place, axis, keepdims=False).astype(F32)
        return own + jnp.sum(dealt.astype(F32), axis=0)

    if planes:
        other, both, small_all = exchange(
            deal(by_section, sides),
            gather(by_dp, jnp.stack([token_ids, target_ids])),
            gather(Group(("section", "tensor"), (sections, shards)), small),
        )
        small_all = small_all.reshape((sections, shards) + small.shape)
        own_side = lax.dynamic_index_in_dim(sides, s, 0, keepdims=False)
        side = [jnp.where(s == l, own_side, other[0]) for l in range(layers)]
        both = jnp.swapaxes(both, 0, 1).reshape(2, shards, sections, groups, part)
        both = lax.dynamic_index_in_dim(
            lax.dynamic_index_in_dim(both, s, 2, keepdims=False), j, 2, keepdims=False
        )
        ids, targets = both[0].reshape(-1), both[1].reshape(-1)
        group_lengths = lax.dynamic_index_in_dim(
            lengths.reshape(shards, sections), s, 1, keepdims=False
        )
        places = jnp.broadcast_to(j * part + jnp.arange(part), (shards, part))
        valid = (places < group_lengths[:, None]).reshape(-1)
    else:
        sides_all, small_all = exchange(gather(by_section, sides), gather(by_section, small))
        small_all = small_all[:, None]
        ids, targets = token_ids[s], target_ids[s]
        valid = jnp.arange(seq) < lengths[my_row]

    outer_gains = [small_all[l, 0, 0] for l in range(layers)]
    outer_offsets = [small_all[l, 0, 1] for l in range(layers)]
    params = []
    for l in range(layers):
        biases = [small_all[l, :, 8 + n, :cols].reshape(-1) for n in range(2)]
        units = small_all[l, :, 10, :hidden].reshape(fan, halves, strip)
        params.append(
            dict(
                gains=small_all[l, 0, 2:4],
                offsets=small_all[l, 0, 4:6],
                row_bias=small_all[l, 0, 6:8],
                bias=jnp.stack(biases),
                up_bias=jnp.swapaxes(units, 0, 1).reshape(1, -1),
            )
        )
        if not planes:
            block = sides_all[l]
            params[l].update(
                qk=block[:, :cols],
                vo=block[:, cols : 2 * cols],
                up=block[0, 2 * cols :],
                down=block[1, 2 * cols :],
            )
    head_number = (
        (jnp.arange(fan)[:, None] if planes else z) * (local_cols // HEAD_DIM)
        + cut_index * (cols // HEAD_DIM)
        + jnp.arange(cols // HEAD_DIM)
    ).reshape(-1)
    slopes = jnp.exp2(-8.0 * (head_number + 1).astype(F32) / HEADS)

    def attn_jobs(l):
        if not planes or l >= layers:
            return []
        return [
            Job("spread", [by_tensor, by_section], side[l][first : first + cols])
            for first in (0, cols)
        ]

    def feed_jobs(l, n):
        if not planes or l >= layers:
            return []
        first = 2 * cols + n * strip
        return [Job("spread", [by_tensor, by_section], side[l][first : first + strip])]

    def take_attn(l, got):
        if got:
            params[l]["qk"], params[l]["vo"] = (
                one.reshape(2, fan * cols, width) for one in got
            )

    def take_feed(l, got):
        if got:
            strips = [one.reshape(2, fan * strip, width) for one in got]
            params[l]["up"], params[l]["down"] = (
                jnp.concatenate([one[n] for one in strips]) for n in range(2)
            )

    def whole(block, *jobs):
        first, *got = exchange(gather(team, block.astype(BF16)), *jobs)
        return first.reshape(seq, width), got

    def summed(terms, *jobs):
        first, *got = exchange(
            Job("reduce", [team], terms.reshape(team.count, part, width)), *jobs
        )
        return first, got

    local_ids = ids - vocab_start
    inside = (local_ids >= 0) & (local_ids < vocab)
    looked = jnp.where(
        inside[:, None], jnp.take(embedding, jnp.clip(local_ids, 0, vocab - 1), axis=0), 0
    )
    group_part = looked.shape[0] // shards
    x, *got = exchange(
        Job("reduce", [by_tensor], looked.reshape(shards, group_part, width)), *attn_jobs(0)
    )
    take_attn(0, got)
    h = layer_norm(x, outer_gains[0], outer_offsets[0])

    kept = []
    strips = []
    for l, p in enumerate(params):
        normed, got = whole(
            layer_norm(h, p["gains"][0], p["offsets"][0]),
            *feed_jobs(l, 0 if l == 0 else 1),
        )
        strips += got
        q, k, v, mixed, lse, back = attend(length, slopes, normed, p["qk"], p["vo"], p["bias"])
        if l > 0:
            take_feed(l, strips)
        total, got = summed(back, *(feed_jobs(l, 1) if l == 0 else []))
        if l == 0:
            take_feed(l, strips + got)
        middle = h + total + p["row_bias"][0]
        second, got = whole(
            layer_norm(middle, p["gains"][1], p["offsets"][1]), *attn_jobs(l + 1)
        )
        take_attn(l + 1, got)
        before, back = feed(second, p["up"], p["down"], p["up_bias"])
        kept.append((h, normed, q, k, v, mixed, lse, middle, second, before))
        total, strips = summed(back, *feed_jobs(l + 1, 0))
        h = middle + total + p["row_bias"][1]

    (final,) = exchange(
        gather(by_tensor, layer_norm(h, outer_gains[-1], outer_offsets[-1]).astype(BF16))
    )
    final = final.reshape(-1, width)
    tokens = final.shape[0]
    columns_of = (targets - vocab_start)[:, None]
    logits, tops, totals, picks = head_logits(final, embedding, columns_of)
    top = jnp.max(tops, axis=1)
    total = jnp.sum(totals * jnp.exp(tops - top[:, None]), axis=1)
    pick = jnp.sum(picks, axis=1)
    (stats,) = exchange(
        gather(by_tensor, jnp.pad(jnp.stack([top, total, pick]), ((0, 5), (0, 0))))
    )
    top_all = jnp.max(stats[:, 0], axis=0)
    log_norm = top_all + jnp.log(jnp.sum(stats[:, 1] * jnp.exp(stats[:, 0] - top_all), axis=0))
    terms = jnp.where(valid, log_norm - jnp.sum(stats[:, 2], axis=0), 0.0)
    loss_part = jnp.sum(
        lax.dynamic_index_in_dim(terms.reshape(shards, -1), z, 0, keepdims=False)
    )
    row_weight = jnp.where(valid, 1.0 / token_count, 0.0)
    grad_logits, back = head_grads(
        logits, embedding, columns_of, log_norm[:, None], row_weight[:, None]
    )
    (grad_final,) = exchange(
        Job("reduce", [by_tensor], back.reshape(shards, group_part, width))
    )
    _, final_back = jax.vjp(layer_norm, h, outer_gains[-1], outer_offsets[-1])
    grad, final_gain, final_offset = final_back(grad_final)

    def section_jobs(pair):
        return [deal(by_section, one) for one in pair] if planes else []

    def section_sums(pair, got):
        out = []
        for one, dealt in zip(pair, got):
            low = own_and_dealt(one, dealt, s).astype(BF16)
            if one.ndim == 4:
                out.append(low.reshape(low.shape[0], fan, cols, width))
            else:
                out.append(low.reshape(halves, fan, strip, width))
        return out

    def tensor_jobs(lows):
        return [deal(by_tensor, low, 1) for low in lows]

    def tensor_sums(lows, got):
        return [
            own_and_dealt(low, dealt, z, 1).astype(BF16) for low, dealt in zip(lows, got)
        ]

    def spread_jobs(pieces):
        return [Job("spread", [by_dp, by_section], piece) for piece in pieces]

    small_rows = [None] * layers
    pairs = [None] * layers
    done = [None] * layers
    lows = None
    for l in reversed(range(layers)):
        p = params[l]
        section_in, normed, q, k, v, mixed, lse, middle, second, before = kept[l]
        late = planes and l + 1 < layers
        gz, got = whole(grad, *(section_jobs(pairs[l + 1]) if late else []))
        if late:
            lows = section_sums(pairs[l + 1], got)
        back, g_feed, up_sum = feed_back(gz, second, before, p["up"], p["down"])
        _, norm_back = jax.vjp(layer_norm, middle, p["gains"][1], p["offsets"][1])
        total, got_a = summed(back, *(tensor_jobs(lows[:1]) if late else []))
        grad_mid, gain_two, offset_two = norm_back(total)
        grad_mid = grad_mid + grad
        gy, got_b = whole(grad_mid, *(tensor_jobs(lows[1:]) if late else []))
        back, g_attn, qv_sum = attend_back(
            length, slopes, gy, normed, p["qk"], p["vo"], q, k, v, mixed, lse
        )
        if late:
            done[l + 1] = tensor_sums(lows, got_a + got_b)
        _, norm_back = jax.vjp(layer_norm, section_in, p["gains"][0], p["offsets"][0])
        total, got = summed(back)
        grad_in, gain_one, offset_one = norm_back(total)
        bias_two = jnp.sum(grad, axis=0)
        grad = grad_in + grad_mid
        pairs[l] = (g_attn.reshape((2, 2) + g_attn.shape[1:]), g_feed)

        def placed(values, size):
            out = jnp.zeros((fan if planes else shards, cut, size), F32)
            at = (0, j, 0) if planes else (z, 0, 0)
            return lax.dynamic_update_slice(out, values.reshape(fan, 1, size), at).reshape(
                -1, width
            )

        units = jnp.swapaxes(up_sum.reshape(halves, fan, strip), 0, 1)
        small_rows[l] = [
            gain_one[None],
            gain_two[None],
            offset_one[None],
            offset_two[None],
            jnp.sum(grad_mid, axis=0)[None],
            bias_two[None],
            placed(qv_sum[0], cols),
            placed(qv_sum[1], cols),
            placed(units, hidden),
        ]

    _, embed_back = jax.vjp(layer_norm, x, outer_gains[0], outer_offsets[0])
    grad_rows, embed_gain, embed_offset = embed_back(grad)
    jobs = [gather(by_tensor, grad_rows.astype(BF16))]
    if planes:
        jobs += section_jobs(pairs[0]) + spread_jobs(done[1])
    grad_rows, *got = exchange(*jobs)
    grad_rows = grad_rows.reshape(tokens, width)

    packed = jnp.concatenate(
        [row for l in range(layers) for row in small_rows[l]]
        + [embed_gain[None], final_gain[None], embed_offset[None], final_offset[None]]
        + [jnp.broadcast_to(loss_part, (1, width))]
    )
    used = packed.shape[0]
    packed = jnp.pad(packed, ((0, -used % 8), (0, 0)))
    packed = all_sum([by_section, by_dp, by_tensor], packed, exchange.ident("small"))
    jobs = []
    if planes:
        lows = section_sums(pairs[0], got[:2])
        spread_one = got[2:]
        jobs = tensor_jobs(lows)
    packed, grad_rows = tie(packed, grad_rows)
    embed_sum, *got = table_sum(
        by_section, by_dp, jobs, grad_logits, ids[:, None] - vocab_start, final, grad_rows,
        exchange.ident("table"),
    )
    if planes:
        spread_zero = exchange(*spread_jobs(tensor_sums(lows, got)))
        attn_sum, feed_sum = (
            jnp.where(s == 0, zero, one) for zero, one in zip(spread_zero, spread_one)
        )
    else:
        chosen = [
            lax.dynamic_index_in_dim(
                lax.psum(jnp.stack([pair[n] for pair in pairs]), ("section", "dp")),
                s, 0, keepdims=False,
            )
            for n in range(2)
        ]
        attn_sum = chosen[0][:, None]
        feed_sum = chosen[1][:, None, None]
    embed_sum = embed_sum.reshape(vocab, width).astype(F32)
    per_layer = (used - 5) // layers
    mine = lax.dynamic_slice_in_dim(packed, s * per_layer, per_layer, 0)
    qv_rows = mine[6:8].reshape(2, -1)
    ff_row = mine[8:].reshape(-1)
    grad_qv = lax.dynamic_slice_in_dim(qv_rows, z * local_cols, local_cols, 1)
    grad_up_bias = lax.dynamic_slice_in_dim(ff_row, z * hidden * cut, hidden * cut, 0)
    base = per_layer * layers
    grad_outer_gain = lax.dynamic_slice_in_dim(packed, base + s, 1, 0)
    grad_outer_bias = lax.dynamic_slice_in_dim(packed, base + 2 + s, 1, 0)
    loss = packed[base + 4, 0] / token_count

    def columns(array):
        return array.astype(F32).reshape(-1, width).T

    grad_qkv = jnp.stack(
        [columns(attn_sum[0, :, 0]), columns(attn_sum[1, :, 0]), columns(attn_sum[0, :, 1])]
    )
    grad_out_mat = attn_sum[1, :, 1].astype(F32).reshape(-1, width)
    grad_up = columns(feed_sum[0])
    grad_down = feed_sum[1].astype(F32).reshape(-1, width)
    return (
        loss,
        embed_sum,
        grad_outer_gain,
        grad_outer_bias,
        mine[0:2][None],
        mine[2:4][None],
        grad_qkv[None],
        grad_qv[None],
        grad_out_mat[None],
        grad_up[None],
        grad_up_bias[None],
        grad_down[None],
        mine[4:6][None],
    )


def solution(mesh):
    return jax.shard_map(
        functools.partial(per_device, dict(mesh.shape)),
        mesh=mesh,
        in_specs=(
            P("dp", None),
            P("dp", None),
            P(),
            P("tensor", None),
            P("section", None),
            P("section", None),
            P("section", None, None),
            P("section", None, None),
            P("section", None, None, "tensor"),
            P("section", None, "tensor"),
            P("section", "tensor", None),
            P("section", None, "tensor"),
            P("section", "tensor"),
            P("section", "tensor", None),
            P("section", None, None),
        ),
        out_specs=(
            P(),
            P("tensor", None),
            P("section", None),
            P("section", None),
            P("section", None, None),
            P("section", None, None),
            P("section", None, None, "tensor"),
            P("section", None, "tensor"),
            P("section", "tensor", None),
            P("section", None, "tensor"),
            P("section", "tensor"),
            P("section", "tensor", None),
            P("section", None, None),
        ),
        check_vma=False,
    )
```

time: 1610 us -> 1360 us (0.84)
  Pallas kernels: 737 us -> 1190 us
  waiting for transfers between devices: 410 us -> 0 us
  matrix products: 161 us -> 0 us
  other arithmetic: 169 us -> 72.9 us
  local copies, waits for them, and re-layouts: 111 us -> 79.6 us
    pallas_call x27 -> x34, Pallas kernels: 676 us -> 1160 us  [the longest x23 729 us: __call__(): pl.pallas_call(functools.partial(exchange_body, jobs), out_shape=tuple((j...]
    psum x1 -> x0, waiting for transfers between devices: 189 us -> none  [per_device(): embed_sum = lax.psum(table.astype(BF16), ('section', 'dp')).astype(F32)]
    all_gather x5 -> x0, waiting for transfers between devices: 174 us -> none  [the longest x2 122 us: spread_weights(): piece = lax.all_gather(piece, 'tensor', axis=0)]
    dot_general x39 -> x0, matrix products: 161 us -> none  [the longest x13 68.8 us: matmul_t(): lax.dot_general(former, latter, (((1,), (1,)), ((), ())), preferred_eleme...]
    reduce_scatter x2 -> x0, waiting for transfers between devices: 45.8 us -> none  [the longest x1 45.8 us: per_device(): lax.psum_scatter(jnp.stack(layer_grads), 'section', scatter_dimension=0,...]
    scatter-add x1 -> x0, other arithmetic: 32.1 us -> none  [per_device(): table.at[jnp.clip(local_ids, 0, vocab - 1)]]
    pallas_call x1, Pallas kernels: 61.5 us -> 30 us  [all_sum(): pl.pallas_call(functools.partial(all_sum_body, groups), out_shape=jax.Sha...]
    convert_element_type x12 -> x19, other arithmetic: 68.6 us -> 37.8 us  [the longest x1 18.8 us: per_device(): embed_sum = embed_sum.reshape(vocab, width).astype(F32)]
  transfers between devices with their start and end apart: 8 -> 0, of which waited for: 5 -> 0; matrix products, arithmetic and copies ran while one was open for 9% -> 0% of each run, Pallas kernels for 19% -> 0%
where the time goes in v2:
time: 1360 us; the launch traced here: 1350 us
  Pallas kernels  1190 us (88%)
  local copies, waits for them, and re-layouts  79.6 us (6%)
  other arithmetic  72.9 us (5%)
    pallas_call x23, Pallas kernels, __call__(): pl.pallas_call(functools.partial(exchange_body, jobs), out_shape=tuple((j...  729 us
    pallas_call x1, Pallas kernels, table_sum(): pl.pallas_call(functools.partial(table_body, by_section, by_dp, jobs), ou...  203 us
    pallas_call x2, Pallas kernels, attend_back(): pl.pallas_call(attend_back_body, out_shape=(jax.ShapeDtypeStruct((seq, mo...  53.9 us
    pallas_call x1, Pallas kernels, head_grads(): pl.pallas_call(head_grads_body, grid=(chunks,), out_shape=(jax.ShapeDtype...  43 us
    unnamed x189, local copies, waits for them, and re-layouts  40.9 us
    pallas_call x2, Pallas kernels, feed_back(): pl.pallas_call(feed_back_body, out_shape=(jax.ShapeDtypeStruct((seq, mode...  40.2 us
    pallas_call x1, Pallas kernels, head_logits(): pl.pallas_call(head_logits_body, grid=(vocab // CHUNK,), out_shape=(jax.S...  39.2 us
    pallas_call x2, Pallas kernels, attend(): pl.pallas_call(attend_body, out_shape=(low, low, low, low, jax.ShapeDtype...  32.1 us

profile of v2, /device:TPU:1, one launch (start us, length us, event | category | flops | bytes accessed | tf_op | source)
XLA Modules:
  0.0 1351.1 jit_solution(9235109450485797855)
XLA Ops:
  6.9 14.8 %shard_map.246 = (bf16[1,384,1024]{2,1,0:T(8,128)(2,1)S(1)}, s32[4,2,2,1024]{3,2,1,0:T(2,128)S(1)}, f32[8,16,1024]{2,1,0:T(8,128)S(1)}) custom-call(bf16[2,384,1024]{2,1,0:T(8,128)(2,1)S(1)} %pad_maximum_fusion.4.refs_0_, s32[2,2,1024]{2,1,0:T(2,128)S(1)} %pad_add_fusion.refs_1_, f32[16,1024]{1,0:T(8,128)S(1)} %concatenate.26.refs_2_), custom_call_target="tpu_custom_call" | custom-call | tf_op jit(solution)/shard_map/pallas_call | solution.py:221
  23.5 13.9 %gather_fusion = bf16[1024,1024]{1,0:T(8,128)(2,1)} fusion(bf16[8192,1024]{1,0:T(8,128)(2,1)} %e_ref.3, s32[1024]{0:T(1024)S(1)} %broadcast_clamp_fusion), kind=kCustom, calls=%fused_computation | custom fusion | bytes 4198400 | tf_op jit(solution)/shard_map/jit(_take)/gather | solution.py:996
  39.3 3.1 broadcast_select_fusion.2
  43.3 72.7 %shard_map.247 = (f32[256,1024]{1,0:T(8,128)S(1)}, bf16[2,4,64,1024]{3,2,1,0:T(8,128)(2,1)S(1)}, bf16[2,4,64,1024]{3,2,1,0:T(8,128)(2,1)S(1)}) custom-call(bf16[4,256,1024]{2,1,0:T(8,128)(2,1)S(1)} %select_select_fusion.refs_0_, bf16[64,1024]{1,0:T(8,128)(2,1)S(1)} %get-tuple-element.236.refs_1_, bf16[64,1024]{1,0:T(8,128)(2,1)S(1)} %get-tuple-element.235.refs_2_), custom_call_target="tpu_custom_call" | custom-call | tf_op jit(solution)/shard_map/pallas_call | solution.py:221
  120.9 32.4 %shard_map.248 = (bf16[4,256,1024]{2,1,0:T(8,128)(2,1)S(1)}, bf16[2,4,128,1024]{3,2,1,0:T(8,128)(2,1)S(1)}) custom-call(bf16[256,1024]{1,0:T(8,128)(2,1)S(1)} %add_convert_fusion.9.refs_0_, bf16[128,1024]{1,0:T(8,128)(2,1)S(1)} %get-tuple-element.234.refs_1_), custom_call_target="tpu_custom_call" | custom-call | tf_op jit(solution)/shard_map/pallas_call | solution.py:221
  157.6 16.1 %shard_map.249 = (bf16[1024,256]{1,0:T(8,128)(2,1)S(1)}, bf16[1024,256]{1,0:T(8,128)(2,1)S(1)}, bf16[1024,256]{1,0:T(8,128)(2,1)S(1)}, bf16[1024,256]{1,0:T(8,12...) custom-call(s32[1]{0:T(128)} %dynamic_slice.119.length_ref, f32[4]{0:T(128)S(1)} %multiply_exponential_fusion.slope_ref, ...), custom_call_target="tpu_custom_call" | custom-call | tf_op jit(solution)/shard_map/pallas_call | solution.py:628
  173.7 2.3 copy-done.25
  176.1 28.8 %shard_map.250 = (f32[256,1024]{1,0:T(8,128)S(1)}, bf16[2,4,128,1024]{3,2,1,0:T(8,128)(2,1)S(1)}) custom-call(bf16[4,256,1024]{2,1,0:T(8,128)(2,1)S(1)} %bitcast.295, bf16[128,1024]{1,0:T(8,128)(2,1)S(1)} %get-tuple-element.233.refs_1_), custom_call_target="tpu_custom_call" | custom-call | tf_op jit(solution)/shard_map/pallas_call | solution.py:221
  211.6 30.4 %shard_map.251 = (bf16[4,256,1024]{2,1,0:T(8,128)(2,1)S(1)}, bf16[2,4,64,1024]{3,2,1,0:T(8,128)(2,1)S(1)}, bf16[2,4,64,1024]{3,2,1,0:T(8,128)(2,1)S(1)}) custom-call(bf16[256,1024]{1,0:T(8,128)(2,1)S(1)} %add_convert_fusion.8.refs_0_, bf16[64,1024]{1,0:T(8,128)(2,1)S(1)} %get-tuple-element.232.refs_1_, bf16[64,1024]{1,0:T(8,128)(2,1)S(1)} %get-tuple-element.231.refs_2_), custom_call_target="tpu_custom_call" | custom-call | tf_op jit(solution)/shard_map/pallas_call | solution.py:221
  242.9 11.5 shard_map.252
  254.5 28.7 %shard_map.253 = (f32[256,1024]{1,0:T(8,128)S(1)}, bf16[2,4,128,1024]{3,2,1,0:T(8,128)(2,1)S(1)}) custom-call(bf16[4,256,1024]{2,1,0:T(8,128)(2,1)S(1)} %bitcast.297, bf16[128,1024]{1,0:T(8,128)(2,1)S(1)} %get-tuple-element.230.refs_1_), custom_call_target="tpu_custom_call" | custom-call | tf_op jit(solution)/shard_map/pallas_call | solution.py:221
  283.9 28.6 %shard_map.254 = (bf16[4,256,1024]{2,1,0:T(8,128)(2,1)S(1)}, bf16[2,4,128,1024]{3,2,1,0:T(8,128)(2,1)S(1)}) custom-call(bf16[256,1024]{1,0:T(8,128)(2,1)S(1)} %add_convert_fusion.7.refs_0_, bf16[128,1024]{1,0:T(8,128)(2,1)S(1)} %get-tuple-element.229.refs_1_), custom_call_target="tpu_custom_call" | custom-call | tf_op jit(solution)/shard_map/pallas_call | solution.py:221
  317.3 16.0 %shard_map.255 = (bf16[1024,256]{1,0:T(8,128)(2,1)S(1)}, bf16[1024,256]{1,0:T(8,128)(2,1)S(1)}, bf16[1024,256]{1,0:T(8,128)(2,1)S(1)}, bf16[1024,256]{1,0:T(8,12...) custom-call(s32[1]{0:T(128)} %dynamic_slice.119.length_ref, f32[4]{0:T(128)S(1)} %multiply_exponential_fusion.slope_ref, ...), custom_call_target="tpu_custom_call" | custom-call | tf_op jit(solution)/shard_map/pallas_call | solution.py:628
  333.4 2.3 copy-done.28
  335.7 26.2 %shard_map.256 = f32[256,1024]{1,0:T(8,128)S(1)} custom-call(bf16[4,256,1024]{2,1,0:T(8,128)(2,1)S(1)} %bitcast.299), custom_call_target="tpu_custom_call" | custom-call | tf_op jit(solution)/shard_map/pallas_call | solution.py:221
  362.8 25.2 %shard_map.257 = bf16[4,256,1024]{2,1,0:T(8,128)(2,1)S(1)} custom-call(bf16[256,1024]{1,0:T(8,128)(2,1)S(1)} %add_convert_fusion.6.refs_0_), custom_call_target="tpu_custom_call" | custom-call | tf_op jit(solution)/shard_map/pallas_call | solution.py:221
  388.0 11.8 shard_map.258
  399.8 24.4 %shard_map.259 = f32[256,1024]{1,0:T(8,128)S(1)} custom-call(bf16[4,256,1024]{2,1,0:T(8,128)(2,1)S(1)} %bitcast.301), custom_call_target="tpu_custom_call" | custom-call | tf_op jit(solution)/shard_map/pallas_call | solution.py:221
  425.0 36.4 %shard_map.260 = bf16[4,256,1024]{2,1,0:T(8,128)(2,1)S(1)} custom-call(bf16[256,1024]{1,0:T(8,128)(2,1)S(1)} %add_convert_fusion.5.refs_0_), custom_call_target="tpu_custom_call" | custom-call | tf_op jit(solution)/shard_map/pallas_call | solution.py:221
  463.7 39.2 %shard_map.261 = (f32[32,1024,256]{2,1,0:T(8,128)}, f32[1024,128]{1,0:T(8,128)S(1)}, f32[1024,128]{1,0:T(8,128)S(1)}, f32[1024,128]{1,0:T(8,128)S(1)}) custom-call(bf16[1024,1024]{1,0:T(8,128)(2,1)S(1)} %bitcast.272, bf16[8192,1024]{1,0:T(8,128)(2,1)} %e_ref.3, s32[1024,1]{1,0:T(8,128)S(1)} %bitcast.304), custom_call_target="tpu_custom_call" | custom-call | flops 17179869184 | bytes 50331648 | tf_op jit(solution)/shard_map/pallas_call | solution.py:509
  509.5 15.0 %shard_map.262 = f32[4,8,1024]{2,1,0:T(8,128)S(1)} custom-call(f32[8,1024]{1,0:T(8,128)S(1)} %select_maximum_fusion.refs_0_), custom_call_target="tpu_custom_call" | custom-call | tf_op jit(solution)/shard_map/pallas_call | solution.py:221
  526.8 43.0 %shard_map.263 = (bf16[32,1024,256]{2,1,0:T(8,128)(2,1)}, bf16[1024,1024]{1,0:T(8,128)(2,1)S(1)}) custom-call(f32[32,1024,256]{2,1,0:T(8,128)} %get-tuple-element.104.logits_ref, bf16[8192,1024]{1,0:T(8,128)(2,1)} %e_ref.3, s32[1024,1]{1,0:T(8,128)S(1)} %bitcast.305, f32[1024,1]{1,0:T(8,128)S(1)} %copy.66.norm_ref, f32[1024,1]{1,0:T(8,128)S(1)} %bitcast.306), custom_call_target="tpu_custom_call" | custom-call | flops 17179869184 | bytes 67108864 | tf_op jit(solution)/shard_map/pallas_call | solution.py:556
  569.8 36.6 %shard_map.264 = f32[256,1024]{1,0:T(8,128)S(1)} custom-call(bf16[4,256,1024]{2,1,0:T(8,128)(2,1)S(1)} %bitcast.300), custom_call_target="tpu_custom_call" | custom-call | tf_op jit(solution)/shard_map/pallas_call | solution.py:221
  607.4 24.2 %shard_map.265 = bf16[4,256,1024]{2,1,0:T(8,128)(2,1)S(1)} custom-call(bf16[256,1024]{1,0:T(8,128)(2,1)S(1)} %get-tuple-element.228.refs_0_), custom_call_target="tpu_custom_call" | custom-call | tf_op jit(solution)/shard_map/pallas_call | solution.py:221
  632.9 20.0 %shard_map.266 = (bf16[1024,1024]{1,0:T(8,128)(2,1)}, f32[2,1024,1024]{2,1,0:T(8,128)}, f32[1,1024]{1,0:T(1,128)S(1)}) custom-call(bf16[1024,1024]{1,0:T(8,128)(2,1)} %bitcast.275, bf16[1024,1024]{1,0:T(8,128)(2,1)} %bitcast.265, f32[1024,1024]{1,0:T(8,128)} %get-tuple-element.109.before_ref, bf16[1024,1024]{1,0:T(8,128)(2,1)} %pad_maximum_fusion.2.up_ref, ...), custom_call_target="tpu_custom_call" | custom-call | tf_op jit(solution)/shard_map/pallas_call | solution.py:792
  654.5 24.4 %shard_map.267 = f32[256,1024]{1,0:T(8,128)S(1)} custom-call(bf16[4,256,1024]{2,1,0:T(8,128)(2,1)S(1)} %bitcast.298), custom_call_target="tpu_custom_call" | custom-call | tf_op jit(solution)/shard_map/pallas_call | solution.py:221
  680.1 24.2 %shard_map.268 = bf16[4,256,1024]{2,1,0:T(8,128)(2,1)S(1)} custom-call(bf16[256,1024]{1,0:T(8,128)(2,1)S(1)} %convert_element_type.182.refs_0_), custom_call_target="tpu_custom_call" | custom-call | tf_op jit(solution)/shard_map/pallas_call | solution.py:221
  705.7 27.2 %shard_map.269 = (bf16[1024,1024]{1,0:T(8,128)(2,1)}, f32[4,256,1024]{2,1,0:T(8,128)}, f32[2,256]{1,0:T(2,128)S(1)}) custom-call(s32[1]{0:T(128)} %dynamic_slice.119.length_ref, f32[4]{0:T(128)S(1)} %multiply_exponential_fusion.slope_ref, bf16[1024,1024]{1,0:T(8,128)(2,1)} %bitcast.274, bf16[1024,1024]{1,0:T(8,128)(2,1)} %bitcast.279, ...), custom_call_target="tpu_custom_call" | custom-call | tf_op jit(solution)/shard_map/pallas_call | solution.py:696
  734.5 24.4 %shard_map.270 = f32[256,1024]{1,0:T(8,128)S(1)} custom-call(bf16[4,256,1024]{2,1,0:T(8,128)(2,1)S(1)} %bitcast.294), custom_call_target="tpu_custom_call" | custom-call | tf_op jit(solution)/shard_map/pallas_call | solution.py:221
  760.9 2.2 copy-done.3
  763.1 25.8 %shard_map.271 = (bf16[4,256,1024]{2,1,0:T(8,128)(2,1)S(1)}, f32[1,2,256,1024]{3,2,1,0:T(8,128)S(1)}, f32[1,1024,1024]{2,1,0:T(8,128)S(1)}) custom-call(bf16[256,1024]{1,0:T(8,128)(2,1)S(1)} %convert_element_type.183.refs_0_, f32[2,2,256,1024]{3,2,1,0:T(8,128)S(1)} %bitcast.268, f32[2,1024,1024]{2,1,0:T(8,128)S(1)} %bitcast.263), custom_call_target="tpu_custom_call" | custom-call | tf_op jit(solution)/shard_map/pallas_call | solution.py:221
  790.7 20.3 %shard_map.272 = (bf16[1024,1024]{1,0:T(8,128)(2,1)}, f32[2,1024,1024]{2,1,0:T(8,128)}, f32[1,1024]{1,0:T(1,128)S(1)}) custom-call(bf16[1024,1024]{1,0:T(8,128)(2,1)} %bitcast.303, bf16[1024,1024]{1,0:T(8,128)(2,1)} %bitcast.281, f32[1024,1024]{1,0:T(8,128)} %get-tuple-element.120.before_ref, bf16[1024,1024]{1,0:T(8,128)(2,1)} %pad_maximum_fusion.up_ref, ...), custom_call_target="tpu_custom_call" | custom-call | tf_op jit(solution)/shard_map/pallas_call | solution.py:792
  812.5 36.3 %shard_map.273 = (f32[256,1024]{1,0:T(8,128)S(1)}, bf16[3,2,64,1024]{3,2,1,0:T(8,128)(2,1)S(1)}) custom-call(bf16[4,256,1024]{2,1,0:T(8,128)(2,1)S(1)} %bitcast.296, bf16[2,4,64,1024]{3,2,1,0:T(8,128)(2,1)S(1)} %bitcast.282), custom_call_target="tpu_custom_call" | custom-call | tf_op jit(solution)/shard_map/pallas_call | solution.py:221
  850.8 36.6 %shard_map.274 = (bf16[4,256,1024]{2,1,0:T(8,128)(2,1)S(1)}, bf16[3,2,128,1024]{3,2,1,0:T(8,128)(2,1)S(1)}) custom-call(bf16[256,1024]{1,0:T(8,128)(2,1)S(1)} %convert_element_type.186.refs_0_, bf16[2,4,128,1024]{3,2,1,0:T(8,128)(2,1)S(1)} %bitcast.266), custom_call_target="tpu_custom_call" | custom-call | tf_op jit(solution)/shard_map/pallas_call | solution.py:221
  892.7 26.7 %shard_map.275 = (bf16[1024,1024]{1,0:T(8,128)(2,1)}, f32[4,256,1024]{2,1,0:T(8,128)}, f32[2,256]{1,0:T(2,128)S(1)}) custom-call(s32[1]{0:T(128)} %dynamic_slice.119.length_ref, f32[4]{0:T(128)S(1)} %multiply_exponential_fusion.slope_ref, bf16[1024,1024]{1,0:T(8,128)(2,1)} %bitcast.302, bf16[1024,1024]{1,0:T(8,128)(2,1)} %bitcast.277, ...), custom_call_target="tpu_custom_call" | custom-call | tf_op jit(solution)/shard_map/pallas_call | solution.py:696
  921.0 24.9 %shard_map.276 = f32[256,1024]{1,0:T(8,128)S(1)} custom-call(bf16[4,256,1024]{2,1,0:T(8,128)(2,1)S(1)} %bitcast.293), custom_call_target="tpu_custom_call" | custom-call | tf_op jit(solution)/shard_map/pallas_call | solution.py:221
  950.6 55.3 %shard_map.278 = (bf16[4,256,1024]{2,1,0:T(8,128)(2,1)S(1)}, f32[1,2,256,1024]{3,2,1,0:T(8,128)S(1)}, f32[1,1024,1024]{2,1,0:T(8,128)S(1)}, bf16[2,4,2,64,1024]{...) custom-call(bf16[256,1024]{1,0:T(8,128)(2,1)S(1)} %add_convert_fusion.4.refs_0_, f32[2,2,256,1024]{3,2,1,0:T(8,128)S(1)} %bitcast.270, ...), custom_call_target="tpu_custom_call" | custom-call | tf_op jit(solution)/shard_map/pallas_call | solution.py:221
  1006.0 2.0 copy-done.12
  1008.0 5.0 add_convert_fusion
  1016.8 30.0 %shard_map.277 = f32[32,1024]{1,0:T(8,128)S(1)} custom-call(f32[32,1024]{1,0:T(8,128)S(1)} %pad.19.x_ref), custom_call_target="tpu_custom_call" | custom-call | tf_op jit(solution)/shard_map/pallas_call | solution.py:268
  1047.8 202.8 %shard_map.279 = (bf16[32,256,1024]{2,1,0:T(8,128)(2,1)}, bf16[3,2,64,1024]{3,2,1,0:T(8,128)(2,1)}, bf16[3,2,128,1024]{3,2,1,0:T(8,128)(2,1)}) custom-call(bf16[32,1024,256]{2,1,0:T(8,128)(2,1)} %get-tuple-element.142.g_ref, s32[1024,1]{1,0:T(8,128)} %copy.76.ids_ref, bf16[1024,1024]{1,0:T(8,128)(2,1)} %bitcast.273, bf16[1024,1024]{1,0:T(8,128)(2,1)} %bitcast.292, ...), custom_call_target="tpu_custom_call" | custom-call | tf_op jit(solution)/shard_map/pallas_call | solution.py:442
  1250.6 1.9 convert_reduce_fusion
  1255.0 52.4 %shard_map.280 = (bf16[2,4,2,64,1024]{4,3,2,1,0:T(8,128)(2,1)S(1)}, bf16[2,4,2,128,1024]{4,3,2,1,0:T(8,128)(2,1)S(1)}) custom-call(bf16[2,64,1024]{2,1,0:T(8,128)(2,1)S(1)} %fusion.4.refs_0_, bf16[2,128,1024]{2,1,0:T(8,128)(2,1)S(1)} %fusion.1.refs_1_), custom_call_target="tpu_custom_call" | custom-call | tf_op jit(solution)/shard_map/pallas_call | solution.py:221
  1311.0 2.6 bitcast_convert_fusion.2
  1313.6 5.3 copy.82
  1318.9 4.2 bitcast_convert_fusion.1
  1324.2 1.9 fusion
  1327.3 18.8 %bitcast_convert_fusion = f32[8192,1024]{1,0:T(8,128)} fusion(bf16[32,256,1024]{2,1,0:T(8,128)(2,1)} %get-tuple-element.146), kind=kLoop, calls=%fused_computation.1 | loop fusion | flops 8388608 | bytes 50331648 | tf_op jit(solution)/shard_map/convert_element_type | solution.py:1172
  (364 shorter events, 86.9 us)
Async XLA Ops:
  3.3 2.6 copy-start.72
  118.3 2.5 copy-start.76
  120.0 37.0 %copy-start.85 = (s32[8]{0:T(128)S(1)}, s32[8]{0:T(128)}, u32[]{:S(2)}) copy-start(s32[8]{0:T(128)} %param.17) | copy-start | bytes 100
  120.0 37.6 %copy-start.15 = (bf16[2,4,64,1024]{3,2,1,0:T(8,128)(2,1)S(1)}, bf16[2,4,64,1024]{3,2,1,0:T(8,128)(2,1)}, u32[]{:S(2)}) copy-start(bf16[2,4,64,1024]{3,2,1,0:T(8,128)(2,1)} %copy-done.14) | copy-start | bytes 3145732
  120.0 37.6 %copy-start.17 = (bf16[2,4,64,1024]{3,2,1,0:T(8,128)(2,1)S(1)}, bf16[2,4,64,1024]{3,2,1,0:T(8,128)(2,1)}, u32[]{:S(2)}) copy-start(bf16[2,4,64,1024]{3,2,1,0:T(8,128)(2,1)} %copy-done.16) | copy-start | bytes 3145732
  173.7 31.5 %copy-start.42 = (bf16[1024,256]{1,0:T(8,128)(2,1)}, bf16[1024,256]{1,0:T(8,128)(2,1)S(1)}, u32[]{:S(2)}) copy-start(bf16[1024,256]{1,0:T(8,128)(2,1)S(1)} %get-tuple-element.126.q_ref) | copy-start | bytes 1572868
  173.7 31.5 %copy-start.44 = (bf16[1024,256]{1,0:T(8,128)(2,1)}, bf16[1024,256]{1,0:T(8,128)(2,1)S(1)}, u32[]{:S(2)}) copy-start(bf16[1024,256]{1,0:T(8,128)(2,1)S(1)} %get-tuple-element.127.k_ref) | copy-start | bytes 1572868
  173.7 31.5 %copy-start.46 = (bf16[1024,256]{1,0:T(8,128)(2,1)}, bf16[1024,256]{1,0:T(8,128)(2,1)S(1)}, u32[]{:S(2)}) copy-start(bf16[1024,256]{1,0:T(8,128)(2,1)S(1)} %get-tuple-element.128.v_ref) | copy-start | bytes 1572868
  173.7 31.5 %copy-start.48 = (bf16[1024,256]{1,0:T(8,128)(2,1)}, bf16[1024,256]{1,0:T(8,128)(2,1)S(1)}, u32[]{:S(2)}) copy-start(bf16[1024,256]{1,0:T(8,128)(2,1)S(1)} %get-tuple-element.129.mixed_ref) | copy-start | bytes 1572868
  173.7 2.4 copy-start.25
  210.1 73.1 %copy-start.57 = (f32[256,1024]{1,0:T(8,128)}, f32[256,1024]{1,0:T(8,128)S(1)}, u32[]{:S(2)}) copy-start(f32[256,1024]{1,0:T(8,128)S(1)} %get-tuple-element.207) | copy-start | bytes 3145732
  242.0 12.4 copy-start.10
  242.1 75.3 %copy-start.18 = (bf16[2,4,64,1024]{3,2,1,0:T(8,128)(2,1)}, bf16[2,4,64,1024]{3,2,1,0:T(8,128)(2,1)S(1)}, u32[]{:S(2)}) copy-start(bf16[2,4,64,1024]{3,2,1,0:T(8,128)(2,1)S(1)} %get-tuple-element.98) | copy-start | bytes 3145732
  242.1 75.3 %copy-start.19 = (bf16[2,4,64,1024]{3,2,1,0:T(8,128)(2,1)}, bf16[2,4,64,1024]{3,2,1,0:T(8,128)(2,1)S(1)}, u32[]{:S(2)}) copy-start(bf16[2,4,64,1024]{3,2,1,0:T(8,128)(2,1)S(1)} %get-tuple-element.99) | copy-start | bytes 3145732
  283.4 29.4 %copy-start.59 = (f32[256,1024]{1,0:T(8,128)}, f32[256,1024]{1,0:T(8,128)S(1)}, u32[]{:S(2)}) copy-start(f32[256,1024]{1,0:T(8,128)S(1)} %get-tuple-element.205) | copy-start | bytes 3145732
  317.3 44.6 %copy-start.60 = (f32[256,1024]{1,0:T(8,128)S(1)}, f32[256,1024]{1,0:T(8,128)}, u32[]{:S(2)}) copy-start(f32[256,1024]{1,0:T(8,128)} %copy-done.59) | copy-start | bytes 3145732
  333.3 28.8 %copy-start.49 = (bf16[1024,256]{1,0:T(8,128)(2,1)}, bf16[1024,256]{1,0:T(8,128)(2,1)S(1)}, u32[]{:S(2)}) copy-start(bf16[1024,256]{1,0:T(8,128)(2,1)S(1)} %get-tuple-element.111.q_ref) | copy-start | bytes 1572868
  333.3 28.8 %copy-start.51 = (bf16[1024,256]{1,0:T(8,128)(2,1)}, bf16[1024,256]{1,0:T(8,128)(2,1)S(1)}, u32[]{:S(2)}) copy-start(bf16[1024,256]{1,0:T(8,128)(2,1)S(1)} %get-tuple-element.112.k_ref) | copy-start | bytes 1572868
  333.3 28.8 %copy-start.53 = (bf16[1024,256]{1,0:T(8,128)(2,1)}, bf16[1024,256]{1,0:T(8,128)(2,1)S(1)}, u32[]{:S(2)}) copy-start(bf16[1024,256]{1,0:T(8,128)(2,1)S(1)} %get-tuple-element.113.v_ref) | copy-start | bytes 1572868
  333.4 28.9 %copy-start.55 = (bf16[1024,256]{1,0:T(8,128)(2,1)}, bf16[1024,256]{1,0:T(8,128)(2,1)S(1)}, u32[]{:S(2)}) copy-start(bf16[1024,256]{1,0:T(8,128)(2,1)S(1)} %get-tuple-element.114.mixed_ref) | copy-start | bytes 1572868
  333.4 2.4 copy-start.28
  362.2 62.0 %copy-start.62 = (f32[256,1024]{1,0:T(8,128)}, f32[256,1024]{1,0:T(8,128)S(1)}, u32[]{:S(2)}) copy-start(f32[256,1024]{1,0:T(8,128)S(1)} %get-tuple-element.203) | copy-start | bytes 3145732
  388.0 11.8 copy-start.2
  424.5 37.0 %copy-start.64 = (f32[256,1024]{1,0:T(8,128)}, f32[256,1024]{1,0:T(8,128)S(1)}, u32[]{:S(2)}) copy-start(f32[256,1024]{1,0:T(8,128)S(1)} %get-tuple-element.201) | copy-start | bytes 3145732
  461.4 41.5 %copy-start.5 = (bf16[4,256,1024]{2,1,0:T(8,128)(2,1)}, bf16[4,256,1024]{2,1,0:T(8,128)(2,1)S(1)}, u32[]{:S(2)}) copy-start(bf16[4,256,1024]{2,1,0:T(8,128)(2,1)S(1)} %shard_map.260) | copy-start | bytes 6291460
  505.3 21.5 %copy-start.40 = (s32[1,1024]{0,1:T(8,128)S(1)}, s32[1,1024]{0,1:T(8,128)}, u32[]{:S(2)}) copy-start(s32[1,1024]{0,1:T(8,128)} %copy.101) | copy-start | bytes 12292
  569.8 36.6 %copy-start.65 = (f32[256,1024]{1,0:T(8,128)S(1)}, f32[256,1024]{1,0:T(8,128)}, u32[]{:S(2)}) copy-start(f32[256,1024]{1,0:T(8,128)} %copy-done.64) | copy-start | bytes 3145732
  632.9 46.0 %copy-start.63 = (f32[256,1024]{1,0:T(8,128)S(1)}, f32[256,1024]{1,0:T(8,128)}, u32[]{:S(2)}) copy-start(f32[256,1024]{1,0:T(8,128)} %copy-done.62) | copy-start | bytes 3145732
  679.9 24.4 %copy-start.68 = (f32[256,1024]{1,0:T(8,128)}, f32[256,1024]{1,0:T(8,128)S(1)}, u32[]{:S(2)}) copy-start(f32[256,1024]{1,0:T(8,128)S(1)} %get-tuple-element.185) | copy-start | bytes 3145732
  680.0 25.7 %copy-start.50 = (bf16[1024,256]{1,0:T(8,128)(2,1)S(1)}, bf16[1024,256]{1,0:T(8,128)(2,1)}, u32[]{:S(2)}) copy-start(bf16[1024,256]{1,0:T(8,128)(2,1)} %copy-done.49) | copy-start | bytes 1572868
  680.0 25.7 %copy-start.52 = (bf16[1024,256]{1,0:T(8,128)(2,1)S(1)}, bf16[1024,256]{1,0:T(8,128)(2,1)}, u32[]{:S(2)}) copy-start(bf16[1024,256]{1,0:T(8,128)(2,1)} %copy-done.51) | copy-start | bytes 1572868
  680.0 25.7 %copy-start.54 = (bf16[1024,256]{1,0:T(8,128)(2,1)S(1)}, bf16[1024,256]{1,0:T(8,128)(2,1)}, u32[]{:S(2)}) copy-start(bf16[1024,256]{1,0:T(8,128)(2,1)} %copy-done.53) | copy-start | bytes 1572868
  705.7 53.2 %copy-start.61 = (f32[256,1024]{1,0:T(8,128)S(1)}, f32[256,1024]{1,0:T(8,128)}, u32[]{:S(2)}) copy-start(f32[256,1024]{1,0:T(8,128)} %copy-done.59) | copy-start | bytes 3145732
  705.7 55.2 %slice-start = ((s8[8388608]{0:T(1024)(128)(4,1)}), s8[4194304]{0:T(1024)(128)(4,1)S(1)}, s32[]{:S(2)}) async-start(s8[8388608]{0:T(1024)(128)(4,1)} %bitcast.262), calls=%async_computation | async-start | bytes 8388608
  734.5 26.4 %slice-start.1 = ((s8[8388608]{0:T(1024)(128)(4,1)}), s8[4194304]{0:T(1024)(128)(4,1)S(1)}, s32[]{:S(2)}) async-start(s8[8388608]{0:T(1024)(128)(4,1)} %bitcast.262), calls=%async_computation.1 | async-start | bytes 8388608
  760.5 2.6 copy-start.3
  760.7 28.2 %copy-start.66 = (f32[256,1024]{1,0:T(8,128)}, f32[256,1024]{1,0:T(8,128)S(1)}, u32[]{:S(2)}) copy-start(f32[256,1024]{1,0:T(8,128)S(1)} %get-tuple-element.187) | copy-start | bytes 3145732
  790.6 20.3 %copy-start.11 = (bf16[1,2,256,1024]{3,2,1,0:T(8,128)(2,1)}, bf16[1,2,256,1024]{3,2,1,0:T(8,128)(2,1)S(1)}, u32[]{:S(2)}) copy-start(bf16[1,2,256,1024]{3,2,1,0:T(8,128)(2,1)S(1)} %add_convert_fusion.3) | copy-start | bytes 3145732
  790.7 58.2 %copy-start.58 = (f32[256,1024]{1,0:T(8,128)S(1)}, f32[256,1024]{1,0:T(8,128)}, u32[]{:S(2)}) copy-start(f32[256,1024]{1,0:T(8,128)} %copy-done.57) | copy-start | bytes 3145732
  850.7 36.7 %copy-start.70 = (f32[256,1024]{1,0:T(8,128)}, f32[256,1024]{1,0:T(8,128)S(1)}, u32[]{:S(2)}) copy-start(f32[256,1024]{1,0:T(8,128)S(1)} %get-tuple-element.189) | copy-start | bytes 3145732
  890.0 2.7 copy-start.43
  890.0 2.7 copy-start.45
  890.0 2.7 copy-start.47
  1008.0 5.0 copy-start.20
  1250.6 3.3 copy-start.77
  1252.5 56.3 %copy-start.13 = (bf16[2,4,2,128,1024]{4,3,2,1,0:T(8,128)(2,1)S(1)}, bf16[2,4,2,128,1024]{4,3,2,1,0:T(8,128)(2,1)}, u32[]{:S(2)}) copy-start(bf16[2,4,2,128,1024]{4,3,2,1,0:T(8,128)(2,1)} %copy-done.12) | copy-start | bytes 12582916
  1318.9 4.2 copy-start.22
  1327.3 22.5 %copy-start.1 = (bf16[1,1024,1024]{2,1,0:T(8,128)(2,1)S(1)}, bf16[1,1024,1024]{2,1,0:T(8,128)(2,1)}, u32[]{:S(2)}) copy-start(bf16[1,1024,1024]{2,1,0:T(8,128)(2,1)} %param.26) | copy-start | bytes 6291460
  (41 other events, 52.8 us)

commit v3 on v2

--- a/solution.py
+++ b/solution.py
@@ -230,51 +230,6 @@
                 vmem_limit_bytes=32 * 2**20,
             ),
         )(*[job.x for job in jobs])
-
-
-def all_sum_body(groups, x_ref, out_ref, *scratch):
-    greet(groups)
-    out_ref[...] = x_ref[...]
-    count = len(groups)
-    for number, group in enumerate(groups):
-        kept, slots, send_sem, recv_sem = scratch[4 * number : 4 * number + 4]
-        kept[...] = out_ref[...]
-        copies = [
-            send(group, peer, step, kept, slots.at[step], send_sem, recv_sem)
-            for step, peer in enumerate(group.peers())
-        ]
-        for copy in copies:
-            copy.wait()
-        me = group.me()
-        total = jnp.zeros_like(out_ref)
-        for place in range(group.count):
-            step = lax.rem(me - place + group.count, group.count) - 1
-            term = slots[jnp.maximum(step, 0)]
-            total = total + jnp.where(place == me, kept[...], term)
-        out_ref[...] = total
-
-
-def all_sum(groups, x, ident):
-    groups = [group for group in groups if group.count > 1]
-    scratch = []
-    for group in groups:
-        others = group.count - 1
-        scratch += [
-            pltpu.VMEM(x.shape, x.dtype),
-            pltpu.VMEM((others,) + x.shape, x.dtype),
-            pltpu.SemaphoreType.DMA((others,)),
-            pltpu.SemaphoreType.DMA((others,)),
-        ]
-    return pl.pallas_call(
-        functools.partial(all_sum_body, groups),
-        out_shape=jax.ShapeDtypeStruct(x.shape, x.dtype),
-        in_specs=[pl.BlockSpec(memory_space=pltpu.VMEM)],
-        out_specs=pl.BlockSpec(memory_space=pltpu.VMEM),
-        scratch_shapes=scratch,
-        compiler_params=pltpu.CompilerParams(
-            collective_id=ident, has_side_effects=True, vmem_limit_bytes=32 * 2**20
-        ),
-    )(x)
 
 
 CHUNK = 256
@@ -590,75 +545,220 @@
 VMEM = pl.BlockSpec(memory_space=pltpu.VMEM)
 
 
-def attend_body(
-    length_ref, slope_ref, a_ref, qk_ref, vo_ref, bias_ref,
-    q_ref, k_ref, v_ref, mixed_ref, lse_ref, part_ref,
-):
-    seq, width = q_ref.shape
-
-    def project(step, carry):
-        rows = pl.ds(pl.multiple_of(step * BLOCK, BLOCK), BLOCK)
-        block = a_ref[rows, :]
-        q_ref[rows, :] = (matmul_t(block, qk_ref[0]) + bias_ref[0:1, :]).astype(BF16)
-        k_ref[rows, :] = matmul_t(block, qk_ref[1]).astype(BF16)
-        v_ref[rows, :] = (matmul_t(block, vo_ref[0]) + bias_ref[1:2, :]).astype(BF16)
+class TeamRows:
+    def __init__(self, team, full, stage, slots, own, ag_send, ag_recv, rs_send, rs_recv):
+        self.team, self.count, self.me = team, team.count, team.me()
+        self.full, self.stage, self.slots, self.own = full, stage, slots, own
+        self.sems = (ag_send, ag_recv, rs_send, rs_recv)
+
+    def peer(self, step):
+        return lax.rem(self.me + 1 + step, self.count)
+
+    def source(self, step):
+        return lax.rem(self.me + self.count - 1 - step, self.count)
+
+    def remote(self, step, src, dst, send_sem, recv_sem):
+        return pltpu.make_async_remote_copy(
+            src_ref=src,
+            dst_ref=dst,
+            send_sem=send_sem.at[step],
+            recv_sem=recv_sem.at[step],
+            device_id=self.team.device(self.peer(step)),
+            device_id_type=MESH,
+        )
+
+    def ag(self, step, x_ref):
+        return self.remote(step, x_ref, self.full.at[self.me], self.sems[0], self.sems[1])
+
+    def rs(self, step):
+        return self.remote(
+            step, self.stage.at[self.peer(step)], self.slots.at[step], self.sems[2], self.sems[3]
+        )
+
+    def send_rows(self, x_ref):
+        for step in range(self.count - 1):
+            self.ag(step, x_ref).start()
+        self.full[self.me] = x_ref[...]
+
+    def each_arrival(self, x_ref, work):
+        work(self.me)
+
+        def one(step, carry):
+            self.ag(step, x_ref).wait_recv()
+            work(self.source(step))
+            return carry
+
+        lax.fori_loop(0, self.count - 1, one, 0)
+
+    def each_arrival_and_back(self, x_ref, term):
+        self.own[...] = term(self.me)
+
+        def one(step, carry):
+            self.ag(step, x_ref).wait_recv()
+            place = self.source(step)
+            self.stage[place] = term(place).astype(BF16)
+            self.rs(self.count - 2 - step).start()
+            return carry
+
+        lax.fori_loop(0, self.count - 1, one, 0)
+
+    def finish(self, x_ref, total_ref):
+        for step in range(self.count - 1):
+            self.rs(step).wait()
+        total = self.own[...]
+        for step in range(self.count - 1):
+            total = total + self.slots[step].astype(F32)
+        total_ref[...] = total
+        for step in range(self.count - 1):
+            self.ag(step, x_ref).wait_send()
+
+
+def team_scratch(team, part, model):
+    count = team.count
+    dma = pltpu.SemaphoreType.DMA
+    return [
+        pltpu.VMEM((count, part, model), BF16),
+        pltpu.VMEM((count, part, model), BF16),
+        pltpu.VMEM((count - 1, part, model), BF16),
+        pltpu.VMEM((part, model), F32),
+    ] + [dma((count - 1,))] * 4
+
+
+def team_call(body, team, ident, jobs, arrays, specs, outs, out_specs, scratch):
+    part, model = arrays[0].shape
+    count_in, count_out, riders = len(arrays), len(outs), len(jobs)
+    own_scratch = team_scratch(team, part, model)
+
+    def kernel(*refs):
+        ins, refs = refs[:count_in], refs[count_in:]
+        xs, refs = refs[:riders], refs[riders:]
+        results, refs = refs[:count_out], refs[count_out:]
+        landings, refs = refs[:riders], refs[riders:]
+        rows = TeamRows(team, *refs[: len(own_scratch)])
+        refs = refs[len(own_scratch) :]
+        mine, refs = refs[: len(scratch)], refs[len(scratch) :]
+        greet([team] + job_groups(jobs))
+        rows.send_rows(ins[0])
+        parts = split_scratch(jobs, refs)
+        ends = [job.start(xs[n], landings[n], *parts[n]) for n, job in enumerate(jobs)]
+        body(rows, ins, results, mine)
+        for end in ends:
+            end()
+
+    out = pl.pallas_call(
+        kernel,
+        out_shape=tuple(outs) + tuple(job.out for job in jobs),
+        in_specs=list(specs) + [job.in_spec for job in jobs],
+        out_specs=tuple(out_specs) + tuple(job.out_spec for job in jobs),
+        scratch_shapes=own_scratch + list(scratch) + [one for job in jobs for one in job.scratch],
+        compiler_params=pltpu.CompilerParams(
+            collective_id=ident, has_side_effects=True, vmem_limit_bytes=58 * 2**20
+        ),
+    )(*arrays, *[job.x for job in jobs])
+    return out[:count_out], list(out[count_out:])
+
+
+def part_rows(place, part):
+    return pl.ds(pl.multiple_of(place * part, part), part)
+
+
+def attend_body(rows, ins, outs, scratch):
+    x_ref, length_ref, slope_ref, qk_ref, vo_ref, bias_ref = ins
+    total_ref, full_out, q_ref, k_ref, v_ref, mixed_ref, lse_ref = outs
+    (full_sem,) = scratch
+    part = x_ref.shape[0]
+    width = q_ref.shape[1]
+
+    def project(place):
+        at = part_rows(place, part)
+        block = rows.full[place]
+        q_ref[at, :] = (matmul_t(block, qk_ref[0]) + bias_ref[0:1, :]).astype(BF16)
+        k_ref[at, :] = matmul_t(block, qk_ref[1]).astype(BF16)
+        v_ref[at, :] = (matmul_t(block, vo_ref[0]) + bias_ref[1:2, :]).astype(BF16)
+
+    rows.each_arrival(x_ref, project)
+    keep = pltpu.make_async_copy(rows.full, full_out, full_sem)
+    keep.start()
+
+    def one(step, carry):
+        place = rows.peer(step)
+        for block in range(rows.count):
+
+            @pl.when(place == block)
+            def _(first=block * part, upto=(block + 1) * part):
+                for head in range(width // HEAD_DIM):
+                    lanes = slice(head * HEAD_DIM, (head + 1) * HEAD_DIM)
+                    scores = masked_scores(
+                        q_ref[first:upto, lanes], k_ref[:upto, lanes], slope_ref[head],
+                        length_ref[0], first,
+                    )
+                    highest = jnp.max(scores, axis=-1, keepdims=True)
+                    powers = jnp.exp(scores - highest)
+                    total = jnp.sum(powers, axis=-1, keepdims=True)
+                    probs = (powers * (1.0 / total)).astype(BF16)
+                    mixed_ref[first:upto, lanes] = matmul(probs, v_ref[:upto, lanes]).astype(BF16)
+                    lse_ref[head, first:upto, :] = highest + jnp.log(total)
+
+        term = matmul(mixed_ref[part_rows(place, part), :], vo_ref[1])
+
+        @pl.when(step < rows.count - 1)
+        def _():
+            rows.stage[place] = term.astype(BF16)
+            rows.rs(step).start()
+
+        @pl.when(step == rows.count - 1)
+        def _():
+            rows.own[...] = term
+
         return carry
 
-    lax.fori_loop(0, seq // BLOCK, project, 0)
-    for first in range(0, seq, BLOCK):
-        upto = first + BLOCK
-        for head in range(width // HEAD_DIM):
-            lanes = slice(head * HEAD_DIM, (head + 1) * HEAD_DIM)
-            scores = masked_scores(
-                q_ref[first:upto, lanes], k_ref[:upto, lanes], slope_ref[head], length_ref[0], first
-            )
-            highest = jnp.max(scores, axis=-1, keepdims=True)
-            powers = jnp.exp(scores - highest)
-            total = jnp.sum(powers, axis=-1, keepdims=True)
-            probs = (powers * (1.0 / total)).astype(BF16)
-            mixed_ref[first:upto, lanes] = matmul(probs, v_ref[:upto, lanes]).astype(BF16)
-            lse_ref[head, first:upto, :] = highest + jnp.log(total)
-        part_ref[first:upto, :] = matmul(mixed_ref[first:upto, :], vo_ref[1]).astype(BF16)
-
-
-def attend(length, slopes, a, qk, vo, bias):
-    seq, model = a.shape
+    lax.fori_loop(0, rows.count, one, 0)
+    rows.finish(x_ref, total_ref)
+    keep.wait()
+
+
+HBM = pl.BlockSpec(memory_space=pl.ANY)
+
+
+def attend(team, ident, jobs, x, length, slopes, qk, vo, bias):
+    part, model = x.shape
+    seq = part * team.count
     width = qk.shape[1]
     low = jax.ShapeDtypeStruct((seq, width), BF16)
-    return pl.pallas_call(
-        attend_body,
-        out_shape=(
+    return team_call(
+        attend_body, team, ident, jobs,
+        [x, length, slopes, qk, vo, bias],
+        [VMEM, SMEM, SMEM, VMEM, VMEM, VMEM],
+        (
+            jax.ShapeDtypeStruct((part, model), F32),
+            jax.ShapeDtypeStruct((team.count, part, model), BF16),
             low, low, low, low,
             jax.ShapeDtypeStruct((width // HEAD_DIM, seq, 1), F32),
-            jax.ShapeDtypeStruct((seq, model), BF16),
         ),
-        in_specs=[SMEM, SMEM, VMEM, VMEM, VMEM, VMEM],
-        out_specs=(VMEM,) * 6,
-        compiler_params=pltpu.CompilerParams(vmem_limit_bytes=48 * 2**20),
-    )(length, slopes, a, qk, vo, bias)
-
-
-def attend_back_body(
-    length_ref, slope_ref, gy_ref, a_ref, qk_ref, vo_ref, q_ref, k_ref, v_ref, mixed_ref, lse_ref,
-    part_ref, grads_ref, sums_ref, go, gq, gk, gv, gk_sum, gv_sum,
-):
+        (VMEM, HBM, VMEM, VMEM, VMEM, VMEM, VMEM),
+        [pltpu.SemaphoreType.DMA],
+    )
+
+
+def attend_back_body(rows, ins, outs, scratch):
+    gy_ref, length_ref, slope_ref, a_ref, qk_ref, vo_ref, q_ref, k_ref, v_ref, mixed_ref, lse_ref = ins
+    total_ref, grads_ref, sums_ref = outs
+    go, gq, gk, gv, gk_sum, gv_sum = scratch
+    part = gy_ref.shape[0]
     seq, width = q_ref.shape
     heads = width // HEAD_DIM
     gk_sum[...] = jnp.zeros_like(gk_sum)
     gv_sum[...] = jnp.zeros_like(gv_sum)
-
-    def open_block(step, carry):
-        rows = pl.ds(pl.multiple_of(step * BLOCK, BLOCK), BLOCK)
-        go[rows, :] = matmul_t(gy_ref[rows, :], vo_ref[1]).astype(BF16)
-        return carry
-
-    lax.fori_loop(0, seq // BLOCK, open_block, 0)
-    grads_ref[3] = outer_sum(mixed_ref[...], gy_ref[...])
-    for head in range(heads):
-        lanes = slice(head * HEAD_DIM, (head + 1) * HEAD_DIM)
-        gq_total = jnp.zeros((1, HEAD_DIM), F32)
-        for first in range(0, seq, BLOCK):
-            upto = first + BLOCK
+    sums_ref[...] = jnp.zeros_like(sums_ref)
+
+    def open_block(place):
+        go[part_rows(place, part), :] = matmul_t(rows.full[place], vo_ref[1]).astype(BF16)
+
+    rows.each_arrival(gy_ref, open_block)
+    for block in reversed(range(rows.count)):
+        first, upto = block * part, (block + 1) * part
+        for head in range(heads):
+            lanes = slice(head * HEAD_DIM, (head + 1) * HEAD_DIM)
             queries, grads = q_ref[first:upto, lanes], go[first:upto, lanes]
             keys, values = k_ref[:upto, lanes], v_ref[:upto, lanes]
             scores = masked_scores(queries, keys, slope_ref[head], length_ref[0], first)
@@ -666,106 +766,119 @@
             grad_probs = matmul_t(grads, values)
             inner = jnp.sum(probs * grad_probs, axis=-1, keepdims=True)
             grad_scores = (probs * (grad_probs - inner) * HEAD_DIM ** (-0.5)).astype(BF16)
-            block = matmul(grad_scores, keys)
-            gq_total = gq_total + jnp.sum(block, axis=0, keepdims=True)
-            gq[first:upto, lanes] = block.astype(BF16)
+            piece = matmul(grad_scores, keys)
+            sums_ref[0:1, lanes] += jnp.sum(piece, axis=0, keepdims=True)
+            gq[first:upto, lanes] = piece.astype(BF16)
             gk_sum[:upto, lanes] += outer_sum(grad_scores, queries)
             gv_sum[:upto, lanes] += outer_sum(probs.astype(BF16), grads)
-        sums_ref[0:1, lanes] = gq_total
+        gk[first:upto, :] = gk_sum[first:upto, :].astype(BF16)
+        gv[first:upto, :] = gv_sum[first:upto, :].astype(BF16)
+        term = (
+            matmul(gq[first:upto, :], qk_ref[0]) + matmul(gk[first:upto, :], qk_ref[1])
+            + matmul(gv[first:upto, :], vo_ref[0])
+        )
+
+        @pl.when(rows.me != block)
+        def _(block=block, term=term):
+            rows.stage[block] = term.astype(BF16)
+            rows.rs(lax.rem(block + rows.count - 1 - rows.me, rows.count)).start()
+
+        @pl.when(rows.me == block)
+        def _(term=term):
+            rows.own[...] = term
+
     sums_ref[1:2, :] = jnp.sum(gv_sum[...], axis=0, keepdims=True)
-    gk[...] = gk_sum[...].astype(BF16)
-    gv[...] = gv_sum[...].astype(BF16)
+    model = gy_ref.shape[1]
+    grads_ref[3] = outer_sum(mixed_ref[...], rows.full[...].reshape(seq, model))
     grads_ref[0] = outer_sum(gq[...], a_ref[...])
     grads_ref[1] = outer_sum(gv[...], a_ref[...])
     grads_ref[2] = outer_sum(gk[...], a_ref[...])
-
-    def close_block(step, carry):
-        rows = pl.ds(pl.multiple_of(step * BLOCK, BLOCK), BLOCK)
-        part_ref[rows, :] = (
-            matmul(gq[rows, :], qk_ref[0]) + matmul(gk[rows, :], qk_ref[1])
-            + matmul(gv[rows, :], vo_ref[0])
-        ).astype(BF16)
-        return carry
-
-    lax.fori_loop(0, seq // BLOCK, close_block, 0)
-
-
-def attend_back(length, slopes, gy, a, qk, vo, q, k, v, mixed, lse):
-    seq, model = a.shape
-    width = qk.shape[1]
-    return pl.pallas_call(
-        attend_back_body,
-        out_shape=(
-            jax.ShapeDtypeStruct((seq, model), BF16),
+    rows.finish(gy_ref, total_ref)
+
+
+def attend_back(team, ident, jobs, gy, length, slopes, a, qk, vo, q, k, v, mixed, lse):
+    part, model = gy.shape
+    seq, width = q.shape
+    return team_call(
+        attend_back_body, team, ident, jobs,
+        [gy, length, slopes, a, qk, vo, q, k, v, mixed, lse],
+        [VMEM, SMEM, SMEM] + [VMEM] * 8,
+        (
+            jax.ShapeDtypeStruct((part, model), F32),
             jax.ShapeDtypeStruct((4, width, model), F32),
             jax.ShapeDtypeStruct((2, width), F32),
         ),
-        in_specs=[SMEM, SMEM] + [VMEM] * 9,
-        out_specs=(VMEM,) * 3,
-        scratch_shapes=[pltpu.VMEM((seq, width), BF16)] * 4 + [pltpu.VMEM((seq, width), F32)] * 2,
-        compiler_params=pltpu.CompilerParams(vmem_limit_bytes=52 * 2**20),
-    )(length, slopes, gy, a, qk, vo, q, k, v, mixed, lse)
+        (VMEM,) * 3,
+        [pltpu.VMEM((seq, width), BF16)] * 4 + [pltpu.VMEM((seq, width), F32)] * 2,
+    )
 
 
 GELU_A = 0.7978845608028654
 GELU_B = 0.044715
 
 
-def feed_body(c_ref, up_ref, down_ref, bias_ref, before_ref, part_ref, total):
-    seq = c_ref.shape[0]
+def feed_body(rows, ins, outs, scratch):
+    x_ref, up_ref, down_ref, bias_ref = ins
+    total_ref, full_out, before_ref = outs
+    (full_sem,) = scratch
+    part = x_ref.shape[0]
     units = up_ref.shape[0]
     tile = min(units, BLOCK)
 
-    def one(step, carry):
-        rows = pl.ds(pl.multiple_of(step * BLOCK, BLOCK), BLOCK)
-        block = c_ref[rows, :]
+    def term(place):
+        at = part_rows(place, part)
+        block = rows.full[place]
+        total = None
         for first in range(0, units, tile):
             lanes = slice(first, first + tile)
             before = matmul_t(block, up_ref[lanes, :]) + bias_ref[:, lanes]
-            before_ref[rows, lanes] = before
+            before_ref[at, lanes] = before
             bend = jnp.tanh(GELU_A * (before + GELU_B * before * before * before))
             active = (0.5 * before * (1.0 + bend)).astype(BF16)
-            term = matmul(active, down_ref[lanes, :])
-            if first == 0:
-                total[...] = term
-            else:
-                total[...] += term
-        part_ref[rows, :] = total[...].astype(BF16)
-        return carry
-
-    lax.fori_loop(0, seq // BLOCK, one, 0)
-
-
-def feed(c, up, down, bias):
-    seq, model = c.shape
+            piece = matmul(active, down_ref[lanes, :])
+            total = piece if total is None else total + piece
+        return total
+
+    rows.each_arrival_and_back(x_ref, term)
+    keep = pltpu.make_async_copy(rows.full, full_out, full_sem)
+    keep.start()
+    rows.finish(x_ref, total_ref)
+    keep.wait()
+
+
+def feed(team, ident, jobs, x, up, down, bias):
+    part, model = x.shape
     units = up.shape[0]
-    return pl.pallas_call(
-        feed_body,
-        out_shape=(
-            jax.ShapeDtypeStruct((seq, units), F32),
-            jax.ShapeDtypeStruct((seq, model), BF16),
+    return team_call(
+        feed_body, team, ident, jobs,
+        [x, up, down, bias],
+        [VMEM] * 4,
+        (
+            jax.ShapeDtypeStruct((part, model), F32),
+            jax.ShapeDtypeStruct((team.count, part, model), BF16),
+            jax.ShapeDtypeStruct((part * team.count, units), F32),
         ),
-        in_specs=[VMEM] * 4,
-        out_specs=(VMEM, VMEM),
-        scratch_shapes=[pltpu.VMEM((BLOCK, model), F32)],
-        compiler_params=pltpu.CompilerParams(vmem_limit_bytes=48 * 2**20),
-    )(c, up, down, bias)
-
-
-def feed_back_body(
-    gz_ref, c_ref, before_ref, up_ref, down_ref, part_ref, grads_ref, sums_ref, active, low
-):
-    seq = c_ref.shape[0]
+        (VMEM, HBM, VMEM),
+        [pltpu.SemaphoreType.DMA],
+    )
+
+
+def feed_back_body(rows, ins, outs, scratch):
+    gz_ref, c_ref, before_ref, up_ref, down_ref = ins
+    total_ref, grads_ref, sums_ref = outs
+    active, low = scratch
+    part, model = gz_ref.shape
+    seq = part * rows.count
     units = up_ref.shape[0]
     tile = min(units, BLOCK)
     sums_ref[...] = jnp.zeros_like(sums_ref)
 
-    def one(step, carry):
-        rows = pl.ds(pl.multiple_of(step * BLOCK, BLOCK), BLOCK)
-        gz = gz_ref[rows, :]
+    def term(place):
+        at = part_rows(place, part)
+        gz = rows.full[place]
         for first in range(0, units, tile):
             lanes = slice(first, first + tile)
-            before = before_ref[rows, lanes]
+            before = before_ref[at, lanes]
             square = before * before
             bend = jnp.tanh(GELU_A * before * (1.0 + GELU_B * square))
             half = 0.5 * (1.0 + bend)
@@ -774,33 +887,34 @@
             )
             grad = matmul_t(gz, down_ref[lanes, :]) * slope
             sums_ref[:, lanes] += jnp.sum(grad, axis=0, keepdims=True)
-            active[rows, lanes] = (before * half).astype(BF16)
-            low[rows, lanes] = grad.astype(BF16)
-        part_ref[rows, :] = matmul(low[rows, :], up_ref[...]).astype(BF16)
-        return carry
-
-    lax.fori_loop(0, seq // BLOCK, one, 0)
+            active[at, lanes] = (before * half).astype(BF16)
+            low[at, lanes] = grad.astype(BF16)
+        return matmul(low[at, :], up_ref[...])
+
+    rows.each_arrival_and_back(gz_ref, term)
     for first in range(0, units, tile):
         lanes = slice(first, first + tile)
         grads_ref[0, lanes, :] = outer_sum(low[:, lanes], c_ref[...])
-        grads_ref[1, lanes, :] = outer_sum(active[:, lanes], gz_ref[...])
-
-
-def feed_back(gz, c, before, up, down):
-    seq, model = c.shape
+        grads_ref[1, lanes, :] = outer_sum(active[:, lanes], rows.full[...].reshape(seq, model))
+    rows.finish(gz_ref, total_ref)
+
+
+def feed_back(team, ident, jobs, gz, c, before, up, down):
+    part, model = gz.shape
+    seq = part * team.count
     units = up.shape[0]
-    return pl.pallas_call(
-        feed_back_body,
-        out_shape=(
-            jax.ShapeDtypeStruct((seq, model), BF16),
+    return team_call(
+        feed_back_body, team, ident, jobs,
+        [gz, c, before, up, down],
+        [VMEM] * 5,
+        (
+            jax.ShapeDtypeStruct((part, model), F32),
             jax.ShapeDtypeStruct((2, units, model), F32),
             jax.ShapeDtypeStruct((1, units), F32),
         ),
-        in_specs=[VMEM] * 5,
-        out_specs=(VMEM,) * 3,
-        scratch_shapes=[pltpu.VMEM((seq, units), BF16)] * 2,
-        compiler_params=pltpu.CompilerParams(vmem_limit_bytes=52 * 2**20),
-    )(gz, c, before, up, down)
+        (VMEM,) * 3,
+        [pltpu.VMEM((seq, units), BF16)] * 2,
+    )
 
 
 def per_device(
@@ -980,15 +1094,8 @@
                 jnp.concatenate([one[n] for one in strips]) for n in range(2)
             )
 
-    def whole(block, *jobs):
-        first, *got = exchange(gather(team, block.astype(BF16)), *jobs)
-        return first.reshape(seq, width), got
-
-    def summed(terms, *jobs):
-        first, *got = exchange(
-            Job("reduce", [team], terms.reshape(team.count, part, width)), *jobs
-        )
-        return first, got
+    def ident(kind, jobs):
+        return exchange.ident((kind,) + tuple(job.key() for job in jobs))
 
     local_ids = ids - vocab_start
     inside = (local_ids >= 0) & (local_ids < vocab)
@@ -1005,25 +1112,21 @@
     kept = []
     strips = []
     for l, p in enumerate(params):
-        normed, got = whole(
-            layer_norm(h, p["gains"][0], p["offsets"][0]),
-            *feed_jobs(l, 0 if l == 0 else 1),
-        )
-        strips += got
-        q, k, v, mixed, lse, back = attend(length, slopes, normed, p["qk"], p["vo"], p["bias"])
-        if l > 0:
-            take_feed(l, strips)
-        total, got = summed(back, *(feed_jobs(l, 1) if l == 0 else []))
-        if l == 0:
-            take_feed(l, strips + got)
+        jobs = (feed_jobs(l, 0) if l == 0 else []) + feed_jobs(l, 1)
+        normed = layer_norm(h, p["gains"][0], p["offsets"][0]).astype(BF16)
+        (total, normed, q, k, v, mixed, lse), got = attend(
+            team, ident("attend", jobs), jobs, normed, length, slopes, p["qk"], p["vo"], p["bias"]
+        )
+        take_feed(l, strips + got)
         middle = h + total + p["row_bias"][0]
-        second, got = whole(
-            layer_norm(middle, p["gains"][1], p["offsets"][1]), *attn_jobs(l + 1)
-        )
-        take_attn(l + 1, got)
-        before, back = feed(second, p["up"], p["down"], p["up_bias"])
-        kept.append((h, normed, q, k, v, mixed, lse, middle, second, before))
-        total, strips = summed(back, *feed_jobs(l + 1, 0))
+        jobs = attn_jobs(l + 1) + feed_jobs(l + 1, 0)
+        second = layer_norm(middle, p["gains"][1], p["offsets"][1]).astype(BF16)
+        (total, second, before), got = feed(
+            team, ident("feed", jobs), jobs, second, p["up"], p["down"], p["up_bias"]
+        )
+        take_attn(l + 1, got[:2])
+        strips = got[2:]
+        kept.append((h, normed.reshape(seq, width), q, k, v, mixed, lse, middle, second, before))
         h = middle + total + p["row_bias"][1]
 
     (final,) = exchange(
@@ -1087,22 +1190,24 @@
         p = params[l]
         section_in, normed, q, k, v, mixed, lse, middle, second, before = kept[l]
         late = planes and l + 1 < layers
-        gz, got = whole(grad, *(section_jobs(pairs[l + 1]) if late else []))
+        jobs = section_jobs(pairs[l + 1]) if late else []
+        (total, g_feed, up_sum), got = feed_back(
+            team, ident("feed back", jobs), jobs, grad.astype(BF16), second.reshape(seq, width),
+            before, p["up"], p["down"],
+        )
         if late:
             lows = section_sums(pairs[l + 1], got)
-        back, g_feed, up_sum = feed_back(gz, second, before, p["up"], p["down"])
         _, norm_back = jax.vjp(layer_norm, middle, p["gains"][1], p["offsets"][1])
-        total, got_a = summed(back, *(tensor_jobs(lows[:1]) if late else []))
         grad_mid, gain_two, offset_two = norm_back(total)
         grad_mid = grad_mid + grad
-        gy, got_b = whole(grad_mid, *(tensor_jobs(lows[1:]) if late else []))
-        back, g_attn, qv_sum = attend_back(
-            length, slopes, gy, normed, p["qk"], p["vo"], q, k, v, mixed, lse
+        jobs = tensor_jobs(lows) if late else []
+        (total, g_attn, qv_sum), got = attend_back(
+            team, ident("attend back", jobs), jobs, grad_mid.astype(BF16), length, slopes, normed,
+            p["qk"], p["vo"], q, k, v, mixed, lse,
         )
         if late:
-            done[l + 1] = tensor_sums(lows, got_a + got_b)
+            done[l + 1] = tensor_sums(lows, got)
         _, norm_back = jax.vjp(layer_norm, section_in, p["gains"][0], p["offsets"][0])
-        total, got = summed(back)
         grad_in, gain_one, offset_one = norm_back(total)
         bias_two = jnp.sum(grad, axis=0)
         grad = grad_in + grad_mid
@@ -1130,12 +1235,6 @@
 
     _, embed_back = jax.vjp(layer_norm, x, outer_gains[0], outer_offsets[0])
     grad_rows, embed_gain, embed_offset = embed_back(grad)
-    jobs = [gather(by_tensor, grad_rows.astype(BF16))]
-    if planes:
-        jobs += section_jobs(pairs[0]) + spread_jobs(done[1])
-    grad_rows, *got = exchange(*jobs)
-    grad_rows = grad_rows.reshape(tokens, width)
-
     packed = jnp.concatenate(
         [row for l in range(layers) for row in small_rows[l]]
         + [embed_gain[None], final_gain[None], embed_offset[None], final_offset[None]]
@@ -1143,17 +1242,22 @@
     )
     used = packed.shape[0]
     packed = jnp.pad(packed, ((0, -used % 8), (0, 0)))
-    packed = all_sum([by_section, by_dp, by_tensor], packed, exchange.ident("small"))
-    jobs = []
+    jobs = [gather(by_tensor, grad_rows.astype(BF16)), gather(by_dp, packed)]
+    if planes:
+        jobs += section_jobs(pairs[0]) + spread_jobs(done[1])
+    grad_rows, packed, *got = exchange(*jobs)
+    grad_rows = grad_rows.reshape(tokens, width)
+    packed = jnp.sum(packed, axis=0)
+    jobs = [gather(Group(("section", "tensor"), (sections, shards)), packed)]
     if planes:
         lows = section_sums(pairs[0], got[:2])
         spread_one = got[2:]
-        jobs = tensor_jobs(lows)
-    packed, grad_rows = tie(packed, grad_rows)
-    embed_sum, *got = table_sum(
+        jobs += tensor_jobs(lows)
+    embed_sum, packed, *got = table_sum(
         by_section, by_dp, jobs, grad_logits, ids[:, None] - vocab_start, final, grad_rows,
         exchange.ident("table"),
     )
+    packed = jnp.sum(packed, axis=0)
     if planes:
         spread_zero = exchange(*spread_jobs(tensor_sums(lows, got)))
         attn_sum, feed_sum = (

time: 1360 us -> 1270 us (0.934)
  Pallas kernels: 1190 us -> 1100 us
  other arithmetic: 72.9 us -> 96.8 us
  local copies, waits for them, and re-layouts: 79.6 us -> 61 us
    pallas_call x23 -> x7, Pallas kernels: 729 us -> 281 us  [__call__(): pl.pallas_call(functools.partial(exchange_body, jobs), out_shape=tuple((j...]
    pallas_call x9 -> x8, Pallas kernels: 180 us -> 526 us  [team_call(): pl.pallas_call(kernel, out_shape=tuple(outs) + tuple((job.out for job in...]
    unnamed x189 -> x127, local copies, waits for them, and re-layouts: 40.9 us -> 16.6 us
where the time goes in v3:
time: 1270 us; the launch traced here: 1260 us
  Pallas kernels  1100 us (87%)
  other arithmetic  96.8 us (8%)
  local copies, waits for them, and re-layouts  61 us (5%)
    pallas_call x8, Pallas kernels, team_call(): pl.pallas_call(kernel, out_shape=tuple(outs) + tuple((job.out for job in...  526 us
    pallas_call x7, Pallas kernels, __call__(): pl.pallas_call(functools.partial(exchange_body, jobs), out_shape=tuple((j...  281 us
    pallas_call x1, Pallas kernels, table_sum(): pl.pallas_call(functools.partial(table_body, by_section, by_dp, jobs), ou...  209 us
    pallas_call x1, Pallas kernels, head_grads(): pl.pallas_call(head_grads_body, grid=(chunks,), out_shape=(jax.ShapeDtype...  43 us
    pallas_call x1, Pallas kernels, head_logits(): pl.pallas_call(head_logits_body, grid=(vocab // CHUNK,), out_shape=(jax.S...  39.2 us

profile of v3, /device:TPU:1, one launch (start us, length us, event | category | flops | bytes accessed | tf_op | source)
XLA Modules:
  0.0 1260.1 jit_solution(3308860727290896236)
XLA Ops:
  0.7 1.6 fusion.43
  6.9 14.8 %shard_map.246 = (bf16[1,384,1024]{2,1,0:T(8,128)(2,1)S(1)}, s32[4,2,2,1024]{3,2,1,0:T(2,128)S(1)}, f32[8,16,1024]{2,1,0:T(8,128)S(1)}) custom-call(bf16[2,384,1024]{2,1,0:T(8,128)(2,1)S(1)} %pad_maximum_fusion.4.refs_0_, s32[2,2,1024]{2,1,0:T(2,128)S(1)} %pad_add_fusion.refs_1_, f32[16,1024]{1,0:T(8,128)S(1)} %concatenate.26.refs_2_), custom_call_target="tpu_custom_call" | custom-call | tf_op jit(solution)/shard_map/pallas_call | solution.py:221
  23.5 13.9 %gather_fusion = bf16[1024,1024]{1,0:T(8,128)(2,1)} fusion(bf16[8192,1024]{1,0:T(8,128)(2,1)} %e_ref.3, s32[1024]{0:T(1024)S(1)} %broadcast_clamp_fusion), kind=kCustom, calls=%fused_computation | custom fusion | bytes 4198400 | tf_op jit(solution)/shard_map/jit(_take)/gather | solution.py:1103
  37.5 1.9 select_select_fusion.refs_0_
  39.4 3.1 broadcast_select_fusion.2
  43.3 72.7 %shard_map.247 = (f32[256,1024]{1,0:T(8,128)S(1)}, bf16[2,4,64,1024]{3,2,1,0:T(8,128)(2,1)S(1)}, bf16[2,4,64,1024]{3,2,1,0:T(8,128)(2,1)S(1)}) custom-call(bf16[4,256,1024]{2,1,0:T(8,128)(2,1)S(1)} %select_select_fusion.refs_0_, bf16[64,1024]{1,0:T(8,128)(2,1)S(1)} %get-tuple-element.228.refs_1_, bf16[64,1024]{1,0:T(8,128)(2,1)S(1)} %get-tuple-element.227.refs_2_), custom_call_target="tpu_custom_call" | custom-call | tf_op jit(solution)/shard_map/pallas_call | solution.py:221
  120.5 1.5 add_convert_fusion.9.refs_0_
  125.4 68.7 %shard_map.248 = (f32[256,1024]{1,0:T(8,128)}, bf16[4,256,1024]{2,1,0:T(8,128)(2,1)}, bf16[1024,256]{1,0:T(8,128)(2,1)}, bf16[1024,256]{1,0:T(8,128)(2,1)}, bf16...) custom-call(bf16[256,1024]{1,0:T(8,128)(2,1)} %add_convert_fusion.9., ...), custom_call_target="tpu_custom_call" | custom-call | tf_op jit(solution)/shard_map/pallas_call | solution.py:648
  194.2 1.9 fusion.41
  196.6 1.5 pad_maximum_fusion.1.refs_2_.refs_4_
  198.1 1.5 pad_maximum_fusion.refs_1_.refs_3_
  204.7 67.0 %shard_map.249 = (f32[256,1024]{1,0:T(8,128)}, bf16[4,256,1024]{2,1,0:T(8,128)(2,1)}, f32[1024,1024]{1,0:T(8,128)}, bf16[2,4,64,1024]{3,2,1,0:T(8,128)(2,1)}, bf...) custom-call(bf16[256,1024]{1,0:T(8,128)(2,1)} %add_convert_fusion.8.refs_0_, ...), custom_call_target="tpu_custom_call" | custom-call | tf_op jit(solution)/shard_map/pallas_call | solution.py:648
  271.7 1.4 fusion.35
  275.2 63.2 %shard_map.250 = (f32[256,1024]{1,0:T(8,128)}, bf16[4,256,1024]{2,1,0:T(8,128)(2,1)}, bf16[1024,256]{1,0:T(8,128)(2,1)}, bf16[1024,256]{1,0:T(8,128)(2,1)}, bf16...) custom-call(bf16[256,1024]{1,0:T(8,128)(2,1)} %add_convert_fusion.7., ...), custom_call_target="tpu_custom_call" | custom-call | tf_op jit(solution)/shard_map/pallas_call | solution.py:648
  338.4 1.9 fusion.40
  340.9 1.5 pad_maximum_fusion.3.refs_2_.refs_4_
  342.3 1.5 pad_maximum_fusion.2.refs_1_.refs_3_
  346.0 59.6 %shard_map.251 = (f32[256,1024]{1,0:T(8,128)}, bf16[4,256,1024]{2,1,0:T(8,128)(2,1)}, f32[1024,1024]{1,0:T(8,128)}) custom-call(bf16[256,1024]{1,0:T(8,128)(2,1)} %add_convert_fusion.6.refs_0_, bf16[1024,1024]{1,0:T(8,128)(2,1)} %pad_maximum_fusion.2.refs_1_.refs_3_, bf16[1024,1024]{1,0:T(8,128)(2,1)} %pad_maximum_fusion.3.refs_2_.refs_4_, f32[1,1024]{1,0:T(1,128)} %bitcast.376), custom_call_target="tpu_custom_call" | custom-call | tf_op jit(solution)/shard_map/pallas_call | solution.py:648
  405.6 1.4 fusion.33
  407.6 36.4 %shard_map.252 = bf16[4,256,1024]{2,1,0:T(8,128)(2,1)S(1)} custom-call(bf16[256,1024]{1,0:T(8,128)(2,1)S(1)} %add_convert_fusion.5.refs_0_), custom_call_target="tpu_custom_call" | custom-call | tf_op jit(solution)/shard_map/pallas_call | solution.py:221
  446.4 39.2 %shard_map.253 = (f32[32,1024,256]{2,1,0:T(8,128)}, f32[1024,128]{1,0:T(8,128)S(1)}, f32[1024,128]{1,0:T(8,128)S(1)}, f32[1024,128]{1,0:T(8,128)S(1)}) custom-call(bf16[1024,1024]{1,0:T(8,128)(2,1)S(1)} %bitcast.252, bf16[8192,1024]{1,0:T(8,128)(2,1)} %e_ref.3, s32[1024,1]{1,0:T(8,128)S(1)} %bitcast.260), custom_call_target="tpu_custom_call" | custom-call | flops 17179869184 | bytes 50331648 | tf_op jit(solution)/shard_map/pallas_call | solution.py:464
  489.4 1.6 multiply_reduce_fusion.18
  492.2 15.0 %shard_map.254 = f32[4,8,1024]{2,1,0:T(8,128)S(1)} custom-call(f32[8,1024]{1,0:T(8,128)S(1)} %select_maximum_fusion.refs_0_), custom_call_target="tpu_custom_call" | custom-call | tf_op jit(solution)/shard_map/pallas_call | solution.py:221
  509.5 43.0 %shard_map.255 = (bf16[32,1024,256]{2,1,0:T(8,128)(2,1)}, bf16[1024,1024]{1,0:T(8,128)(2,1)S(1)}) custom-call(f32[32,1024,256]{2,1,0:T(8,128)} %get-tuple-element.95.logits_ref, bf16[8192,1024]{1,0:T(8,128)(2,1)} %e_ref.3, s32[1024,1]{1,0:T(8,128)S(1)} %bitcast.261, f32[1024,1]{1,0:T(8,128)S(1)} %copy.66.norm_ref, f32[1024,1]{1,0:T(8,128)S(1)} %bitcast.262), custom_call_target="tpu_custom_call" | custom-call | flops 17179869184 | bytes 67108864 | tf_op jit(solution)/shard_map/pallas_call | solution.py:511
  552.5 37.2 %shard_map.256 = f32[256,1024]{1,0:T(8,128)S(1)} custom-call(bf16[4,256,1024]{2,1,0:T(8,128)(2,1)S(1)} %bitcast.259), custom_call_target="tpu_custom_call" | custom-call | tf_op jit(solution)/shard_map/pallas_call | solution.py:221
  591.5 55.2 %shard_map.257 = (f32[256,1024]{1,0:T(8,128)}, f32[2,1024,1024]{2,1,0:T(8,128)}, f32[1,1024]{1,0:T(1,128)}) custom-call(bf16[256,1024]{1,0:T(8,128)(2,1)} %get-tuple-element.220.refs_0_, bf16[1024,1024]{1,0:T(8,128)(2,1)} %bitcast.298, f32[1024,1024]{1,0:T(8,128)} %get-tuple-element.102.refs_2_, bf16[1024,1024]{1,0:T(8,128)(2,1)} %pad_maximum_fusion.2.refs_1_.refs_3_, ...), custom_call_target="tpu_custom_call" | custom-call | tf_op jit(solution)/shard_map/pallas_call | solution.py:648
  646.8 1.7 multiply_reduce_fusion.2
  650.0 71.8 %shard_map.258 = (f32[256,1024]{1,0:T(8,128)}, f32[4,256,1024]{2,1,0:T(8,128)}, f32[2,256]{1,0:T(2,128)}) custom-call(bf16[256,1024]{1,0:T(8,128)(2,1)} %convert_element_type.182.refs_0_, s32[1]{0:T(128)} %dynamic_slice.119.refs_1_, f32[4]{0:T(128)} %multiply_exponential_fusion.refs_2_, bf16[1024,1024]{1,0:T(8,128)(2,1)} %bitcast.292, ...), custom_call_target="tpu_custom_call" | custom-call | tf_op jit(solution)/shard_map/pallas_call | solution.py:648
  721.8 1.7 multiply_reduce_fusion.3
  725.0 59.5 %shard_map.259 = (f32[256,1024]{1,0:T(8,128)}, f32[2,1024,1024]{2,1,0:T(8,128)}, f32[1,1024]{1,0:T(1,128)}, f32[1,2,256,1024]{3,2,1,0:T(8,128)}, f32[1,1024,1024]{2,1,0:T(8,128)}) custom-call(bf16[256,1024]{1,0:T(8,128)(2,1)} %convert_element_type.183.refs_0_, bf16[1024,1024]{1,0:T(8,128)(2,1)} %bitcast.291, f32[1024,1024]{1,0:T(8,128)} %get-tuple-element.112.refs_2_, ...), custom_call_target="tpu_custom_call" | custom-call | tf_op jit(solution)/shard_map/pallas_call | solution.py:648
  784.5 5.7 add_convert_fusion.1
  794.0 81.0 %shard_map.260 = (f32[256,1024]{1,0:T(8,128)}, f32[4,256,1024]{2,1,0:T(8,128)}, f32[2,256]{1,0:T(2,128)}, bf16[3,2,64,1024]{3,2,1,0:T(8,128)(2,1)}, bf16[3,2,128,1024]{3,2,1,0:T(8,128)(2,1)}) custom-call(bf16[256,1024]{1,0:T(8,128)(2,1)} %convert_element_type.184.refs_0_, s32[1]{0:T(128)} %dynamic_slice.119.refs_1_, f32[4]{0:T(128)} %multiply_exponential_fusion.refs_2_, ...), custom_call_target="tpu_custom_call" | custom-call | tf_op jit(solution)/shard_map/pallas_call | solution.py:648
  875.1 2.8 convert_reduce_fusion.1
  877.9 1.6 fusion.2.refs_5_
  882.1 1.4 multiply_reduce_fusion.1
  886.1 1.8 fusion.27
  888.6 52.2 %shard_map.261 = (bf16[4,256,1024]{2,1,0:T(8,128)(2,1)S(1)}, f32[4,32,1024]{2,1,0:T(8,128)S(1)}, f32[1,2,256,1024]{3,2,1,0:T(8,128)S(1)}, f32[1,1024,1024]{2,1,0...) custom-call(bf16[256,1024]{1,0:T(8,128)(2,1)S(1)} %add_convert_fusion.4.refs_0_, ...), custom_call_target="tpu_custom_call" | custom-call | tf_op jit(solution)/shard_map/pallas_call | solution.py:221
  940.8 2.0 copy-done.6
  942.8 5.0 add_convert_fusion
  950.8 208.7 %shard_map.262 = (bf16[32,256,1024]{2,1,0:T(8,128)(2,1)}, f32[8,32,1024]{2,1,0:T(8,128)}, bf16[3,2,64,1024]{3,2,1,0:T(8,128)(2,1)}, bf16[3,2,128,1024]{3,2,1,0:T(8,128)(2,1)}) custom-call(bf16[32,1024,256]{2,1,0:T(8,128)(2,1)} %get-tuple-element.99.g_ref, s32[1024,1]{1,0:T(8,128)} %copy.76.ids_ref, bf16[1024,1024]{1,0:T(8,128)(2,1)} %bitcast.253, ...), custom_call_target="tpu_custom_call" | custom-call | tf_op jit(solution)/shard_map/pallas_call | solution.py:397
  1159.5 1.9 convert_reduce_fusion
  1163.9 52.4 %shard_map.263 = (bf16[2,4,2,64,1024]{4,3,2,1,0:T(8,128)(2,1)S(1)}, bf16[2,4,2,128,1024]{4,3,2,1,0:T(8,128)(2,1)S(1)}) custom-call(bf16[2,64,1024]{2,1,0:T(8,128)(2,1)S(1)} %fusion.4.refs_0_, bf16[2,128,1024]{2,1,0:T(8,128)(2,1)S(1)} %fusion.1.refs_1_), custom_call_target="tpu_custom_call" | custom-call | tf_op jit(solution)/shard_map/pallas_call | solution.py:221
  1218.1 1.8 fusion.37
  1219.9 2.6 bitcast_convert_fusion.2
  1222.5 5.3 copy.82
  1227.8 4.2 bitcast_convert_fusion.1
  1233.1 1.9 fusion
  1236.2 18.8 %bitcast_convert_fusion = f32[8192,1024]{1,0:T(8,128)} fusion(bf16[32,256,1024]{2,1,0:T(8,128)(2,1)} %get-tuple-element.138), kind=kLoop, calls=%fused_computation.1 | loop fusion | flops 8388608 | bytes 50331648 | tf_op jit(solution)/shard_map/convert_element_type | solution.py:1276
  (286 shorter events, 61.6 us)
Async XLA Ops:
  0.6 2.3 copy-start
  3.3 2.6 copy-start.28
  5.6 1.1 copy-start.57
  5.6 1.1 copy-start.45
  5.6 1.1 copy-start.46
  5.6 1.1 copy-start.47
  5.6 1.1 copy-start.50
  5.7 1.1 copy-start.51
  5.7 1.2 copy-start.48
  5.7 1.2 copy-start.49
  37.5 1.9 copy-start.13
  118.4 5.1 copy-start.36
  120.0 4.3 copy-start.56
  194.2 2.2 copy-start.38
  198.1 1.5 copy-start.42
  200.1 71.6 %copy-start.19 = (f32[256,1024]{1,0:T(8,128)}, f32[256,1024]{1,0:T(8,128)S(1)}, u32[]{:S(2)}) copy-start(f32[256,1024]{1,0:T(8,128)S(1)} %get-tuple-element.199) | copy-start | bytes 3145732
  200.1 1.7 copy-start.34
  273.1 70.7 %copy-start.21 = (f32[256,1024]{1,0:T(8,128)}, f32[256,1024]{1,0:T(8,128)S(1)}, u32[]{:S(2)}) copy-start(f32[256,1024]{1,0:T(8,128)S(1)} %get-tuple-element.197) | copy-start | bytes 3145732
  338.4 2.2 copy-start.37
  342.3 1.5 copy-start.40
  344.1 61.5 %copy-start.23 = (f32[256,1024]{1,0:T(8,128)}, f32[256,1024]{1,0:T(8,128)S(1)}, u32[]{:S(2)}) copy-start(f32[256,1024]{1,0:T(8,128)S(1)} %get-tuple-element.195) | copy-start | bytes 3145732
  407.0 37.0 %copy-start.25 = (f32[256,1024]{1,0:T(8,128)}, f32[256,1024]{1,0:T(8,128)S(1)}, u32[]{:S(2)}) copy-start(f32[256,1024]{1,0:T(8,128)S(1)} %get-tuple-element.193) | copy-start | bytes 3145732
  444.0 41.6 %copy-start.3 = (bf16[4,256,1024]{2,1,0:T(8,128)(2,1)}, bf16[4,256,1024]{2,1,0:T(8,128)(2,1)S(1)}, u32[]{:S(2)}) copy-start(bf16[4,256,1024]{2,1,0:T(8,128)(2,1)S(1)} %shard_map.252) | copy-start | bytes 6291460
  488.1 21.4 %copy-start.16 = (s32[1,1024]{0,1:T(8,128)S(1)}, s32[1,1024]{0,1:T(8,128)}, u32[]{:S(2)}) copy-start(s32[1,1024]{0,1:T(8,128)} %copy.101) | copy-start | bytes 12292
  552.5 37.2 %copy-start.26 = (f32[256,1024]{1,0:T(8,128)S(1)}, f32[256,1024]{1,0:T(8,128)}, u32[]{:S(2)}) copy-start(f32[256,1024]{1,0:T(8,128)} %copy-done.25) | copy-start | bytes 3145732
  591.5 55.2 %copy-start.24 = (f32[256,1024]{1,0:T(8,128)S(1)}, f32[256,1024]{1,0:T(8,128)}, u32[]{:S(2)}) copy-start(f32[256,1024]{1,0:T(8,128)} %copy-done.23) | copy-start | bytes 3145732
  646.8 1.7 copy-start.32
  650.0 71.8 %copy-start.22 = (f32[256,1024]{1,0:T(8,128)S(1)}, f32[256,1024]{1,0:T(8,128)}, u32[]{:S(2)}) copy-start(f32[256,1024]{1,0:T(8,128)} %copy-done.21) | copy-start | bytes 3145732
  721.8 1.7 copy-start.31
  784.5 5.7 copy-start.27
  784.5 5.7 copy-start.39
  790.2 1.3 copy-start.20
  790.2 1.9 copy-start.30
  875.1 4.5 copy-start.43
  877.9 2.8 copy-start.33
  882.0 1.5 copy-start.55
  882.0 1.9 copy-start.53
  882.0 2.0 copy-start.54
  882.0 2.4 copy-start.52
  886.0 2.5 copy-start.2
  940.8 2.0 copy-start.6
  942.8 5.0 copy-start.8
  1159.5 3.3 copy-start.44
  1161.4 56.3 %copy-start.7 = (bf16[2,4,2,128,1024]{4,3,2,1,0:T(8,128)(2,1)S(1)}, bf16[2,4,2,128,1024]{4,3,2,1,0:T(8,128)(2,1)}, u32[]{:S(2)}) copy-start(bf16[2,4,2,128,1024]{4,3,2,1,0:T(8,128)(2,1)} %copy-done.6) | copy-start | bytes 12582916
  1216.3 1.3 copy-start.9
  1227.8 4.2 copy-start.10
  1236.2 18.8 %copy-start.41 = (f32[8,32,1024]{2,1,0:T(8,128)S(1)}, f32[8,32,1024]{2,1,0:T(8,128)}, u32[]{:S(2)}) copy-start(f32[8,32,1024]{2,1,0:T(8,128)} %get-tuple-element.137) | copy-start | bytes 3145732
  1236.2 22.5 %copy-start.1 = (bf16[1,1024,1024]{2,1,0:T(8,128)(2,1)S(1)}, bf16[1,1024,1024]{2,1,0:T(8,128)(2,1)}, u32[]{:S(2)}) copy-start(bf16[1,1024,1024]{2,1,0:T(8,128)(2,1)} %param.26) | copy-start | bytes 6291460
  (10 other events, 9.0 us)

commit v4 on v3

--- a/solution.py
+++ b/solution.py
@@ -44,7 +44,8 @@
 
 
 class Group:
-    def __init__(self, axes, sizes):
+    def __init__(self, axes, sizes, square=False):
+        self.square = square
         self.axes = axes
         self.sizes = sizes
         self.count = math.prod(sizes)
@@ -111,7 +112,10 @@
             self.out = jax.ShapeDtypeStruct((count,) + x.shape, x.dtype)
         elif kind == "spread":
             self.out = jax.ShapeDtypeStruct((groups[1].count, count) + x.shape, x.dtype)
-            self.scratch += [dma((count,)), dma((count,))]
+            copies = 7 if groups[0].square else count
+            if groups[0].square:
+                self.scratch = [dma((6,)), dma((6,)), dma]
+            self.scratch += [dma((copies,)), dma((copies,))]
         elif kind == "deal":
             self.out = jax.ShapeDtypeStruct((count - 1,) + rest, x.dtype)
         else:
@@ -138,6 +142,52 @@
             def finish():
                 for copy in copies + [own]:
                     copy.wait()
+
+        elif self.kind == "spread" and group.square:
+            pair = self.groups[1]
+            side = pair.me()
+            fw_send, fw_recv = more
+            size = self.x.shape[0] // 2
+            near = [across(me, 0), across(me, 1)]
+
+            def copy_of(number):
+                at = pl.ds(SQUARE_HALF[number] * size, size)
+                place = me if number < 4 else near[number - 4]
+                dst = out.at[side, place, at]
+                src = x.at[at] if number < 4 else dst
+                copy = pltpu.make_async_remote_copy(
+                    src_ref=src, dst_ref=dst, send_sem=send_sem.at[number],
+                    recv_sem=recv_sem.at[number], device_id=group.device(near[SQUARE_STEP[number]]),
+                    device_id_type=MESH,
+                )
+                origin = near[SQUARE_STEP[number]] if number < 4 else across(me, 2)
+                return copy, out.at[side, origin, at]
+
+            copies = [copy_of(number) for number in range(6)]
+            for number in (0, 2, 1, 3):
+                copies[number][0].start()
+            passed = [send(pair, 1 - side, 6, x, out.at[side, me], fw_send, fw_recv)]
+            own = pltpu.make_async_copy(x, out.at[side, me], own_sem)
+            own.start()
+
+            def arrived(number):
+                copy, landed = copies[number]
+                copy.wait_recv()
+                passed.append(send(pair, 1 - side, number, landed, landed, fw_send, fw_recv))
+
+            def finish():
+                for number in (0, 2):
+                    copies[number][0].wait_recv()
+                    copies[4 + number // 2][0].start()
+                    landed = copies[number][1]
+                    passed.append(send(pair, 1 - side, number, landed, landed, fw_send, fw_recv))
+                for number in (1, 3, 4, 5):
+                    arrived(number)
+                for copy in passed:
+                    copy.wait()
+                for copy, _ in copies:
+                    copy.wait_send()
+                own.wait()
 
         elif self.kind == "spread":
             pair = self.groups[1]
@@ -329,9 +379,9 @@
                     fetch(index + 1, 0, 1 - slot).start()
 
             base = chunk(half, peers[number], sub) * CHUNK
-            place = base + lax.broadcasted_iota(jnp.int32, (tokens, CHUNK), 1)
+            place = base + lax.broadcasted_iota(jnp.int32, (CHUNK, tokens), 0)
             chosen = jnp.where(place == ids_ref[...], 1.0, 0.0).astype(BF16)
-            term = outer_sum(g_buf[slot], u_ref[...]) + outer_sum(chosen, gx_ref[...])
+            term = outer_sum(g_buf[slot], u_ref[...]) + matmul(chosen, gx_ref[...])
             if away == 0:
                 to_partner[number, rows(sub), :] = term.astype(BF16)
                 partner_copy(number, sub).start()
@@ -384,6 +434,202 @@
         end()
 
 
+def across(me, step):
+    bits = jnp.int32(step + 1)
+    x, y = lax.rem(me, 2), lax.div(me, 2)
+    return 2 * lax.rem(y + lax.div(bits, 2), 2) + lax.rem(x + lax.rem(bits, 2), 2)
+
+
+SQUARE_HALF = (0, 1, 1, 0, 0, 1)
+SQUARE_STEP = (0, 0, 1, 1, 1, 0)
+
+
+def table_square_body(by_section, by_dp, jobs, g_ref, ids_ref, u_ref, gx_ref, *refs):
+    riders = len(jobs)
+    xs, (out_ref, *outs), refs = refs[:riders], refs[riders : 2 * riders + 1], refs[2 * riders + 1 :]
+    (
+        g_buf, to_partner, from_partner, to_dp, hop_land, from_dp, own, result,
+        g_sem, ps_send, ps_recv, hop_send, hop_recv, dp_send, dp_recv, ag_send, ag_recv,
+        fw_send, fw_recv, own_sem,
+    ) = refs[:20]
+    s, j = by_section.me(), by_dp.me()
+    partner = 1 - s
+    near_x, near_y, far = (across(j, step) for step in range(3))
+    peers = [far, near_y, near_x, j]
+    count = 4
+    block = own.shape[0]
+    subs = block // CHUNK
+    half_rows = CHUNK // 2
+    tokens = u_ref.shape[0]
+    greet([by_section, by_dp] + job_groups(jobs))
+    parts = split_scratch(jobs, refs[20:])
+    ends = [job.start(xs[n], outs[n], *parts[n]) for n, job in enumerate(jobs)]
+
+    def chunk(half, place, sub):
+        return (half * count + place) * subs + sub
+
+    order = [(number, away) for number in range(count) for away in (0, 1)]
+
+    def fetch(index, sub, slot):
+        number, away = order[index]
+        half = partner if away == 0 else s
+        return pltpu.make_async_copy(
+            g_ref.at[chunk(half, peers[number], sub)], g_buf.at[slot], g_sem.at[slot]
+        )
+
+    def remote(group, peer, number, sub, src, dst, send_sem, recv_sem):
+        return pltpu.make_async_remote_copy(
+            src_ref=src,
+            dst_ref=dst,
+            send_sem=send_sem.at[number, sub],
+            recv_sem=recv_sem.at[number, sub],
+            device_id=group.device(peer),
+            device_id_type=MESH,
+        )
+
+    def rows(sub):
+        return pl.ds(pl.multiple_of(sub * CHUNK, CHUNK), CHUNK)
+
+    def half_of(sub, which):
+        return pl.ds(pl.multiple_of(sub * CHUNK + which * half_rows, half_rows), half_rows)
+
+    def partner_copy(number, sub):
+        return remote(
+            by_section, partner, number, sub,
+            to_partner.at[number, rows(sub)], from_partner.at[number, rows(sub)],
+            ps_send, ps_recv,
+        )
+
+    def hop_copy(which, sub):
+        return remote(
+            by_dp, (near_x, near_y)[which], which, sub,
+            to_dp.at[0, half_of(sub, which)], hop_land.at[half_of(sub, which)], hop_send, hop_recv,
+        )
+
+    def chip_copy(number, sub):
+        return remote(
+            by_dp, (near_y, near_x)[number], number, sub,
+            to_dp.at[number + 1, rows(sub)], from_dp.at[number, rows(sub)], dp_send, dp_recv,
+        )
+
+    def spread_copy(number, sub):
+        which = SQUARE_HALF[number]
+        place = j if number < 4 else (near_x, near_y)[number - 4]
+        dst = out_ref.at[chunk(s, place, sub), pl.ds(which * half_rows, half_rows)]
+        src = result.at[half_of(sub, which)] if number < 4 else dst
+        peer = (near_x, near_y)[SQUARE_STEP[number]]
+        return remote(by_dp, peer, number, sub, src, dst, ag_send, ag_recv)
+
+    sources = [near_x, near_y, far, j]
+
+    def forward_copy(number, sub):
+        target = out_ref.at[chunk(s, sources[number], sub)]
+        origin = result.at[rows(sub)] if number == count - 1 else target
+        return remote(by_section, partner, number, sub, origin, target, fw_send, fw_recv)
+
+    def own_copy(sub):
+        return pltpu.make_async_copy(
+            result.at[rows(sub)], out_ref.at[chunk(s, j, sub)], own_sem.at[sub]
+        )
+
+    fetch(0, 0, 0).start()
+    for index, (number, away) in enumerate(order):
+        half = partner if away == 0 else s
+
+        def one(sub, carry, index=index, number=number, away=away, half=half):
+            slot = lax.rem(sub, 2)
+            fetch(index, sub, slot).wait()
+
+            @pl.when(sub + 1 < subs)
+            def _():
+                fetch(index, sub + 1, 1 - slot).start()
+
+            if index + 1 < len(order):
+
+                @pl.when(sub + 1 == subs)
+                def _():
+                    fetch(index + 1, 0, 1 - slot).start()
+
+            base = chunk(half, peers[number], sub) * CHUNK
+            place = base + lax.broadcasted_iota(jnp.int32, (CHUNK, tokens), 0)
+            chosen = jnp.where(place == ids_ref[...], 1.0, 0.0).astype(BF16)
+            term = outer_sum(g_buf[slot], u_ref[...]) + matmul(chosen, gx_ref[...])
+            if away == 0:
+                to_partner[number, rows(sub), :] = term.astype(BF16)
+                partner_copy(number, sub).start()
+                return carry
+            partner_copy(number, sub).wait_recv()
+            term = term + from_partner[number, rows(sub), :].astype(F32)
+            if number == 0:
+                to_dp[0, rows(sub), :] = term.astype(BF16)
+                for which in range(2):
+                    hop_copy(which, sub).start()
+            elif number < 3:
+                which = number - 1
+                hop_copy(which, sub).wait_recv()
+                mine = slice(which * half_rows, (which + 1) * half_rows)
+                rest = slice((1 - which) * half_rows, (2 - which) * half_rows)
+                to_dp[number, half_of(sub, which), :] = (
+                    term[mine] + hop_land[half_of(sub, which), :].astype(F32)
+                ).astype(BF16)
+                to_dp[number, half_of(sub, 1 - which), :] = term[rest].astype(BF16)
+                chip_copy(which, sub).start()
+            else:
+                own[rows(sub), :] = term
+            return carry
+
+        lax.fori_loop(0, subs, one, 0)
+
+    def finish(sub, carry):
+        term = own[rows(sub), :]
+        for number in range(2):
+            chip_copy(number, sub).wait_recv()
+            term = term + from_dp[number, rows(sub), :].astype(F32)
+        result[rows(sub), :] = term.astype(BF16)
+        for number in (0, 2, 1, 3):
+            spread_copy(number, sub).start()
+        forward_copy(count - 1, sub).start()
+        own_copy(sub).start()
+        return carry
+
+    lax.fori_loop(0, subs, finish, 0)
+
+    def pass_on(sub, carry):
+        for number in (0, 2):
+            spread_copy(number, sub).wait_recv()
+            spread_copy(4 + number // 2, sub).start()
+        for number in (0, 1):
+            spread_copy(2 * number + 1, sub).wait_recv()
+            forward_copy(number, sub).start()
+        return carry
+
+    lax.fori_loop(0, subs, pass_on, 0)
+
+    def last(sub, carry):
+        for number in (4, 5):
+            spread_copy(number, sub).wait_recv()
+        forward_copy(2, sub).start()
+        return carry
+
+    lax.fori_loop(0, subs, last, 0)
+
+    def drain(sub, carry):
+        own_copy(sub).wait()
+        for number in range(count):
+            partner_copy(number, sub).wait_send()
+            forward_copy(number, sub).wait()
+        for number in range(2):
+            hop_copy(number, sub).wait_send()
+            chip_copy(number, sub).wait_send()
+        for number in range(6):
+            spread_copy(number, sub).wait_send()
+        return carry
+
+    lax.fori_loop(0, subs, drain, 0)
+    for end in ends:
+        end()
+
+
 def table_sum(by_section, by_dp, jobs, grads, ids, final, grad_rows, ident):
     chunks, tokens, _ = grads.shape
     width = final.shape[1]
@@ -391,35 +637,32 @@
     subs = chunks // (2 * count)
     block = subs * CHUNK
     assert subs % 2 == 0
+    dma = pltpu.SemaphoreType.DMA
+    low = functools.partial(pltpu.VMEM, dtype=BF16)
+    square = by_dp.square
+    scratch = [
+        low((2, tokens, CHUNK)),
+        low((count, block, width)),
+        low((count, block, width)),
+        low((count - 1, block, width)),
+    ]
+    scratch += [low((block, width)), low((2, block, width))] if square else [
+        low((count - 1, block, width))
+    ]
+    scratch += [pltpu.VMEM((block, width), F32), low((block, width)), dma((2,))]
+    copies = (count, 2, 2, 6, count) if square else (count, count - 1, count - 1, count)
+    scratch += [dma((copy, subs)) for copy in copies for _ in range(2)] + [dma((subs,))]
     vmem = pl.BlockSpec(memory_space=pltpu.VMEM)
     hbm = pl.BlockSpec(memory_space=pl.ANY)
-    dma = pltpu.SemaphoreType.DMA
     return pl.pallas_call(
-        functools.partial(table_body, by_section, by_dp, jobs),
+        functools.partial(
+            table_square_body if by_dp.square else table_body, by_section, by_dp, jobs
+        ),
         out_shape=(jax.ShapeDtypeStruct((chunks, CHUNK, width), BF16),)
         + tuple(job.out for job in jobs),
         in_specs=[hbm, vmem, vmem, vmem] + [job.in_spec for job in jobs],
         out_specs=(hbm,) + tuple(job.out_spec for job in jobs),
-        scratch_shapes=[
-            pltpu.VMEM((2, tokens, CHUNK), BF16),
-            pltpu.VMEM((count, block, width), BF16),
-            pltpu.VMEM((count, block, width), BF16),
-            pltpu.VMEM((count - 1, block, width), BF16),
-            pltpu.VMEM((count - 1, block, width), BF16),
-            pltpu.VMEM((block, width), F32),
-            pltpu.VMEM((block, width), BF16),
-            dma((2,)),
-            dma((count, subs)),
-            dma((count, subs)),
-            dma((count - 1, subs)),
-            dma((count - 1, subs)),
-            dma((count - 1, subs)),
-            dma((count - 1, subs)),
-            dma((count, subs)),
-            dma((count, subs)),
-            dma((subs,)),
-        ]
-        + [one for job in jobs for one in job.scratch],
+        scratch_shapes=scratch + [one for job in jobs for one in job.scratch],
         compiler_params=pltpu.CompilerParams(
             collective_id=ident, has_side_effects=True, vmem_limit_bytes=56 * 2**20
         ),
@@ -546,82 +789,133 @@
 
 
 class TeamRows:
-    def __init__(self, team, full, stage, slots, own, ag_send, ag_recv, rs_send, rs_recv):
+    def __init__(self, team, x_ref, full, stage, slots, own, ag_send, ag_recv, rs_send, rs_recv):
         self.team, self.count, self.me = team, team.count, team.me()
-        self.full, self.stage, self.slots, self.own = full, stage, slots, own
-        self.sems = (ag_send, ag_recv, rs_send, rs_recv)
+        self.x_ref, self.full, self.stage, self.slots, self.own = x_ref, full, stage, slots, own
+        self.ag_sems, self.rs_sems = (ag_send, ag_recv), (rs_send, rs_recv)
+
+    def shifted(self, step):
+        return across(self.me, step)
 
     def peer(self, step):
+        if self.team.square:
+            return self.shifted(step)
         return lax.rem(self.me + 1 + step, self.count)
 
     def source(self, step):
+        if self.team.square:
+            return self.shifted(step)
         return lax.rem(self.me + self.count - 1 - step, self.count)
 
-    def remote(self, step, src, dst, send_sem, recv_sem):
+    def back_step(self, place):
+        if self.team.square:
+            flip_x = lax.rem(lax.rem(self.me, 2) + lax.rem(place, 2), 2)
+            flip_y = lax.rem(lax.div(self.me, 2) + lax.div(place, 2), 2)
+            return 2 * flip_y + flip_x - 1
+        return lax.rem(place + self.count - 1 - self.me, self.count)
+
+    def remote(self, number, peer, src, dst, sems):
         return pltpu.make_async_remote_copy(
             src_ref=src,
             dst_ref=dst,
-            send_sem=send_sem.at[step],
-            recv_sem=recv_sem.at[step],
-            device_id=self.team.device(self.peer(step)),
+            send_sem=sems[0].at[number],
+            recv_sem=sems[1].at[number],
+            device_id=self.team.device(peer),
             device_id_type=MESH,
         )
 
-    def ag(self, step, x_ref):
-        return self.remote(step, x_ref, self.full.at[self.me], self.sems[0], self.sems[1])
+    def ag(self, number):
+        if not self.team.square:
+            return self.remote(
+                number, self.peer(number), self.x_ref, self.full.at[self.me], self.ag_sems
+            )
+        half = self.x_ref.shape[0] // 2
+        which = SQUARE_HALF[number]
+        rows = pl.ds(which * half, half)
+        peer = self.shifted(SQUARE_STEP[number])
+        if number < 4:
+            src, place = self.x_ref.at[rows], self.me
+        else:
+            place = self.shifted(number - 4)
+            src = self.full.at[place, rows]
+        return self.remote(number, peer, src, self.full.at[place, rows], self.ag_sems)
 
     def rs(self, step):
         return self.remote(
-            step, self.stage.at[self.peer(step)], self.slots.at[step], self.sems[2], self.sems[3]
-        )
-
-    def send_rows(self, x_ref):
-        for step in range(self.count - 1):
-            self.ag(step, x_ref).start()
-        self.full[self.me] = x_ref[...]
-
-    def each_arrival(self, x_ref, work):
+            step, self.peer(step), self.stage.at[self.peer(step)], self.slots.at[step], self.rs_sems
+        )
+
+    def send_rows(self):
+        for number in (0, 2, 1, 3) if self.team.square else range(self.count - 1):
+            self.ag(number).start()
+        self.full[self.me] = self.x_ref[...]
+
+    def pass_on(self):
+        if self.team.square:
+            for number in (0, 2):
+                self.ag(number).wait_recv()
+                self.ag(4 + number // 2).start()
+
+    def wait_rows(self, step):
+        if not self.team.square:
+            self.ag(step).wait_recv()
+            return
+        for number, these in enumerate(((1,), (3,), (4, 5))):
+
+            @pl.when(step == number)
+            def _(these=these):
+                for one in these:
+                    self.ag(one).wait_recv()
+
+    def each_arrival(self, work):
         work(self.me)
+        self.pass_on()
 
         def one(step, carry):
-            self.ag(step, x_ref).wait_recv()
+            self.wait_rows(step)
             work(self.source(step))
             return carry
 
         lax.fori_loop(0, self.count - 1, one, 0)
 
-    def each_arrival_and_back(self, x_ref, term):
+    def each_arrival_and_back(self, term):
         self.own[...] = term(self.me)
+        self.pass_on()
 
         def one(step, carry):
-            self.ag(step, x_ref).wait_recv()
+            self.wait_rows(step)
             place = self.source(step)
             self.stage[place] = term(place).astype(BF16)
-            self.rs(self.count - 2 - step).start()
+            self.rs(self.back_step(place)).start()
             return carry
 
         lax.fori_loop(0, self.count - 1, one, 0)
 
-    def finish(self, x_ref, total_ref):
+    def finish(self, total_ref):
         for step in range(self.count - 1):
             self.rs(step).wait()
         total = self.own[...]
         for step in range(self.count - 1):
             total = total + self.slots[step].astype(F32)
         total_ref[...] = total
-        for step in range(self.count - 1):
-            self.ag(step, x_ref).wait_send()
+        for number in range(6 if self.team.square else self.count - 1):
+            self.ag(number).wait_send()
 
 
 def team_scratch(team, part, model):
     count = team.count
     dma = pltpu.SemaphoreType.DMA
+    copies = 6 if team.square else count - 1
     return [
         pltpu.VMEM((count, part, model), BF16),
         pltpu.VMEM((count, part, model), BF16),
         pltpu.VMEM((count - 1, part, model), BF16),
         pltpu.VMEM((part, model), F32),
-    ] + [dma((count - 1,))] * 4
+        dma((copies,)),
+        dma((copies,)),
+        dma((count - 1,)),
+        dma((count - 1,)),
+    ]
 
 
 def team_call(body, team, ident, jobs, arrays, specs, outs, out_specs, scratch):
@@ -634,11 +928,11 @@
         xs, refs = refs[:riders], refs[riders:]
         results, refs = refs[:count_out], refs[count_out:]
         landings, refs = refs[:riders], refs[riders:]
-        rows = TeamRows(team, *refs[: len(own_scratch)])
+        rows = TeamRows(team, ins[0], *refs[: len(own_scratch)])
         refs = refs[len(own_scratch) :]
         mine, refs = refs[: len(scratch)], refs[len(scratch) :]
         greet([team] + job_groups(jobs))
-        rows.send_rows(ins[0])
+        rows.send_rows()
         parts = split_scratch(jobs, refs)
         ends = [job.start(xs[n], landings[n], *parts[n]) for n, job in enumerate(jobs)]
         body(rows, ins, results, mine)
@@ -676,11 +970,12 @@
         k_ref[at, :] = matmul_t(block, qk_ref[1]).astype(BF16)
         v_ref[at, :] = (matmul_t(block, vo_ref[0]) + bias_ref[1:2, :]).astype(BF16)
 
-    rows.each_arrival(x_ref, project)
+    rows.each_arrival(project)
     keep = pltpu.make_async_copy(rows.full, full_out, full_sem)
     keep.start()
 
-    def one(step, carry):
+    def one(turn, carry):
+        step = lax.rem(2 * rows.count - 2 - turn, rows.count)
         place = rows.peer(step)
         for block in range(rows.count):
 
@@ -713,7 +1008,7 @@
         return carry
 
     lax.fori_loop(0, rows.count, one, 0)
-    rows.finish(x_ref, total_ref)
+    rows.finish(total_ref)
     keep.wait()
 
 
@@ -754,7 +1049,7 @@
     def open_block(place):
         go[part_rows(place, part), :] = matmul_t(rows.full[place], vo_ref[1]).astype(BF16)
 
-    rows.each_arrival(gy_ref, open_block)
+    rows.each_arrival(open_block)
     for block in reversed(range(rows.count)):
         first, upto = block * part, (block + 1) * part
         for head in range(heads):
@@ -781,7 +1076,7 @@
         @pl.when(rows.me != block)
         def _(block=block, term=term):
             rows.stage[block] = term.astype(BF16)
-            rows.rs(lax.rem(block + rows.count - 1 - rows.me, rows.count)).start()
+            rows.rs(rows.back_step(block)).start()
 
         @pl.when(rows.me == block)
         def _(term=term):
@@ -793,7 +1088,7 @@
     grads_ref[0] = outer_sum(gq[...], a_ref[...])
     grads_ref[1] = outer_sum(gv[...], a_ref[...])
     grads_ref[2] = outer_sum(gk[...], a_ref[...])
-    rows.finish(gy_ref, total_ref)
+    rows.finish(total_ref)
 
 
 def attend_back(team, ident, jobs, gy, length, slopes, a, qk, vo, q, k, v, mixed, lse):
@@ -839,10 +1134,10 @@
             total = piece if total is None else total + piece
         return total
 
-    rows.each_arrival_and_back(x_ref, term)
+    rows.each_arrival_and_back(term)
     keep = pltpu.make_async_copy(rows.full, full_out, full_sem)
     keep.start()
-    rows.finish(x_ref, total_ref)
+    rows.finish(total_ref)
     keep.wait()
 
 
@@ -891,12 +1186,12 @@
             low[at, lanes] = grad.astype(BF16)
         return matmul(low[at, :], up_ref[...])
 
-    rows.each_arrival_and_back(gz_ref, term)
+    rows.each_arrival_and_back(term)
     for first in range(0, units, tile):
         lanes = slice(first, first + tile)
         grads_ref[0, lanes, :] = outer_sum(low[:, lanes], c_ref[...])
         grads_ref[1, lanes, :] = outer_sum(active[:, lanes], rows.full[...].reshape(seq, model))
-    rows.finish(gz_ref, total_ref)
+    rows.finish(total_ref)
 
 
 def feed_back(team, ident, jobs, gz, c, before, up, down):
@@ -947,6 +1242,7 @@
     rows = token_ids.shape[0] * groups
     local_cols = qkv_weight.shape[-1]
     planes = rows == sections * shards and local_cols % (groups * HEAD_DIM) == 0
+    by_dp.square = planes and groups == 4
     team = by_dp if planes else by_tensor
     cut = groups if planes else 1
     fan = shards if planes else 1
@@ -1185,28 +1481,31 @@
     small_rows = [None] * layers
     pairs = [None] * layers
     done = [None] * layers
-    lows = None
+    feed_low = [None] * layers
     for l in reversed(range(layers)):
         p = params[l]
         section_in, normed, q, k, v, mixed, lse, middle, second, before = kept[l]
         late = planes and l + 1 < layers
-        jobs = section_jobs(pairs[l + 1]) if late else []
+        jobs = section_jobs([pairs[l + 1][0]]) + tensor_jobs(feed_low[l + 1]) if late else []
         (total, g_feed, up_sum), got = feed_back(
             team, ident("feed back", jobs), jobs, grad.astype(BF16), second.reshape(seq, width),
             before, p["up"], p["down"],
         )
         if late:
-            lows = section_sums(pairs[l + 1], got)
+            attn_low = section_sums([pairs[l + 1][0]], got[:1])
+            feed_done = tensor_sums(feed_low[l + 1], got[1:])
         _, norm_back = jax.vjp(layer_norm, middle, p["gains"][1], p["offsets"][1])
         grad_mid, gain_two, offset_two = norm_back(total)
         grad_mid = grad_mid + grad
-        jobs = tensor_jobs(lows) if late else []
+        jobs = section_jobs([g_feed]) + (tensor_jobs(attn_low) if late else [])
         (total, g_attn, qv_sum), got = attend_back(
             team, ident("attend back", jobs), jobs, grad_mid.astype(BF16), length, slopes, normed,
             p["qk"], p["vo"], q, k, v, mixed, lse,
         )
+        if planes:
+            feed_low[l] = section_sums([g_feed], got[:1])
         if late:
-            done[l + 1] = tensor_sums(lows, got)
+            done[l + 1] = tensor_sums(attn_low, got[1:]) + feed_done
         _, norm_back = jax.vjp(layer_norm, section_in, p["gains"][0], p["offsets"][0])
         grad_in, gain_one, offset_one = norm_back(total)
         bias_two = jnp.sum(grad, axis=0)
@@ -1244,17 +1543,17 @@
     packed = jnp.pad(packed, ((0, -used % 8), (0, 0)))
     jobs = [gather(by_tensor, grad_rows.astype(BF16)), gather(by_dp, packed)]
     if planes:
-        jobs += section_jobs(pairs[0]) + spread_jobs(done[1])
+        jobs += section_jobs(pairs[0][:1]) + spread_jobs(done[1])
     grad_rows, packed, *got = exchange(*jobs)
     grad_rows = grad_rows.reshape(tokens, width)
     packed = jnp.sum(packed, axis=0)
     jobs = [gather(Group(("section", "tensor"), (sections, shards)), packed)]
     if planes:
-        lows = section_sums(pairs[0], got[:2])
-        spread_one = got[2:]
+        lows = section_sums(pairs[0][:1], got[:1]) + feed_low[0]
+        spread_one = got[1:]
         jobs += tensor_jobs(lows)
     embed_sum, packed, *got = table_sum(
-        by_section, by_dp, jobs, grad_logits, ids[:, None] - vocab_start, final, grad_rows,
+        by_section, by_dp, jobs, grad_logits, ids[None, :] - vocab_start, final, grad_rows,
         exchange.ident("table"),
     )
     packed = jnp.sum(packed, axis=0)

time: 1270 us -> 1160 us (0.913)
  Pallas kernels: 1100 us -> 990 us
    pallas_call x8, Pallas kernels: 526 us -> 473 us  [team_call(): pl.pallas_call(kernel, out_shape=tuple(outs) + tuple((job.out for job in...]
    pallas_call x1, Pallas kernels: 209 us -> 170 us  [table_sum(): pl.pallas_call(functools.partial(table_square_body if by_dp.square else t...]
    pallas_call x7, Pallas kernels: 281 us -> 264 us  [__call__(): pl.pallas_call(functools.partial(exchange_body, jobs), out_shape=tuple((j...]
where the time goes in v4:
time: 1160 us; the launch traced here: 1150 us
  Pallas kernels  990 us (85%)
  other arithmetic  97.2 us (8%)
  local copies, waits for them, and re-layouts  60.1 us (5%)
    pallas_call x8, Pallas kernels, team_call(): pl.pallas_call(kernel, out_shape=tuple(outs) + tuple((job.out for job in...  473 us
    pallas_call x7, Pallas kernels, __call__(): pl.pallas_call(functools.partial(exchange_body, jobs), out_shape=tuple((j...  264 us
    pallas_call x1, Pallas kernels, table_sum(): pl.pallas_call(functools.partial(table_square_body if by_dp.square else t...  170 us
    pallas_call x1, Pallas kernels, head_grads(): pl.pallas_call(head_grads_body, grid=(chunks,), out_shape=(jax.ShapeDtype...  43 us
    pallas_call x1, Pallas kernels, head_logits(): pl.pallas_call(head_logits_body, grid=(vocab // CHUNK,), out_shape=(jax.S...  39.2 us

profile of v4, /device:TPU:1, one launch (start us, length us, event | category | flops | bytes accessed | tf_op | source)
XLA Modules:
  0.0 1151.5 jit_solution(16257240895479960839)
XLA Ops:
  0.7 1.6 fusion.43
  6.9 14.8 %shard_map.246 = (bf16[1,384,1024]{2,1,0:T(8,128)(2,1)S(1)}, s32[4,2,2,1024]{3,2,1,0:T(2,128)S(1)}, f32[8,16,1024]{2,1,0:T(8,128)S(1)}) custom-call(bf16[2,384,1024]{2,1,0:T(8,128)(2,1)S(1)} %pad_maximum_fusion.4.refs_0_, s32[2,2,1024]{2,1,0:T(2,128)S(1)} %pad_add_fusion.refs_1_, f32[16,1024]{1,0:T(8,128)S(1)} %concatenate.26.refs_2_), custom_call_target="tpu_custom_call" | custom-call | tf_op jit(solution)/shard_map/pallas_call | solution.py:271
  23.5 13.9 %gather_fusion = bf16[1024,1024]{1,0:T(8,128)(2,1)} fusion(bf16[8192,1024]{1,0:T(8,128)(2,1)} %e_ref.3, s32[1024]{0:T(1024)S(1)} %broadcast_clamp_fusion), kind=kCustom, calls=%fused_computation | custom fusion | bytes 4198400 | tf_op jit(solution)/shard_map/jit(_take)/gather | solution.py:1399
  37.5 1.9 select_select_fusion.refs_0_
  39.4 3.1 broadcast_select_fusion.2
  43.3 72.7 %shard_map.247 = (f32[256,1024]{1,0:T(8,128)S(1)}, bf16[2,4,64,1024]{3,2,1,0:T(8,128)(2,1)S(1)}, bf16[2,4,64,1024]{3,2,1,0:T(8,128)(2,1)S(1)}) custom-call(bf16[4,256,1024]{2,1,0:T(8,128)(2,1)S(1)} %select_select_fusion.refs_0_, bf16[64,1024]{1,0:T(8,128)(2,1)S(1)} %get-tuple-element.228.refs_1_, bf16[64,1024]{1,0:T(8,128)(2,1)S(1)} %get-tuple-element.227.refs_2_), custom_call_target="tpu_custom_call" | custom-call | tf_op jit(solution)/shard_map/pallas_call | solution.py:271
  120.4 1.5 add_convert_fusion.9.refs_0_
  125.4 63.0 %shard_map.248 = (f32[256,1024]{1,0:T(8,128)}, bf16[4,256,1024]{2,1,0:T(8,128)(2,1)}, bf16[1024,256]{1,0:T(8,128)(2,1)}, bf16[1024,256]{1,0:T(8,128)(2,1)}, bf16...) custom-call(bf16[256,1024]{1,0:T(8,128)(2,1)} %add_convert_fusion.9., ...), custom_call_target="tpu_custom_call" | custom-call | tf_op jit(solution)/shard_map/pallas_call | solution.py:942
  188.5 1.9 fusion.41
  190.9 1.5 pad_maximum_fusion.1.refs_2_.refs_4_
  192.4 1.5 pad_maximum_fusion.refs_1_.refs_3_
  198.9 55.1 %shard_map.249 = (f32[256,1024]{1,0:T(8,128)}, bf16[4,256,1024]{2,1,0:T(8,128)(2,1)}, f32[1024,1024]{1,0:T(8,128)}, bf16[2,4,64,1024]{3,2,1,0:T(8,128)(2,1)}, bf...) custom-call(bf16[256,1024]{1,0:T(8,128)(2,1)} %add_convert_fusion.8.refs_0_, ...), custom_call_target="tpu_custom_call" | custom-call | tf_op jit(solution)/shard_map/pallas_call | solution.py:942
  254.0 1.4 fusion.35
  257.5 57.0 %shard_map.250 = (f32[256,1024]{1,0:T(8,128)}, bf16[4,256,1024]{2,1,0:T(8,128)(2,1)}, bf16[1024,256]{1,0:T(8,128)(2,1)}, bf16[1024,256]{1,0:T(8,128)(2,1)}, bf16...) custom-call(bf16[256,1024]{1,0:T(8,128)(2,1)} %add_convert_fusion.7., ...), custom_call_target="tpu_custom_call" | custom-call | tf_op jit(solution)/shard_map/pallas_call | solution.py:942
  314.5 1.9 fusion.40
  317.0 1.5 pad_maximum_fusion.3.refs_2_.refs_4_
  318.4 1.5 pad_maximum_fusion.2.refs_1_.refs_3_
  322.2 47.4 %shard_map.251 = (f32[256,1024]{1,0:T(8,128)}, bf16[4,256,1024]{2,1,0:T(8,128)(2,1)}, f32[1024,1024]{1,0:T(8,128)}) custom-call(bf16[256,1024]{1,0:T(8,128)(2,1)} %add_convert_fusion.6.refs_0_, bf16[1024,1024]{1,0:T(8,128)(2,1)} %pad_maximum_fusion.2.refs_1_.refs_3_, bf16[1024,1024]{1,0:T(8,128)(2,1)} %pad_maximum_fusion.3.refs_2_.refs_4_, f32[1,1024]{1,0:T(1,128)} %bitcast.381), custom_call_target="tpu_custom_call" | custom-call | tf_op jit(solution)/shard_map/pallas_call | solution.py:942
  369.6 1.4 fusion.33
  371.6 36.4 %shard_map.252 = bf16[4,256,1024]{2,1,0:T(8,128)(2,1)S(1)} custom-call(bf16[256,1024]{1,0:T(8,128)(2,1)S(1)} %add_convert_fusion.5.refs_0_), custom_call_target="tpu_custom_call" | custom-call | tf_op jit(solution)/shard_map/pallas_call | solution.py:271
  410.3 39.2 %shard_map.253 = (f32[32,1024,256]{2,1,0:T(8,128)}, f32[1024,128]{1,0:T(8,128)S(1)}, f32[1024,128]{1,0:T(8,128)S(1)}, f32[1024,128]{1,0:T(8,128)S(1)}) custom-call(bf16[1024,1024]{1,0:T(8,128)(2,1)S(1)} %bitcast.257, bf16[8192,1024]{1,0:T(8,128)(2,1)} %e_ref.3, s32[1024,1]{1,0:T(8,128)S(1)} %bitcast.265), custom_call_target="tpu_custom_call" | custom-call | flops 17179869184 | bytes 50331648 | tf_op jit(solution)/shard_map/pallas_call | solution.py:707
  453.3 1.6 multiply_reduce_fusion.18
  456.1 15.0 %shard_map.254 = f32[4,8,1024]{2,1,0:T(8,128)S(1)} custom-call(f32[8,1024]{1,0:T(8,128)S(1)} %select_maximum_fusion.refs_0_), custom_call_target="tpu_custom_call" | custom-call | tf_op jit(solution)/shard_map/pallas_call | solution.py:271
  473.4 43.0 %shard_map.255 = (bf16[32,1024,256]{2,1,0:T(8,128)(2,1)}, bf16[1024,1024]{1,0:T(8,128)(2,1)S(1)}) custom-call(f32[32,1024,256]{2,1,0:T(8,128)} %get-tuple-element.95.logits_ref, bf16[8192,1024]{1,0:T(8,128)(2,1)} %e_ref.3, s32[1024,1]{1,0:T(8,128)S(1)} %bitcast.266, f32[1024,1]{1,0:T(8,128)S(1)} %copy.66.norm_ref, f32[1024,1]{1,0:T(8,128)S(1)} %bitcast.267), custom_call_target="tpu_custom_call" | custom-call | flops 17179869184 | bytes 67108864 | tf_op jit(solution)/shard_map/pallas_call | solution.py:754
  516.4 37.3 %shard_map.256 = f32[256,1024]{1,0:T(8,128)S(1)} custom-call(bf16[4,256,1024]{2,1,0:T(8,128)(2,1)S(1)} %bitcast.264), custom_call_target="tpu_custom_call" | custom-call | tf_op jit(solution)/shard_map/pallas_call | solution.py:271
  555.5 48.8 %shard_map.257 = (f32[256,1024]{1,0:T(8,128)}, f32[2,1024,1024]{2,1,0:T(8,128)}, f32[1,1024]{1,0:T(1,128)}) custom-call(bf16[256,1024]{1,0:T(8,128)(2,1)} %get-tuple-element.220.refs_0_, bf16[1024,1024]{1,0:T(8,128)(2,1)} %bitcast.303, f32[1024,1024]{1,0:T(8,128)} %get-tuple-element.102.refs_2_, bf16[1024,1024]{1,0:T(8,128)(2,1)} %pad_maximum_fusion.2.refs_1_.refs_3_, ...), custom_call_target="tpu_custom_call" | custom-call | tf_op jit(solution)/shard_map/pallas_call | solution.py:942
  604.3 1.7 multiply_reduce_fusion.2
  607.5 67.7 %shard_map.258 = (f32[256,1024]{1,0:T(8,128)}, f32[4,256,1024]{2,1,0:T(8,128)}, f32[2,256]{1,0:T(2,128)}, f32[1,1024,1024]{2,1,0:T(8,128)}) custom-call(bf16[256,1024]{1,0:T(8,128)(2,1)} %convert_element_type.182.refs_0_, s32[1]{0:T(128)} %dynamic_slice.119.refs_1_, f32[4]{0:T(128)} %multiply_exponential_fusion.refs_2_, bf16[1024,1024]{1,0:T(8,128)(2,1)} %bitcast.298, ...), custom_call_target="tpu_custom_call" | custom-call | tf_op jit(solution)/shard_map/pallas_call | solution.py:942
  675.3 5.6 add_convert_fusion.1
  682.9 57.3 %shard_map.259 = (f32[256,1024]{1,0:T(8,128)}, f32[2,1024,1024]{2,1,0:T(8,128)}, f32[1,1024]{1,0:T(1,128)}, f32[1,2,256,1024]{3,2,1,0:T(8,128)}, bf16[3,2,128,1024]{3,2,1,0:T(8,128)(2,1)}) custom-call(bf16[256,1024]{1,0:T(8,128)(2,1)} %convert_element_type.183.refs_0_, bf16[1024,1024]{1,0:T(8,128)(2,1)} %bitcast.297, ...), custom_call_target="tpu_custom_call" | custom-call | tf_op jit(solution)/shard_map/pallas_call | solution.py:942
  740.2 3.7 add_convert_fusion.3
  745.8 77.1 %shard_map.260 = (f32[256,1024]{1,0:T(8,128)}, f32[4,256,1024]{2,1,0:T(8,128)}, f32[2,256]{1,0:T(2,128)}, f32[1,1024,1024]{2,1,0:T(8,128)}, bf16[3,2,64,1024]{3,2,1,0:T(8,128)(2,1)}) custom-call(bf16[256,1024]{1,0:T(8,128)(2,1)} %convert_element_type.186.refs_0_, s32[1]{0:T(128)} %dynamic_slice.119.refs_1_, f32[4]{0:T(128)} %multiply_exponential_fusion.refs_2_, ...), custom_call_target="tpu_custom_call" | custom-call | tf_op jit(solution)/shard_map/pallas_call | solution.py:942
  822.9 5.6 add_convert_fusion
  829.8 1.6 fusion.2.refs_4_
  833.9 1.4 multiply_reduce_fusion.1
  838.1 1.8 fusion.27
  840.6 53.9 %shard_map.261 = (bf16[4,256,1024]{2,1,0:T(8,128)(2,1)S(1)}, f32[4,32,1024]{2,1,0:T(8,128)S(1)}, f32[1,2,256,1024]{3,2,1,0:T(8,128)S(1)}, bf16[2,4,2,64,1024]{4,...) custom-call(bf16[256,1024]{1,0:T(8,128)(2,1)S(1)} %add_convert_fusion.4.refs_0_, f32[32,1024]{1,0:T(8,128)S(1)} %pad.19.refs_1_, ...), custom_call_target="tpu_custom_call" | custom-call | tf_op jit(solution)/shard_map/pallas_call | solution.py:271
  895.8 1.5 add_convert_fusion.2
  899.4 169.9 %shard_map.262 = (bf16[32,256,1024]{2,1,0:T(8,128)(2,1)}, f32[8,32,1024]{2,1,0:T(8,128)}, bf16[3,2,64,1024]{3,2,1,0:T(8,128)(2,1)}, bf16[3,2,128,1024]{3,2,1,0:T(8,128)(2,1)}) custom-call(bf16[32,1024,256]{2,1,0:T(8,128)(2,1)} %get-tuple-element.99.g_ref, s32[1,1024]{1,0:T(1,128)} %bitcast.369, bf16[1024,1024]{1,0:T(8,128)(2,1)} %bitcast.258, ...), custom_call_target="tpu_custom_call" | custom-call | tf_op jit(solution)/shard_map/pallas_call | solution.py:657
  1069.2 1.9 convert_reduce_fusion
  1071.1 1.3 fusion.1.refs_1_
  1073.6 34.1 %shard_map.263 = (bf16[2,4,2,64,1024]{4,3,2,1,0:T(8,128)(2,1)S(1)}, bf16[2,4,2,128,1024]{4,3,2,1,0:T(8,128)(2,1)S(1)}) custom-call(bf16[2,64,1024]{2,1,0:T(8,128)(2,1)S(1)} %fusion.4.refs_0_, bf16[2,128,1024]{2,1,0:T(8,128)(2,1)S(1)} %fusion.1.refs_1_), custom_call_target="tpu_custom_call" | custom-call | tf_op jit(solution)/shard_map/pallas_call | solution.py:271
  1109.5 1.8 fusion.37
  1111.3 2.6 bitcast_convert_fusion.2
  1113.9 5.3 copy.81
  1119.3 4.2 bitcast_convert_fusion.1
  1124.6 1.9 fusion
  1127.6 18.8 %bitcast_convert_fusion = f32[8192,1024]{1,0:T(8,128)} fusion(bf16[32,256,1024]{2,1,0:T(8,128)(2,1)} %get-tuple-element.138), kind=kLoop, calls=%fused_computation.1 | loop fusion | flops 8388608 | bytes 50331648 | tf_op jit(solution)/shard_map/convert_element_type | solution.py:1575
  (284 shorter events, 60.5 us)
Async XLA Ops:
  0.6 2.3 copy-start
  3.3 2.6 copy-start.27
  5.6 1.1 copy-start.56
  5.6 1.1 copy-start.44
  5.6 1.1 copy-start.45
  5.6 1.1 copy-start.46
  5.6 1.1 copy-start.49
  5.7 1.1 copy-start.50
  5.7 1.2 copy-start.47
  5.7 1.2 copy-start.48
  37.5 1.9 copy-start.13
  118.3 5.1 copy-start.35
  120.0 4.3 copy-start.55
  188.5 2.2 copy-start.37
  192.4 1.5 copy-start.41
  194.4 59.6 %copy-start.19 = (f32[256,1024]{1,0:T(8,128)}, f32[256,1024]{1,0:T(8,128)S(1)}, u32[]{:S(2)}) copy-start(f32[256,1024]{1,0:T(8,128)S(1)} %get-tuple-element.199) | copy-start | bytes 3145732
  194.4 1.7 copy-start.33
  255.4 64.5 %copy-start.21 = (f32[256,1024]{1,0:T(8,128)}, f32[256,1024]{1,0:T(8,128)S(1)}, u32[]{:S(2)}) copy-start(f32[256,1024]{1,0:T(8,128)S(1)} %get-tuple-element.197) | copy-start | bytes 3145732
  314.5 2.2 copy-start.36
  318.4 1.5 copy-start.39
  320.2 49.4 %copy-start.23 = (f32[256,1024]{1,0:T(8,128)}, f32[256,1024]{1,0:T(8,128)S(1)}, u32[]{:S(2)}) copy-start(f32[256,1024]{1,0:T(8,128)S(1)} %get-tuple-element.195) | copy-start | bytes 3145732
  371.0 37.0 %copy-start.25 = (f32[256,1024]{1,0:T(8,128)}, f32[256,1024]{1,0:T(8,128)S(1)}, u32[]{:S(2)}) copy-start(f32[256,1024]{1,0:T(8,128)S(1)} %get-tuple-element.193) | copy-start | bytes 3145732
  408.0 41.5 %copy-start.3 = (bf16[4,256,1024]{2,1,0:T(8,128)(2,1)}, bf16[4,256,1024]{2,1,0:T(8,128)(2,1)S(1)}, u32[]{:S(2)}) copy-start(bf16[4,256,1024]{2,1,0:T(8,128)(2,1)S(1)} %shard_map.252) | copy-start | bytes 6291460
  409.3 1.0 copy-start.15
  452.0 21.4 %copy-start.16 = (s32[1,1024]{0,1:T(8,128)S(1)}, s32[1,1024]{0,1:T(8,128)}, u32[]{:S(2)}) copy-start(s32[1,1024]{0,1:T(8,128)} %copy.100) | copy-start | bytes 12292
  516.4 37.3 %copy-start.26 = (f32[256,1024]{1,0:T(8,128)S(1)}, f32[256,1024]{1,0:T(8,128)}, u32[]{:S(2)}) copy-start(f32[256,1024]{1,0:T(8,128)} %copy-done.25) | copy-start | bytes 3145732
  555.5 48.8 %copy-start.24 = (f32[256,1024]{1,0:T(8,128)S(1)}, f32[256,1024]{1,0:T(8,128)}, u32[]{:S(2)}) copy-start(f32[256,1024]{1,0:T(8,128)} %copy-done.23) | copy-start | bytes 3145732
  604.3 1.7 copy-start.31
  675.2 5.7 copy-start.22
  675.3 5.7 copy-start.29
  740.2 3.7 copy-start.20
  740.2 3.7 copy-start.30
  822.9 5.6 copy-start.38
  828.5 2.9 copy-start.42
  829.8 2.8 copy-start.32
  833.9 1.5 copy-start.54
  833.9 1.9 copy-start.52
  833.9 2.0 copy-start.53
  833.9 2.4 copy-start.51
  838.1 2.5 copy-start.2
  894.4 1.3 copy-start.8
  895.8 2.3 copy-start.6
  1069.2 3.3 copy-start.43
  1071.1 38.0 %copy-start.7 = (bf16[2,4,2,128,1024]{4,3,2,1,0:T(8,128)(2,1)S(1)}, bf16[2,4,2,128,1024]{4,3,2,1,0:T(8,128)(2,1)}, u32[]{:S(2)}) copy-start(bf16[2,4,2,128,1024]{4,3,2,1,0:T(8,128)(2,1)} %copy-done.6) | copy-start | bytes 12582916
  1107.8 1.3 copy-start.9
  1119.3 4.2 copy-start.10
  1127.6 18.8 %copy-start.40 = (f32[8,32,1024]{2,1,0:T(8,128)S(1)}, f32[8,32,1024]{2,1,0:T(8,128)}, u32[]{:S(2)}) copy-start(f32[8,32,1024]{2,1,0:T(8,128)} %get-tuple-element.137) | copy-start | bytes 3145732
  1127.6 22.5 %copy-start.1 = (bf16[1,1024,1024]{2,1,0:T(8,128)(2,1)S(1)}, bf16[1,1024,1024]{2,1,0:T(8,128)(2,1)}, u32[]{:S(2)}) copy-start(bf16[1,1024,1024]{2,1,0:T(8,128)(2,1)} %param.26) | copy-start | bytes 6291460
  (9 other events, 8.0 us)

commit v5 on v4

--- a/solution.py
+++ b/solution.py
@@ -44,8 +44,9 @@
 
 
 class Group:
-    def __init__(self, axes, sizes, square=False):
+    def __init__(self, axes, sizes, square=False, line=False):
         self.square = square
+        self.line = line
         self.axes = axes
         self.sizes = sizes
         self.count = math.prod(sizes)
@@ -97,8 +98,132 @@
     return lax.optimization_barrier(arrays)
 
 
+class LineRows:
+    def __init__(self, group, x, full, send_sem, recv_sem):
+        self.group, self.count, self.me = group, group.count, group.me()
+        self.x, self.full, self.sems = x, full, (send_sem, recv_sem)
+
+    def copy(self, up, step):
+        place = self.me - step if up else self.me + step
+        place = jnp.clip(place, 0, self.count - 1)
+        number = step if up else self.count - 1 + step
+        src = self.x if step == 0 else self.full.at[place]
+        return pltpu.make_async_remote_copy(
+            src_ref=src,
+            dst_ref=self.full.at[place],
+            send_sem=self.sems[0].at[number],
+            recv_sem=self.sems[1].at[number],
+            device_id=self.group.device(
+                jnp.clip(self.me + 1 if up else self.me - 1, 0, self.count - 1)
+            ),
+            device_id_type=MESH,
+        )
+
+    def leaves(self, up, step):
+        if up:
+            return (self.me - step >= 0) & (self.me < self.count - 1)
+        return (self.me + step < self.count) & (self.me > 0)
+
+    def arrives(self, up, step):
+        return self.me - 1 - step >= 0 if up else self.me + 1 + step < self.count
+
+    def start(self):
+        for up in (True, False):
+
+            @pl.when(self.leaves(up, 0))
+            def _(up=up):
+                self.copy(up, 0).start()
+
+    def step(self, step):
+        for up in (True, False):
+
+            @pl.when(self.arrives(up, step - 1))
+            def _(up=up):
+                self.copy(up, step - 1).wait_recv()
+
+            if step < self.count - 1:
+
+                @pl.when(self.leaves(up, step))
+                def _(up=up):
+                    self.copy(up, step).start()
+
+    def wait_sends(self):
+        for step in range(self.count - 1):
+            for up in (True, False):
+
+                @pl.when(self.leaves(up, step))
+                def _(up=up, step=step):
+                    self.copy(up, step).wait_send()
+
+    def finish(self):
+        for step in range(1, self.count):
+            self.step(step)
+        self.wait_sends()
+
+
+class LineSum:
+    def __init__(self, group, x, stage, land, send_sem, recv_sem):
+        self.group, self.count, self.me = group, group.count, group.me()
+        self.x, self.stage, self.land, self.sems = x, stage, land, (send_sem, recv_sem)
+
+    def copy(self, up, step):
+        side = 0 if up else 1
+        return pltpu.make_async_remote_copy(
+            src_ref=self.stage.at[side, step],
+            dst_ref=self.land.at[side, step],
+            send_sem=self.sems[0].at[side, step],
+            recv_sem=self.sems[1].at[side, step],
+            device_id=self.group.device(
+                jnp.clip(self.me + 1 if up else self.me - 1, 0, self.count - 1)
+            ),
+            device_id_type=MESH,
+        )
+
+    def leaves(self, up, step):
+        return self.me < self.count - 1 - step if up else self.me > step
+
+    def behind(self, up):
+        return self.me > 0 if up else self.me < self.count - 1
+
+    def step(self, step):
+        for up in (True, False):
+            place = self.count - 1 - step if up else step
+            side = 0 if up else 1
+
+            @pl.when(self.leaves(up, step) & self.behind(up))
+            def _(up=up, place=place, side=side):
+                self.copy(up, step).wait_recv()
+                total = self.x[place].astype(F32) + self.land[side, step].astype(F32)
+                self.stage[side, step] = total.astype(self.stage.dtype)
+                self.copy(up, step).start()
+
+            @pl.when(self.leaves(up, step) & jnp.logical_not(self.behind(up)))
+            def _(up=up, place=place, side=side):
+                self.stage[side, step] = self.x[place]
+                self.copy(up, step).start()
+
+    def finish(self, out):
+        out[...] = self.x[self.me].astype(F32)
+        for up in (True, False):
+            side = 0 if up else 1
+            for step in range(self.count - 1):
+
+                @pl.when(self.behind(up) & (self.me == (self.count - 1 - step if up else step)))
+                def _(up=up, step=step, side=side):
+                    self.copy(up, step).wait_recv()
+                    out[...] += self.land[side, step].astype(F32)
+
+        for up in (True, False):
+            for step in range(self.count - 1):
+
+                @pl.when(self.leaves(up, step))
+                def _(up=up, step=step):
+                    self.copy(up, step).wait_send()
+
+
 class Job:
-    def __init__(self, kind, groups, x, axis=0):
+    def __init__(self, kind, groups, x, axis=0, late=False):
+        self.late = late
         self.kind, self.groups, self.x, self.axis = kind, groups, x, axis
         count = groups[0].count
         rest = x.shape[:axis] + x.shape[axis + 1 :]
@@ -108,6 +233,8 @@
         self.scratch = [dma((count - 1,)), dma((count - 1,)), dma]
         if kind in ("gather", "spread"):
             self.in_spec = pl.BlockSpec(memory_space=pltpu.VMEM)
+        if kind == "gather" and groups[0].line:
+            self.scratch = [dma((2 * count - 2,)), dma((2 * count - 2,)), dma]
         if kind == "gather":
             self.out = jax.ShapeDtypeStruct((count,) + x.shape, x.dtype)
         elif kind == "spread":
@@ -121,7 +248,14 @@
         else:
             self.out = jax.ShapeDtypeStruct(rest, F32)
             self.out_spec = pl.BlockSpec(memory_space=pltpu.VMEM)
-            self.scratch += [pltpu.VMEM(rest, x.dtype), pltpu.VMEM((count - 1,) + rest, x.dtype)]
+            if groups[0].line:
+                self.in_spec = pl.BlockSpec(memory_space=pltpu.VMEM)
+                self.scratch = [dma((2, count - 1)), dma((2, count - 1)), dma]
+                self.scratch += [pltpu.VMEM((2, count - 1) + rest, x.dtype)] * 2
+            else:
+                self.scratch += [
+                    pltpu.VMEM(rest, x.dtype), pltpu.VMEM((count - 1,) + rest, x.dtype)
+                ]
 
     def key(self):
         return (self.kind, tuple(g.axes for g in self.groups), self.x.shape, str(self.x.dtype), self.axis)
@@ -134,7 +268,26 @@
         def block(place):
             return x.at[(slice(None),) * self.axis + (place,)]
 
-        if self.kind == "gather":
+        if self.kind == "gather" and group.line:
+            line = LineRows(group, x, out, send_sem, recv_sem)
+            line.start()
+            own = pltpu.make_async_copy(x, out.at[me], own_sem)
+            own.start()
+
+            def finish():
+                line.finish()
+                own.wait()
+
+        elif self.kind == "reduce" and group.line:
+            line = LineSum(group, x, *more, send_sem, recv_sem)
+            line.step(0)
+
+            def finish():
+                for step in range(1, group.count - 1):
+                    line.step(step)
+                line.finish(out)
+
+        elif self.kind == "gather":
             copies = [send(group, p, k, x, out.at[me], send_sem, recv_sem) for k, p in peers]
             own = pltpu.make_async_copy(x, out.at[me], own_sem)
             own.start()
@@ -282,17 +435,27 @@
         )(*[job.x for job in jobs])
 
 
-CHUNK = 256
+CHUNK = 512
+
+
+def start_rows(group, x_ref, full, send_sem, recv_sem):
+    me = group.me()
+    full[me] = x_ref[...]
+    return [
+        send(group, peer, step, x_ref, full.at[me], send_sem, recv_sem)
+        for step, peer in enumerate(group.peers())
+    ]
 
 
 def table_body(
-    by_section, by_dp, jobs, g_ref, ids_ref, u_ref, gx_ref, *refs
+    by_section, by_dp, by_tensor, jobs, g_ref, ids_ref, u_ref, gx_ref, *refs
 ):
     riders = len(jobs)
     xs, (out_ref, *outs), refs = refs[:riders], refs[riders : 2 * riders + 1], refs[2 * riders + 1 :]
     (g_buf, to_partner, from_partner, to_dp, from_dp, own, result,
     g_sem, ps_send, ps_recv, dp_send, dp_recv, ag_send, ag_recv, fw_send, fw_recv, own_sem,
     ) = refs[:17]
+    gx_full, gx_send, gx_recv = refs[17:20]
     s, j = by_section.me(), by_dp.me()
     partner = 1 - s
     peers = by_dp.peers() + [j]
@@ -300,8 +463,9 @@
     block = own.shape[0]
     subs = block // CHUNK
     tokens = u_ref.shape[0]
-    greet([by_section, by_dp] + job_groups(jobs))
-    parts = split_scratch(jobs, refs[17:])
+    greet([by_section, by_dp, by_tensor] + job_groups(jobs))
+    gx_copies = start_rows(by_tensor, gx_ref, gx_full, gx_send, gx_recv)
+    parts = split_scratch(jobs, refs[20:])
     ends = [job.start(xs[n], outs[n], *parts[n]) for n, job in enumerate(jobs)]
 
     def chunk(half, place, sub):
@@ -360,6 +524,8 @@
             result.at[rows(sub)], out_ref.at[chunk(s, j, sub)], own_sem.at[sub]
         )
 
+    for copy in gx_copies:
+        copy.wait()
     fetch(0, 0, 0).start()
     for index, (number, away) in enumerate(order):
         half = partner if away == 0 else s
@@ -381,7 +547,9 @@
             base = chunk(half, peers[number], sub) * CHUNK
             place = base + lax.broadcasted_iota(jnp.int32, (CHUNK, tokens), 0)
             chosen = jnp.where(place == ids_ref[...], 1.0, 0.0).astype(BF16)
-            term = outer_sum(g_buf[slot], u_ref[...]) + matmul(chosen, gx_ref[...])
+            term = outer_sum(g_buf[slot], u_ref[...]) + matmul(
+                chosen, gx_full[...].reshape(tokens, gx_full.shape[2])
+            )
             if away == 0:
                 to_partner[number, rows(sub), :] = term.astype(BF16)
                 partner_copy(number, sub).start()
@@ -444,7 +612,7 @@
 SQUARE_STEP = (0, 0, 1, 1, 1, 0)
 
 
-def table_square_body(by_section, by_dp, jobs, g_ref, ids_ref, u_ref, gx_ref, *refs):
+def table_square_body(by_section, by_dp, by_tensor, jobs, g_ref, ids_ref, u_ref, gx_ref, *refs):
     riders = len(jobs)
     xs, (out_ref, *outs), refs = refs[:riders], refs[riders : 2 * riders + 1], refs[2 * riders + 1 :]
     (
@@ -452,6 +620,7 @@
         g_sem, ps_send, ps_recv, hop_send, hop_recv, dp_send, dp_recv, ag_send, ag_recv,
         fw_send, fw_recv, own_sem,
     ) = refs[:20]
+    gx_full, gx_send, gx_recv = refs[20:23]
     s, j = by_section.me(), by_dp.me()
     partner = 1 - s
     near_x, near_y, far = (across(j, step) for step in range(3))
@@ -461,9 +630,14 @@
     subs = block // CHUNK
     half_rows = CHUNK // 2
     tokens = u_ref.shape[0]
-    greet([by_section, by_dp] + job_groups(jobs))
-    parts = split_scratch(jobs, refs[20:])
-    ends = [job.start(xs[n], outs[n], *parts[n]) for n, job in enumerate(jobs)]
+    greet([by_section, by_dp, by_tensor] + job_groups(jobs))
+    line = LineRows(by_tensor, gx_ref, gx_full, gx_send, gx_recv)
+    line.start()
+    gx_full[line.me] = gx_ref[...]
+    parts = split_scratch(jobs, refs[23:])
+    ends = [
+        job.start(xs[n], outs[n], *parts[n]) for n, job in enumerate(jobs) if not job.late
+    ]
 
     def chunk(half, place, sub):
         return (half * count + place) * subs + sub
@@ -532,11 +706,18 @@
             result.at[rows(sub)], out_ref.at[chunk(s, j, sub)], own_sem.at[sub]
         )
 
+    def slot_of(number, away):
+        if away == 0:
+            return to_partner.at[number]
+        return to_dp.at[number] if number < 3 else own
+
     fetch(0, 0, 0).start()
+    stops = {(step * len(order)) // line.count: step for step in range(1, line.count - 1)}
     for index, (number, away) in enumerate(order):
-        half = partner if away == 0 else s
-
-        def one(sub, carry, index=index, number=number, away=away, half=half):
+        if index in stops:
+            line.step(stops[index])
+
+        def share(sub, carry, index=index, number=number, away=away):
             slot = lax.rem(sub, 2)
             fetch(index, sub, slot).wait()
 
@@ -550,10 +731,24 @@
                 def _():
                     fetch(index + 1, 0, 1 - slot).start()
 
+            held = slot_of(number, away)
+            held[rows(sub), :] = outer_sum(g_buf[slot], u_ref[...]).astype(held.dtype)
+            return carry
+
+        lax.fori_loop(0, subs, share, 0)
+    line.step(line.count - 1)
+    line.wait_sends()
+    ends += [job.start(xs[n], outs[n], *parts[n]) for n, job in enumerate(jobs) if job.late]
+
+    for index, (number, away) in enumerate(order):
+        half = partner if away == 0 else s
+
+        def one(sub, carry, number=number, away=away, half=half):
             base = chunk(half, peers[number], sub) * CHUNK
             place = base + lax.broadcasted_iota(jnp.int32, (CHUNK, tokens), 0)
             chosen = jnp.where(place == ids_ref[...], 1.0, 0.0).astype(BF16)
-            term = outer_sum(g_buf[slot], u_ref[...]) + matmul(chosen, gx_ref[...])
+            term = matmul(chosen, gx_full[...].reshape(tokens, gx_full.shape[2]))
+            term = term + slot_of(number, away)[rows(sub), :].astype(F32)
             if away == 0:
                 to_partner[number, rows(sub), :] = term.astype(BF16)
                 partner_copy(number, sub).start()
@@ -630,7 +825,7 @@
         end()
 
 
-def table_sum(by_section, by_dp, jobs, grads, ids, final, grad_rows, ident):
+def table_sum(by_section, by_dp, by_tensor, jobs, grads, ids, final, grad_rows, ident):
     chunks, tokens, _ = grads.shape
     width = final.shape[1]
     count = by_dp.count
@@ -652,11 +847,13 @@
     scratch += [pltpu.VMEM((block, width), F32), low((block, width)), dma((2,))]
     copies = (count, 2, 2, 6, count) if square else (count, count - 1, count - 1, count)
     scratch += [dma((copy, subs)) for copy in copies for _ in range(2)] + [dma((subs,))]
+    scratch += [low((by_tensor.count,) + grad_rows.shape)]
+    scratch += [dma(((by_tensor.count - 1) * (2 if square else 1),))] * 2
     vmem = pl.BlockSpec(memory_space=pltpu.VMEM)
     hbm = pl.BlockSpec(memory_space=pl.ANY)
     return pl.pallas_call(
         functools.partial(
-            table_square_body if by_dp.square else table_body, by_section, by_dp, jobs
+            table_square_body if by_dp.square else table_body, by_section, by_dp, by_tensor, jobs
         ),
         out_shape=(jax.ShapeDtypeStruct((chunks, CHUNK, width), BF16),)
         + tuple(job.out for job in jobs),
@@ -918,7 +1115,24 @@
     ]
 
 
-def team_call(body, team, ident, jobs, arrays, specs, outs, out_specs, scratch):
+class LateDeal:
+    def __init__(self, pair, landing, send_sem, recv_sem):
+        self.pair, self.landing, self.sems = pair, landing, (send_sem, recv_sem)
+
+    def other(self):
+        return 1 - self.pair.me()
+
+    def start(self, src):
+        self.copy = send(self.pair, self.other(), 0, src, self.landing, *self.sems)
+
+    def wait(self):
+        self.copy.wait()
+
+
+def team_call(body, team, ident, jobs, arrays, specs, outs, out_specs, scratch, pair=None, dealt=None):
+    if pair is not None:
+        outs, out_specs = tuple(outs) + (dealt,), tuple(out_specs) + (HBM,)
+        scratch = list(scratch) + [pltpu.SemaphoreType.DMA((1,))] * 2
     part, model = arrays[0].shape
     count_in, count_out, riders = len(arrays), len(outs), len(jobs)
     own_scratch = team_scratch(team, part, model)
@@ -931,11 +1145,14 @@
         rows = TeamRows(team, ins[0], *refs[: len(own_scratch)])
         refs = refs[len(own_scratch) :]
         mine, refs = refs[: len(scratch)], refs[len(scratch) :]
-        greet([team] + job_groups(jobs))
+        greet([team] + job_groups(jobs) + ([] if pair is None else [pair]))
         rows.send_rows()
         parts = split_scratch(jobs, refs)
         ends = [job.start(xs[n], landings[n], *parts[n]) for n, job in enumerate(jobs)]
-        body(rows, ins, results, mine)
+        if pair is None:
+            body(rows, ins, results, mine)
+        else:
+            body(rows, ins, results[:-1], mine[:-2], LateDeal(pair, results[-1], *mine[-2:]))
         for end in ends:
             end()
 
@@ -1035,7 +1252,7 @@
     )
 
 
-def attend_back_body(rows, ins, outs, scratch):
+def attend_back_body(rows, ins, outs, scratch, late=None):
     gy_ref, length_ref, slope_ref, a_ref, qk_ref, vo_ref, q_ref, k_ref, v_ref, mixed_ref, lse_ref = ins
     total_ref, grads_ref, sums_ref = outs
     go, gq, gk, gv, gk_sum, gv_sum = scratch
@@ -1088,10 +1305,14 @@
     grads_ref[0] = outer_sum(gq[...], a_ref[...])
     grads_ref[1] = outer_sum(gv[...], a_ref[...])
     grads_ref[2] = outer_sum(gk[...], a_ref[...])
+    if late is not None:
+        late.start(grads_ref.at[pl.ds(2 * late.other(), 2)])
     rows.finish(total_ref)
-
-
-def attend_back(team, ident, jobs, gy, length, slopes, a, qk, vo, q, k, v, mixed, lse):
+    if late is not None:
+        late.wait()
+
+
+def attend_back(team, ident, jobs, pair, gy, length, slopes, a, qk, vo, q, k, v, mixed, lse):
     part, model = gy.shape
     seq, width = q.shape
     return team_call(
@@ -1105,6 +1326,8 @@
         ),
         (VMEM,) * 3,
         [pltpu.VMEM((seq, width), BF16)] * 4 + [pltpu.VMEM((seq, width), F32)] * 2,
+        pair,
+        jax.ShapeDtypeStruct((2, width, model), F32),
     )
 
 
@@ -1158,7 +1381,7 @@
     )
 
 
-def feed_back_body(rows, ins, outs, scratch):
+def feed_back_body(rows, ins, outs, scratch, late=None):
     gz_ref, c_ref, before_ref, up_ref, down_ref = ins
     total_ref, grads_ref, sums_ref = outs
     active, low = scratch
@@ -1191,10 +1414,14 @@
         lanes = slice(first, first + tile)
         grads_ref[0, lanes, :] = outer_sum(low[:, lanes], c_ref[...])
         grads_ref[1, lanes, :] = outer_sum(active[:, lanes], rows.full[...].reshape(seq, model))
+    if late is not None:
+        late.start(grads_ref.at[late.other()])
     rows.finish(total_ref)
-
-
-def feed_back(team, ident, jobs, gz, c, before, up, down):
+    if late is not None:
+        late.wait()
+
+
+def feed_back(team, ident, jobs, pair, gz, c, before, up, down):
     part, model = gz.shape
     seq = part * team.count
     units = up.shape[0]
@@ -1209,6 +1436,8 @@
         ),
         (VMEM,) * 3,
         [pltpu.VMEM((seq, units), BF16)] * 2,
+        pair,
+        jax.ShapeDtypeStruct((units, model), F32),
     )
 
 
@@ -1243,6 +1472,7 @@
     local_cols = qkv_weight.shape[-1]
     planes = rows == sections * shards and local_cols % (groups * HEAD_DIM) == 0
     by_dp.square = planes and groups == 4
+    by_tensor.line = planes
     team = by_dp if planes else by_tensor
     cut = groups if planes else 1
     fan = shards if planes else 1
@@ -1454,9 +1684,6 @@
     _, final_back = jax.vjp(layer_norm, h, outer_gains[-1], outer_offsets[-1])
     grad, final_gain, final_offset = final_back(grad_final)
 
-    def section_jobs(pair):
-        return [deal(by_section, one) for one in pair] if planes else []
-
     def section_sums(pair, got):
         out = []
         for one, dealt in zip(pair, got):
@@ -1480,37 +1707,38 @@
 
     small_rows = [None] * layers
     pairs = [None] * layers
-    done = [None] * layers
-    feed_low = [None] * layers
+    attn_low, attn_done, feed_done = ([None] * layers for _ in range(3))
     for l in reversed(range(layers)):
         p = params[l]
         section_in, normed, q, k, v, mixed, lse, middle, second, before = kept[l]
+        pair = by_section if planes else None
         late = planes and l + 1 < layers
-        jobs = section_jobs([pairs[l + 1][0]]) + tensor_jobs(feed_low[l + 1]) if late else []
-        (total, g_feed, up_sum), got = feed_back(
-            team, ident("feed back", jobs), jobs, grad.astype(BF16), second.reshape(seq, width),
-            before, p["up"], p["down"],
+        jobs = tensor_jobs(attn_low[l + 1]) if late else []
+        (total, g_feed, up_sum, *dealt), got = feed_back(
+            team, ident("feed back", jobs), jobs, pair, grad.astype(BF16),
+            second.reshape(seq, width), before, p["up"], p["down"],
         )
         if late:
-            attn_low = section_sums([pairs[l + 1][0]], got[:1])
-            feed_done = tensor_sums(feed_low[l + 1], got[1:])
+            attn_done[l + 1] = tensor_sums(attn_low[l + 1], got)
+        if planes:
+            feed_low = section_sums([g_feed], [one[None] for one in dealt])
         _, norm_back = jax.vjp(layer_norm, middle, p["gains"][1], p["offsets"][1])
         grad_mid, gain_two, offset_two = norm_back(total)
         grad_mid = grad_mid + grad
-        jobs = section_jobs([g_feed]) + (tensor_jobs(attn_low) if late else [])
-        (total, g_attn, qv_sum), got = attend_back(
-            team, ident("attend back", jobs), jobs, grad_mid.astype(BF16), length, slopes, normed,
-            p["qk"], p["vo"], q, k, v, mixed, lse,
-        )
+        jobs = tensor_jobs(feed_low) if planes else []
+        (total, g_attn, qv_sum, *dealt), got = attend_back(
+            team, ident("attend back", jobs), jobs, pair, grad_mid.astype(BF16), length, slopes,
+            normed, p["qk"], p["vo"], q, k, v, mixed, lse,
+        )
+        g_attn = g_attn.reshape((2, 2) + g_attn.shape[1:])
         if planes:
-            feed_low[l] = section_sums([g_feed], got[:1])
-        if late:
-            done[l + 1] = tensor_sums(attn_low, got[1:]) + feed_done
+            feed_done[l] = tensor_sums(feed_low, got)
+            attn_low[l] = section_sums([g_attn], [one[None] for one in dealt])
         _, norm_back = jax.vjp(layer_norm, section_in, p["gains"][0], p["offsets"][0])
         grad_in, gain_one, offset_one = norm_back(total)
         bias_two = jnp.sum(grad, axis=0)
         grad = grad_in + grad_mid
-        pairs[l] = (g_attn.reshape((2, 2) + g_attn.shape[1:]), g_feed)
+        pairs[l] = (g_attn, g_feed)
 
         def placed(values, size):
             out = jnp.zeros((fan if planes else shards, cut, size), F32)
@@ -1541,24 +1769,22 @@
     )
     used = packed.shape[0]
     packed = jnp.pad(packed, ((0, -used % 8), (0, 0)))
-    jobs = [gather(by_tensor, grad_rows.astype(BF16)), gather(by_dp, packed)]
+    jobs = [Job("gather", [Group(("section", "tensor"), (sections, shards))], packed, late=True)]
     if planes:
-        jobs += section_jobs(pairs[0][:1]) + spread_jobs(done[1])
-    grad_rows, packed, *got = exchange(*jobs)
-    grad_rows = grad_rows.reshape(tokens, width)
+        jobs += spread_jobs(attn_done[1] + feed_done[1])
+        jobs += [Job("deal", [by_tensor], low, 1, late=True) for low in attn_low[0]]
+    embed_sum, packed, *got = table_sum(
+        by_section, by_dp, by_tensor, jobs, grad_logits, ids[None, :] - vocab_start, final,
+        grad_rows.astype(BF16), exchange.ident("table"),
+    )
     packed = jnp.sum(packed, axis=0)
-    jobs = [gather(Group(("section", "tensor"), (sections, shards)), packed)]
+    jobs = [gather(by_dp, packed)]
     if planes:
-        lows = section_sums(pairs[0][:1], got[:1]) + feed_low[0]
-        spread_one = got[1:]
-        jobs += tensor_jobs(lows)
-    embed_sum, packed, *got = table_sum(
-        by_section, by_dp, jobs, grad_logits, ids[None, :] - vocab_start, final, grad_rows,
-        exchange.ident("table"),
-    )
+        spread_one = got[:2]
+        jobs += spread_jobs(tensor_sums(attn_low[0], got[2:]) + feed_done[0])
+    packed, *spread_zero = exchange(*jobs)
     packed = jnp.sum(packed, axis=0)
     if planes:
-        spread_zero = exchange(*spread_jobs(tensor_sums(lows, got)))
         attn_sum, feed_sum = (
             jnp.where(s == 0, zero, one) for zero, one in zip(spread_zero, spread_one)
         )

time: 1160 us -> 1140 us (0.983)
  Pallas kernels: 990 us -> 957 us
  local copies, waits for them, and re-layouts: 60.1 us -> 78.3 us
    pallas_call x7 -> x6, Pallas kernels: 264 us -> 207 us  [__call__(): pl.pallas_call(functools.partial(exchange_body, jobs), out_shape=tuple((j...]
    pallas_call x1, Pallas kernels: 170 us -> 217 us  [table_sum(): pl.pallas_call(functools.partial(table_square_body if by_dp.square else t...]
    convert_element_type x4, other arithmetic: 16.5 us -> 3.25 us  [section_sums(): low = own_and_dealt(one, dealt, s).astype(BF16)]
where the time goes in v5:
time: 1140 us; the launch traced here: 1130 us
  Pallas kernels  957 us (84%)
  other arithmetic  87.6 us (8%)
  local copies, waits for them, and re-layouts  78.3 us (7%)
    pallas_call x8, Pallas kernels, team_call(): pl.pallas_call(kernel, out_shape=tuple(outs) + tuple((job.out for job in...  468 us
    pallas_call x1, Pallas kernels, table_sum(): pl.pallas_call(functools.partial(table_square_body if by_dp.square else t...  217 us
    pallas_call x6, Pallas kernels, __call__(): pl.pallas_call(functools.partial(exchange_body, jobs), out_shape=tuple((j...  207 us
    pallas_call x1, Pallas kernels, head_grads(): pl.pallas_call(head_grads_body, grid=(chunks,), out_shape=(jax.ShapeDtype...  34 us
    pallas_call x1, Pallas kernels, head_logits(): pl.pallas_call(head_logits_body, grid=(vocab // CHUNK,), out_shape=(jax.S...  31 us

profile of v5, /device:TPU:1, one launch (start us, length us, event | category | flops | bytes accessed | tf_op | source)
XLA Modules:
  0.0 1127.8 jit_solution(3783675107122674967)
XLA Ops:
  0.7 1.6 fusion.47
  6.9 14.8 %shard_map.246 = (bf16[1,384,1024]{2,1,0:T(8,128)(2,1)S(1)}, s32[4,2,2,1024]{3,2,1,0:T(2,128)S(1)}, f32[8,16,1024]{2,1,0:T(8,128)S(1)}) custom-call(bf16[2,384,1024]{2,1,0:T(8,128)(2,1)S(1)} %pad_maximum_fusion.4.refs_0_, s32[2,2,1024]{2,1,0:T(2,128)S(1)} %pad_add_fusion.refs_1_, f32[16,1024]{1,0:T(8,128)S(1)} %concatenate.26.refs_2_), custom_call_target="tpu_custom_call" | custom-call | tf_op jit(solution)/shard_map/pallas_call | solution.py:424
  23.5 13.9 %gather_fusion = bf16[1024,1024]{1,0:T(8,128)(2,1)} fusion(bf16[8192,1024]{1,0:T(8,128)(2,1)} %e_ref.3, s32[1024]{0:T(1024)S(1)} %broadcast_clamp_fusion), kind=kCustom, calls=%fused_computation | custom fusion | bytes 4198400 | tf_op jit(solution)/shard_map/jit(_take)/gather | solution.py:1629
  37.5 1.9 select_select_fusion.refs_0_
  39.4 3.1 broadcast_select_fusion.2
  43.3 77.7 %shard_map.247 = (f32[256,1024]{1,0:T(8,128)S(1)}, bf16[2,4,64,1024]{3,2,1,0:T(8,128)(2,1)S(1)}, bf16[2,4,64,1024]{3,2,1,0:T(8,128)(2,1)S(1)}) custom-call(bf16[4,256,1024]{2,1,0:T(8,128)(2,1)S(1)} %select_select_fusion.refs_0_, bf16[64,1024]{1,0:T(8,128)(2,1)S(1)} %get-tuple-element.226.refs_1_, bf16[64,1024]{1,0:T(8,128)(2,1)S(1)} %get-tuple-element.225.refs_2_), custom_call_target="tpu_custom_call" | custom-call | tf_op jit(solution)/shard_map/pallas_call | solution.py:424
  125.5 1.5 add_convert_fusion.5.refs_0_
  130.5 61.4 %shard_map.248 = (f32[256,1024]{1,0:T(8,128)}, bf16[4,256,1024]{2,1,0:T(8,128)(2,1)}, bf16[1024,256]{1,0:T(8,128)(2,1)}, bf16[1024,256]{1,0:T(8,128)(2,1)}, bf16...) custom-call(bf16[256,1024]{1,0:T(8,128)(2,1)} %add_convert_fusion.5., ...), custom_call_target="tpu_custom_call" | custom-call | tf_op jit(solution)/shard_map/pallas_call | solution.py:1159
  192.0 1.9 fusion.45
  194.4 1.5 pad_maximum_fusion.1.refs_2_.refs_4_
  195.9 1.5 pad_maximum_fusion.refs_1_.refs_3_
  202.4 55.4 %shard_map.249 = (f32[256,1024]{1,0:T(8,128)}, bf16[4,256,1024]{2,1,0:T(8,128)(2,1)}, f32[1024,1024]{1,0:T(8,128)}, bf16[2,4,64,1024]{3,2,1,0:T(8,128)(2,1)}, bf...) custom-call(bf16[256,1024]{1,0:T(8,128)(2,1)} %add_convert_fusion.4.refs_0_, ...), custom_call_target="tpu_custom_call" | custom-call | tf_op jit(solution)/shard_map/pallas_call | solution.py:1159
  261.3 56.9 %shard_map.250 = (f32[256,1024]{1,0:T(8,128)}, bf16[4,256,1024]{2,1,0:T(8,128)(2,1)}, bf16[1024,256]{1,0:T(8,128)(2,1)}, bf16[1024,256]{1,0:T(8,128)(2,1)}, bf16...) custom-call(bf16[256,1024]{1,0:T(8,128)(2,1)} %add_convert_fusion.3., ...), custom_call_target="tpu_custom_call" | custom-call | tf_op jit(solution)/shard_map/pallas_call | solution.py:1159
  318.3 1.9 fusion.44
  320.7 1.5 pad_maximum_fusion.3.refs_2_.refs_4_
  322.2 1.5 pad_maximum_fusion.2.refs_1_.refs_3_
  325.9 47.4 %shard_map.251 = (f32[256,1024]{1,0:T(8,128)}, bf16[4,256,1024]{2,1,0:T(8,128)(2,1)}, f32[1024,1024]{1,0:T(8,128)}) custom-call(bf16[256,1024]{1,0:T(8,128)(2,1)} %add_convert_fusion.2.refs_0_, bf16[1024,1024]{1,0:T(8,128)(2,1)} %pad_maximum_fusion.2.refs_1_.refs_3_, bf16[1024,1024]{1,0:T(8,128)(2,1)} %pad_maximum_fusion.3.refs_2_.refs_4_, f32[1,1024]{1,0:T(1,128)} %bitcast.373), custom_call_target="tpu_custom_call" | custom-call | tf_op jit(solution)/shard_map/pallas_call | solution.py:1159
  375.4 35.1 %shard_map.252 = bf16[4,256,1024]{2,1,0:T(8,128)(2,1)S(1)} custom-call(bf16[256,1024]{1,0:T(8,128)(2,1)S(1)} %add_convert_fusion.1.refs_0_), custom_call_target="tpu_custom_call" | custom-call | tf_op jit(solution)/shard_map/pallas_call | solution.py:424
  412.8 31.0 %shard_map.253 = (f32[16,1024,512]{2,1,0:T(8,128)}, f32[1024,128]{1,0:T(8,128)S(1)}, f32[1024,128]{1,0:T(8,128)S(1)}, f32[1024,128]{1,0:T(8,128)S(1)}) custom-call(bf16[1024,1024]{1,0:T(8,128)(2,1)S(1)} %bitcast.250, bf16[8192,1024]{1,0:T(8,128)(2,1)} %e_ref.3, s32[1024,1]{1,0:T(8,128)S(1)} %bitcast.257), custom_call_target="tpu_custom_call" | custom-call | flops 17179869184 | bytes 50331648 | tf_op jit(solution)/shard_map/pallas_call | solution.py:904
  447.5 1.6 multiply_reduce_fusion.18
  450.3 7.9 shard_map.254
  460.5 34.0 %shard_map.255 = (bf16[16,1024,512]{2,1,0:T(8,128)(2,1)}, bf16[1024,1024]{1,0:T(8,128)(2,1)S(1)}) custom-call(f32[16,1024,512]{2,1,0:T(8,128)} %get-tuple-element.94.logits_ref, bf16[8192,1024]{1,0:T(8,128)(2,1)} %e_ref.3, s32[1024,1]{1,0:T(8,128)S(1)} %bitcast.258, f32[1024,1]{1,0:T(8,128)S(1)} %copy.66.norm_ref, f32[1024,1]{1,0:T(8,128)S(1)} %bitcast.259), custom_call_target="tpu_custom_call" | custom-call | flops 17179869184 | bytes 67108864 | tf_op jit(solution)/shard_map/pallas_call | solution.py:951
  494.5 31.8 %shard_map.256 = f32[256,1024]{1,0:T(8,128)S(1)} custom-call(bf16[4,256,1024]{2,1,0:T(8,128)(2,1)S(1)} %bitcast.256), custom_call_target="tpu_custom_call" | custom-call | tf_op jit(solution)/shard_map/pallas_call | solution.py:424
  528.1 67.8 %shard_map.257 = (f32[256,1024]{1,0:T(8,128)}, f32[2,1024,1024]{2,1,0:T(8,128)}, f32[1,1024]{1,0:T(1,128)}, f32[1024,1024]{1,0:T(8,128)}) custom-call(bf16[256,1024]{1,0:T(8,128)(2,1)} %get-tuple-element.218.refs_0_, bf16[1024,1024]{1,0:T(8,128)(2,1)} %bitcast.293, f32[1024,1024]{1,0:T(8,128)} %get-tuple-element.101.refs_2_, ...), custom_call_target="tpu_custom_call" | custom-call | tf_op jit(solution)/shard_map/pallas_call | solution.py:1159
  596.0 2.7 constant_dynamic-slice_fusion.8
  600.6 1.5 copy.70.refs_11_
  605.6 64.0 %shard_map.258 = (f32[256,1024]{1,0:T(8,128)}, f32[4,256,1024]{2,1,0:T(8,128)}, f32[2,256]{1,0:T(2,128)}, f32[2,256,1024]{2,1,0:T(8,128)}, bf16[3,2,128,1024]{3,2,1,0:T(8,128)(2,1)}) custom-call(bf16[256,1024]{1,0:T(8,128)(2,1)} %convert_element_type.170.refs_0_, s32[1]{0:T(128)} %dynamic_slice.119.refs_1_, f32[4]{0:T(128)} %multiply_exponential_fusion.refs_2_, ...), custom_call_target="tpu_custom_call" | custom-call | tf_op jit(solution)/shard_map/pallas_call | solution.py:1159
  669.6 1.9 constant_dynamic-slice_fusion.7
  676.6 48.4 %shard_map.259 = (f32[256,1024]{1,0:T(8,128)}, f32[2,1024,1024]{2,1,0:T(8,128)}, f32[1,1024]{1,0:T(1,128)}, f32[1024,1024]{1,0:T(8,128)}, bf16[3,2,64,1024]{3,2,1,0:T(8,128)(2,1)}) custom-call(bf16[256,1024]{1,0:T(8,128)(2,1)} %convert_element_type.172.refs_0_, bf16[1024,1024]{1,0:T(8,128)(2,1)} %bitcast.291, f32[1024,1024]{1,0:T(8,128)} %get-tuple-element.113.refs_2_, ...), custom_call_target="tpu_custom_call" | custom-call | tf_op jit(solution)/shard_map/pallas_call | solution.py:1159
  725.0 2.7 constant_dynamic-slice_fusion.6
  729.6 1.5 copy.76.refs_11_
  734.6 66.3 %shard_map.260 = (f32[256,1024]{1,0:T(8,128)}, f32[4,256,1024]{2,1,0:T(8,128)}, f32[2,256]{1,0:T(2,128)}, f32[2,256,1024]{2,1,0:T(8,128)}, bf16[3,2,128,1024]{3,2,1,0:T(8,128)(2,1)}) custom-call(bf16[256,1024]{1,0:T(8,128)(2,1)} %convert_element_type.174.refs_0_, s32[1]{0:T(128)} %dynamic_slice.119.refs_1_, f32[4]{0:T(128)} %multiply_exponential_fusion.refs_2_, ...), custom_call_target="tpu_custom_call" | custom-call | tf_op jit(solution)/shard_map/pallas_call | solution.py:1159
  800.9 2.8 convert_reduce_fusion
  803.7 1.5 fusion.5.refs_2_
  805.2 1.9 constant_dynamic-slice_fusion.4
  810.4 2.1 fusion.6.refs_2_
  812.7 1.7 fusion.9.refs_1_
  815.7 1.4 multiply_reduce_fusion.1
  820.4 1.6 fusion.31
  823.5 217.0 %shard_map.261 = (bf16[16,512,1024]{2,1,0:T(8,128)(2,1)}, f32[8,32,1024]{2,1,0:T(8,128)}, bf16[2,4,2,64,1024]{4,3,2,1,0:T(8,128)(2,1)}, bf16[2,4,2,128,1024]{4,3,2,1,0:T(8,128)(2,1)}, bf16[3,2,64,1024]{3,2,1,0:T(8,128)(2,1)}) custom-call(bf16[16,1024,512]{2,1,0:T(8,128)(2,1)} %get-tuple-element.98.g_ref, s32[1,1024]{1,0:T(1,128)} %bitcast.361, ...), custom_call_target="tpu_custom_call" | custom-call | tf_op jit(solution)/shard_map/pallas_call | solution.py:854
  1043.0 39.8 %shard_map.262 = (f32[4,32,1024]{2,1,0:T(8,128)S(1)}, bf16[2,4,2,64,1024]{4,3,2,1,0:T(8,128)(2,1)S(1)}, bf16[2,4,2,128,1024]{4,3,2,1,0:T(8,128)(2,1)S(1)}) custom-call(f32[32,1024]{1,0:T(8,128)S(1)} %reduce_sum.560.refs_0_, bf16[2,64,1024]{2,1,0:T(8,128)(2,1)S(1)} %fusion.8.refs_1_, bf16[2,128,1024]{2,1,0:T(8,128)(2,1)S(1)} %fusion.5.refs_2_), custom_call_target="tpu_custom_call" | custom-call | tf_op jit(solution)/shard_map/pallas_call | solution.py:424
  1082.9 2.7 broadcast_select_fusion
  1085.6 1.8 fusion.41
  1087.4 2.6 bitcast_convert_fusion.2
  1090.0 5.3 copy.89
  1095.4 4.2 bitcast_convert_fusion.1
  1100.7 1.9 fusion.4
  1103.7 18.8 %bitcast_convert_fusion = f32[8192,1024]{1,0:T(8,128)} fusion(bf16[16,512,1024]{2,1,0:T(8,128)(2,1)} %get-tuple-element.138), kind=kLoop, calls=%fused_computation.1 | loop fusion | flops 8388608 | bytes 50331648 | tf_op jit(solution)/shard_map/convert_element_type | solution.py:1801
  (295 shorter events, 72.1 us)
Async XLA Ops:
  0.6 2.3 copy-start
  3.3 2.6 copy-start.23
  5.6 1.1 copy-start.46
  5.6 1.1 copy-start.47
  5.6 1.1 copy-start.48
  5.6 1.1 copy-start.51
  5.7 1.1 copy-start.52
  5.7 1.2 copy-start.49
  5.7 1.2 copy-start.50
  37.5 1.9 copy-start.7
  123.4 5.2 copy-start.35
  125.1 4.3 copy-start.57
  191.9 2.2 copy-start.39
  195.9 1.5 copy-start.43
  197.9 60.0 %copy-start.13 = (f32[256,1024]{1,0:T(8,128)}, f32[256,1024]{1,0:T(8,128)S(1)}, u32[]{:S(2)}) copy-start(f32[256,1024]{1,0:T(8,128)S(1)} %get-tuple-element.197) | copy-start | bytes 3145732
  197.9 1.7 copy-start.33
  259.3 64.5 %copy-start.15 = (f32[256,1024]{1,0:T(8,128)}, f32[256,1024]{1,0:T(8,128)S(1)}, u32[]{:S(2)}) copy-start(f32[256,1024]{1,0:T(8,128)S(1)} %get-tuple-element.195) | copy-start | bytes 3145732
  318.3 2.2 copy-start.37
  322.2 1.5 copy-start.42
  324.0 49.4 %copy-start.17 = (f32[256,1024]{1,0:T(8,128)}, f32[256,1024]{1,0:T(8,128)S(1)}, u32[]{:S(2)}) copy-start(f32[256,1024]{1,0:T(8,128)S(1)} %get-tuple-element.193) | copy-start | bytes 3145732
  374.8 35.7 %copy-start.19 = (f32[256,1024]{1,0:T(8,128)}, f32[256,1024]{1,0:T(8,128)S(1)}, u32[]{:S(2)}) copy-start(f32[256,1024]{1,0:T(8,128)S(1)} %get-tuple-element.191) | copy-start | bytes 3145732
  410.5 33.3 %copy-start.2 = (bf16[4,256,1024]{2,1,0:T(8,128)(2,1)}, bf16[4,256,1024]{2,1,0:T(8,128)(2,1)S(1)}, u32[]{:S(2)}) copy-start(bf16[4,256,1024]{2,1,0:T(8,128)(2,1)S(1)} %shard_map.252) | copy-start | bytes 6291460
  446.2 14.3 %copy-start.10 = (s32[1,1024]{0,1:T(8,128)S(1)}, s32[1,1024]{0,1:T(8,128)}, u32[]{:S(2)}) copy-start(s32[1,1024]{0,1:T(8,128)} %copy.104) | copy-start | bytes 12292
  494.5 31.9 %copy-start.20 = (f32[256,1024]{1,0:T(8,128)S(1)}, f32[256,1024]{1,0:T(8,128)}, u32[]{:S(2)}) copy-start(f32[256,1024]{1,0:T(8,128)} %copy-done.19) | copy-start | bytes 3145732
  596.0 3.5 copy-start.31
  600.5 2.1 copy-start.21
  600.6 2.1 copy-start.18
  600.6 3.0 copy-start.29
  669.6 2.2 copy-start.40
  672.3 2.7 copy-start.26
  672.3 2.0 copy-start.16
  672.3 2.3 copy-start.27
  725.0 3.5 copy-start.30
  729.6 2.1 copy-start.22
  729.6 2.1 copy-start.14
  729.6 3.0 copy-start.28
  805.2 2.2 copy-start.38
  807.9 2.5 copy-start.25
  807.9 2.2 copy-start.41
  810.1 2.4 copy-start.45
  810.4 4.0 copy-start.32
  815.7 1.5 copy-start.56
  815.7 1.9 copy-start.54
  815.7 2.0 copy-start.55
  815.7 2.4 copy-start.53
  1040.5 2.4 copy-start.44
  1095.4 4.2 copy-start.36
  1103.7 22.5 %copy-start.1 = (bf16[1,1024,1024]{2,1,0:T(8,128)(2,1)S(1)}, bf16[1,1024,1024]{2,1,0:T(8,128)(2,1)}, u32[]{:S(2)}) copy-start(bf16[1,1024,1024]{2,1,0:T(8,128)(2,1)} %param.26) | copy-start | bytes 6291460
  (11 other events, 10.0 us)

commit v6 on v5

--- a/solution.py
+++ b/solution.py
@@ -185,21 +185,30 @@
     def behind(self, up):
         return self.me > 0 if up else self.me < self.count - 1
 
-    def step(self, step):
+    def first(self, step):
         for up in (True, False):
             place = self.count - 1 - step if up else step
             side = 0 if up else 1
 
-            @pl.when(self.leaves(up, step) & self.behind(up))
+            @pl.when(self.leaves(up, step) & jnp.logical_not(self.behind(up)))
+            def _(up=up, place=place, side=side):
+                self.stage[side, step] = self.x[place]
+                self.copy(up, step).start()
+
+    def rest(self, step, near=None):
+        for up in (True, False):
+            place = self.count - 1 - step if up else step
+            side = 0 if up else 1
+            here = self.leaves(up, step) & self.behind(up)
+            if near is not None:
+                by_end = self.me == (1 if up else self.count - 2)
+                here = here & (by_end if near else jnp.logical_not(by_end))
+
+            @pl.when(here)
             def _(up=up, place=place, side=side):
                 self.copy(up, step).wait_recv()
                 total = self.x[place].astype(F32) + self.land[side, step].astype(F32)
                 self.stage[side, step] = total.astype(self.stage.dtype)
-                self.copy(up, step).start()
-
-            @pl.when(self.leaves(up, step) & jnp.logical_not(self.behind(up)))
-            def _(up=up, place=place, side=side):
-                self.stage[side, step] = self.x[place]
                 self.copy(up, step).start()
 
     def finish(self, out):
@@ -280,11 +289,12 @@
 
         elif self.kind == "reduce" and group.line:
             line = LineSum(group, x, *more, send_sem, recv_sem)
-            line.step(0)
+            for step in range(group.count - 1):
+                line.first(step)
 
             def finish():
-                for step in range(1, group.count - 1):
-                    line.step(step)
+                for step in range(group.count - 1):
+                    line.rest(step)
                 line.finish(out)
 
         elif self.kind == "gather":
@@ -1335,12 +1345,17 @@
 GELU_B = 0.044715
 
 
+def strip_rows(strips, which, first, size):
+    length = strips[0].shape[1]
+    return strips[first // length][which, first % length : first % length + size, :]
+
+
 def feed_body(rows, ins, outs, scratch):
-    x_ref, up_ref, down_ref, bias_ref = ins
+    x_ref, bias_ref, *strips = ins
     total_ref, full_out, before_ref = outs
     (full_sem,) = scratch
     part = x_ref.shape[0]
-    units = up_ref.shape[0]
+    units = bias_ref.shape[1]
     tile = min(units, BLOCK)
 
     def term(place):
@@ -1349,11 +1364,11 @@
         total = None
         for first in range(0, units, tile):
             lanes = slice(first, first + tile)
-            before = matmul_t(block, up_ref[lanes, :]) + bias_ref[:, lanes]
+            before = matmul_t(block, strip_rows(strips, 0, first, tile)) + bias_ref[:, lanes]
             before_ref[at, lanes] = before
             bend = jnp.tanh(GELU_A * (before + GELU_B * before * before * before))
             active = (0.5 * before * (1.0 + bend)).astype(BF16)
-            piece = matmul(active, down_ref[lanes, :])
+            piece = matmul(active, strip_rows(strips, 1, first, tile))
             total = piece if total is None else total + piece
         return total
 
@@ -1364,13 +1379,13 @@
     keep.wait()
 
 
-def feed(team, ident, jobs, x, up, down, bias):
+def feed(team, ident, jobs, x, strips, bias):
     part, model = x.shape
-    units = up.shape[0]
+    units = bias.shape[1]
     return team_call(
         feed_body, team, ident, jobs,
-        [x, up, down, bias],
-        [VMEM] * 4,
+        [x, bias] + strips,
+        [VMEM] * (2 + len(strips)),
         (
             jax.ShapeDtypeStruct((part, model), F32),
             jax.ShapeDtypeStruct((team.count, part, model), BF16),
@@ -1382,12 +1397,12 @@
 
 
 def feed_back_body(rows, ins, outs, scratch, late=None):
-    gz_ref, c_ref, before_ref, up_ref, down_ref = ins
+    gz_ref, c_ref, before_ref, *strips = ins
     total_ref, grads_ref, sums_ref = outs
     active, low = scratch
     part, model = gz_ref.shape
     seq = part * rows.count
-    units = up_ref.shape[0]
+    units = before_ref.shape[1]
     tile = min(units, BLOCK)
     sums_ref[...] = jnp.zeros_like(sums_ref)
 
@@ -1403,11 +1418,15 @@
             slope = half + 0.5 * before * (1.0 - bend * bend) * (
                 GELU_A * (1.0 + 3.0 * GELU_B * square)
             )
-            grad = matmul_t(gz, down_ref[lanes, :]) * slope
+            grad = matmul_t(gz, strip_rows(strips, 1, first, tile)) * slope
             sums_ref[:, lanes] += jnp.sum(grad, axis=0, keepdims=True)
             active[at, lanes] = (before * half).astype(BF16)
             low[at, lanes] = grad.astype(BF16)
-        return matmul(low[at, :], up_ref[...])
+        length = strips[0].shape[1]
+        return sum(
+            matmul(low[at, n * length : (n + 1) * length], strip[0])
+            for n, strip in enumerate(strips)
+        )
 
     rows.each_arrival_and_back(term)
     for first in range(0, units, tile):
@@ -1421,14 +1440,14 @@
         late.wait()
 
 
-def feed_back(team, ident, jobs, pair, gz, c, before, up, down):
+def feed_back(team, ident, jobs, pair, gz, c, before, strips):
     part, model = gz.shape
     seq = part * team.count
-    units = up.shape[0]
+    units = before.shape[1]
     return team_call(
         feed_back_body, team, ident, jobs,
-        [gz, c, before, up, down],
-        [VMEM] * 5,
+        [gz, c, before] + strips,
+        [VMEM] * (3 + len(strips)),
         (
             jax.ShapeDtypeStruct((part, model), F32),
             jax.ShapeDtypeStruct((2, units, model), F32),
@@ -1439,6 +1458,271 @@
         pair,
         jax.ShapeDtypeStruct((units, model), F32),
     )
+
+
+def line_head_logits_body(
+    group, x_ref, e_ref, ids_ref, logits_ref, full_out, stats_out,
+    full, table, staged, top, total, pick, stats,
+    ag_send, ag_recv, e_sem, out_sem, full_sem, st_send, st_recv,
+):
+    count, me = group.count, group.me()
+    part = x_ref.shape[0]
+    tiles = e_ref.shape[0] // CHUNK
+    line = LineRows(group, x_ref, full, ag_send, ag_recv)
+    greet([group])
+    line.start()
+    full[me] = x_ref[...]
+    top[...] = jnp.full_like(top, NEG)
+    total[...] = jnp.zeros_like(total)
+    pick[...] = jnp.zeros_like(pick)
+
+    def rows_of(tile):
+        return pl.ds(pl.multiple_of(tile * CHUNK, CHUNK), CHUNK)
+
+    def load(tile):
+        return pltpu.make_async_copy(
+            e_ref.at[rows_of(tile)], table.at[rows_of(tile)], e_sem.at[tile]
+        )
+
+    def leave(tile, place, slot):
+        return pltpu.make_async_copy(
+            staged.at[slot], logits_ref.at[tile, part_rows(place, part)], out_sem.at[slot]
+        )
+
+    for tile in range(tiles):
+        load(tile).start()
+
+    def work(place, first):
+        at = part_rows(place, part)
+        ids = ids_ref[at, :]
+
+        def one(pair, carry):
+            for slot in range(2):
+                tile = 2 * pair + slot
+                if first:
+                    load(tile).wait()
+
+                    @pl.when(pair > 0)
+                    def _(slot=slot, tile=tile):
+                        leave(tile, place, slot).wait()
+
+                else:
+                    leave(tile, place, slot).wait()
+                logits = matmul_t(full[place], table[rows_of(tile), :])
+                staged[slot] = logits
+                leave(tile, place, slot).start()
+                column = tile * CHUNK + lax.broadcasted_iota(jnp.int32, (part, CHUNK), 1)
+                picked = jnp.where(column == ids, logits, 0.0)
+                pieces = [logits[:, at : at + LANES] for at in range(0, CHUNK, LANES)]
+                before = top[at, :]
+                high = functools.reduce(jnp.maximum, pieces, before)
+                sums = total[at, :] * jnp.exp(before - high)
+                found = pick[at, :]
+                for number, piece in enumerate(pieces):
+                    sums = sums + jnp.exp(piece - high)
+                    found = found + picked[:, number * LANES : (number + 1) * LANES]
+                top[at, :] = high
+                total[at, :] = sums
+                pick[at, :] = found
+            return carry
+
+        lax.fori_loop(0, tiles // 2, one, 0)
+
+    work(me, True)
+    for step in range(1, count):
+        line.step(step)
+
+        @pl.when(me >= step)
+        def _(step=step):
+            work(me - step, False)
+
+        @pl.when(me + step < count)
+        def _(step=step):
+            work(me + step, False)
+
+    keep = pltpu.make_async_copy(full, full_out, full_sem)
+    keep.start()
+    tall = top[...].T
+    high = jnp.max(tall, axis=0, keepdims=True)
+    stats[me] = jnp.zeros(stats.shape[1:], F32)
+    stats[me, 0:1, :] = high
+    stats[me, 1:2, :] = jnp.sum(total[...].T * jnp.exp(tall - high), axis=0, keepdims=True)
+    stats[me, 2:3, :] = jnp.sum(pick[...].T, axis=0, keepdims=True)
+    copies = [
+        send(group, peer, step, stats.at[me], stats.at[me], st_send, st_recv)
+        for step, peer in enumerate(group.peers())
+    ]
+    for slot in range(2):
+        leave(0, me, slot).wait()
+    line.wait_sends()
+    for copy in copies:
+        copy.wait()
+    stats_out[...] = stats[...]
+    keep.wait()
+
+
+def line_head_logits(group, ident, x, embedding, ids):
+    part, width = x.shape
+    vocab = embedding.shape[0]
+    count = group.count
+    tokens = part * count
+    tiles = vocab // CHUNK
+    assert tiles % 2 == 0
+    dma = pltpu.SemaphoreType.DMA
+    return pl.pallas_call(
+        functools.partial(line_head_logits_body, group),
+        out_shape=(
+            jax.ShapeDtypeStruct((tiles, tokens, CHUNK), F32),
+            jax.ShapeDtypeStruct((count, part, width), BF16),
+            jax.ShapeDtypeStruct((count, 8, tokens), F32),
+        ),
+        in_specs=[VMEM, HBM, VMEM],
+        out_specs=(HBM, HBM, VMEM),
+        scratch_shapes=[
+            pltpu.VMEM((count, part, width), BF16),
+            pltpu.VMEM((vocab, width), BF16),
+            pltpu.VMEM((2, part, CHUNK), F32),
+            pltpu.VMEM((tokens, LANES), F32),
+            pltpu.VMEM((tokens, LANES), F32),
+            pltpu.VMEM((tokens, LANES), F32),
+            pltpu.VMEM((count, 8, tokens), F32),
+            dma((2 * count - 2,)),
+            dma((2 * count - 2,)),
+            dma((tiles,)),
+            dma((2,)),
+            dma,
+            dma((count - 1,)),
+            dma((count - 1,)),
+        ],
+        compiler_params=pltpu.CompilerParams(
+            collective_id=ident, has_side_effects=True, vmem_limit_bytes=56 * 2**20
+        ),
+    )(x, embedding, ids)
+
+
+def line_head_grads_body(
+    group, logits_ref, e_ref, ids_ref, norm_ref, weight_ref, grads_ref, total_ref,
+    terms, stage, land, table, staged, low, acc,
+    rs_send, rs_recv, e_sem, in_sem, out_sem,
+):
+    count, me = group.count, group.me()
+    part = terms.shape[1]
+    tiles = e_ref.shape[0] // CHUNK
+    line = LineSum(group, terms, stage, land, rs_send, rs_recv)
+    greet([group])
+
+    def rows_of(tile):
+        return pl.ds(pl.multiple_of(tile * CHUNK, CHUNK), CHUNK)
+
+    def load(tile):
+        return pltpu.make_async_copy(
+            e_ref.at[rows_of(tile)], table.at[rows_of(tile)], e_sem.at[tile]
+        )
+
+    def enter(tile, place, slot):
+        return pltpu.make_async_copy(
+            logits_ref.at[tile, part_rows(place, part)], staged.at[slot], in_sem.at[slot]
+        )
+
+    def leave(tile, place, slot):
+        return pltpu.make_async_copy(
+            low.at[:, pl.ds(slot * CHUNK, CHUNK)],
+            grads_ref.at[tile, part_rows(place, part)],
+            out_sem.at[slot],
+        )
+
+    for tile in range(tiles):
+        load(tile).start()
+    for tile in range(tiles):
+        load(tile).wait()
+
+    def work(place):
+        at = part_rows(place, part)
+        ids, norm, weight = ids_ref[at, :], norm_ref[at, :], weight_ref[at, :]
+        for slot in range(2):
+            enter(slot, place, slot).start()
+        acc[...] = jnp.zeros_like(acc)
+
+        def one(pair, carry):
+            for slot in range(2):
+                tile = 2 * pair + slot
+                enter(tile, place, slot).wait()
+                column = tile * CHUNK + lax.broadcasted_iota(jnp.int32, (part, CHUNK), 1)
+                probs = jnp.exp(staged[slot] - norm)
+                grads = (jnp.where(column == ids, probs - 1.0, probs) * weight).astype(BF16)
+
+                @pl.when(pair > 0)
+                def _(slot=slot, tile=tile):
+                    leave(tile, place, slot).wait()
+
+                low[:, slot * CHUNK : (slot + 1) * CHUNK] = grads
+                leave(tile, place, slot).start()
+
+                @pl.when(pair + 1 < tiles // 2)
+                def _(slot=slot, tile=tile):
+                    enter(tile + 2, place, slot).start()
+
+            rows = pl.ds(pl.multiple_of(pair * 2 * CHUNK, 2 * CHUNK), 2 * CHUNK)
+            acc[...] += matmul(low[...], table[rows, :])
+            return carry
+
+        lax.fori_loop(0, tiles // 2, one, 0)
+        for slot in range(2):
+            leave(0, place, slot).wait()
+        terms[place] = acc[...].astype(BF16)
+
+    for step in range(count - 1):
+
+        @pl.when(me < count - 1 - step)
+        def _(step=step):
+            work(count - 1 - step)
+
+        @pl.when(me > step)
+        def _(step=step):
+            work(step)
+
+        line.first(step)
+        if step == 1:
+            line.rest(0, near=True)
+    work(me)
+    line.rest(0, near=False)
+    for step in range(1, count - 1):
+        line.rest(step)
+    line.finish(total_ref)
+
+
+def line_head_grads(group, ident, logits, embedding, ids, norm, weight):
+    tiles, tokens, _ = logits.shape
+    vocab, width = embedding.shape
+    count = group.count
+    part = tokens // count
+    dma = pltpu.SemaphoreType.DMA
+    return pl.pallas_call(
+        functools.partial(line_head_grads_body, group),
+        out_shape=(
+            jax.ShapeDtypeStruct(logits.shape, BF16),
+            jax.ShapeDtypeStruct((part, width), F32),
+        ),
+        in_specs=[HBM, HBM, VMEM, VMEM, VMEM],
+        out_specs=(HBM, VMEM),
+        scratch_shapes=[
+            pltpu.VMEM((count, part, width), BF16),
+            pltpu.VMEM((2, count - 1, part, width), BF16),
+            pltpu.VMEM((2, count - 1, part, width), BF16),
+            pltpu.VMEM((vocab, width), BF16),
+            pltpu.VMEM((2, part, CHUNK), F32),
+            pltpu.VMEM((part, 2 * CHUNK), BF16),
+            pltpu.VMEM((part, width), F32),
+            dma((2, count - 1)),
+            dma((2, count - 1)),
+            dma((tiles,)),
+            dma((2,)),
+            dma((2,)),
+        ],
+        compiler_params=pltpu.CompilerParams(
+            collective_id=ident, has_side_effects=True, vmem_limit_bytes=56 * 2**20
+        ),
+    )(logits, embedding, ids, norm, weight)
 
 
 def per_device(
@@ -1583,8 +1867,7 @@
             params[l].update(
                 qk=block[:, :cols],
                 vo=block[:, cols : 2 * cols],
-                up=block[0, 2 * cols :],
-                down=block[1, 2 * cols :],
+                strips=[block[:, 2 * cols :]],
             )
     head_number = (
         (jnp.arange(fan)[:, None] if planes else z) * (local_cols // HEAD_DIM)
@@ -1615,10 +1898,7 @@
 
     def take_feed(l, got):
         if got:
-            strips = [one.reshape(2, fan * strip, width) for one in got]
-            params[l]["up"], params[l]["down"] = (
-                jnp.concatenate([one[n] for one in strips]) for n in range(2)
-            )
+            params[l]["strips"] = [one.reshape(2, fan * strip, width) for one in got]
 
     def ident(kind, jobs):
         return exchange.ident((kind,) + tuple(job.key() for job in jobs))
@@ -1648,26 +1928,31 @@
         jobs = attn_jobs(l + 1) + feed_jobs(l + 1, 0)
         second = layer_norm(middle, p["gains"][1], p["offsets"][1]).astype(BF16)
         (total, second, before), got = feed(
-            team, ident("feed", jobs), jobs, second, p["up"], p["down"], p["up_bias"]
+            team, ident("feed", jobs), jobs, second, p["strips"], p["up_bias"]
         )
         take_attn(l + 1, got[:2])
         strips = got[2:]
         kept.append((h, normed.reshape(seq, width), q, k, v, mixed, lse, middle, second, before))
         h = middle + total + p["row_bias"][1]
 
-    (final,) = exchange(
-        gather(by_tensor, layer_norm(h, outer_gains[-1], outer_offsets[-1]).astype(BF16))
-    )
-    final = final.reshape(-1, width)
+    final = layer_norm(h, outer_gains[-1], outer_offsets[-1]).astype(BF16)
+    columns_of = (targets - vocab_start)[:, None]
+    if planes:
+        logits, final, stats = line_head_logits(
+            by_tensor, exchange.ident("head logits"), final, embedding, columns_of
+        )
+        final = final.reshape(-1, width)
+    else:
+        (final,) = exchange(gather(by_tensor, final))
+        final = final.reshape(-1, width)
+        logits, tops, totals, picks = head_logits(final, embedding, columns_of)
+        top = jnp.max(tops, axis=1)
+        total = jnp.sum(totals * jnp.exp(tops - top[:, None]), axis=1)
+        pick = jnp.sum(picks, axis=1)
+        (stats,) = exchange(
+            gather(by_tensor, jnp.pad(jnp.stack([top, total, pick]), ((0, 5), (0, 0))))
+        )
     tokens = final.shape[0]
-    columns_of = (targets - vocab_start)[:, None]
-    logits, tops, totals, picks = head_logits(final, embedding, columns_of)
-    top = jnp.max(tops, axis=1)
-    total = jnp.sum(totals * jnp.exp(tops - top[:, None]), axis=1)
-    pick = jnp.sum(picks, axis=1)
-    (stats,) = exchange(
-        gather(by_tensor, jnp.pad(jnp.stack([top, total, pick]), ((0, 5), (0, 0))))
-    )
     top_all = jnp.max(stats[:, 0], axis=0)
     log_norm = top_all + jnp.log(jnp.sum(stats[:, 1] * jnp.exp(stats[:, 0] - top_all), axis=0))
     terms = jnp.where(valid, log_norm - jnp.sum(stats[:, 2], axis=0), 0.0)
@@ -1675,12 +1960,18 @@
         lax.dynamic_index_in_dim(terms.reshape(shards, -1), z, 0, keepdims=False)
     )
     row_weight = jnp.where(valid, 1.0 / token_count, 0.0)
-    grad_logits, back = head_grads(
-        logits, embedding, columns_of, log_norm[:, None], row_weight[:, None]
-    )
-    (grad_final,) = exchange(
-        Job("reduce", [by_tensor], back.reshape(shards, group_part, width))
-    )
+    if planes:
+        grad_logits, grad_final = line_head_grads(
+            by_tensor, exchange.ident("head grads"), logits, embedding, columns_of,
+            log_norm[:, None], row_weight[:, None],
+        )
+    else:
+        grad_logits, back = head_grads(
+            logits, embedding, columns_of, log_norm[:, None], row_weight[:, None]
+        )
+        (grad_final,) = exchange(
+            Job("reduce", [by_tensor], back.reshape(shards, group_part, width))
+        )
     _, final_back = jax.vjp(layer_norm, h, outer_gains[-1], outer_offsets[-1])
     grad, final_gain, final_offset = final_back(grad_final)
 
@@ -1716,7 +2007,7 @@
         jobs = tensor_jobs(attn_low[l + 1]) if late else []
         (total, g_feed, up_sum, *dealt), got = feed_back(
             team, ident("feed back", jobs), jobs, pair, grad.astype(BF16),
-            second.reshape(seq, width), before, p["up"], p["down"],
+            second.reshape(seq, width), before, p["strips"],
         )
         if late:
             attn_done[l + 1] = tensor_sums(attn_low[l + 1], got)
@@ -1771,7 +2062,7 @@
     packed = jnp.pad(packed, ((0, -used % 8), (0, 0)))
     jobs = [Job("gather", [Group(("section", "tensor"), (sections, shards))], packed, late=True)]
     if planes:
-        jobs += spread_jobs(attn_done[1] + feed_done[1])
+        jobs += spread_jobs(attn_done[1] + feed_done[1] + feed_done[0])
         jobs += [Job("deal", [by_tensor], low, 1, late=True) for low in attn_low[0]]
     embed_sum, packed, *got = table_sum(
         by_section, by_dp, by_tensor, jobs, grad_logits, ids[None, :] - vocab_start, final,
@@ -1781,10 +2072,11 @@
     jobs = [gather(by_dp, packed)]
     if planes:
         spread_one = got[:2]
-        jobs += spread_jobs(tensor_sums(attn_low[0], got[2:]) + feed_done[0])
+        jobs += spread_jobs(tensor_sums(attn_low[0], got[3:]))
     packed, *spread_zero = exchange(*jobs)
     packed = jnp.sum(packed, axis=0)
     if planes:
+        spread_zero.append(got[2])
         attn_sum, feed_sum = (
             jnp.where(s == 0, zero, one) for zero, one in zip(spread_zero, spread_one)
         )

time: 1140 us -> 1080 us (0.947)
  Pallas kernels: 957 us -> 913 us
    pallas_call x6 -> x3, Pallas kernels: 207 us -> 101 us  [__call__(): pl.pallas_call(functools.partial(exchange_body, jobs), out_shape=tuple((j...]
    pallas_call x2, Pallas kernels: 65 us -> 128 us  [the longest x1 66.6 us: line_head_grads(): pl.pallas_call(functools.partial(line_head_grads_body, group), out_shape=...]
    pallas_call x8, Pallas kernels: 468 us -> 454 us  [team_call(): pl.pallas_call(kernel, out_shape=tuple(outs) + tuple((job.out for job in...]
    pallas_call x1, Pallas kernels: 217 us -> 230 us  [table_sum(): pl.pallas_call(functools.partial(table_square_body if by_dp.square else t...]
where the time goes in v6:
time: 1080 us; the launch traced here: 1070 us
  Pallas kernels  913 us (85%)
  other arithmetic  79.9 us (7%)
  local copies, waits for them, and re-layouts  70.7 us (7%)
    pallas_call x8, Pallas kernels, team_call(): pl.pallas_call(kernel, out_shape=tuple(outs) + tuple((job.out for job in...  454 us
    pallas_call x1, Pallas kernels, table_sum(): pl.pallas_call(functools.partial(table_square_body if by_dp.square else t...  230 us
    pallas_call x3, Pallas kernels, __call__(): pl.pallas_call(functools.partial(exchange_body, jobs), out_shape=tuple((j...  101 us
    pallas_call x1, Pallas kernels, line_head_grads(): pl.pallas_call(functools.partial(line_head_grads_body, group), out_shape=...  66.6 us
    pallas_call x1, Pallas kernels, line_head_logits(): pl.pallas_call(functools.partial(line_head_logits_body, group), out_shape...  61.1 us

profile of v6, /device:TPU:1, one launch (start us, length us, event | category | flops | bytes accessed | tf_op | source)
XLA Modules:
  0.0 1068.6 jit_solution(4531074683627242105)
XLA Ops:
  0.7 1.6 fusion.41
  3.4 1.2 dynamic-slice_bitcast_fusion
  6.9 14.8 %shard_map.246 = (bf16[1,384,1024]{2,1,0:T(8,128)(2,1)S(1)}, s32[4,2,2,1024]{3,2,1,0:T(2,128)S(1)}, f32[8,16,1024]{2,1,0:T(8,128)S(1)}) custom-call(bf16[2,384,1024]{2,1,0:T(8,128)(2,1)S(1)} %pad_maximum_fusion.refs_0_, s32[2,2,1024]{2,1,0:T(2,128)S(1)} %pad_add_fusion.refs_1_, f32[16,1024]{1,0:T(8,128)S(1)} %concatenate.14.refs_2_), custom_call_target="tpu_custom_call" | custom-call | tf_op jit(solution)/shard_map/pallas_call | solution.py:434
  23.5 13.9 %gather_fusion = bf16[1024,1024]{1,0:T(8,128)(2,1)} fusion(bf16[8192,1024]{1,0:T(8,128)(2,1)} %e_ref.3, s32[1024]{0:T(1024)S(1)} %broadcast_clamp_fusion), kind=kCustom, calls=%fused_computation | custom fusion | bytes 4198400 | tf_op jit(solution)/shard_map/jit(_take)/gather | solution.py:1909
  37.5 1.9 select_select_fusion.refs_0_
  39.3 2.9 broadcast_select_fusion.2
  43.1 68.1 %shard_map.247 = (f32[256,1024]{1,0:T(8,128)S(1)}, bf16[2,4,64,1024]{3,2,1,0:T(8,128)(2,1)S(1)}, bf16[2,4,64,1024]{3,2,1,0:T(8,128)(2,1)S(1)}) custom-call(bf16[4,256,1024]{2,1,0:T(8,128)(2,1)S(1)} %select_select_fusion.refs_0_, bf16[64,1024]{1,0:T(8,128)(2,1)S(1)} %get-tuple-element.214.refs_1_, bf16[64,1024]{1,0:T(8,128)(2,1)S(1)} %get-tuple-element.213.refs_2_), custom_call_target="tpu_custom_call" | custom-call | tf_op jit(solution)/shard_map/pallas_call | solution.py:434
  113.5 1.3 fusion.42
  115.6 1.5 add_convert_fusion.5.refs_0_
  120.6 60.6 %shard_map.248 = (f32[256,1024]{1,0:T(8,128)}, bf16[4,256,1024]{2,1,0:T(8,128)(2,1)}, bf16[1024,256]{1,0:T(8,128)(2,1)}, bf16[1024,256]{1,0:T(8,128)(2,1)}, bf16...) custom-call(bf16[256,1024]{1,0:T(8,128)(2,1)} %add_convert_fusion.5., ...), custom_call_target="tpu_custom_call" | custom-call | tf_op jit(solution)/shard_map/pallas_call | solution.py:1169
  181.2 1.6 fusion.38
  187.1 55.1 %shard_map.249 = (f32[256,1024]{1,0:T(8,128)}, bf16[4,256,1024]{2,1,0:T(8,128)(2,1)}, f32[1024,1024]{1,0:T(8,128)}, bf16[2,4,64,1024]{3,2,1,0:T(8,128)(2,1)}, bf...) custom-call(bf16[256,1024]{1,0:T(8,128)(2,1)} %add_convert_fusion.4.refs_0_, f32[1,1024]{1,0:T(1,128)} %bitcast.357, ...), custom_call_target="tpu_custom_call" | custom-call | tf_op jit(solution)/shard_map/pallas_call | solution.py:1169
  242.2 1.4 fusion.37
  245.7 56.9 %shard_map.250 = (f32[256,1024]{1,0:T(8,128)}, bf16[4,256,1024]{2,1,0:T(8,128)(2,1)}, bf16[1024,256]{1,0:T(8,128)(2,1)}, bf16[1024,256]{1,0:T(8,128)(2,1)}, bf16...) custom-call(bf16[256,1024]{1,0:T(8,128)(2,1)} %add_convert_fusion.3., ...), custom_call_target="tpu_custom_call" | custom-call | tf_op jit(solution)/shard_map/pallas_call | solution.py:1169
  302.6 1.4 fusion.36
  306.0 47.5 %shard_map.251 = (f32[256,1024]{1,0:T(8,128)}, bf16[4,256,1024]{2,1,0:T(8,128)(2,1)}, f32[1024,1024]{1,0:T(8,128)}) custom-call(bf16[256,1024]{1,0:T(8,128)(2,1)} %add_convert_fusion.2.refs_0_, f32[1,1024]{1,0:T(1,128)} %bitcast.358, bf16[2,512,1024]{2,1,0:T(8,128)(2,1)} %bitcast.257, bf16[2,512,1024]{2,1,0:T(8,128)(2,1)} %bitcast.259), custom_call_target="tpu_custom_call" | custom-call | tf_op jit(solution)/shard_map/pallas_call | solution.py:1169
  353.5 1.4 fusion.35
  358.0 61.1 %shard_map.252 = (f32[16,1024,512]{2,1,0:T(8,128)}, bf16[4,256,1024]{2,1,0:T(8,128)(2,1)}, f32[4,8,1024]{2,1,0:T(8,128)}) custom-call(bf16[256,1024]{1,0:T(8,128)(2,1)} %add_convert_fusion.1.x_ref, bf16[8192,1024]{1,0:T(8,128)(2,1)} %e_ref.3, s32[1024,1]{1,0:T(8,128)} %bitcast.261), custom_call_target="tpu_custom_call" | custom-call | tf_op jit(solution)/shard_map/pallas_call | solution.py:1572
  425.0 66.6 %shard_map.253 = (bf16[16,1024,512]{2,1,0:T(8,128)(2,1)}, f32[256,1024]{1,0:T(8,128)}) custom-call(f32[16,1024,512]{2,1,0:T(8,128)} %get-tuple-element.93.logits_ref, bf16[8192,1024]{1,0:T(8,128)(2,1)} %e_ref.3, s32[1024,1]{1,0:T(8,128)} %bitcast.262, f32[1024,1]{1,0:T(8,128)} %copy.66.norm_ref, f32[1024,1]{1,0:T(8,128)} %bitcast.270), custom_call_target="tpu_custom_call" | custom-call | tf_op jit(solution)/shard_map/pallas_call | solution.py:1700
  491.6 1.7 multiply_reduce_fusion
  494.7 54.6 %shard_map.254 = (f32[256,1024]{1,0:T(8,128)}, f32[2,1024,1024]{2,1,0:T(8,128)}, f32[1,1024]{1,0:T(1,128)}, f32[1024,1024]{1,0:T(8,128)}) custom-call(bf16[256,1024]{1,0:T(8,128)(2,1)} %get-tuple-element.206.refs_0_, bf16[1024,1024]{1,0:T(8,128)(2,1)} %bitcast.281, f32[1024,1024]{1,0:T(8,128)} %get-tuple-element.99.refs_2_, bf16[2,512,1024]{2,1,0:T(8,128)(2,1)} %bitcast.258, ...), custom_call_target="tpu_custom_call" | custom-call | tf_op jit(solution)/shard_map/pallas_call | solution.py:1169
  549.3 2.7 constant_dynamic-slice_fusion.8
  552.7 1.1 fusion.1
  553.9 1.5 copy.70.refs_11_
  558.9 64.6 %shard_map.255 = (f32[256,1024]{1,0:T(8,128)}, f32[4,256,1024]{2,1,0:T(8,128)}, f32[2,256]{1,0:T(2,128)}, f32[2,256,1024]{2,1,0:T(8,128)}, bf16[3,2,128,1024]{3,2,1,0:T(8,128)(2,1)}) custom-call(bf16[256,1024]{1,0:T(8,128)(2,1)} %convert_element_type.168.refs_0_, s32[1]{0:T(128)} %dynamic_slice.119.refs_1_, f32[4]{0:T(128)} %multiply_exponential_fusion.refs_2_, ...), custom_call_target="tpu_custom_call" | custom-call | tf_op jit(solution)/shard_map/pallas_call | solution.py:1169
  623.5 1.9 constant_dynamic-slice_fusion.7
  630.2 48.4 %shard_map.256 = (f32[256,1024]{1,0:T(8,128)}, f32[2,1024,1024]{2,1,0:T(8,128)}, f32[1,1024]{1,0:T(1,128)}, f32[1024,1024]{1,0:T(8,128)}, bf16[3,2,64,1024]{3,2,1,0:T(8,128)(2,1)}) custom-call(bf16[256,1024]{1,0:T(8,128)(2,1)} %convert_element_type.170.refs_0_, bf16[1024,1024]{1,0:T(8,128)(2,1)} %bitcast.279, f32[1024,1024]{1,0:T(8,128)} %get-tuple-element.111.refs_2_, ...), custom_call_target="tpu_custom_call" | custom-call | tf_op jit(solution)/shard_map/pallas_call | solution.py:1169
  678.5 2.7 constant_dynamic-slice_fusion.6
  682.0 1.1 fusion
  683.1 1.5 copy.76.refs_11_
  687.1 66.3 %shard_map.257 = (f32[256,1024]{1,0:T(8,128)}, f32[4,256,1024]{2,1,0:T(8,128)}, f32[2,256]{1,0:T(2,128)}, f32[2,256,1024]{2,1,0:T(8,128)}, bf16[3,2,128,1024]{3,2,1,0:T(8,128)(2,1)}) custom-call(bf16[256,1024]{1,0:T(8,128)(2,1)} %convert_element_type.172.refs_0_, s32[1]{0:T(128)} %dynamic_slice.119.refs_1_, f32[4]{0:T(128)} %multiply_exponential_fusion.refs_2_, ...), custom_call_target="tpu_custom_call" | custom-call | tf_op jit(solution)/shard_map/pallas_call | solution.py:1169
  753.4 1.9 constant_dynamic-slice_fusion.4
  757.9 1.3 convert_reduce_fusion
  759.2 2.4 fusion.5.refs_3_
  761.9 2.1 fusion.6.refs_2_
  764.2 1.7 fusion.9.refs_1_
  767.2 1.4 multiply_reduce_fusion.1
  771.8 1.6 fusion.29
  775.0 230.1 %shard_map.258 = (bf16[16,512,1024]{2,1,0:T(8,128)(2,1)}, f32[8,32,1024]{2,1,0:T(8,128)}, bf16[2,4,2,64,1024]{4,3,2,1,0:T(8,128)(2,1)}, bf16[2,4,2,128,1024]{4,3...) custom-call(bf16[16,1024,512]{2,1,0:T(8,128)(2,1)} %get-tuple-element.95.g_ref, ...), custom_call_target="tpu_custom_call" | custom-call | tf_op jit(solution)/shard_map/pallas_call | solution.py:864
  1005.0 2.6 broadcast_select_fusion
  1008.3 2.6 bitcast_convert_fusion.2
  1010.9 5.3 copy.89
  1016.3 2.6 bitcast_convert_fusion.1
  1020.2 18.6 %shard_map.259 = (f32[4,32,1024]{2,1,0:T(8,128)S(1)}, bf16[2,4,2,64,1024]{4,3,2,1,0:T(8,128)(2,1)S(1)}) custom-call(f32[32,1024]{1,0:T(8,128)S(1)} %reduce_sum.540.refs_0_, bf16[2,64,1024]{2,1,0:T(8,128)(2,1)S(1)} %fusion.8.refs_1_), custom_call_target="tpu_custom_call" | custom-call | tf_op jit(solution)/shard_map/pallas_call | solution.py:434
  1038.8 1.8 broadcast_select_fusion.1
  1041.4 1.9 fusion.4
  1043.3 1.1 bitcast_convert_fusion.3
  1044.5 18.8 %bitcast_convert_fusion = f32[8192,1024]{1,0:T(8,128)} fusion(bf16[16,512,1024]{2,1,0:T(8,128)(2,1)} %get-tuple-element.136), kind=kLoop, calls=%fused_computation.1 | loop fusion | flops 8388608 | bytes 50331648 | tf_op jit(solution)/shard_map/convert_element_type | solution.py:2093
  (256 shorter events, 57.1 us)
Async XLA Ops:
  0.6 2.3 copy-start
  3.3 2.6 copy-start.13
  5.6 1.1 copy-start.45
  5.6 1.1 copy-start.33
  5.6 1.1 copy-start.34
  5.6 1.1 copy-start.35
  5.6 1.1 copy-start.38
  5.6 1.1 copy-start.39
  5.7 1.2 copy-start.36
  5.7 1.2 copy-start.37
  5.7 1.0 copy-start.14
  21.6 0.9 copy-start.4
  22.5 0.8 copy-start.6
  37.4 1.9 copy-start.5
  42.2 0.9 copy-start.24
  111.2 1.0 copy-start.2
  112.1 1.0 copy-start.3
  113.5 5.1 copy-start.25
  115.1 4.3 copy-start.44
  182.8 1.3 copy-start.23
  304.1 49.4 %copy-start.7 = (f32[256,1024]{1,0:T(8,128)}, f32[256,1024]{1,0:T(8,128)S(1)}, u32[]{:S(2)}) copy-start(f32[256,1024]{1,0:T(8,128)S(1)} %get-tuple-element.189) | copy-start | bytes 3145732
  354.9 1.0 copy-start.9
  425.0 66.7 %copy-start.10 = (f32[256,1024]{1,0:T(8,128)S(1)}, f32[256,1024]{1,0:T(8,128)}, u32[]{:S(2)}) copy-start(f32[256,1024]{1,0:T(8,128)} %copy-done.9) | copy-start | bytes 3145732
  491.6 1.7 copy-start.19
  549.3 3.5 copy-start.21
  553.9 2.1 copy-start.11
  553.9 2.1 copy-start.8
  553.9 3.0 copy-start.18
  623.5 2.2 copy-start.27
  626.2 2.4 copy-start.15
  626.2 2.0 copy-start.16
  678.5 3.5 copy-start.20
  683.1 2.0 copy-start.12
  683.1 2.0 copy-start.17
  753.4 2.2 copy-start.26
  756.1 1.8 copy-start.29
  759.2 2.4 copy-start.28
  761.6 2.4 copy-start.31
  761.9 4.0 copy-start.22
  767.2 1.5 copy-start.43
  767.2 1.9 copy-start.41
  767.2 2.0 copy-start.42
  767.2 2.4 copy-start.40
  1016.2 2.6 copy-start.32
  1018.9 1.2 copy-start.30
  1044.5 22.5 %copy-start.1 = (bf16[1,1024,1024]{2,1,0:T(8,128)(2,1)S(1)}, bf16[1,1024,1024]{2,1,0:T(8,128)(2,1)}, u32[]{:S(2)}) copy-start(bf16[1,1024,1024]{2,1,0:T(8,128)(2,1)} %param.26) | copy-start | bytes 6291460

commit v7 on v6

--- a/solution.py
+++ b/solution.py
@@ -746,9 +746,11 @@
             return carry
 
         lax.fori_loop(0, subs, share, 0)
+    for end in ends:
+        end()
     line.step(line.count - 1)
     line.wait_sends()
-    ends += [job.start(xs[n], outs[n], *parts[n]) for n, job in enumerate(jobs) if job.late]
+    ends = [job.start(xs[n], outs[n], *parts[n]) for n, job in enumerate(jobs) if job.late]
 
     for index, (number, away) in enumerate(order):
         half = partner if away == 0 else s
@@ -1099,6 +1101,8 @@
         lax.fori_loop(0, self.count - 1, one, 0)
 
     def finish(self, total_ref):
+        for end in self.ends:
+            end()
         for step in range(self.count - 1):
             self.rs(step).wait()
         total = self.own[...]
@@ -1139,7 +1143,7 @@
         self.copy.wait()
 
 
-def team_call(body, team, ident, jobs, arrays, specs, outs, out_specs, scratch, pair=None, dealt=None):
+def team_call(body, team, ident, jobs, arrays, specs, outs, out_specs, scratch, pair=None, dealt=None, ahead=0):
     if pair is not None:
         outs, out_specs = tuple(outs) + (dealt,), tuple(out_specs) + (HBM,)
         scratch = list(scratch) + [pltpu.SemaphoreType.DMA((1,))] * 2
@@ -1158,13 +1162,26 @@
         greet([team] + job_groups(jobs) + ([] if pair is None else [pair]))
         rows.send_rows()
         parts = split_scratch(jobs, refs)
-        ends = [job.start(xs[n], landings[n], *parts[n]) for n, job in enumerate(jobs)]
+
+        def start(numbers):
+            return [jobs[n].start(xs[n], landings[n], *parts[n]) for n in numbers]
+
+        rows.landings = landings
+        first = start(range(ahead if ahead else riders))
+        if ahead:
+
+            def ready():
+                for end in first:
+                    end()
+                rows.ends = start(range(ahead, riders))
+
+            rows.ready = ready
+        else:
+            rows.ends = first
         if pair is None:
             body(rows, ins, results, mine)
         else:
             body(rows, ins, results[:-1], mine[:-2], LateDeal(pair, results[-1], *mine[-2:]))
-        for end in ends:
-            end()
 
     out = pl.pallas_call(
         kernel,
@@ -1184,18 +1201,34 @@
 
 
 def attend_body(rows, ins, outs, scratch):
-    x_ref, length_ref, slope_ref, qk_ref, vo_ref, bias_ref = ins
+    x_ref, length_ref, slope_ref, bias_ref, *weights = ins
     total_ref, full_out, q_ref, k_ref, v_ref, mixed_ref, lse_ref = outs
-    (full_sem,) = scratch
+    full_sem, *buffers = scratch
+    if not weights:
+        *weights, sems = buffers
+        rows.ready()
+        copies = [
+            pltpu.make_async_copy(rows.landings[n], weights[n], sems.at[n]) for n in range(2)
+        ]
+        for copy in copies:
+            copy.start()
+        for copy in copies:
+            copy.wait()
+    qk_ref, vo_ref = weights
+
+    def weight(ref, n):
+        block = ref[n]
+        return block.reshape(-1, block.shape[-1])
+
     part = x_ref.shape[0]
     width = q_ref.shape[1]
 
     def project(place):
         at = part_rows(place, part)
         block = rows.full[place]
-        q_ref[at, :] = (matmul_t(block, qk_ref[0]) + bias_ref[0:1, :]).astype(BF16)
-        k_ref[at, :] = matmul_t(block, qk_ref[1]).astype(BF16)
-        v_ref[at, :] = (matmul_t(block, vo_ref[0]) + bias_ref[1:2, :]).astype(BF16)
+        q_ref[at, :] = (matmul_t(block, weight(qk_ref, 0)) + bias_ref[0:1, :]).astype(BF16)
+        k_ref[at, :] = matmul_t(block, weight(qk_ref, 1)).astype(BF16)
+        v_ref[at, :] = (matmul_t(block, weight(vo_ref, 0)) + bias_ref[1:2, :]).astype(BF16)
 
     rows.each_arrival(project)
     keep = pltpu.make_async_copy(rows.full, full_out, full_sem)
@@ -1221,7 +1254,7 @@
                     mixed_ref[first:upto, lanes] = matmul(probs, v_ref[:upto, lanes]).astype(BF16)
                     lse_ref[head, first:upto, :] = highest + jnp.log(total)
 
-        term = matmul(mixed_ref[part_rows(place, part), :], vo_ref[1])
+        term = matmul(mixed_ref[part_rows(place, part), :], weight(vo_ref, 1))
 
         @pl.when(step < rows.count - 1)
         def _():
@@ -1242,15 +1275,19 @@
 HBM = pl.BlockSpec(memory_space=pl.ANY)
 
 
-def attend(team, ident, jobs, x, length, slopes, qk, vo, bias):
+def attend(team, ident, jobs, x, length, slopes, bias, weights):
     part, model = x.shape
     seq = part * team.count
-    width = qk.shape[1]
+    width = bias.shape[1]
+    scratch = [pltpu.SemaphoreType.DMA]
+    if not weights:
+        scratch += [pltpu.VMEM(job.out.shape, BF16) for job in jobs[:2]]
+        scratch.append(pltpu.SemaphoreType.DMA((2,)))
     low = jax.ShapeDtypeStruct((seq, width), BF16)
     return team_call(
         attend_body, team, ident, jobs,
-        [x, length, slopes, qk, vo, bias],
-        [VMEM, SMEM, SMEM, VMEM, VMEM, VMEM],
+        [x, length, slopes, bias] + weights,
+        [VMEM, SMEM, SMEM, VMEM] + [VMEM] * len(weights),
         (
             jax.ShapeDtypeStruct((part, model), F32),
             jax.ShapeDtypeStruct((team.count, part, model), BF16),
@@ -1258,7 +1295,8 @@
             jax.ShapeDtypeStruct((width // HEAD_DIM, seq, 1), F32),
         ),
         (VMEM, HBM, VMEM, VMEM, VMEM, VMEM, VMEM),
-        [pltpu.SemaphoreType.DMA],
+        scratch,
+        ahead=0 if weights else 2,
     )
 
 
@@ -1633,10 +1671,8 @@
 
     for tile in range(tiles):
         load(tile).start()
-    for tile in range(tiles):
-        load(tile).wait()
-
-    def work(place):
+
+    def work(place, fresh=False):
         at = part_rows(place, part)
         ids, norm, weight = ids_ref[at, :], norm_ref[at, :], weight_ref[at, :]
         for slot in range(2):
@@ -1647,6 +1683,8 @@
             for slot in range(2):
                 tile = 2 * pair + slot
                 enter(tile, place, slot).wait()
+                if fresh:
+                    load(tile).wait()
                 column = tile * CHUNK + lax.broadcasted_iota(jnp.int32, (part, CHUNK), 1)
                 probs = jnp.exp(staged[slot] - norm)
                 grads = (jnp.where(column == ids, probs - 1.0, probs) * weight).astype(BF16)
@@ -1675,9 +1713,15 @@
 
         @pl.when(me < count - 1 - step)
         def _(step=step):
-            work(count - 1 - step)
-
-        @pl.when(me > step)
+            work(count - 1 - step, fresh=step == 0)
+
+        if step == 0:
+
+            @pl.when(me == count - 1)
+            def _():
+                work(0, fresh=True)
+
+        @pl.when((me > step) & ((me < count - 1) | (step > 0)))
         def _(step=step):
             work(step)
 
@@ -1909,20 +1953,21 @@
         inside[:, None], jnp.take(embedding, jnp.clip(local_ids, 0, vocab - 1), axis=0), 0
     )
     group_part = looked.shape[0] // shards
-    x, *got = exchange(
-        Job("reduce", [by_tensor], looked.reshape(shards, group_part, width)), *attn_jobs(0)
-    )
-    take_attn(0, got)
+    (x,) = exchange(Job("reduce", [by_tensor], looked.reshape(shards, group_part, width)))
     h = layer_norm(x, outer_gains[0], outer_offsets[0])
 
     kept = []
     strips = []
     for l, p in enumerate(params):
-        jobs = (feed_jobs(l, 0) if l == 0 else []) + feed_jobs(l, 1)
+        jobs = (attn_jobs(l) + feed_jobs(l, 0) if l == 0 else []) + feed_jobs(l, 1)
         normed = layer_norm(h, p["gains"][0], p["offsets"][0]).astype(BF16)
         (total, normed, q, k, v, mixed, lse), got = attend(
-            team, ident("attend", jobs), jobs, normed, length, slopes, p["qk"], p["vo"], p["bias"]
-        )
+            team, ident("attend", jobs), jobs, normed, length, slopes, p["bias"],
+            [p["qk"], p["vo"]] if "qk" in p else [],
+        )
+        if "qk" not in p:
+            take_attn(l, got[:2])
+            got = got[2:]
         take_feed(l, strips + got)
         middle = h + total + p["row_bias"][0]
         jobs = attn_jobs(l + 1) + feed_jobs(l + 1, 0)

time: 1080 us -> 1070 us (level)
    pallas_call x8, Pallas kernels: 454 us -> 478 us  [team_call(): pl.pallas_call(kernel, out_shape=tuple(outs) + tuple((job.out for job in...]
    pallas_call x3, Pallas kernels: 101 us -> 84.2 us  [__call__(): pl.pallas_call(functools.partial(exchange_body, jobs), out_shape=tuple((j...]
where the time goes in v7:
time: 1070 us; the launch traced here: 1060 us
  Pallas kernels  908 us (85%)
  other arithmetic  80 us (7%)
  local copies, waits for them, and re-layouts  64.1 us (6%)
    pallas_call x8, Pallas kernels, team_call(): pl.pallas_call(kernel, out_shape=tuple(outs) + tuple((job.out for job in...  478 us
    pallas_call x1, Pallas kernels, table_sum(): pl.pallas_call(functools.partial(table_square_body if by_dp.square else t...  220 us
    pallas_call x3, Pallas kernels, __call__(): pl.pallas_call(functools.partial(exchange_body, jobs), out_shape=tuple((j...  84.2 us
    pallas_call x1, Pallas kernels, line_head_grads(): pl.pallas_call(functools.partial(line_head_grads_body, group), out_shape=...  65.3 us
    pallas_call x1, Pallas kernels, line_head_logits(): pl.pallas_call(functools.partial(line_head_logits_body, group), out_shape...  60.2 us

profile of v7, /device:TPU:1, one launch (start us, length us, event | category | flops | bytes accessed | tf_op | source)
XLA Modules:
  0.0 1056.5 jit_solution(10204238850671943485)
XLA Ops:
  0.7 1.6 fusion.41
  3.4 1.2 dynamic-slice_bitcast_fusion
  6.9 14.8 %shard_map.246 = (bf16[1,384,1024]{2,1,0:T(8,128)(2,1)S(1)}, s32[4,2,2,1024]{3,2,1,0:T(2,128)S(1)}, f32[8,16,1024]{2,1,0:T(8,128)S(1)}) custom-call(bf16[2,384,1024]{2,1,0:T(8,128)(2,1)S(1)} %pad_maximum_fusion.refs_0_, s32[2,2,1024]{2,1,0:T(2,128)S(1)} %pad_add_fusion.refs_1_, f32[16,1024]{1,0:T(8,128)S(1)} %concatenate.14.refs_2_), custom_call_target="tpu_custom_call" | custom-call | tf_op jit(solution)/shard_map/pallas_call | solution.py:434
  21.8 13.9 %gather_fusion = bf16[1024,1024]{1,0:T(8,128)(2,1)} fusion(bf16[8192,1024]{1,0:T(8,128)(2,1)} %e_ref.3, s32[1024]{0:T(1024)S(1)} %broadcast_clamp_fusion), kind=kCustom, calls=%fused_computation | custom fusion | bytes 4198400 | tf_op jit(solution)/shard_map/jit(_take)/gather | solution.py:1953
  35.8 1.8 select_select_fusion.refs_0_
  37.6 49.1 %shard_map.247 = f32[256,1024]{1,0:T(8,128)S(1)} custom-call(bf16[4,256,1024]{2,1,0:T(8,128)(2,1)S(1)} %select_select_fusion.refs_0_), custom_call_target="tpu_custom_call" | custom-call | tf_op jit(solution)/shard_map/pallas_call | solution.py:434
  87.9 1.5 add_convert_fusion.5.refs_0_
  90.2 3.0 broadcast_select_fusion.2
  95.8 80.4 %shard_map.248 = (f32[256,1024]{1,0:T(8,128)}, bf16[4,256,1024]{2,1,0:T(8,128)(2,1)}, bf16[1024,256]{1,0:T(8,128)(2,1)}, bf16[1024,256]{1,0:T(8,128)(2,1)}, bf16...) custom-call(bf16[256,1024]{1,0:T(8,128)(2,1)} %add_convert_fusion.5., ...), custom_call_target="tpu_custom_call" | custom-call | tf_op jit(solution)/shard_map/pallas_call | solution.py:1186
  176.3 1.6 fusion.38
  181.4 56.5 %shard_map.249 = (f32[256,1024]{1,0:T(8,128)}, bf16[4,256,1024]{2,1,0:T(8,128)(2,1)}, f32[1024,1024]{1,0:T(8,128)}, bf16[2,4,64,1024]{3,2,1,0:T(8,128)(2,1)}, bf...) custom-call(bf16[256,1024]{1,0:T(8,128)(2,1)} %add_convert_fusion.4.refs_0_, f32[1,1024]{1,0:T(1,128)} %bitcast.355, ...), custom_call_target="tpu_custom_call" | custom-call | tf_op jit(solution)/shard_map/pallas_call | solution.py:1186
  237.9 1.4 fusion.37
  241.4 58.7 %shard_map.250 = (f32[256,1024]{1,0:T(8,128)}, bf16[4,256,1024]{2,1,0:T(8,128)(2,1)}, bf16[1024,256]{1,0:T(8,128)(2,1)}, bf16[1024,256]{1,0:T(8,128)(2,1)}, bf16...) custom-call(bf16[256,1024]{1,0:T(8,128)(2,1)} %add_convert_fusion.3., ...), custom_call_target="tpu_custom_call" | custom-call | tf_op jit(solution)/shard_map/pallas_call | solution.py:1186
  300.2 1.4 fusion.36
  303.5 47.9 %shard_map.251 = (f32[256,1024]{1,0:T(8,128)}, bf16[4,256,1024]{2,1,0:T(8,128)(2,1)}, f32[1024,1024]{1,0:T(8,128)}) custom-call(bf16[256,1024]{1,0:T(8,128)(2,1)} %add_convert_fusion.2.refs_0_, f32[1,1024]{1,0:T(1,128)} %bitcast.356, bf16[2,512,1024]{2,1,0:T(8,128)(2,1)} %bitcast.253, bf16[2,512,1024]{2,1,0:T(8,128)(2,1)} %bitcast.255), custom_call_target="tpu_custom_call" | custom-call | tf_op jit(solution)/shard_map/pallas_call | solution.py:1186
  351.4 1.4 fusion.35
  355.9 60.2 %shard_map.252 = (f32[16,1024,512]{2,1,0:T(8,128)}, bf16[4,256,1024]{2,1,0:T(8,128)(2,1)}, f32[4,8,1024]{2,1,0:T(8,128)}) custom-call(bf16[256,1024]{1,0:T(8,128)(2,1)} %add_convert_fusion.1.x_ref, bf16[8192,1024]{1,0:T(8,128)(2,1)} %e_ref.3, s32[1024,1]{1,0:T(8,128)} %bitcast.257), custom_call_target="tpu_custom_call" | custom-call | tf_op jit(solution)/shard_map/pallas_call | solution.py:1610
  421.9 65.3 %shard_map.253 = (bf16[16,1024,512]{2,1,0:T(8,128)(2,1)}, f32[256,1024]{1,0:T(8,128)}) custom-call(f32[16,1024,512]{2,1,0:T(8,128)} %get-tuple-element.89.logits_ref, bf16[8192,1024]{1,0:T(8,128)(2,1)} %e_ref.3, s32[1024,1]{1,0:T(8,128)} %bitcast.258, f32[1024,1]{1,0:T(8,128)} %copy.66.norm_ref, f32[1024,1]{1,0:T(8,128)} %bitcast.266), custom_call_target="tpu_custom_call" | custom-call | tf_op jit(solution)/shard_map/pallas_call | solution.py:1744
  487.2 1.7 multiply_reduce_fusion
  490.3 54.4 %shard_map.254 = (f32[256,1024]{1,0:T(8,128)}, f32[2,1024,1024]{2,1,0:T(8,128)}, f32[1,1024]{1,0:T(1,128)}, f32[1024,1024]{1,0:T(8,128)}) custom-call(bf16[256,1024]{1,0:T(8,128)(2,1)} %get-tuple-element.204.refs_0_, bf16[1024,1024]{1,0:T(8,128)(2,1)} %bitcast.277, f32[1024,1024]{1,0:T(8,128)} %get-tuple-element.95.refs_2_, bf16[2,512,1024]{2,1,0:T(8,128)(2,1)} %bitcast.254, ...), custom_call_target="tpu_custom_call" | custom-call | tf_op jit(solution)/shard_map/pallas_call | solution.py:1186
  544.7 2.7 constant_dynamic-slice_fusion.8
  548.1 1.1 fusion.1
  549.3 1.5 copy.70.refs_11_
  554.3 63.4 %shard_map.255 = (f32[256,1024]{1,0:T(8,128)}, f32[4,256,1024]{2,1,0:T(8,128)}, f32[2,256]{1,0:T(2,128)}, f32[2,256,1024]{2,1,0:T(8,128)}, bf16[3,2,128,1024]{3,2,1,0:T(8,128)(2,1)}) custom-call(bf16[256,1024]{1,0:T(8,128)(2,1)} %convert_element_type.168.refs_0_, s32[1]{0:T(128)} %dynamic_slice.118.refs_1_, f32[4]{0:T(128)} %multiply_exponential_fusion.refs_2_, ...), custom_call_target="tpu_custom_call" | custom-call | tf_op jit(solution)/shard_map/pallas_call | solution.py:1186
  617.7 1.9 constant_dynamic-slice_fusion.7
  624.4 48.6 %shard_map.256 = (f32[256,1024]{1,0:T(8,128)}, f32[2,1024,1024]{2,1,0:T(8,128)}, f32[1,1024]{1,0:T(1,128)}, f32[1024,1024]{1,0:T(8,128)}, bf16[3,2,64,1024]{3,2,1,0:T(8,128)(2,1)}) custom-call(bf16[256,1024]{1,0:T(8,128)(2,1)} %convert_element_type.170.refs_0_, bf16[1024,1024]{1,0:T(8,128)(2,1)} %bitcast.275, f32[1024,1024]{1,0:T(8,128)} %get-tuple-element.107.refs_2_, ...), custom_call_target="tpu_custom_call" | custom-call | tf_op jit(solution)/shard_map/pallas_call | solution.py:1186
  673.0 2.7 constant_dynamic-slice_fusion.6
  676.4 1.1 fusion
  677.6 1.5 copy.76.refs_11_
  681.5 68.6 %shard_map.257 = (f32[256,1024]{1,0:T(8,128)}, f32[4,256,1024]{2,1,0:T(8,128)}, f32[2,256]{1,0:T(2,128)}, f32[2,256,1024]{2,1,0:T(8,128)}, bf16[3,2,128,1024]{3,2,1,0:T(8,128)(2,1)}) custom-call(bf16[256,1024]{1,0:T(8,128)(2,1)} %convert_element_type.172.refs_0_, s32[1]{0:T(128)} %dynamic_slice.118.refs_1_, f32[4]{0:T(128)} %multiply_exponential_fusion.refs_2_, ...), custom_call_target="tpu_custom_call" | custom-call | tf_op jit(solution)/shard_map/pallas_call | solution.py:1186
  750.0 1.9 constant_dynamic-slice_fusion.4
  752.8 1.1 copy.85.refs_4_
  754.6 1.3 convert_reduce_fusion
  755.8 2.4 fusion.5.refs_3_
  758.6 2.1 fusion.6.refs_2_
  760.8 1.7 fusion.9.refs_1_
  763.9 1.4 multiply_reduce_fusion.1
  768.5 1.6 fusion.29
  771.7 219.5 %shard_map.258 = (bf16[16,512,1024]{2,1,0:T(8,128)(2,1)}, f32[8,32,1024]{2,1,0:T(8,128)}, bf16[2,4,2,64,1024]{4,3,2,1,0:T(8,128)(2,1)}, bf16[2,4,2,128,1024]{4,3...) custom-call(bf16[16,1024,512]{2,1,0:T(8,128)(2,1)} %get-tuple-element.91.g_ref, ...), custom_call_target="tpu_custom_call" | custom-call | tf_op jit(solution)/shard_map/pallas_call | solution.py:866
  991.2 2.6 broadcast_select_fusion
  994.5 2.6 bitcast_convert_fusion.2
  997.1 5.3 copy.89
  1002.4 2.6 bitcast_convert_fusion.1
  1006.3 20.4 %shard_map.259 = (f32[4,32,1024]{2,1,0:T(8,128)S(1)}, bf16[2,4,2,64,1024]{4,3,2,1,0:T(8,128)(2,1)S(1)}) custom-call(f32[32,1024]{1,0:T(8,128)S(1)} %reduce_sum.540.refs_0_, bf16[2,64,1024]{2,1,0:T(8,128)(2,1)S(1)} %fusion.8.refs_1_), custom_call_target="tpu_custom_call" | custom-call | tf_op jit(solution)/shard_map/pallas_call | solution.py:434
  1026.7 1.8 broadcast_select_fusion.1
  1029.4 1.9 fusion.4
  1031.3 1.1 bitcast_convert_fusion.3
  1032.4 18.8 %bitcast_convert_fusion = f32[8192,1024]{1,0:T(8,128)} fusion(bf16[16,512,1024]{2,1,0:T(8,128)(2,1)} %get-tuple-element.134), kind=kLoop, calls=%fused_computation.1 | loop fusion | flops 8388608 | bytes 50331648 | tf_op jit(solution)/shard_map/convert_element_type | solution.py:2138
  (242 shorter events, 50.6 us)
Async XLA Ops:
  0.6 2.3 copy-start
  3.3 2.6 copy-start.8
  5.6 1.1 copy-start.38
  5.6 1.1 copy-start.26
  5.6 1.1 copy-start.27
  5.6 1.1 copy-start.28
  5.6 1.1 copy-start.31
  5.7 1.1 copy-start.32
  5.7 1.2 copy-start.29
  5.7 1.2 copy-start.30
  5.7 1.0 copy-start.9
  90.2 4.5 copy-start.37
  177.9 1.3 copy-start.18
  301.6 49.8 %copy-start.2 = (f32[256,1024]{1,0:T(8,128)}, f32[256,1024]{1,0:T(8,128)S(1)}, u32[]{:S(2)}) copy-start(f32[256,1024]{1,0:T(8,128)S(1)} %get-tuple-element.187) | copy-start | bytes 3145732
  352.8 1.0 copy-start.4
  421.9 65.3 %copy-start.5 = (f32[256,1024]{1,0:T(8,128)S(1)}, f32[256,1024]{1,0:T(8,128)}, u32[]{:S(2)}) copy-start(f32[256,1024]{1,0:T(8,128)} %copy-done.4) | copy-start | bytes 3145732
  487.2 1.7 copy-start.14
  544.7 3.5 copy-start.16
  549.2 2.1 copy-start.6
  549.3 2.1 copy-start.3
  549.3 3.0 copy-start.13
  617.7 2.2 copy-start.20
  620.4 2.4 copy-start.10
  620.4 2.0 copy-start.11
  672.9 3.5 copy-start.15
  677.5 2.0 copy-start.7
  677.5 2.0 copy-start.12
  750.0 2.2 copy-start.19
  752.8 1.8 copy-start.22
  755.8 2.4 copy-start.21
  758.3 2.4 copy-start.24
  758.6 4.0 copy-start.17
  763.8 1.5 copy-start.36
  763.9 1.9 copy-start.34
  763.9 2.0 copy-start.35
  763.9 2.4 copy-start.33
  1002.4 2.6 copy-start.25
  1005.0 1.2 copy-start.23
  1032.4 22.5 %copy-start.1 = (bf16[1,1024,1024]{2,1,0:T(8,128)(2,1)S(1)}, bf16[1,1024,1024]{2,1,0:T(8,128)(2,1)}, u32[]{:S(2)}) copy-start(bf16[1,1024,1024]{2,1,0:T(8,128)(2,1)} %param.26) | copy-start | bytes 6291460

commit v8 on v7

--- a/solution.py
+++ b/solution.py
@@ -338,12 +338,14 @@
                 copy.wait_recv()
                 passed.append(send(pair, 1 - side, number, landed, landed, fw_send, fw_recv))
 
-            def finish():
+            def middle():
                 for number in (0, 2):
                     copies[number][0].wait_recv()
                     copies[4 + number // 2][0].start()
                     landed = copies[number][1]
                     passed.append(send(pair, 1 - side, number, landed, landed, fw_send, fw_recv))
+
+            def finish():
                 for number in (1, 3, 4, 5):
                     arrived(number)
                 for copy in passed:
@@ -351,6 +353,8 @@
                 for copy, _ in copies:
                     copy.wait_send()
                 own.wait()
+
+            return middle, finish
 
         elif self.kind == "spread":
             pair = self.groups[1]
@@ -396,7 +400,18 @@
                     total = total + slots[k].astype(F32)
                 out[...] = total
 
-        return finish
+        return None, finish
+
+
+def pass_on(ends):
+    for middle, _ in ends:
+        if middle is not None:
+            middle()
+
+
+def finish_jobs(ends):
+    for _, finish in ends:
+        finish()
 
 
 def job_groups(jobs):
@@ -418,8 +433,8 @@
     ends = [
         job.start(refs[n], refs[count + n], *parts[n]) for n, job in enumerate(jobs)
     ]
-    for end in ends:
-        end()
+    pass_on(ends)
+    finish_jobs(ends)
 
 
 class Exchanges:
@@ -608,8 +623,8 @@
         return carry
 
     lax.fori_loop(0, subs, drain, 0)
-    for end in ends:
-        end()
+    pass_on(ends)
+    finish_jobs(ends)
 
 
 def across(me, step):
@@ -746,11 +761,10 @@
             return carry
 
         lax.fori_loop(0, subs, share, 0)
-    for end in ends:
-        end()
+    pass_on(ends)
     line.step(line.count - 1)
     line.wait_sends()
-    ends = [job.start(xs[n], outs[n], *parts[n]) for n, job in enumerate(jobs) if job.late]
+    late = [job.start(xs[n], outs[n], *parts[n]) for n, job in enumerate(jobs) if job.late]
 
     for index, (number, away) in enumerate(order):
         half = partner if away == 0 else s
@@ -801,7 +815,7 @@
 
     lax.fori_loop(0, subs, finish, 0)
 
-    def pass_on(sub, carry):
+    def pass_chunk(sub, carry):
         for number in (0, 2):
             spread_copy(number, sub).wait_recv()
             spread_copy(4 + number // 2, sub).start()
@@ -810,7 +824,7 @@
             forward_copy(number, sub).start()
         return carry
 
-    lax.fori_loop(0, subs, pass_on, 0)
+    lax.fori_loop(0, subs, pass_chunk, 0)
 
     def last(sub, carry):
         for number in (4, 5):
@@ -833,8 +847,9 @@
         return carry
 
     lax.fori_loop(0, subs, drain, 0)
-    for end in ends:
-        end()
+    finish_jobs(ends)
+    pass_on(late)
+    finish_jobs(late)
 
 
 def table_sum(by_section, by_dp, by_tensor, jobs, grads, ids, final, grad_rows, ident):
@@ -1101,8 +1116,8 @@
         lax.fori_loop(0, self.count - 1, one, 0)
 
     def finish(self, total_ref):
-        for end in self.ends:
-            end()
+        pass_on(self.ends)
+        finish_jobs(self.ends)
         for step in range(self.count - 1):
             self.rs(step).wait()
         total = self.own[...]
@@ -1171,8 +1186,8 @@
         if ahead:
 
             def ready():
-                for end in first:
-                    end()
+                pass_on(first)
+                finish_jobs(first)
                 rows.ends = start(range(ahead, riders))
 
             rows.ready = ready
@@ -1845,16 +1860,10 @@
     qv_piece = lax.dynamic_slice_in_dim(qv_bias[0], cut_index * cols, cols, 1)
     up_piece = lax.dynamic_slice_in_dim(up_bias[0], cut_index * hidden, hidden, 0)
     small = jnp.concatenate(
-        [
-            outer_gain,
-            outer_bias,
-            norm_gain[0],
-            norm_bias[0],
-            row_bias[0],
-            pad_rows(qv_piece, 2),
-            pad_rows(up_piece[None], 6),
-        ]
+        [outer_gain, outer_bias, norm_gain[0], norm_bias[0], row_bias[0]]
     )
+    bias_piece = jnp.concatenate([qv_piece[0], qv_piece[1], up_piece])
+    bias_piece = jnp.pad(bias_piece, (0, -bias_piece.shape[0] % 1024)).reshape(-1, 128)
 
     def gather(group, x):
         return Job("gather", [group], x)
@@ -1867,12 +1876,13 @@
         return own + jnp.sum(dealt.astype(F32), axis=0)
 
     if planes:
-        other, both, small_all = exchange(
+        other, both, small_all, bias_all = exchange(
             deal(by_section, sides),
             gather(by_dp, jnp.stack([token_ids, target_ids])),
-            gather(Group(("section", "tensor"), (sections, shards)), small),
-        )
-        small_all = small_all.reshape((sections, shards) + small.shape)
+            gather(by_section, small),
+            gather(Group(("section", "tensor"), (sections, shards)), bias_piece),
+        )
+        bias_all = bias_all.reshape(sections, shards, -1)
         own_side = lax.dynamic_index_in_dim(sides, s, 0, keepdims=False)
         side = [jnp.where(s == l, own_side, other[0]) for l in range(layers)]
         both = jnp.swapaxes(both, 0, 1).reshape(2, shards, sections, groups, part)
@@ -1886,22 +1896,24 @@
         places = jnp.broadcast_to(j * part + jnp.arange(part), (shards, part))
         valid = (places < group_lengths[:, None]).reshape(-1)
     else:
-        sides_all, small_all = exchange(gather(by_section, sides), gather(by_section, small))
-        small_all = small_all[:, None]
+        sides_all, small_all, bias_all = exchange(
+            gather(by_section, sides), gather(by_section, small), gather(by_section, bias_piece)
+        )
+        bias_all = bias_all.reshape(sections, 1, -1)
         ids, targets = token_ids[s], target_ids[s]
         valid = jnp.arange(seq) < lengths[my_row]
 
-    outer_gains = [small_all[l, 0, 0] for l in range(layers)]
-    outer_offsets = [small_all[l, 0, 1] for l in range(layers)]
+    outer_gains = [small_all[l, 0] for l in range(layers)]
+    outer_offsets = [small_all[l, 1] for l in range(layers)]
     params = []
     for l in range(layers):
-        biases = [small_all[l, :, 8 + n, :cols].reshape(-1) for n in range(2)]
-        units = small_all[l, :, 10, :hidden].reshape(fan, halves, strip)
+        biases = [bias_all[l, :, n * cols : (n + 1) * cols].reshape(-1) for n in range(2)]
+        units = bias_all[l, :, 2 * cols : 2 * cols + hidden].reshape(fan, halves, strip)
         params.append(
             dict(
-                gains=small_all[l, 0, 2:4],
-                offsets=small_all[l, 0, 4:6],
-                row_bias=small_all[l, 0, 6:8],
+                gains=small_all[l, 2:4],
+                offsets=small_all[l, 4:6],
+                row_bias=small_all[l, 6:8],
                 bias=jnp.stack(biases),
                 up_bias=jnp.swapaxes(units, 0, 1).reshape(1, -1),
             )

time: 1070 us -> 1050 us (0.981)
  Pallas kernels: 908 us -> 888 us
    pallas_call x3, Pallas kernels: 84.2 us -> 70.5 us  [__call__(): pl.pallas_call(functools.partial(exchange_body, jobs), out_shape=tuple((j...]
where the time goes in v8:
time: 1050 us; the launch traced here: 1040 us
  Pallas kernels  888 us (85%)
  other arithmetic  80.9 us (8%)
  local copies, waits for them, and re-layouts  65.7 us (6%)
    pallas_call x8, Pallas kernels, team_call(): pl.pallas_call(kernel, out_shape=tuple(outs) + tuple((job.out for job in...  479 us
    pallas_call x1, Pallas kernels, table_sum(): pl.pallas_call(functools.partial(table_square_body if by_dp.square else t...  213 us
    pallas_call x3, Pallas kernels, __call__(): pl.pallas_call(functools.partial(exchange_body, jobs), out_shape=tuple((j...  70.5 us
    pallas_call x1, Pallas kernels, line_head_grads(): pl.pallas_call(functools.partial(line_head_grads_body, group), out_shape=...  65.3 us
    pallas_call x1, Pallas kernels, line_head_logits(): pl.pallas_call(functools.partial(line_head_logits_body, group), out_shape...  60.2 us

profile of v8, /device:TPU:1, one launch (start us, length us, event | category | flops | bytes accessed | tf_op | source)
XLA Modules:
  0.0 1039.3 jit_solution(6666391778566186857)
XLA Ops:
  0.7 1.6 fusion.41
  6.6 1.1 dynamic-slice_bitcast_fusion
  9.9 8.8 shard_map.246
  19.8 13.9 %gather_fusion = bf16[1024,1024]{1,0:T(8,128)(2,1)} fusion(bf16[8192,1024]{1,0:T(8,128)(2,1)} %e_ref.3, s32[1024]{0:T(1024)S(1)} %broadcast_clamp_fusion), kind=kCustom, calls=%fused_computation | custom fusion | bytes 4198400 | tf_op jit(solution)/shard_map/jit(_take)/gather | solution.py:1965
  33.7 1.8 select_select_fusion.refs_0_
  35.5 43.1 %shard_map.247 = f32[256,1024]{1,0:T(8,128)S(1)} custom-call(bf16[4,256,1024]{2,1,0:T(8,128)(2,1)S(1)} %select_select_fusion.refs_0_), custom_call_target="tpu_custom_call" | custom-call | tf_op jit(solution)/shard_map/pallas_call | solution.py:449
  79.8 1.5 add_convert_fusion.5.refs_0_
  81.3 2.9 broadcast_select_fusion.2
  86.9 80.8 %shard_map.248 = (f32[256,1024]{1,0:T(8,128)}, bf16[4,256,1024]{2,1,0:T(8,128)(2,1)}, bf16[1024,256]{1,0:T(8,128)(2,1)}, bf16[1024,256]{1,0:T(8,128)(2,1)}, bf16...) custom-call(bf16[256,1024]{1,0:T(8,128)(2,1)} %add_convert_fusion.5., ...), custom_call_target="tpu_custom_call" | custom-call | tf_op jit(solution)/shard_map/pallas_call | solution.py:1201
  167.7 1.7 fusion.38
  172.8 57.0 %shard_map.249 = (f32[256,1024]{1,0:T(8,128)}, bf16[4,256,1024]{2,1,0:T(8,128)(2,1)}, f32[1024,1024]{1,0:T(8,128)}, bf16[2,4,64,1024]{3,2,1,0:T(8,128)(2,1)}, bf...) custom-call(bf16[256,1024]{1,0:T(8,128)(2,1)} %add_convert_fusion.4.refs_0_, f32[1,1024]{1,0:T(1,128)} %bitcast.345, ...), custom_call_target="tpu_custom_call" | custom-call | tf_op jit(solution)/shard_map/pallas_call | solution.py:1201
  229.8 1.4 fusion.37
  233.3 58.7 %shard_map.250 = (f32[256,1024]{1,0:T(8,128)}, bf16[4,256,1024]{2,1,0:T(8,128)(2,1)}, bf16[1024,256]{1,0:T(8,128)(2,1)}, bf16[1024,256]{1,0:T(8,128)(2,1)}, bf16...) custom-call(bf16[256,1024]{1,0:T(8,128)(2,1)} %add_convert_fusion.3., ...), custom_call_target="tpu_custom_call" | custom-call | tf_op jit(solution)/shard_map/pallas_call | solution.py:1201
  292.1 1.4 fusion.36
  294.8 47.9 %shard_map.251 = (f32[256,1024]{1,0:T(8,128)}, bf16[4,256,1024]{2,1,0:T(8,128)(2,1)}, f32[1024,1024]{1,0:T(8,128)}) custom-call(bf16[256,1024]{1,0:T(8,128)(2,1)} %add_convert_fusion.2.refs_0_, f32[1,1024]{1,0:T(1,128)} %bitcast.344, bf16[2,512,1024]{2,1,0:T(8,128)(2,1)} %bitcast.242, bf16[2,512,1024]{2,1,0:T(8,128)(2,1)} %bitcast.244), custom_call_target="tpu_custom_call" | custom-call | tf_op jit(solution)/shard_map/pallas_call | solution.py:1201
  342.7 1.4 fusion.35
  347.2 60.2 %shard_map.252 = (f32[16,1024,512]{2,1,0:T(8,128)}, bf16[4,256,1024]{2,1,0:T(8,128)(2,1)}, f32[4,8,1024]{2,1,0:T(8,128)}) custom-call(bf16[256,1024]{1,0:T(8,128)(2,1)} %add_convert_fusion.1.x_ref, bf16[8192,1024]{1,0:T(8,128)(2,1)} %e_ref.3, s32[1024,1]{1,0:T(8,128)} %bitcast.246), custom_call_target="tpu_custom_call" | custom-call | tf_op jit(solution)/shard_map/pallas_call | solution.py:1625
  413.2 65.3 %shard_map.253 = (bf16[16,1024,512]{2,1,0:T(8,128)(2,1)}, f32[256,1024]{1,0:T(8,128)}) custom-call(f32[16,1024,512]{2,1,0:T(8,128)} %get-tuple-element.91.logits_ref, bf16[8192,1024]{1,0:T(8,128)(2,1)} %e_ref.3, s32[1024,1]{1,0:T(8,128)} %bitcast.247, f32[1024,1]{1,0:T(8,128)} %copy.58.norm_ref, f32[1024,1]{1,0:T(8,128)} %bitcast.255), custom_call_target="tpu_custom_call" | custom-call | tf_op jit(solution)/shard_map/pallas_call | solution.py:1759
  478.5 1.7 multiply_reduce_fusion
  481.6 54.4 %shard_map.254 = (f32[256,1024]{1,0:T(8,128)}, f32[2,1024,1024]{2,1,0:T(8,128)}, f32[1,1024]{1,0:T(1,128)}, f32[1024,1024]{1,0:T(8,128)}) custom-call(bf16[256,1024]{1,0:T(8,128)(2,1)} %get-tuple-element.206.refs_0_, bf16[1024,1024]{1,0:T(8,128)(2,1)} %bitcast.266, f32[1024,1024]{1,0:T(8,128)} %get-tuple-element.97.refs_2_, bf16[2,512,1024]{2,1,0:T(8,128)(2,1)} %bitcast.243, ...), custom_call_target="tpu_custom_call" | custom-call | tf_op jit(solution)/shard_map/pallas_call | solution.py:1201
  536.0 2.7 constant_dynamic-slice_fusion.8
  539.5 1.1 fusion.1
  540.6 1.5 copy.62.refs_11_
  545.6 63.4 %shard_map.255 = (f32[256,1024]{1,0:T(8,128)}, f32[4,256,1024]{2,1,0:T(8,128)}, f32[2,256]{1,0:T(2,128)}, f32[2,256,1024]{2,1,0:T(8,128)}, bf16[3,2,128,1024]{3,2,1,0:T(8,128)(2,1)}) custom-call(bf16[256,1024]{1,0:T(8,128)(2,1)} %convert_element_type.166.refs_0_, s32[1]{0:T(128)} %dynamic_slice.118.refs_1_, f32[4]{0:T(128)} %multiply_exponential_fusion.refs_2_, ...), custom_call_target="tpu_custom_call" | custom-call | tf_op jit(solution)/shard_map/pallas_call | solution.py:1201
  609.1 1.9 constant_dynamic-slice_fusion.7
  615.7 48.6 %shard_map.256 = (f32[256,1024]{1,0:T(8,128)}, f32[2,1024,1024]{2,1,0:T(8,128)}, f32[1,1024]{1,0:T(1,128)}, f32[1024,1024]{1,0:T(8,128)}, bf16[3,2,64,1024]{3,2,1,0:T(8,128)(2,1)}) custom-call(bf16[256,1024]{1,0:T(8,128)(2,1)} %convert_element_type.168.refs_0_, bf16[1024,1024]{1,0:T(8,128)(2,1)} %bitcast.264, f32[1024,1024]{1,0:T(8,128)} %get-tuple-element.109.refs_2_, ...), custom_call_target="tpu_custom_call" | custom-call | tf_op jit(solution)/shard_map/pallas_call | solution.py:1201
  664.3 2.7 constant_dynamic-slice_fusion.6
  667.8 1.1 fusion
  668.9 1.5 copy.68.refs_11_
  672.8 68.6 %shard_map.257 = (f32[256,1024]{1,0:T(8,128)}, f32[4,256,1024]{2,1,0:T(8,128)}, f32[2,256]{1,0:T(2,128)}, f32[2,256,1024]{2,1,0:T(8,128)}, bf16[3,2,128,1024]{3,2,1,0:T(8,128)(2,1)}) custom-call(bf16[256,1024]{1,0:T(8,128)(2,1)} %convert_element_type.170.refs_0_, s32[1]{0:T(128)} %dynamic_slice.118.refs_1_, f32[4]{0:T(128)} %multiply_exponential_fusion.refs_2_, ...), custom_call_target="tpu_custom_call" | custom-call | tf_op jit(solution)/shard_map/pallas_call | solution.py:1201
  741.4 1.9 constant_dynamic-slice_fusion.4
  744.1 1.1 copy.77.refs_4_
  745.9 1.3 convert_reduce_fusion
  747.2 2.4 fusion.5.refs_3_
  749.9 2.1 fusion.6.refs_2_
  752.2 1.7 fusion.9.refs_1_
  755.2 1.4 multiply_reduce_fusion.1
  759.9 1.6 fusion.29
  763.0 212.8 %shard_map.258 = (bf16[16,512,1024]{2,1,0:T(8,128)(2,1)}, f32[8,32,1024]{2,1,0:T(8,128)}, bf16[2,4,2,64,1024]{4,3,2,1,0:T(8,128)(2,1)}, bf16[2,4,2,128,1024]{4,3...) custom-call(bf16[16,1024,512]{2,1,0:T(8,128)(2,1)} %get-tuple-element.93.g_ref, ...), custom_call_target="tpu_custom_call" | custom-call | tf_op jit(solution)/shard_map/pallas_call | solution.py:881
  975.8 2.6 broadcast_select_fusion
  979.1 2.6 bitcast_convert_fusion.2
  981.7 5.3 copy.81
  987.0 2.6 bitcast_convert_fusion.1
  990.9 18.6 %shard_map.259 = (f32[4,32,1024]{2,1,0:T(8,128)S(1)}, bf16[2,4,2,64,1024]{4,3,2,1,0:T(8,128)(2,1)S(1)}) custom-call(f32[32,1024]{1,0:T(8,128)S(1)} %reduce_sum.540.refs_0_, bf16[2,64,1024]{2,1,0:T(8,128)(2,1)S(1)} %fusion.8.refs_1_), custom_call_target="tpu_custom_call" | custom-call | tf_op jit(solution)/shard_map/pallas_call | solution.py:449
  1009.5 1.8 broadcast_select_fusion.1
  1012.2 1.9 fusion.4
  1014.1 1.1 bitcast_convert_fusion.3
  1015.2 18.8 %bitcast_convert_fusion = f32[8192,1024]{1,0:T(8,128)} fusion(bf16[16,512,1024]{2,1,0:T(8,128)(2,1)} %get-tuple-element.136), kind=kLoop, calls=%fused_computation.1 | loop fusion | flops 8388608 | bytes 50331648 | tf_op jit(solution)/shard_map/convert_element_type | solution.py:2150
  (239 shorter events, 53.3 us)
Async XLA Ops:
  0.6 3.6 copy-start
  8.6 1.0 copy-start.37
  8.6 1.2 copy-start.27
  8.6 1.2 copy-start.28
  8.6 1.2 copy-start.29
  8.6 1.2 copy-start.30
  8.7 1.2 copy-start.31
  8.7 1.2 copy-start.25
  8.7 1.2 copy-start.26
  8.8 1.1 copy-start.8
  81.3 4.4 copy-start.36
  169.3 1.3 copy-start.17
  293.5 49.2 %copy-start.2 = (f32[256,1024]{1,0:T(8,128)}, f32[256,1024]{1,0:T(8,128)S(1)}, u32[]{:S(2)}) copy-start(f32[256,1024]{1,0:T(8,128)S(1)} %get-tuple-element.189) | copy-start | bytes 3145732
  344.1 1.0 copy-start.4
  413.2 65.3 %copy-start.5 = (f32[256,1024]{1,0:T(8,128)S(1)}, f32[256,1024]{1,0:T(8,128)}, u32[]{:S(2)}) copy-start(f32[256,1024]{1,0:T(8,128)} %copy-done.4) | copy-start | bytes 3145732
  478.5 1.7 copy-start.13
  536.0 3.5 copy-start.15
  540.6 2.1 copy-start.6
  540.6 2.1 copy-start.3
  540.6 3.0 copy-start.12
  609.0 2.2 copy-start.19
  611.8 2.4 copy-start.9
  611.8 2.0 copy-start.10
  664.3 3.5 copy-start.14
  668.9 2.0 copy-start.7
  668.9 2.0 copy-start.11
  741.4 2.2 copy-start.18
  744.1 1.8 copy-start.21
  747.2 2.4 copy-start.20
  749.6 2.4 copy-start.23
  749.9 4.0 copy-start.16
  755.2 1.5 copy-start.35
  755.2 1.9 copy-start.33
  755.2 2.0 copy-start.34
  755.2 2.4 copy-start.32
  987.0 2.6 copy-start.24
  989.6 1.2 copy-start.22
  1015.2 22.5 %copy-start.1 = (bf16[1,1024,1024]{2,1,0:T(8,128)(2,1)S(1)}, bf16[1,1024,1024]{2,1,0:T(8,128)(2,1)}, u32[]{:S(2)}) copy-start(bf16[1,1024,1024]{2,1,0:T(8,128)(2,1)} %param.26) | copy-start | bytes 6291460

commit v9 on v8

--- a/solution.py
+++ b/solution.py
@@ -1969,9 +1969,8 @@
     h = layer_norm(x, outer_gains[0], outer_offsets[0])
 
     kept = []
-    strips = []
     for l, p in enumerate(params):
-        jobs = (attn_jobs(l) + feed_jobs(l, 0) if l == 0 else []) + feed_jobs(l, 1)
+        jobs = (attn_jobs(l) if l == 0 else []) + feed_jobs(l, 0) + feed_jobs(l, 1)
         normed = layer_norm(h, p["gains"][0], p["offsets"][0]).astype(BF16)
         (total, normed, q, k, v, mixed, lse), got = attend(
             team, ident("attend", jobs), jobs, normed, length, slopes, p["bias"],
@@ -1980,15 +1979,14 @@
         if "qk" not in p:
             take_attn(l, got[:2])
             got = got[2:]
-        take_feed(l, strips + got)
+        take_feed(l, got)
         middle = h + total + p["row_bias"][0]
-        jobs = attn_jobs(l + 1) + feed_jobs(l + 1, 0)
+        jobs = attn_jobs(l + 1)
         second = layer_norm(middle, p["gains"][1], p["offsets"][1]).astype(BF16)
         (total, second, before), got = feed(
             team, ident("feed", jobs), jobs, second, p["strips"], p["up_bias"]
         )
-        take_attn(l + 1, got[:2])
-        strips = got[2:]
+        take_attn(l + 1, got)
         kept.append((h, normed.reshape(seq, width), q, k, v, mixed, lse, middle, second, before))
         h = middle + total + p["row_bias"][1]
 
@@ -2160,7 +2158,7 @@
     loss = packed[base + 4, 0] / token_count
 
     def columns(array):
-        return array.astype(F32).reshape(-1, width).T
+        return array.reshape(-1, width).T.astype(F32)
 
     grad_qkv = jnp.stack(
         [columns(attn_sum[0, :, 0]), columns(attn_sum[1, :, 0]), columns(attn_sum[0, :, 1])]

time: 1050 us -> 1040 us (level)
    pallas_call x8, Pallas kernels: 479 us -> 469 us  [team_call(): pl.pallas_call(kernel, out_shape=tuple(outs) + tuple((job.out for job in...]
where the time goes in v9:
time: 1040 us
  Pallas kernels  882 us (85%)
  other arithmetic  80.9 us (8%)
  local copies, waits for them, and re-layouts  67.6 us (6%)
    pallas_call x8, Pallas kernels, team_call(): pl.pallas_call(kernel, out_shape=tuple(outs) + tuple((job.out for job in...  469 us
    pallas_call x1, Pallas kernels, table_sum(): pl.pallas_call(functools.partial(table_square_body if by_dp.square else t...  212 us
    pallas_call x3, Pallas kernels, __call__(): pl.pallas_call(functools.partial(exchange_body, jobs), out_shape=tuple((j...  70.5 us
    pallas_call x1, Pallas kernels, line_head_grads(): pl.pallas_call(functools.partial(line_head_grads_body, group), out_shape=...  66.3 us
    pallas_call x1, Pallas kernels, line_head_logits(): pl.pallas_call(functools.partial(line_head_logits_body, group), out_shape...  64.5 us

profile of v9, /device:TPU:1, one launch (start us, length us, event | category | flops | bytes accessed | tf_op | source)
XLA Modules:
  0.0 1035.3 jit_solution(17641561017938182806)
XLA Ops:
  0.7 1.6 fusion.41
  9.9 8.8 shard_map.246
  19.8 13.9 %gather_fusion = bf16[1024,1024]{1,0:T(8,128)(2,1)} fusion(bf16[8192,1024]{1,0:T(8,128)(2,1)} %e_ref.3, s32[1024]{0:T(1024)S(1)} %broadcast_clamp_fusion), kind=kCustom, calls=%fused_computation | custom fusion | bytes 4198400 | tf_op jit(solution)/shard_map/jit(_take)/gather | solution.py:1965
  33.7 1.8 select_select_fusion.refs_0_
  35.5 43.1 %shard_map.247 = f32[256,1024]{1,0:T(8,128)S(1)} custom-call(bf16[4,256,1024]{2,1,0:T(8,128)(2,1)S(1)} %select_select_fusion.refs_0_), custom_call_target="tpu_custom_call" | custom-call | tf_op jit(solution)/shard_map/pallas_call | solution.py:449
  79.8 1.5 add_convert_fusion.5.refs_0_
  81.3 2.9 broadcast_select_fusion.2
  86.9 80.8 %shard_map.248 = (f32[256,1024]{1,0:T(8,128)}, bf16[4,256,1024]{2,1,0:T(8,128)(2,1)}, bf16[1024,256]{1,0:T(8,128)(2,1)}, bf16[1024,256]{1,0:T(8,128)(2,1)}, bf16...) custom-call(bf16[256,1024]{1,0:T(8,128)(2,1)} %add_convert_fusion.5., ...), custom_call_target="tpu_custom_call" | custom-call | tf_op jit(solution)/shard_map/pallas_call | solution.py:1201
  167.7 1.7 fusion.38
  170.6 1.7 slice_bitcast_fusion.4
  172.9 55.2 %shard_map.249 = (f32[256,1024]{1,0:T(8,128)}, bf16[4,256,1024]{2,1,0:T(8,128)(2,1)}, f32[1024,1024]{1,0:T(8,128)}, bf16[2,4,64,1024]{3,2,1,0:T(8,128)(2,1)}, bf16[2,4,64,1024]{3,2,1,0:T(8,128)(2,1)}) custom-call(bf16[256,1024]{1,0:T(8,128)(2,1)} %add_convert_fusion.4.refs_0_, f32[1,1024]{1,0:T(1,128)} %bitcast.345, bf16[2,512,1024]{2,1,0:T(8,128)(2,1)} %bitcast.238, ...), custom_call_target="tpu_custom_call" | custom-call | tf_op jit(solution)/shard_map/pallas_call | solution.py:1201
  228.1 1.4 fusion.37
  231.6 1.9 slice_bitcast_fusion
  233.5 52.0 %shard_map.250 = (f32[256,1024]{1,0:T(8,128)}, bf16[4,256,1024]{2,1,0:T(8,128)(2,1)}, bf16[1024,256]{1,0:T(8,128)(2,1)}, bf16[1024,256]{1,0:T(8,128)(2,1)}, bf16...) custom-call(bf16[256,1024]{1,0:T(8,128)(2,1)} %add_convert_fusion.3., ...), custom_call_target="tpu_custom_call" | custom-call | tf_op jit(solution)/shard_map/pallas_call | solution.py:1201
  285.5 1.4 fusion.36
  288.2 47.6 %shard_map.251 = (f32[256,1024]{1,0:T(8,128)}, bf16[4,256,1024]{2,1,0:T(8,128)(2,1)}, f32[1024,1024]{1,0:T(8,128)}) custom-call(bf16[256,1024]{1,0:T(8,128)(2,1)} %add_convert_fusion.2.refs_0_, f32[1,1024]{1,0:T(1,128)} %bitcast.344, bf16[2,512,1024]{2,1,0:T(8,128)(2,1)} %bitcast.242, bf16[2,512,1024]{2,1,0:T(8,128)(2,1)} %bitcast.244), custom_call_target="tpu_custom_call" | custom-call | tf_op jit(solution)/shard_map/pallas_call | solution.py:1201
  335.9 1.4 fusion.35
  340.4 64.5 %shard_map.252 = (f32[16,1024,512]{2,1,0:T(8,128)}, bf16[4,256,1024]{2,1,0:T(8,128)(2,1)}, f32[4,8,1024]{2,1,0:T(8,128)}) custom-call(bf16[256,1024]{1,0:T(8,128)(2,1)} %add_convert_fusion.1.x_ref, bf16[8192,1024]{1,0:T(8,128)(2,1)} %e_ref.3, s32[1024,1]{1,0:T(8,128)} %bitcast.246), custom_call_target="tpu_custom_call" | custom-call | tf_op jit(solution)/shard_map/pallas_call | solution.py:1625
  410.7 66.3 %shard_map.253 = (bf16[16,1024,512]{2,1,0:T(8,128)(2,1)}, f32[256,1024]{1,0:T(8,128)}) custom-call(f32[16,1024,512]{2,1,0:T(8,128)} %get-tuple-element.91.logits_ref, bf16[8192,1024]{1,0:T(8,128)(2,1)} %e_ref.3, s32[1024,1]{1,0:T(8,128)} %bitcast.247, f32[1024,1]{1,0:T(8,128)} %copy.58.norm_ref, f32[1024,1]{1,0:T(8,128)} %bitcast.255), custom_call_target="tpu_custom_call" | custom-call | tf_op jit(solution)/shard_map/pallas_call | solution.py:1759
  477.0 1.7 multiply_reduce_fusion
  480.1 53.0 %shard_map.254 = (f32[256,1024]{1,0:T(8,128)}, f32[2,1024,1024]{2,1,0:T(8,128)}, f32[1,1024]{1,0:T(1,128)}, f32[1024,1024]{1,0:T(8,128)}) custom-call(bf16[256,1024]{1,0:T(8,128)(2,1)} %get-tuple-element.206.refs_0_, bf16[1024,1024]{1,0:T(8,128)(2,1)} %bitcast.266, f32[1024,1024]{1,0:T(8,128)} %get-tuple-element.97.refs_2_, bf16[2,512,1024]{2,1,0:T(8,128)(2,1)} %bitcast.243, ...), custom_call_target="tpu_custom_call" | custom-call | tf_op jit(solution)/shard_map/pallas_call | solution.py:1201
  533.1 2.7 constant_dynamic-slice_fusion.8
  536.6 1.1 fusion.1
  537.7 1.5 copy.62.refs_11_
  542.7 64.5 %shard_map.255 = (f32[256,1024]{1,0:T(8,128)}, f32[4,256,1024]{2,1,0:T(8,128)}, f32[2,256]{1,0:T(2,128)}, f32[2,256,1024]{2,1,0:T(8,128)}, bf16[3,2,128,1024]{3,2,1,0:T(8,128)(2,1)}) custom-call(bf16[256,1024]{1,0:T(8,128)(2,1)} %convert_element_type.174.refs_0_, s32[1]{0:T(128)} %dynamic_slice.118.refs_1_, f32[4]{0:T(128)} %multiply_exponential_fusion.refs_2_, ...), custom_call_target="tpu_custom_call" | custom-call | tf_op jit(solution)/shard_map/pallas_call | solution.py:1201
  607.2 1.9 constant_dynamic-slice_fusion.7
  613.9 48.7 %shard_map.256 = (f32[256,1024]{1,0:T(8,128)}, f32[2,1024,1024]{2,1,0:T(8,128)}, f32[1,1024]{1,0:T(1,128)}, f32[1024,1024]{1,0:T(8,128)}, bf16[3,2,64,1024]{3,2,1,0:T(8,128)(2,1)}) custom-call(bf16[256,1024]{1,0:T(8,128)(2,1)} %convert_element_type.176.refs_0_, bf16[1024,1024]{1,0:T(8,128)(2,1)} %bitcast.264, f32[1024,1024]{1,0:T(8,128)} %get-tuple-element.109.refs_2_, ...), custom_call_target="tpu_custom_call" | custom-call | tf_op jit(solution)/shard_map/pallas_call | solution.py:1201
  662.6 2.7 constant_dynamic-slice_fusion.6
  666.0 1.1 fusion
  667.2 1.5 copy.68.refs_11_
  671.1 66.8 %shard_map.257 = (f32[256,1024]{1,0:T(8,128)}, f32[4,256,1024]{2,1,0:T(8,128)}, f32[2,256]{1,0:T(2,128)}, f32[2,256,1024]{2,1,0:T(8,128)}, bf16[3,2,128,1024]{3,2,1,0:T(8,128)(2,1)}) custom-call(bf16[256,1024]{1,0:T(8,128)(2,1)} %convert_element_type.178.refs_0_, s32[1]{0:T(128)} %dynamic_slice.118.refs_1_, f32[4]{0:T(128)} %multiply_exponential_fusion.refs_2_, ...), custom_call_target="tpu_custom_call" | custom-call | tf_op jit(solution)/shard_map/pallas_call | solution.py:1201
  737.9 1.9 constant_dynamic-slice_fusion.4
  742.4 1.3 convert_reduce_fusion
  743.7 2.4 fusion.5.refs_3_
  746.4 2.1 fusion.6.refs_2_
  748.7 1.7 fusion.9.refs_1_
  751.8 1.4 multiply_reduce_fusion.1
  756.4 1.6 fusion.29
  759.6 212.2 %shard_map.258 = (bf16[16,512,1024]{2,1,0:T(8,128)(2,1)}, f32[8,32,1024]{2,1,0:T(8,128)}, bf16[2,4,2,64,1024]{4,3,2,1,0:T(8,128)(2,1)}, bf16[2,4,2,128,1024]{4,3...) custom-call(bf16[16,1024,512]{2,1,0:T(8,128)(2,1)} %get-tuple-element.93.g_ref, ...), custom_call_target="tpu_custom_call" | custom-call | tf_op jit(solution)/shard_map/pallas_call | solution.py:881
  971.8 2.6 broadcast_select_fusion
  975.0 2.6 bitcast_convert_fusion.2
  977.6 5.3 copy.81
  983.0 2.6 bitcast_convert_fusion.1
  986.9 18.6 %shard_map.259 = (f32[4,32,1024]{2,1,0:T(8,128)S(1)}, bf16[2,4,2,64,1024]{4,3,2,1,0:T(8,128)(2,1)S(1)}) custom-call(f32[32,1024]{1,0:T(8,128)S(1)} %reduce_sum.540.refs_0_, bf16[2,64,1024]{2,1,0:T(8,128)(2,1)S(1)} %fusion.8.refs_1_), custom_call_target="tpu_custom_call" | custom-call | tf_op jit(solution)/shard_map/pallas_call | solution.py:449
  1005.5 1.8 broadcast_select_fusion.1
  1008.2 1.9 fusion.4
  1010.1 1.1 bitcast_convert_fusion.3
  1011.2 18.8 %bitcast_convert_fusion = f32[8192,1024]{1,0:T(8,128)} fusion(bf16[16,512,1024]{2,1,0:T(8,128)(2,1)} %get-tuple-element.136), kind=kLoop, calls=%fused_computation.1 | loop fusion | flops 8388608 | bytes 50331648 | tf_op jit(solution)/shard_map/convert_element_type | solution.py:2148
  (237 shorter events, 54.0 us)
Async XLA Ops:
  0.6 3.6 copy-start
  8.6 1.0 copy-start.36
  8.6 1.2 copy-start.26
  8.6 1.2 copy-start.27
  8.6 1.2 copy-start.28
  8.6 1.2 copy-start.29
  8.7 1.2 copy-start.30
  8.7 1.2 copy-start.24
  8.7 1.2 copy-start.25
  8.8 1.1 copy-start.8
  81.3 4.4 copy-start.35
  286.9 48.9 %copy-start.2 = (f32[256,1024]{1,0:T(8,128)}, f32[256,1024]{1,0:T(8,128)S(1)}, u32[]{:S(2)}) copy-start(f32[256,1024]{1,0:T(8,128)S(1)} %get-tuple-element.189) | copy-start | bytes 3145732
  337.3 1.0 copy-start.4
  410.7 66.3 %copy-start.5 = (f32[256,1024]{1,0:T(8,128)S(1)}, f32[256,1024]{1,0:T(8,128)}, u32[]{:S(2)}) copy-start(f32[256,1024]{1,0:T(8,128)} %copy-done.4) | copy-start | bytes 3145732
  477.0 1.7 copy-start.13
  533.1 3.5 copy-start.15
  537.7 2.1 copy-start.6
  537.7 2.1 copy-start.3
  537.7 3.0 copy-start.12
  607.2 2.2 copy-start.18
  609.9 2.4 copy-start.9
  609.9 2.0 copy-start.10
  662.6 3.5 copy-start.14
  667.1 2.0 copy-start.7
  667.2 2.0 copy-start.11
  737.9 2.2 copy-start.17
  740.6 1.8 copy-start.20
  743.7 2.4 copy-start.19
  746.1 2.4 copy-start.22
  746.4 4.0 copy-start.16
  751.7 1.5 copy-start.34
  751.7 1.9 copy-start.32
  751.7 2.0 copy-start.33
  751.7 2.4 copy-start.31
  983.0 2.6 copy-start.23
  985.6 1.2 copy-start.21
  1011.2 22.5 %copy-start.1 = (bf16[1,1024,1024]{2,1,0:T(8,128)(2,1)S(1)}, bf16[1,1024,1024]{2,1,0:T(8,128)(2,1)}, u32[]{:S(2)}) copy-start(bf16[1,1024,1024]{2,1,0:T(8,128)(2,1)} %param.26) | copy-start | bytes 6291460

commit v10 on v9

--- a/solution.py
+++ b/solution.py
@@ -1564,8 +1564,9 @@
                 logits = matmul_t(full[place], table[rows_of(tile), :])
                 staged[slot] = logits
                 leave(tile, place, slot).start()
-                column = tile * CHUNK + lax.broadcasted_iota(jnp.int32, (part, CHUNK), 1)
-                picked = jnp.where(column == ids, logits, 0.0)
+                column = lax.broadcasted_iota(jnp.int32, (part, CHUNK), 1)
+                wanted = ids - tile * CHUNK
+                picked = jnp.where(column == wanted, logits, 0.0)
                 pieces = [logits[:, at : at + LANES] for at in range(0, CHUNK, LANES)]
                 before = top[at, :]
                 high = functools.reduce(jnp.maximum, pieces, before)
@@ -1700,9 +1701,10 @@
                 enter(tile, place, slot).wait()
                 if fresh:
                     load(tile).wait()
-                column = tile * CHUNK + lax.broadcasted_iota(jnp.int32, (part, CHUNK), 1)
+                column = lax.broadcasted_iota(jnp.int32, (part, CHUNK), 1)
+                wanted = ids - tile * CHUNK
                 probs = jnp.exp(staged[slot] - norm)
-                grads = (jnp.where(column == ids, probs - 1.0, probs) * weight).astype(BF16)
+                grads = (jnp.where(column == wanted, probs - 1.0, probs) * weight).astype(BF16)
 
                 @pl.when(pair > 0)
                 def _(slot=slot, tile=tile):

time: 1040 us -> 1050 us (level)
  no operation moved by 1% of the time
where the time goes in v10:
time: 1050 us; the launch traced here: 1040 us
  Pallas kernels  883 us (84%)
  other arithmetic  80.9 us (8%)
  local copies, waits for them, and re-layouts  67.6 us (6%)
    pallas_call x8, Pallas kernels, team_call(): pl.pallas_call(kernel, out_shape=tuple(outs) + tuple((job.out for job in...  469 us
    pallas_call x1, Pallas kernels, table_sum(): pl.pallas_call(functools.partial(table_square_body if by_dp.square else t...  212 us
    pallas_call x3, Pallas kernels, __call__(): pl.pallas_call(functools.partial(exchange_body, jobs), out_shape=tuple((j...  70.5 us
    pallas_call x1, Pallas kernels, line_head_grads(): pl.pallas_call(functools.partial(line_head_grads_body, group), out_shape=...  66.6 us
    pallas_call x1, Pallas kernels, line_head_logits(): pl.pallas_call(functools.partial(line_head_logits_body, group), out_shape...  64.7 us

profile of v10, /device:TPU:1, one launch (start us, length us, event | category | flops | bytes accessed | tf_op | source)
XLA Modules:
  0.0 1035.8 jit_solution(12887399591832245314)
XLA Ops:
  0.7 1.6 fusion.41
  9.9 8.8 shard_map.246
  19.8 13.9 %gather_fusion = bf16[1024,1024]{1,0:T(8,128)(2,1)} fusion(bf16[8192,1024]{1,0:T(8,128)(2,1)} %e_ref.3, s32[1024]{0:T(1024)S(1)} %broadcast_clamp_fusion), kind=kCustom, calls=%fused_computation | custom fusion | bytes 4198400 | tf_op jit(solution)/shard_map/jit(_take)/gather | solution.py:1967
  33.7 1.8 select_select_fusion.refs_0_
  35.5 43.1 %shard_map.247 = f32[256,1024]{1,0:T(8,128)S(1)} custom-call(bf16[4,256,1024]{2,1,0:T(8,128)(2,1)S(1)} %select_select_fusion.refs_0_), custom_call_target="tpu_custom_call" | custom-call | tf_op jit(solution)/shard_map/pallas_call | solution.py:449
  79.8 1.5 add_convert_fusion.5.refs_0_
  81.3 2.9 broadcast_select_fusion.2
  86.9 80.8 %shard_map.248 = (f32[256,1024]{1,0:T(8,128)}, bf16[4,256,1024]{2,1,0:T(8,128)(2,1)}, bf16[1024,256]{1,0:T(8,128)(2,1)}, bf16[1024,256]{1,0:T(8,128)(2,1)}, bf16...) custom-call(bf16[256,1024]{1,0:T(8,128)(2,1)} %add_convert_fusion.5., ...), custom_call_target="tpu_custom_call" | custom-call | tf_op jit(solution)/shard_map/pallas_call | solution.py:1201
  167.7 1.7 fusion.38
  170.6 1.7 slice_bitcast_fusion.4
  172.9 55.2 %shard_map.249 = (f32[256,1024]{1,0:T(8,128)}, bf16[4,256,1024]{2,1,0:T(8,128)(2,1)}, f32[1024,1024]{1,0:T(8,128)}, bf16[2,4,64,1024]{3,2,1,0:T(8,128)(2,1)}, bf16[2,4,64,1024]{3,2,1,0:T(8,128)(2,1)}) custom-call(bf16[256,1024]{1,0:T(8,128)(2,1)} %add_convert_fusion.4.refs_0_, f32[1,1024]{1,0:T(1,128)} %bitcast.345, bf16[2,512,1024]{2,1,0:T(8,128)(2,1)} %bitcast.238, ...), custom_call_target="tpu_custom_call" | custom-call | tf_op jit(solution)/shard_map/pallas_call | solution.py:1201
  228.1 1.4 fusion.37
  231.6 1.9 slice_bitcast_fusion
  233.5 52.0 %shard_map.250 = (f32[256,1024]{1,0:T(8,128)}, bf16[4,256,1024]{2,1,0:T(8,128)(2,1)}, bf16[1024,256]{1,0:T(8,128)(2,1)}, bf16[1024,256]{1,0:T(8,128)(2,1)}, bf16...) custom-call(bf16[256,1024]{1,0:T(8,128)(2,1)} %add_convert_fusion.3., ...), custom_call_target="tpu_custom_call" | custom-call | tf_op jit(solution)/shard_map/pallas_call | solution.py:1201
  285.5 1.4 fusion.36
  288.2 47.6 %shard_map.251 = (f32[256,1024]{1,0:T(8,128)}, bf16[4,256,1024]{2,1,0:T(8,128)(2,1)}, f32[1024,1024]{1,0:T(8,128)}) custom-call(bf16[256,1024]{1,0:T(8,128)(2,1)} %add_convert_fusion.2.refs_0_, f32[1,1024]{1,0:T(1,128)} %bitcast.344, bf16[2,512,1024]{2,1,0:T(8,128)(2,1)} %bitcast.242, bf16[2,512,1024]{2,1,0:T(8,128)(2,1)} %bitcast.244), custom_call_target="tpu_custom_call" | custom-call | tf_op jit(solution)/shard_map/pallas_call | solution.py:1201
  335.9 1.4 fusion.35
  340.4 64.7 %shard_map.252 = (f32[16,1024,512]{2,1,0:T(8,128)}, bf16[4,256,1024]{2,1,0:T(8,128)(2,1)}, f32[4,8,1024]{2,1,0:T(8,128)}) custom-call(bf16[256,1024]{1,0:T(8,128)(2,1)} %add_convert_fusion.1.x_ref, bf16[8192,1024]{1,0:T(8,128)(2,1)} %e_ref.3, s32[1024,1]{1,0:T(8,128)} %bitcast.246), custom_call_target="tpu_custom_call" | custom-call | tf_op jit(solution)/shard_map/pallas_call | solution.py:1626
  410.9 66.6 %shard_map.253 = (bf16[16,1024,512]{2,1,0:T(8,128)(2,1)}, f32[256,1024]{1,0:T(8,128)}) custom-call(f32[16,1024,512]{2,1,0:T(8,128)} %get-tuple-element.91.logits_ref, bf16[8192,1024]{1,0:T(8,128)(2,1)} %e_ref.3, s32[1024,1]{1,0:T(8,128)} %bitcast.247, f32[1024,1]{1,0:T(8,128)} %copy.58.norm_ref, f32[1024,1]{1,0:T(8,128)} %bitcast.255), custom_call_target="tpu_custom_call" | custom-call | tf_op jit(solution)/shard_map/pallas_call | solution.py:1761
  477.6 1.7 multiply_reduce_fusion
  480.6 53.0 %shard_map.254 = (f32[256,1024]{1,0:T(8,128)}, f32[2,1024,1024]{2,1,0:T(8,128)}, f32[1,1024]{1,0:T(1,128)}, f32[1024,1024]{1,0:T(8,128)}) custom-call(bf16[256,1024]{1,0:T(8,128)(2,1)} %get-tuple-element.206.refs_0_, bf16[1024,1024]{1,0:T(8,128)(2,1)} %bitcast.266, f32[1024,1024]{1,0:T(8,128)} %get-tuple-element.97.refs_2_, bf16[2,512,1024]{2,1,0:T(8,128)(2,1)} %bitcast.243, ...), custom_call_target="tpu_custom_call" | custom-call | tf_op jit(solution)/shard_map/pallas_call | solution.py:1201
  533.6 2.7 constant_dynamic-slice_fusion.8
  537.1 1.1 fusion.1
  538.2 1.5 copy.62.refs_11_
  543.2 64.4 %shard_map.255 = (f32[256,1024]{1,0:T(8,128)}, f32[4,256,1024]{2,1,0:T(8,128)}, f32[2,256]{1,0:T(2,128)}, f32[2,256,1024]{2,1,0:T(8,128)}, bf16[3,2,128,1024]{3,2,1,0:T(8,128)(2,1)}) custom-call(bf16[256,1024]{1,0:T(8,128)(2,1)} %convert_element_type.174.refs_0_, s32[1]{0:T(128)} %dynamic_slice.118.refs_1_, f32[4]{0:T(128)} %multiply_exponential_fusion.refs_2_, ...), custom_call_target="tpu_custom_call" | custom-call | tf_op jit(solution)/shard_map/pallas_call | solution.py:1201
  607.6 1.9 constant_dynamic-slice_fusion.7
  614.3 48.7 %shard_map.256 = (f32[256,1024]{1,0:T(8,128)}, f32[2,1024,1024]{2,1,0:T(8,128)}, f32[1,1024]{1,0:T(1,128)}, f32[1024,1024]{1,0:T(8,128)}, bf16[3,2,64,1024]{3,2,1,0:T(8,128)(2,1)}) custom-call(bf16[256,1024]{1,0:T(8,128)(2,1)} %convert_element_type.176.refs_0_, bf16[1024,1024]{1,0:T(8,128)(2,1)} %bitcast.264, f32[1024,1024]{1,0:T(8,128)} %get-tuple-element.109.refs_2_, ...), custom_call_target="tpu_custom_call" | custom-call | tf_op jit(solution)/shard_map/pallas_call | solution.py:1201
  663.0 2.7 constant_dynamic-slice_fusion.6
  666.5 1.1 fusion
  667.6 1.5 copy.68.refs_11_
  671.5 67.1 %shard_map.257 = (f32[256,1024]{1,0:T(8,128)}, f32[4,256,1024]{2,1,0:T(8,128)}, f32[2,256]{1,0:T(2,128)}, f32[2,256,1024]{2,1,0:T(8,128)}, bf16[3,2,128,1024]{3,2,1,0:T(8,128)(2,1)}) custom-call(bf16[256,1024]{1,0:T(8,128)(2,1)} %convert_element_type.178.refs_0_, s32[1]{0:T(128)} %dynamic_slice.118.refs_1_, f32[4]{0:T(128)} %multiply_exponential_fusion.refs_2_, ...), custom_call_target="tpu_custom_call" | custom-call | tf_op jit(solution)/shard_map/pallas_call | solution.py:1201
  738.6 1.9 constant_dynamic-slice_fusion.4
  743.1 1.3 convert_reduce_fusion
  744.4 2.4 fusion.5.refs_3_
  747.2 2.1 fusion.6.refs_2_
  749.4 1.7 fusion.9.refs_1_
  752.5 1.4 multiply_reduce_fusion.1
  757.1 1.6 fusion.29
  760.3 212.0 %shard_map.258 = (bf16[16,512,1024]{2,1,0:T(8,128)(2,1)}, f32[8,32,1024]{2,1,0:T(8,128)}, bf16[2,4,2,64,1024]{4,3,2,1,0:T(8,128)(2,1)}, bf16[2,4,2,128,1024]{4,3...) custom-call(bf16[16,1024,512]{2,1,0:T(8,128)(2,1)} %get-tuple-element.93.g_ref, ...), custom_call_target="tpu_custom_call" | custom-call | tf_op jit(solution)/shard_map/pallas_call | solution.py:881
  972.3 2.6 broadcast_select_fusion
  975.6 2.6 bitcast_convert_fusion.2
  978.2 5.3 copy.81
  983.5 2.6 bitcast_convert_fusion.1
  987.4 18.6 %shard_map.259 = (f32[4,32,1024]{2,1,0:T(8,128)S(1)}, bf16[2,4,2,64,1024]{4,3,2,1,0:T(8,128)(2,1)S(1)}) custom-call(f32[32,1024]{1,0:T(8,128)S(1)} %reduce_sum.540.refs_0_, bf16[2,64,1024]{2,1,0:T(8,128)(2,1)S(1)} %fusion.8.refs_1_), custom_call_target="tpu_custom_call" | custom-call | tf_op jit(solution)/shard_map/pallas_call | solution.py:449
  1006.0 1.8 broadcast_select_fusion.1
  1008.7 1.9 fusion.4
  1010.6 1.1 bitcast_convert_fusion.3
  1011.7 18.8 %bitcast_convert_fusion = f32[8192,1024]{1,0:T(8,128)} fusion(bf16[16,512,1024]{2,1,0:T(8,128)(2,1)} %get-tuple-element.136), kind=kLoop, calls=%fused_computation.1 | loop fusion | flops 8388608 | bytes 50331648 | tf_op jit(solution)/shard_map/convert_element_type | solution.py:2150
  (237 shorter events, 54.0 us)
Async XLA Ops:
  0.6 3.6 copy-start
  8.6 1.0 copy-start.36
  8.6 1.2 copy-start.26
  8.6 1.2 copy-start.27
  8.6 1.2 copy-start.28
  8.6 1.2 copy-start.29
  8.7 1.2 copy-start.30
  8.7 1.2 copy-start.24
  8.7 1.2 copy-start.25
  8.8 1.1 copy-start.8
  81.3 4.4 copy-start.35
  286.9 48.9 %copy-start.2 = (f32[256,1024]{1,0:T(8,128)}, f32[256,1024]{1,0:T(8,128)S(1)}, u32[]{:S(2)}) copy-start(f32[256,1024]{1,0:T(8,128)S(1)} %get-tuple-element.189) | copy-start | bytes 3145732
  337.3 1.0 copy-start.4
  410.9 66.6 %copy-start.5 = (f32[256,1024]{1,0:T(8,128)S(1)}, f32[256,1024]{1,0:T(8,128)}, u32[]{:S(2)}) copy-start(f32[256,1024]{1,0:T(8,128)} %copy-done.4) | copy-start | bytes 3145732
  477.5 1.7 copy-start.13
  533.6 3.5 copy-start.15
  538.2 2.1 copy-start.6
  538.2 2.1 copy-start.3
  538.2 3.0 copy-start.12
  607.6 2.2 copy-start.18
  610.4 2.4 copy-start.9
  610.4 2.0 copy-start.10
  663.0 3.5 copy-start.14
  667.6 2.0 copy-start.7
  667.6 2.0 copy-start.11
  738.6 2.2 copy-start.17
  741.3 1.8 copy-start.20
  744.4 2.4 copy-start.19
  746.8 2.4 copy-start.22
  747.1 4.0 copy-start.16
  752.4 1.5 copy-start.34
  752.4 1.9 copy-start.32
  752.4 2.0 copy-start.33
  752.5 2.4 copy-start.31
  983.5 2.6 copy-start.23
  986.1 1.2 copy-start.21
  1011.7 22.5 %copy-start.1 = (bf16[1,1024,1024]{2,1,0:T(8,128)(2,1)S(1)}, bf16[1,1024,1024]{2,1,0:T(8,128)(2,1)}, u32[]{:S(2)}) copy-start(bf16[1,1024,1024]{2,1,0:T(8,128)(2,1)} %param.26) | copy-start | bytes 6291460
